TPU v7x, 512 devices: a whole 4x8x8 slice. The times are simulated.
512 devices in a mesh: batch: 16 (over y_hi, x, core), ctx: 32 (over y_lo, z).
Axes of the slice: x: 4, y: 8 (y_hi: 2, y_lo: 4; y = y_hi * 4 + y_lo), z: 8, core: 2. Of those that a mesh axis runs over, the one named last changes fastest.
Arguments:
- hist_query: bfloat16 [131072, 512], P(('batch', 'ctx')), may hold values from -6 to 6
- hist_key: bfloat16 [131072, 512], P(('batch', 'ctx')), may hold values from -6 to 6
- hist_value: bfloat16 [131072, 512], P(('batch', 'ctx')), may hold values from -6 to 6
- hist_gate: bfloat16 [131072, 512], P(('batch', 'ctx')), may hold values from -6 to 6
- hist_input: bfloat16 [131072, 1024], P(('batch', 'ctx')), may hold values from -6 to 6
- cand_query: bfloat16 [16384, 512], P(('batch', 'ctx')), may hold values from -6 to 6
- cand_key: bfloat16 [16384, 512], P(('batch', 'ctx')), may hold values from -6 to 6
- cand_value: bfloat16 [16384, 512], P(('batch', 'ctx')), may hold values from -6 to 6
- cand_gate: bfloat16 [16384, 512], P(('batch', 'ctx')), may hold values from -6 to 6
- cand_input: bfloat16 [16384, 1024], P(('batch', 'ctx')), may hold values from -6 to 6
- cand_user: int32 [16384], P('batch'), may hold values from 0 to 1
- hist_len: int32 [32], P('batch'), may hold values from 1 to 8064, as said below
- hist_start: int32 [32], P('batch'), may hold values from 0 to 8064, as said below
- out_weight: bfloat16 [512, 1024], replicated, may hold values from -0.25 to 0.25
Outputs:
- hist_out: bfloat16 [131072, 1024], P(('batch', 'ctx'))
- cand_out: bfloat16 [16384, 1024], P(('batch', 'ctx'))
Inputs may be any that keep to these rules, and one draw needn't show every extreme that they name: `hist_len`: in each group the users take whole consecutive blocks of 128 slots: the first user starts at slot 0, the next at the block after the first user's last block; a user with b blocks has a length above (b - 1) * 128; slots after the last user's history are padding, and some groups use every block. `hist_start`: multiples of 128; the first user of every group starts at 0. `cand_user`: index of a user of the candidate's own group.
All inputs are finite; a program needn't handle non-finite values.
Results may differ from a plain program's by a relative error of at most 0.006.
Values may be sent and summed in bfloat16 or wider, within the bound.
No kernel may reach another device: no remote copies, remote signals or barrier semaphores. Data moves between devices by JAX's collectives and lax.ppermute only.
A program may use at most 128 MiB of HBM per device.

v0:
```python
import math

import jax
import jax.numpy as jnp
from jax import lax
from jax.sharding import PartitionSpec as P

HEADS = 4
DH = 128


def owners(events, lens, starts):
    result = jnp.full(events.shape, -1, jnp.int32)
    for user in range(lens.shape[0]):
        inside = (events >= starts[user]) & (events < starts[user] + lens[user])
        result = jnp.where(inside, jnp.int32(user), result)
    return result


def pointwise(queries, keys, values, mask):
    rows = queries.shape[0]
    width = queries.shape[1]
    q_heads = queries.reshape(rows, HEADS, DH)
    k_heads = keys.reshape(keys.shape[0], HEADS, DH)
    v_heads = values.reshape(values.shape[0], HEADS, DH)
    scores = jnp.einsum("qhd,khd->hqk", q_heads, k_heads, preferred_element_type=jnp.float32) * (
        1.0 / math.sqrt(DH)
    )
    weights = jnp.where(mask[None], jax.nn.silu(scores), 0.0).astype(jnp.bfloat16)
    out = jnp.einsum("hqk,khd->qhd", weights, v_heads, preferred_element_type=jnp.float32)
    return out.reshape(rows, width)


def self_term(queries, keys, values):
    rows = queries.shape[0]
    q_heads = queries.reshape(rows, HEADS, DH).astype(jnp.float32)
    k_heads = keys.reshape(rows, HEADS, DH).astype(jnp.float32)
    v_heads = values.reshape(rows, HEADS, DH).astype(jnp.float32)
    scores = jnp.sum(q_heads * k_heads, axis=-1) * (1.0 / math.sqrt(DH))
    weights = jax.nn.silu(scores).astype(jnp.bfloat16).astype(jnp.float32)
    return (weights[:, :, None] * v_heads).reshape(rows, HEADS * DH)


def finish(total, gate, inputs, out_weight):
    mean = jnp.mean(total, axis=-1, keepdims=True)
    centered = total - mean
    spread = jnp.mean(centered * centered, axis=-1, keepdims=True)
    normed = centered * lax.rsqrt(spread + 1e-05)
    gated = (normed * gate.astype(jnp.float32)).astype(jnp.bfloat16)
    mixed = jnp.dot(gated, out_weight, preferred_element_type=jnp.float32)
    return (inputs.astype(jnp.float32) + mixed).astype(jnp.bfloat16)


def on_device(
    hist_query,
    hist_key,
    hist_value,
    hist_gate,
    hist_input,
    cand_query,
    cand_key,
    cand_value,
    cand_gate,
    cand_input,
    cand_user,
    hist_len,
    hist_start,
    out_weight,
):
    block_rows = hist_query.shape[0]
    cand_rows = cand_query.shape[0]
    place = lax.axis_index("ctx")
    events = place * block_rows + jnp.arange(block_rows, dtype=jnp.int32)
    owner = owners(events, hist_len, hist_start)
    mine = lax.dynamic_slice_in_dim(cand_user, place * cand_rows, cand_rows)
    piece = (
        lax.all_gather(hist_key, "ctx", axis=0, tiled=True),
        lax.all_gather(hist_value, "ctx", axis=0, tiled=True),
    )
    keys, values = piece
    key_events = jnp.arange(keys.shape[0], dtype=jnp.int32)
    key_owner = owners(key_events, hist_len, hist_start)
    mask = (
        (owner[:, None] == key_owner[None, :])
        & (owner[:, None] >= 0)
        & (key_events[None, :] <= events[:, None])
    )
    hist_term, key_owner = (pointwise(hist_query, keys, values, mask), key_owner)
    cand_mask = mine[:, None] == key_owner[None, :]
    cand_total = pointwise(cand_query, piece[0], piece[1], cand_mask)
    cand_total = cand_total + self_term(cand_query, cand_key, cand_value)
    return (
        finish(hist_term, hist_gate, hist_input, out_weight),
        finish(cand_total, cand_gate, cand_input, out_weight),
    )


def solution(mesh):
    return jax.shard_map(
        on_device,
        mesh=mesh,
        in_specs=(
            P(("batch", "ctx"), None),
            P(("batch", "ctx"), None),
            P(("batch", "ctx"), None),
            P(("batch", "ctx"), None),
            P(("batch", "ctx"), None),
            P(("batch", "ctx"), None),
            P(("batch", "ctx"), None),
            P(("batch", "ctx"), None),
            P(("batch", "ctx"), None),
            P(("batch", "ctx"), None),
            P("batch"),
            P("batch"),
            P("batch"),
            P(),
        ),
        out_specs=(P(("batch", "ctx"), None), P(("batch", "ctx"), None)),
        check_vma=False,
    )
```

profile of v0, /device:TPU:56, one launch (start us, length us, event | category | flops | bytes accessed | tf_op | source)
XLA Modules:
  0.0 397.4 jit_solution(4261656535237916895)
XLA Ops:
  7.2 0.7 all-gather.5.cloned.1.call-update
  8.0 1.8 copy.40
  9.8 0.8 reshape.194
  10.6 0.8 reshape.192
  11.3 0.1 multiply_reduce_fusion.1
  11.5 0.1 copy.50
  11.6 1.3 fusion.34
  13.0 1.3 fusion.33
  16.9 0.8 dynamic_slice.3
  17.6 1.3 broadcast_compare_fusion.1
  18.9 1.3 select_select_fusion
  20.2 0.2 broadcast_compare_fusion
  20.4 2.5 fusion
  22.9 153.6 %all-gather.5.cloned.1.call-done = bf16[8192,512]{1,0:T(8,128)(2,1)} async-done(((bf16[256,512]{1,0:T(8,128)(2,1)}), bf16[8192,512]{1,0:T(8,128)(2,1)}) %all-gather.5.cloned.1.call-update) | async-done | bytes 8388624 | tf_op jit(solution)/shard_map/all_gather | solution.py:78
  176.5 12.0 %copy.43 = bf16[8192,512]{0,1:T(8,128)(2,1)} copy(bf16[8192,512]{1,0:T(8,128)(2,1)} %all-gather.5.cloned.1.call-done) | data formatting | bytes 16777216 | tf_op jit(solution)/shard_map/all_gather | solution.py:78
  188.5 167.8 %all-gather.3.cloned.1.call-done = bf16[8192,512]{0,1:T(8,128)(2,1)} async-done(((bf16[256,512]{0,1:T(8,128)(2,1)}), bf16[8192,512]{0,1:T(8,128)(2,1)}) %all-gather.3.cloned.1.call-update) | async-done | bytes 8388624 | tf_op jit(solution)/shard_map/all_gather | solution.py:77
  356.3 20.5 %fusion.35 = (f32[256]{0:T(256)S(1)}, f32[4,256,128]{1,2,0:T(8,128)}) fusion(bf16[8192,4,128]{0,2,1:T(8,128)(2,1)} %bitcast.52, bf16[8192,4,128]{0,2,1:T(8,128)(2,1)} %bitcast.56, pred[256,8192]{1,0:T(8,128)(4,1)S(1)} %fusion, bf16[256,512]{1,0:T(8,128)(2,1)} %param.14), kind=kOutput, calls=%fused_computation.57 | convolution fusion | flops 4353818624 | bytes 19661824 | tf_op jit(solution)/shard_map/hqk,khd->qhd/dot_general | solution.py:30
  376.8 1.2 copy.44
  378.1 1.1 fusion.7
  379.3 8.4 %fusion.5 = f32[4,4,8,128]{3,2,1,0:T(8,128)S(1)} fusion(bf16[8192,4,128]{0,2,1:T(8,128)(2,1)} %bitcast.53, bf16[8192,4,128]{0,2,1:T(8,128)(2,1)} %bitcast.57, pred[32,8192]{1,0:T(8,128)(4,1)S(1)} %broadcast_compare_fusion, bf16[32,512]{1,0:T(8,128)(2,1)S(1)} %copy-done.6), kind=kOutput, calls=%fused_computation.11 | convolution fusion | flops 544210944 | bytes 17137664 | tf_op jit(solution)/shard_map/hqk,khd->qhd/dot_general | solution.py:30
  387.9 0.1 fusion.31
  388.0 0.2 multiply_reduce_fusion
  388.2 1.0 fusion.4
  389.2 1.3 fusion.2
  (25 shorter events, 0.3 us)
Async XLA Ops:
  7.2 381.0 %copy-start = (bf16[512,1024]{1,0:T(8,128)(2,1)S(1)}, bf16[512,1024]{1,0:T(8,128)(2,1)}, u32[]{:S(2)}) copy-start(bf16[512,1024]{1,0:T(8,128)(2,1)} %param.27) | copy-start | bytes 3145732
  7.2 169.3 %all-gather.5.cloned.1.call-start = ((), (), s32[]{:S(2)}) async-start(), calls=%async_computation.1 | async-start | bytes 8650752 | tf_op jit(solution)/shard_map/all_gather | solution.py:78
  7.9 348.4 %all-gather.3.cloned.1.call-start = ((), (), s32[]{:S(2)}) async-start(), calls=%async_computation | async-start | bytes 8650752 | tf_op jit(solution)/shard_map/all_gather | solution.py:77
  356.3 22.9 %copy-start.6 = (bf16[32,512]{1,0:T(8,128)(2,1)S(1)}, bf16[32,512]{1,0:T(8,128)(2,1)}, u32[]{:S(2)}) copy-start(bf16[32,512]{1,0:T(8,128)(2,1)} %param.19) | copy-start | bytes 98308
  379.3 8.6 %copy-start.4 = (bf16[32,512]{1,0:T(8,128)(2,1)S(1)}, bf16[32,512]{1,0:T(8,128)(2,1)}, u32[]{:S(2)}) copy-start(bf16[32,512]{1,0:T(8,128)(2,1)} %param.21) | copy-start | bytes 98308
  379.3 8.9 %copy-start.3 = (bf16[32,1024]{1,0:T(8,128)(2,1)S(1)}, bf16[32,1024]{1,0:T(8,128)(2,1)}, u32[]{:S(2)}) copy-start(bf16[32,1024]{1,0:T(8,128)(2,1)} %param.23) | copy-start | bytes 196612
  379.3 8.9 %copy-start.5 = (bf16[32,512]{1,0:T(8,128)(2,1)S(1)}, bf16[32,512]{1,0:T(8,128)(2,1)}, u32[]{:S(2)}) copy-start(bf16[32,512]{1,0:T(8,128)(2,1)} %param.22) | copy-start | bytes 98308
  379.3 9.9 %copy-start.1 = (bf16[256,1024]{1,0:T(8,128)(2,1)S(1)}, bf16[256,1024]{1,0:T(8,128)(2,1)}, u32[]{:S(2)}) copy-start(bf16[256,1024]{1,0:T(8,128)(2,1)} %param.18) | copy-start | bytes 1572868
  379.3 9.9 %copy-start.2 = (bf16[256,512]{1,0:T(8,128)(2,1)S(1)}, bf16[256,512]{1,0:T(8,128)(2,1)}, u32[]{:S(2)}) copy-start(bf16[256,512]{1,0:T(8,128)(2,1)} %param.17) | copy-start | bytes 786436
Sparse Core Ops, SparseCore 0:
  10.1 166.3 all-gather.4
  179.1 177.2 all-gather.2
where the time goes:
time: 399 us; the launch traced here: 397 us
  waiting for transfers between devices  322 us (81%)
  matrix products  31.2 us (8%)
  local copies, waits for them, and re-layouts  20.3 us (5%)
  between operations  16.8 us (4%)
  other arithmetic  6.82 us (2%)
    all_gather x1, waiting for transfers between devices, on_device(): lax.all_gather(hist_key, 'ctx', axis=0, tiled=True)  168 us
    all_gather x1, waiting for transfers between devices, on_device(): lax.all_gather(hist_value, 'ctx', axis=0, tiled=True)  154 us
    dot_general x2, matrix products, pointwise(): jnp.einsum('hqk,khd->qhd', weights, v_heads, preferred_element_type=jnp.f...  29 us
    all_gather x1, local copies, waits for them, and re-layouts, on_device(): lax.all_gather(hist_value, 'ctx', axis=0, tiled=True)  12 us
  transfers between devices with their start and end apart: 2, of which 2 were waited for; matrix products, arithmetic and copies ran while one was open for 6% of the time, Pallas kernels for 0%

commit v1 on v0

v1 whole, which is shorter than its diff:
```python
import functools
import math

import jax
import jax.numpy as jnp
from jax import lax
from jax.experimental import pallas as pl
from jax.experimental.pallas import tpu as pltpu
from jax.sharding import Mesh, PartitionSpec as P

HEADS = 4
DH = 128
NY = 4
NZ = 8
ROWS = 256
CROWS = 32
QROWS = ROWS + CROWS
STRIP = NZ * ROWS
HALF = 1.0 / (2.0 * math.sqrt(DH))
VMEM_LIMIT = 48 * 1024 * 1024


def contract_lanes(a, b):
    return lax.dot_general(a, b, (((1,), (1,)), ((), ())), preferred_element_type=jnp.float32)


def silu_weight(scores):
    half = scores * HALF
    return half * jnp.tanh(half) + half


def attend_kernel(heads, place_ref, start_ref, len_ref, q0, q1, q2, q3, kv_ref, cu_ref, own_ref, o1, o2, o3, acc, cq, cacc):
    width = heads * DH
    y = place_ref[0]
    z = place_ref[1]
    starts = [start_ref[u] for u in range(2)]
    ends = [start_ref[u] + len_ref[u] for u in range(2)]
    strip0 = y * STRIP
    qs = (q0, q1, q2, q3)

    def cols(h):
        return slice(h * DH, (h + 1) * DH)

    def vcols(h):
        return slice(width + h * DH, width + (h + 1) * DH)

    def plain(slot, first, keys):
        out = []
        for h in range(heads):
            k = kv_ref[pl.ds(first, keys), cols(h)]
            w = silu_weight(contract_lanes(qs[slot][0:ROWS, cols(h)], k)).astype(jnp.bfloat16)
            v = kv_ref[pl.ds(first, keys), vcols(h)]
            out.append(jnp.dot(w, v, preferred_element_type=jnp.float32))
        for h in range(heads):
            acc[:, cols(h)] += out[h]

    for slot in range(NY):
        q_first = ((y + slot) * NZ + z) * ROWS
        acc[...] = jnp.zeros_like(acc)

        def general(slot=slot, q_first=q_first):
            def step(b, carry):
                k_first = strip0 + b * ROWS
                full = jnp.bool_(False)
                some = jnp.bool_(False)
                for s, t in zip(starts, ends):
                    full = full | ((s <= k_first) & (t >= q_first + ROWS))
                    some = some | ((s < k_first + ROWS) & (t > k_first) & (s < q_first + ROWS) & (t > q_first))
                full = full & (k_first < q_first)
                some = some & (k_first <= q_first) & jnp.logical_not(full)

                @pl.when(full)
                def _():
                    plain(slot, pl.multiple_of(b * ROWS, ROWS), ROWS)

                @pl.when(some)
                def _():
                    first = pl.multiple_of(b * ROWS, ROWS)
                    row = q_first + lax.broadcasted_iota(jnp.int32, (ROWS, ROWS), 0)
                    col = k_first + lax.broadcasted_iota(jnp.int32, (ROWS, ROWS), 1)
                    mask = jnp.zeros((ROWS, ROWS), jnp.bool_)
                    for s, t in zip(starts, ends):
                        mask = mask | ((row >= s) & (row < t) & (col >= s))
                    mask = mask & (col <= row)
                    for h in range(heads):
                        k = kv_ref[pl.ds(first, ROWS), cols(h)]
                        w = silu_weight(contract_lanes(qs[slot][0:ROWS, cols(h)], k))
                        w = jnp.where(mask, w, 0.0).astype(jnp.bfloat16)
                        v = kv_ref[pl.ds(first, ROWS), vcols(h)]
                        acc[:, cols(h)] += jnp.dot(w, v, preferred_element_type=jnp.float32)

                return carry

            lax.fori_loop(0, NZ, step, 0)

        if slot == 0:
            general()
            own_ref[0:ROWS, :] = acc[...]
        else:
            valid = y + slot < NY
            whole = jnp.bool_(False)
            for s, t in zip(starts, ends):
                whole = whole | ((s <= strip0) & (t >= q_first + ROWS))

            @pl.when(valid & whole)
            def _(slot=slot):
                def step(b, carry):
                    plain(slot, pl.multiple_of(b * 2 * ROWS, 2 * ROWS), 2 * ROWS)
                    return carry

                lax.fori_loop(0, NZ // 2, step, 0)

            @pl.when(valid & jnp.logical_not(whole))
            def _(general=general):
                general()

            (o1, o2, o3)[slot - 1][0:ROWS, :] = acc[...].astype(jnp.bfloat16)

    lows, highs = [], []
    for slot in range(NY):
        cq[slot * CROWS : (slot + 1) * CROWS, :] = qs[slot][ROWS:QROWS, :]
        first = pl.multiple_of((lax.rem(y + slot, NY) * NZ + z) * CROWS, CROWS)
        user = cu_ref[pl.ds(first, CROWS), :]
        lows.append(jnp.where(user == 0, starts[0], starts[1]))
        highs.append(jnp.where(user == 0, ends[0], ends[1]))
    low = jnp.concatenate(lows, 0)
    high = jnp.concatenate(highs, 0)
    cacc[...] = jnp.zeros_like(cacc)

    def cstep(b, carry):
        first = pl.multiple_of(b * ROWS, ROWS)
        col = strip0 + first + lax.broadcasted_iota(jnp.int32, (NY * CROWS, ROWS), 1)
        mask = (col >= low) & (col < high)
        for h in range(heads):
            k = kv_ref[pl.ds(first, ROWS), cols(h)]
            w = silu_weight(contract_lanes(cq[:, cols(h)], k))
            w = jnp.where(mask, w, 0.0).astype(jnp.bfloat16)
            v = kv_ref[pl.ds(first, ROWS), vcols(h)]
            cacc[:, cols(h)] += jnp.dot(w, v, preferred_element_type=jnp.float32)
        return carry

    lax.fori_loop(0, NZ, cstep, 0)
    own_ref[ROWS:QROWS, :] = cacc[0:CROWS, :]
    for slot in range(1, NY):
        (o1, o2, o3)[slot - 1][ROWS:QROWS, :] = cacc[slot * CROWS : (slot + 1) * CROWS, :].astype(jnp.bfloat16)


def attend(heads, head_block, place, starts, lens, queries, kv, users):
    width = heads * DH
    smem = pl.BlockSpec(memory_space=pltpu.SMEM)
    vmem = pl.BlockSpec(memory_space=pltpu.VMEM)
    q_spec = pl.BlockSpec((QROWS, width), lambda i: (0, head_block))
    whole = lambda shape: pl.BlockSpec(shape, lambda i: (0, 0))
    return pl.pallas_call(
        functools.partial(attend_kernel, heads),
        grid=(1,),
        in_specs=[smem, smem, smem, q_spec, q_spec, q_spec, q_spec, vmem, vmem],
        out_specs=[whole((QROWS, width))] * 4,
        out_shape=[jax.ShapeDtypeStruct((QROWS, width), jnp.float32)]
        + [jax.ShapeDtypeStruct((QROWS, width), jnp.bfloat16)] * 3,
        scratch_shapes=[
            pltpu.VMEM((ROWS, width), jnp.float32),
            pltpu.VMEM((NY * CROWS, width), jnp.bfloat16),
            pltpu.VMEM((NY * CROWS, width), jnp.float32),
        ],
        compiler_params=pltpu.CompilerParams(vmem_limit_bytes=VMEM_LIMIT),
        cost_estimate=pl.CostEstimate(flops=heads * 2 * 2 * QROWS * 4 * STRIP * DH, bytes_accessed=4 << 20, transcendentals=0),
        name="attend",
    )(place, starts, lens, *queries, kv, users)


def finish_kernel(parts, *refs):
    n = parts * 4
    totals = refs[:n]
    hg, hx, cq, ck, cv, cg, cx, w_ref, ho, co = refs[n:]
    sums = []
    for p in range(parts):
        total = totals[4 * p][...]
        for i in range(1, 4):
            total = total + totals[4 * p + i][...].astype(jnp.float32)
        sums.append(total)
    total = sums[0] if parts == 1 else jnp.concatenate(sums, axis=1)
    own = []
    for h in range(HEADS):
        at = slice(h * DH, (h + 1) * DH)
        scores = jnp.sum(cq[:, at].astype(jnp.float32) * ck[:, at].astype(jnp.float32), axis=-1, keepdims=True)
        weight = silu_weight(scores).astype(jnp.bfloat16).astype(jnp.float32)
        own.append(weight * cv[:, at].astype(jnp.float32))

    def tail(rows, gate, inputs, out):
        mean = jnp.mean(rows, axis=-1, keepdims=True)
        centered = rows - mean
        spread = jnp.mean(centered * centered, axis=-1, keepdims=True)
        normed = centered * lax.rsqrt(spread + 1e-05)
        gated = (normed * gate[...].astype(jnp.float32)).astype(jnp.bfloat16)
        mixed = jnp.dot(gated, w_ref[...], preferred_element_type=jnp.float32)
        out[...] = (inputs[...].astype(jnp.float32) + mixed).astype(jnp.bfloat16)

    tail(total[0:ROWS], hg, hx, ho)
    tail(total[ROWS:QROWS] + jnp.concatenate(own, axis=1), cg, cx, co)


def finish(totals, parts, hg, hx, cq, ck, cv, cg, cx, w):
    vmem = pl.BlockSpec(memory_space=pltpu.VMEM)
    return pl.pallas_call(
        functools.partial(finish_kernel, parts),
        in_specs=[vmem] * (len(totals) + 8),
        out_specs=[vmem] * 2,
        out_shape=[jax.ShapeDtypeStruct(hx.shape, jnp.bfloat16), jax.ShapeDtypeStruct(cx.shape, jnp.bfloat16)],
        compiler_params=pltpu.CompilerParams(vmem_limit_bytes=VMEM_LIMIT),
        name="finish",
    )(*totals, hg, hx, cq, ck, cv, cg, cx, w)


def turn(array, axis, count, step):
    return lax.ppermute(array, axis, [(i, (i + step) % count) for i in range(count)])


def on_device(
    hist_query, hist_key, hist_value, hist_gate, hist_input,
    cand_query, cand_key, cand_value, cand_gate, cand_input,
    cand_user, hist_len, hist_start, out_weight,
):
    place = jnp.stack([lax.axis_index("y"), lax.axis_index("z")]).astype(jnp.int32)
    users = cand_user.reshape(-1, 1)
    kv = lax.all_gather(jnp.concatenate([hist_key, hist_value], axis=1), "z", axis=0, tiled=True)
    mine = jnp.concatenate([hist_query, cand_query], axis=0)
    queries = [mine] + [turn(mine, "y", NY, -k) for k in (1, 2, 3)]
    own, *away = attend(HEADS, 0, place, hist_start, hist_len, queries, kv, users)
    back = [turn(a, "y", NY, k) for k, a in zip((1, 2, 3), away)]
    return finish(
        [own] + back, 1, hist_gate, hist_input, cand_query, cand_key, cand_value, cand_gate, cand_input, out_weight
    )


def solution(mesh):
    grid = Mesh(mesh.devices.reshape(-1, NY, NZ), ("batch", "y", "z"))
    rows = P(("batch", "y", "z"), None)
    return jax.shard_map(
        on_device,
        mesh=grid,
        in_specs=(rows,) * 10 + (P("batch"), P("batch"), P("batch"), P()),
        out_specs=(rows, rows),
        check_vma=False,
    )
```

time: 399 us -> 131 us (0.33)
  waiting for transfers between devices: 322 us -> 71.2 us
  matrix products: 31.2 us -> 0 us
  starting transfers between devices: 0.08 us -> 28.8 us
  local copies, waits for them, and re-layouts: 20.3 us -> 3.99 us
  Pallas kernels: 0 us -> 9.4 us
  other arithmetic: 6.82 us -> 1.95 us
    all_gather x2 -> x1, waiting for transfers between devices: 321 us -> 31.7 us  [on_device(): lax.all_gather(jnp.concatenate([hist_key, hist_value], axis=1), 'z', axis...]
    ppermute x0 -> x6, waiting for transfers between devices: none -> 39.5 us  [turn(): lax.ppermute(array, axis, [(i, (i + step) % count) for i in range(count)])]
    dot_general x4 -> x0, matrix products: 31.2 us -> none  [the longest x2 29 us: pointwise(): jnp.einsum('hqk,khd->qhd', weights, v_heads, preferred_element_type=jnp.f...]
    ppermute x0 -> x6, starting transfers between devices: none -> 28.7 us  [turn(): lax.ppermute(array, axis, [(i, (i + step) % count) for i in range(count)])]
    all_gather x1 -> x0, local copies, waits for them, and re-layouts: 12 us -> none  [on_device(): lax.all_gather(hist_value, 'ctx', axis=0, tiled=True)]
    pallas_call x0 -> x2, Pallas kernels: none -> 9.4 us  [the longest x1 7.9 us: attend(): pl.pallas_call(functools.partial(attend_kernel, heads), grid=(1,), in_spe...]
  transfers between devices with their start and end apart: 2 -> 7, of which waited for: 2 -> 4; matrix products, arithmetic and copies ran while one was open for 6% -> 2% of each run, Pallas kernels for 0% -> 0%
where the time goes in v1:
time: 131 us; the launch traced here: 130 us
  waiting for transfers between devices  71.2 us (54%)
  starting transfers between devices  28.8 us (22%)
  between operations  14.2 us (11%)
  Pallas kernels  9.4 us (7%)
  local copies, waits for them, and re-layouts  3.99 us (3%)
  other arithmetic  1.95 us (1%)
    ppermute x6, waiting for transfers between devices, turn(): lax.ppermute(array, axis, [(i, (i + step) % count) for i in range(count)])  39.5 us
    all_gather x1, waiting for transfers between devices, on_device(): lax.all_gather(jnp.concatenate([hist_key, hist_value], axis=1), 'z', axis...  31.7 us
    ppermute x6, starting transfers between devices, turn(): lax.ppermute(array, axis, [(i, (i + step) % count) for i in range(count)])  28.7 us
    pallas_call x1, Pallas kernels, attend(): pl.pallas_call(functools.partial(attend_kernel, heads), grid=(1,), in_spe...  7.9 us
  transfers between devices with their start and end apart: 7, of which 4 were waited for; matrix products, arithmetic and copies ran while one was open for 2% of the time, Pallas kernels for 0%

profile of v1, /device:TPU:56, one launch (start us, length us, event | category | flops | bytes accessed | tf_op | source)
XLA Modules:
  0.0 129.6 jit_solution(1192636173875094979)
XLA Ops:
  7.2 0.0 all-gather.2.cloned.1.call-start
  7.2 1.9 %pad_maximum_fusion = bf16[256,1024]{1,0:T(8,128)(2,1)} fusion(bf16[256,512]{1,0:T(8,128)(2,1)} %param.16, bf16[256,512]{1,0:T(8,128)(2,1)} %param.15), kind=kLoop, calls=%fused_computation | loop fusion | flops 1048576 | bytes 1048576 | tf_op jit(solution)/shard_map/concatenate | solution.py:226
  9.1 0.0 all-gather.2.cloned.1.call-update
  9.1 1.0 constant_dynamic-update-slice_fusion.1
  10.1 0.8 constant_dynamic-update-slice_fusion.q0
  10.8 4.8 %collective-permute-start.2 = (bf16[288,512]{1,0:T(8,128)(2,1)S(1)}, bf16[288,512]{1,0:T(8,128)(2,1)S(1)}, u32[]{:S(2)}, u32[]{:S(2)}) collective-permute-start(bf16[288,512]{1,0:T(8,128)(2,1)S(1)} %constant_dynamic-update-slice_fusion.q0), channel_id=1, source_target_pairs={{0,8},{8,16},{16,24},{24,0},{1,9},{9,17},{17,25},{25,1},{2,10},{10... | collective-permute-start | bytes 884744 | tf_op jit(solution)/shard_map/ppermute | solution.py:216
  15.7 1.9 %collective-permute-start.1 = (bf16[288,512]{1,0:T(8,128)(2,1)S(1)}, bf16[288,512]{1,0:T(8,128)(2,1)S(1)}, u32[]{:S(2)}, u32[]{:S(2)}) collective-permute-start(bf16[288,512]{1,0:T(8,128)(2,1)S(1)} %constant_dynamic-update-slice_fusion.q0), channel_id=1, source_target_pairs={{0,16},{8,24},{16,0},{24,8},{1,17},{9,25},{17,1},{25,9},{2,18},{10... | collective-permute-start | bytes 884744 | tf_op jit(solution)/shard_map/ppermute | solution.py:216
  17.6 3.1 %collective-permute-start = (bf16[288,512]{1,0:T(8,128)(2,1)S(1)}, bf16[288,512]{1,0:T(8,128)(2,1)}, u32[]{:S(2)}, u32[]{:S(2)}) collective-permute-start(bf16[288,512]{1,0:T(8,128)(2,1)S(1)} %constant_dynamic-update-slice_fusion.q0), channel_id=1, source_target_pairs={{0,24},{8,0},{16,8},{24,16},{1,25},{9,1},{17,9},{25,17},{2,26},{10... | collective-permute-start | bytes 884744 | tf_op jit(solution)/shard_map/ppermute | solution.py:216
  20.7 0.9 copy.16.cu_ref
  21.7 0.1 pad_add_fusion.place_ref
  21.8 0.0 copy-start.4
  21.8 0.0 copy-start.5
  21.8 0.0 copy-start.7
  21.8 1.3 %collective-permute-done.2.q3 = bf16[288,512]{1,0:T(8,128)(2,1)S(1)} collective-permute-done((bf16[288,512]{1,0:T(8,128)(2,1)S(1)}, bf16[288,512]{1,0:T(8,128)(2,1)S(1)}, u32[]{:S(2)}, u32[]{:S(2)}) %collective-permute-start.2) | collective-permute-done | bytes 294944 | tf_op jit(solution)/shard_map/ppermute | solution.py:216
  23.1 18.1 %collective-permute-done.1.q2 = bf16[288,512]{1,0:T(8,128)(2,1)S(1)} collective-permute-done((bf16[288,512]{1,0:T(8,128)(2,1)S(1)}, bf16[288,512]{1,0:T(8,128)(2,1)S(1)}, u32[]{:S(2)}, u32[]{:S(2)}) %collective-permute-start.1) | collective-permute-done | bytes 294944 | tf_op jit(solution)/shard_map/ppermute | solution.py:216
  41.2 31.7 %all-gather.2.cloned.1.call-done.kv_ref = bf16[2048,1024]{1,0:T(8,128)(2,1)} async-done(((bf16[256,1024]{1,0:T(8,128)(2,1)}), bf16[2048,1024]{1,0:T(8,128)(2,1)}) %all-gather.2.cloned.1.call-update) | async-done | bytes 4194320 | tf_op jit(solution)/shard_map/all_gather | solution.py:226
  73.0 0.7 copy-done.8
  73.6 0.7 copy-done.9
  74.3 7.9 %attend.1 = (f32[288,512]{1,0:T(8,128)S(1)}, bf16[288,512]{1,0:T(8,128)(2,1)S(1)}, bf16[288,512]{1,0:T(8,128)(2,1)S(1)}, bf16[288,512]{1,0:T(8,128)(2,1)S(1)}) custom-call(s32[2]{0:T(128)S(1)} %pad_add_fusion.place_ref, s32[2]{0:T(128)S(1)} %copy-done.8, s32[2]{0:T(128)S(1)} %copy-done.9, bf16[288,512]{1,0:T(8,128)(2,1)S(1)} %constant_dynamic-update-slice_fusion.q0, ...), custom_call_target="tpu_custom_call" | custom-call | flops 4831838208 | bytes 4194304 | tf_op jit(solution)/shard_map/attend/pallas_call | solution.py:154
  82.2 5.7 %collective-permute-start.3 = (bf16[288,512]{1,0:T(8,128)(2,1)S(1)}, bf16[288,512]{1,0:T(8,128)(2,1)S(1)}, u32[]{:S(2)}, u32[]{:S(2)}) collective-permute-start(bf16[288,512]{1,0:T(8,128)(2,1)S(1)} %get-tuple-element.7), channel_id=1, source_target_pairs={{0,8},{8,16},{16,24},{24,0},{1,9},{9,17},{17,25},{25,1},{2,10},{10... | collective-permute-start | bytes 884744 | tf_op jit(solution)/shard_map/ppermute | solution.py:216
  87.8 9.3 %collective-permute-start.4 = (bf16[288,512]{1,0:T(8,128)(2,1)S(1)}, bf16[288,512]{1,0:T(8,128)(2,1)S(1)}, u32[]{:S(2)}, u32[]{:S(2)}) collective-permute-start(bf16[288,512]{1,0:T(8,128)(2,1)S(1)} %get-tuple-element.8), channel_id=1, source_target_pairs={{0,16},{8,24},{16,0},{24,8},{1,17},{9,25},{17,1},{25,9},{2,18},{10... | collective-permute-start | bytes 884744 | tf_op jit(solution)/shard_map/ppermute | solution.py:216
  97.1 3.9 %collective-permute-start.5 = (bf16[288,512]{1,0:T(8,128)(2,1)S(1)}, bf16[288,512]{1,0:T(8,128)(2,1)S(1)}, u32[]{:S(2)}, u32[]{:S(2)}) collective-permute-start(bf16[288,512]{1,0:T(8,128)(2,1)S(1)} %get-tuple-element.9), channel_id=1, source_target_pairs={{0,24},{8,0},{16,8},{24,16},{1,25},{9,1},{17,9},{25,17},{2,26},{10... | collective-permute-start | bytes 884744 | tf_op jit(solution)/shard_map/ppermute | solution.py:216
  101.1 20.1 %collective-permute-done.4.refs_2_ = bf16[288,512]{1,0:T(8,128)(2,1)S(1)} collective-permute-done((bf16[288,512]{1,0:T(8,128)(2,1)S(1)}, bf16[288,512]{1,0:T(8,128)(2,1)S(1)}, u32[]{:S(2)}, u32[]{:S(2)}) %collective-permute-start.4) | collective-permute-done | bytes 294944 | tf_op jit(solution)/shard_map/ppermute | solution.py:216
  121.2 1.5 %finish.1 = (bf16[256,1024]{1,0:T(8,128)(2,1)}, bf16[32,1024]{1,0:T(8,128)(2,1)}) custom-call(f32[288,512]{1,0:T(8,128)S(1)} %get-tuple-element.6.refs_0_, bf16[288,512]{1,0:T(8,128)(2,1)S(1)} %collective-permute-done.3.refs_1_, bf16[288,512]{1,0:T(8,128)(2,1)S(1)} %collective-permute-done.4.refs_2_, bf16[288,512]{1,0:T(8,128)(2,1)S(1)} %collective-permute-done.5.refs_3_, ...), custom_call_target="tpu_custom_call" | custom-call | tf_op jit(solution)/shard_map/finish/pallas_call | solution.py:205
  (18 shorter events, 0.0 us)
Async XLA Ops:
  7.2 65.8 %all-gather.2.cloned.1.call-start = ((), (), s32[]{:S(2)}) async-start(), calls=%async_computation | async-start | bytes 4718592 | tf_op jit(solution)/shard_map/all_gather | solution.py:226
  10.8 12.3 %collective-permute-start.2 = (bf16[288,512]{1,0:T(8,128)(2,1)S(1)}, bf16[288,512]{1,0:T(8,128)(2,1)S(1)}, u32[]{:S(2)}, u32[]{:S(2)}) collective-permute-start(bf16[288,512]{1,0:T(8,128)(2,1)S(1)} %constant_dynamic-update-slice_fusion.q0), channel_id=1, source_target_pairs={{0,8},{8,16},{16,24},{24,0},{1,9},{9,17},{17,25},{25,1},{2,10},{10... | collective-permute-start | bytes 884744 | tf_op jit(solution)/shard_map/ppermute | solution.py:216
  15.7 25.6 %collective-permute-start.1 = (bf16[288,512]{1,0:T(8,128)(2,1)S(1)}, bf16[288,512]{1,0:T(8,128)(2,1)S(1)}, u32[]{:S(2)}, u32[]{:S(2)}) collective-permute-start(bf16[288,512]{1,0:T(8,128)(2,1)S(1)} %constant_dynamic-update-slice_fusion.q0), channel_id=1, source_target_pairs={{0,16},{8,24},{16,0},{24,8},{1,17},{9,25},{17,1},{25,9},{2,18},{10... | collective-permute-start | bytes 884744 | tf_op jit(solution)/shard_map/ppermute | solution.py:216
  17.6 23.6 %collective-permute-start = (bf16[288,512]{1,0:T(8,128)(2,1)S(1)}, bf16[288,512]{1,0:T(8,128)(2,1)}, u32[]{:S(2)}, u32[]{:S(2)}) collective-permute-start(bf16[288,512]{1,0:T(8,128)(2,1)S(1)} %constant_dynamic-update-slice_fusion.q0), channel_id=1, source_target_pairs={{0,24},{8,0},{16,8},{24,16},{1,25},{9,1},{17,9},{25,17},{2,26},{10... | collective-permute-start | bytes 884744 | tf_op jit(solution)/shard_map/ppermute | solution.py:216
  21.7 99.4 %copy-start = (bf16[512,1024]{1,0:T(8,128)(2,1)S(1)}, bf16[512,1024]{1,0:T(8,128)(2,1)}, u32[]{:S(2)}) copy-start(bf16[512,1024]{1,0:T(8,128)(2,1)} %refs_11_.1) | copy-start | bytes 3145732
  21.7 99.4 %copy-start.1 = (bf16[256,1024]{1,0:T(8,128)(2,1)S(1)}, bf16[256,1024]{1,0:T(8,128)(2,1)}, u32[]{:S(2)}) copy-start(bf16[256,1024]{1,0:T(8,128)(2,1)} %refs_5_.1) | copy-start | bytes 1572868
  21.7 99.4 %copy-start.2 = (bf16[256,512]{1,0:T(8,128)(2,1)S(1)}, bf16[256,512]{1,0:T(8,128)(2,1)}, u32[]{:S(2)}) copy-start(bf16[256,512]{1,0:T(8,128)(2,1)} %refs_4_.1) | copy-start | bytes 786436
  21.7 99.4 %copy-start.3 = (bf16[32,512]{1,0:T(8,128)(2,1)S(1)}, bf16[32,512]{1,0:T(8,128)(2,1)}, u32[]{:S(2)}) copy-start(bf16[32,512]{1,0:T(8,128)(2,1)} %refs_6_.1) | copy-start | bytes 98308
  21.8 99.4 %copy-start.4 = (bf16[32,1024]{1,0:T(8,128)(2,1)S(1)}, bf16[32,1024]{1,0:T(8,128)(2,1)}, u32[]{:S(2)}) copy-start(bf16[32,1024]{1,0:T(8,128)(2,1)} %refs_10_.1) | copy-start | bytes 196612
  21.8 99.4 %copy-start.5 = (bf16[32,512]{1,0:T(8,128)(2,1)S(1)}, bf16[32,512]{1,0:T(8,128)(2,1)}, u32[]{:S(2)}) copy-start(bf16[32,512]{1,0:T(8,128)(2,1)} %refs_7_.1) | copy-start | bytes 98308
  21.8 99.4 %copy-start.6 = (bf16[32,512]{1,0:T(8,128)(2,1)S(1)}, bf16[32,512]{1,0:T(8,128)(2,1)}, u32[]{:S(2)}) copy-start(bf16[32,512]{1,0:T(8,128)(2,1)} %refs_8_.1) | copy-start | bytes 98308
  21.8 99.4 %copy-start.7 = (bf16[32,512]{1,0:T(8,128)(2,1)S(1)}, bf16[32,512]{1,0:T(8,128)(2,1)}, u32[]{:S(2)}) copy-start(bf16[32,512]{1,0:T(8,128)(2,1)} %refs_9_.1) | copy-start | bytes 98308
  73.0 0.7 copy-start.8
  73.6 0.7 copy-start.9
  82.2 18.9 %collective-permute-start.3 = (bf16[288,512]{1,0:T(8,128)(2,1)S(1)}, bf16[288,512]{1,0:T(8,128)(2,1)S(1)}, u32[]{:S(2)}, u32[]{:S(2)}) collective-permute-start(bf16[288,512]{1,0:T(8,128)(2,1)S(1)} %get-tuple-element.7), channel_id=1, source_target_pairs={{0,8},{8,16},{16,24},{24,0},{1,9},{9,17},{17,25},{25,1},{2,10},{10... | collective-permute-start | bytes 884744 | tf_op jit(solution)/shard_map/ppermute | solution.py:216
  87.8 33.3 %collective-permute-start.4 = (bf16[288,512]{1,0:T(8,128)(2,1)S(1)}, bf16[288,512]{1,0:T(8,128)(2,1)S(1)}, u32[]{:S(2)}, u32[]{:S(2)}) collective-permute-start(bf16[288,512]{1,0:T(8,128)(2,1)S(1)} %get-tuple-element.8), channel_id=1, source_target_pairs={{0,16},{8,24},{16,0},{24,8},{1,17},{9,25},{17,1},{25,9},{2,18},{10... | collective-permute-start | bytes 884744 | tf_op jit(solution)/shard_map/ppermute | solution.py:216
  97.1 24.0 %collective-permute-start.5 = (bf16[288,512]{1,0:T(8,128)(2,1)S(1)}, bf16[288,512]{1,0:T(8,128)(2,1)S(1)}, u32[]{:S(2)}, u32[]{:S(2)}) collective-permute-start(bf16[288,512]{1,0:T(8,128)(2,1)S(1)} %get-tuple-element.9), channel_id=1, source_target_pairs={{0,24},{8,0},{16,8},{24,16},{1,25},{9,1},{17,9},{25,17},{2,26},{10... | collective-permute-start | bytes 884744 | tf_op jit(solution)/shard_map/ppermute | solution.py:216
Sparse Core Ops, SparseCore 0:
  10.7 62.2 all-gather.1

commit v2 on v1

v2 whole, which is shorter than its diff:
```python
import functools
import math

import jax
import jax.numpy as jnp
from jax import lax
from jax.experimental import pallas as pl
from jax.experimental.pallas import tpu as pltpu
from jax.sharding import Mesh, PartitionSpec as P

HEADS = 4
DH = 128
NY = 4
NZ = 8
ROWS = 256
CROWS = 32
QROWS = ROWS + CROWS
STRIP = NZ * ROWS
BLOCK = 128
HALF_HEADS = 2
WIDTH = HALF_HEADS * DH
CKEYS = 1024
HALF = 1.0 / (2.0 * math.sqrt(DH))
VMEM_LIMIT = 48 * 1024 * 1024


def contract_lanes(a, b):
    return lax.dot_general(a, b, (((1,), (1,)), ((), ())), preferred_element_type=jnp.float32)


def silu_weight(scores):
    half = scores * HALF
    return half * jnp.tanh(half) + half


def attend_kernel(pieces, place_ref, start_ref, len_ref, q0, q1, q2, q3, cu_ref, *refs):
    kv_refs = refs[:pieces]
    own_ref, o1, o2, o3, kv, qs, acc, cq, cacc = refs[pieces:]
    y = place_ref[0]
    z = place_ref[1]
    starts = [start_ref[u] for u in range(2)]
    ends = [start_ref[u] + len_ref[u] for u in range(2)]
    strip0 = y * STRIP

    def kcols(h):
        return slice(h * DH, (h + 1) * DH)

    def vcols(h):
        return slice(WIDTH + h * DH, WIDTH + (h + 1) * DH)

    if pieces == 1:
        kv = kv_refs[0]
    else:
        for piece, ref in enumerate(kv_refs):
            block = lax.rem(z + piece, NZ)
            kv[pl.ds(pl.multiple_of(block * ROWS, ROWS), ROWS), :] = ref[...]
    for slot, ref in enumerate((q0, q1, q2, q3)):
        qs[slot * ROWS : (slot + 1) * ROWS, :] = ref[0:ROWS, :]
        cq[slot * CROWS : (slot + 1) * CROWS, :] = ref[ROWS:QROWS, :]
    acc[...] = jnp.zeros_like(acc)

    def body(row, rows, first, keys, triangle=False):
        mask = None
        if triangle:
            mask = lax.broadcasted_iota(jnp.int32, (rows, keys), 0) >= lax.broadcasted_iota(jnp.int32, (rows, keys), 1)
        out = []
        for h in range(HALF_HEADS):
            w = silu_weight(contract_lanes(qs[pl.ds(row, rows), kcols(h)], kv[pl.ds(first, keys), kcols(h)]))
            if triangle:
                w = jnp.where(mask, w, 0.0)
            out.append(jnp.dot(w.astype(jnp.bfloat16), kv[pl.ds(first, keys), vcols(h)], preferred_element_type=jnp.float32))
        for h in range(HALF_HEADS):
            acc[pl.ds(row, rows), kcols(h)] += out[h]

    def run(row, rows, low, count):
        count = jnp.maximum(count, 0)
        wide = count // 8

        def step(i, carry):
            body(row, rows, pl.multiple_of((low + 8 * i) * BLOCK, BLOCK), 8 * BLOCK)
            return carry

        lax.fori_loop(0, wide, step, 0)
        done = low + 8 * wide
        for size in (4, 2, 1):
            here = (count // size) % 2 == 1

            @pl.when(here)
            def _(done=done, size=size):
                body(row, rows, pl.multiple_of(done * BLOCK, BLOCK), size * BLOCK)

            done = done + jnp.where(here, size, 0)

    def owner_of(event):
        low, end = jnp.int32(-1), jnp.int32(-1)
        for s, t in zip(starts, ends):
            inside = (s <= event) & (event < t)
            low = jnp.where(inside, s, low)
            end = jnp.where(inside, t, end)
        return low, end

    def slot_step(slot, carry):
        event = ((y + slot) * NZ + z) * ROWS
        row = pl.multiple_of(slot * ROWS, ROWS)
        low0, _ = owner_of(event)
        low1, _ = owner_of(event + BLOCK)
        near = slot == 0
        same = (low0 == low1) & (low0 >= 0)
        top = jnp.where(near, 2 * z, NZ * ROWS // BLOCK)

        @pl.when(same)
        def _():
            low = jnp.maximum(low0 - strip0, 0) // BLOCK
            run(row, ROWS, low, top - low)

            @pl.when(near)
            def _():
                body(row, ROWS, pl.multiple_of(z * ROWS, ROWS), ROWS, triangle=True)

        @pl.when(jnp.logical_not(same))
        def _():
            def half_step(half, carry):
                start = jnp.where(half == 0, low0, low1)

                @pl.when(start >= 0)
                def _():
                    low = jnp.maximum(start - strip0, 0) // BLOCK
                    upto = jnp.where(near, 2 * z + half, top)
                    at = pl.multiple_of(row + half * BLOCK, BLOCK)
                    run(at, BLOCK, low, upto - low)

                    @pl.when(near)
                    def _():
                        body(at, BLOCK, pl.multiple_of((2 * z + half) * BLOCK, BLOCK), BLOCK, triangle=True)

                return carry

            lax.fori_loop(0, 2, half_step, 0)

        return carry

    lax.fori_loop(0, NY - y, slot_step, 0)

    for slot in range(NY):
        event = ((y + slot) * NZ + z) * ROWS
        _, end0 = owner_of(event)
        _, end1 = owner_of(event + BLOCK)
        at = lax.broadcasted_iota(jnp.int32, (ROWS, WIDTH), 0)
        end = jnp.where(at < BLOCK, end0, end1)
        rows = jnp.where(event + at < end, acc[slot * ROWS : (slot + 1) * ROWS, :], 0.0)
        if slot == 0:
            own_ref[0:ROWS, :] = rows
        else:
            (o1, o2, o3)[slot - 1][0:ROWS, :] = rows.astype(jnp.bfloat16)

    lows, highs = [], []
    for slot in range(NY):
        first = pl.multiple_of((lax.rem(y + slot, NY) * NZ + z) * CROWS, CROWS)
        user = cu_ref[pl.ds(first, CROWS), :]
        lows.append(jnp.where(user == 0, starts[0], starts[1]) - strip0)
        highs.append(jnp.where(user == 0, ends[0], ends[1]) - strip0)
    low = jnp.concatenate(lows, 0)
    high = jnp.concatenate(highs, 0)
    cacc[...] = jnp.zeros_like(cacc)

    def cand_step(i, carry):
        first = pl.multiple_of(i * CKEYS, CKEYS)
        col = first + lax.broadcasted_iota(jnp.int32, (NY * CROWS, CKEYS), 1)
        mask = (col >= low) & (col < high)
        out = []
        for h in range(HALF_HEADS):
            w = silu_weight(contract_lanes(cq[:, kcols(h)], kv[pl.ds(first, CKEYS), kcols(h)]))
            w = jnp.where(mask, w, 0.0).astype(jnp.bfloat16)
            out.append(jnp.dot(w, kv[pl.ds(first, CKEYS), vcols(h)], preferred_element_type=jnp.float32))
        for h in range(HALF_HEADS):
            cacc[:, kcols(h)] += out[h]
        return carry

    lax.fori_loop(0, STRIP // CKEYS, cand_step, 0)
    own_ref[ROWS:QROWS, :] = cacc[0:CROWS, :]
    for slot in range(1, NY):
        (o1, o2, o3)[slot - 1][ROWS:QROWS, :] = cacc[slot * CROWS : (slot + 1) * CROWS, :].astype(jnp.bfloat16)


def attend(part, place, starts, lens, queries, pieces, users):
    smem = pl.BlockSpec(memory_space=pltpu.SMEM)
    vmem = pl.BlockSpec(memory_space=pltpu.VMEM)
    q_spec = pl.BlockSpec((QROWS, WIDTH), lambda i: (0, part))
    o_spec = pl.BlockSpec((QROWS, WIDTH), lambda i: (0, 0))
    return pl.pallas_call(
        functools.partial(attend_kernel, len(pieces)),
        grid=(1,),
        in_specs=[smem, smem, smem, q_spec, q_spec, q_spec, q_spec] + [vmem] * (1 + len(pieces)),
        out_specs=[o_spec] * 4,
        out_shape=[jax.ShapeDtypeStruct((QROWS, WIDTH), jnp.float32)]
        + [jax.ShapeDtypeStruct((QROWS, WIDTH), jnp.bfloat16)] * 3,
        scratch_shapes=[
            pltpu.VMEM((STRIP if len(pieces) > 1 else 16, 2 * WIDTH), jnp.bfloat16),
            pltpu.VMEM((NY * ROWS, WIDTH), jnp.bfloat16),
            pltpu.VMEM((NY * ROWS, WIDTH), jnp.float32),
            pltpu.VMEM((NY * CROWS, WIDTH), jnp.bfloat16),
            pltpu.VMEM((NY * CROWS, WIDTH), jnp.float32),
        ],
        compiler_params=pltpu.CompilerParams(vmem_limit_bytes=VMEM_LIMIT),
        cost_estimate=pl.CostEstimate(
            flops=2 * HALF_HEADS * 2 * QROWS * 4 * STRIP * DH, bytes_accessed=4 << 20, transcendentals=0
        ),
        name="attend",
    )(place, starts, lens, *queries, users, *pieces)


def finish_kernel(parts, *refs):
    n = parts * 4
    totals = refs[:n]
    hg, hx, cq, ck, cv, cg, cx, w_ref, ho, co = refs[n:]
    sums = []
    for p in range(parts):
        total = totals[4 * p][...]
        for i in range(1, 4):
            total = total + totals[4 * p + i][...].astype(jnp.float32)
        sums.append(total)
    total = sums[0] if parts == 1 else jnp.concatenate(sums, axis=1)
    own = []
    for h in range(HEADS):
        at = slice(h * DH, (h + 1) * DH)
        scores = jnp.sum(cq[:, at].astype(jnp.float32) * ck[:, at].astype(jnp.float32), axis=-1, keepdims=True)
        weight = silu_weight(scores).astype(jnp.bfloat16).astype(jnp.float32)
        own.append(weight * cv[:, at].astype(jnp.float32))

    def tail(rows, gate, inputs, out):
        mean = jnp.mean(rows, axis=-1, keepdims=True)
        centered = rows - mean
        spread = jnp.mean(centered * centered, axis=-1, keepdims=True)
        normed = centered * lax.rsqrt(spread + 1e-05)
        gated = (normed * gate[...].astype(jnp.float32)).astype(jnp.bfloat16)
        mixed = jnp.dot(gated, w_ref[...], preferred_element_type=jnp.float32)
        out[...] = (inputs[...].astype(jnp.float32) + mixed).astype(jnp.bfloat16)

    tail(total[0:ROWS], hg, hx, ho)
    tail(total[ROWS:QROWS] + jnp.concatenate(own, axis=1), cg, cx, co)


def finish(totals, parts, hg, hx, cq, ck, cv, cg, cx, w):
    vmem = pl.BlockSpec(memory_space=pltpu.VMEM)
    return pl.pallas_call(
        functools.partial(finish_kernel, parts),
        in_specs=[vmem] * (len(totals) + 8),
        out_specs=[vmem] * 2,
        out_shape=[jax.ShapeDtypeStruct(hx.shape, jnp.bfloat16), jax.ShapeDtypeStruct(cx.shape, jnp.bfloat16)],
        compiler_params=pltpu.CompilerParams(vmem_limit_bytes=VMEM_LIMIT),
        name="finish",
    )(*totals, hg, hx, cq, ck, cv, cg, cx, w)


def turn(array, axis, count, step):
    return lax.ppermute(array, axis, [(i, (i + step) % count) for i in range(count)])


def on_device(
    hist_query, hist_key, hist_value, hist_gate, hist_input,
    cand_query, cand_key, cand_value, cand_gate, cand_input,
    cand_user, hist_len, hist_start, out_weight,
):
    place = jnp.stack([lax.axis_index("y"), lax.axis_index("z")]).astype(jnp.int32)
    users = cand_user.reshape(-1, 1)
    left = jnp.concatenate([hist_key[:, :WIDTH], hist_value[:, :WIDTH]], axis=1)
    right = jnp.concatenate([hist_key[:, WIDTH:], hist_value[:, WIDTH:]], axis=1)
    strip = lax.all_gather(right, "z", axis=0, tiled=True)
    up, down = [left], [left]
    for _ in range(3):
        up.append(turn(up[-1], "z", NZ, 1))
        down.append(turn(down[-1], "z", NZ, -1))
    across = turn(up[-1], "z", NZ, 1)
    blocks = down + [across] + up[:0:-1]
    mine = jnp.concatenate([hist_query, cand_query], axis=0)
    queries = [mine] + [turn(mine, "y", NY, -k) for k in (1, 2, 3)]
    totals = []
    for part, pieces in enumerate((blocks, [strip])):
        own, *away = attend(part, place, hist_start, hist_len, queries, pieces, users)
        totals += [own] + [turn(a, "y", NY, k) for k, a in zip((1, 2, 3), away)]
    return finish(
        totals, 2, hist_gate, hist_input, cand_query, cand_key, cand_value, cand_gate, cand_input, out_weight
    )


def solution(mesh):
    grid = Mesh(mesh.devices.reshape(-1, NY, NZ), ("batch", "y", "z"))
    rows = P(("batch", "y", "z"), None)
    return jax.shard_map(
        on_device,
        mesh=grid,
        in_specs=(rows,) * 10 + (P("batch"), P("batch"), P("batch"), P()),
        out_specs=(rows, rows),
        check_vma=False,
    )
```

time: 131 us -> 131 us (level)
  waiting for transfers between devices: 71.2 us -> 32.9 us
  starting transfers between devices: 28.8 us -> 63.2 us
  local copies, waits for them, and re-layouts: 3.99 us -> 9.05 us
    ppermute x6 -> x16, starting transfers between devices: 28.7 us -> 63.2 us  [turn(): lax.ppermute(array, axis, [(i, (i + step) % count) for i in range(count)])]
    all_gather x1, waiting for transfers between devices: 31.7 us -> 0.02 us  [on_device(): strip = lax.all_gather(right, 'z', axis=0, tiled=True)]
    ppermute x6 -> x16, waiting for transfers between devices: 39.5 us -> 32.9 us  [turn(): lax.ppermute(array, axis, [(i, (i + step) % count) for i in range(count)])]
    unnamed x21 -> x51, local copies, waits for them, and re-layouts: 2.32 us -> 7.66 us
    pallas_call x1 -> x2, Pallas kernels: 7.9 us -> 7.08 us  [attend(): pl.pallas_call(functools.partial(attend_kernel, len(pieces)), grid=(1,),...]
  transfers between devices with their start and end apart: 7 -> 17, of which waited for: 4 -> 4; matrix products, arithmetic and copies ran while one was open for 2% -> 0% of each run, Pallas kernels for 0% -> 5%
where the time goes in v2:
time: 131 us; the launch traced here: 129 us
  starting transfers between devices  63.2 us (48%)
  waiting for transfers between devices  32.9 us (25%)
  between operations  14.5 us (11%)
  local copies, waits for them, and re-layouts  9.05 us (7%)
  Pallas kernels  8.59 us (7%)
    ppermute x16, starting transfers between devices, turn(): lax.ppermute(array, axis, [(i, (i + step) % count) for i in range(count)])  63.2 us
    ppermute x16, waiting for transfers between devices, turn(): lax.ppermute(array, axis, [(i, (i + step) % count) for i in range(count)])  32.9 us
    unnamed x51, local copies, waits for them, and re-layouts  7.66 us
    pallas_call x2, Pallas kernels, attend(): pl.pallas_call(functools.partial(attend_kernel, len(pieces)), grid=(1,),...  7.08 us
  transfers between devices with their start and end apart: 17, of which 4 were waited for; matrix products, arithmetic and copies ran while one was open for 0% of the time, Pallas kernels for 5%

profile of v2, /device:TPU:56, one launch (start us, length us, event | category | flops | bytes accessed | tf_op | source)
XLA Modules:
  0.0 129.2 jit_solution(10144343645366013370)
XLA Ops:
  9.2 4.3 %collective-permute-start.6 = (bf16[256,512]{1,0:T(8,128)(2,1)S(1)}, bf16[256,512]{1,0:T(8,128)(2,1)S(1)}, u32[]{:S(2)}, u32[]{:S(2)}) collective-permute-start(bf16[256,512]{1,0:T(8,128)(2,1)S(1)} %pad_maximum_fusion.refs_0_), channel_id=1, source_target_pairs={{0,1},{1,2},{2,3},{3,4},{4,5},{5,6},{6,7},{7,0},{8,9},{9,10},{10,1... | collective-permute-start | bytes 786440 | tf_op jit(solution)/shard_map/ppermute | solution.py:256
  13.5 8.6 %collective-permute-start.3 = (bf16[256,512]{1,0:T(8,128)(2,1)S(1)}, bf16[256,512]{1,0:T(8,128)(2,1)S(1)}, u32[]{:S(2)}, u32[]{:S(2)}) collective-permute-start(bf16[256,512]{1,0:T(8,128)(2,1)S(1)} %pad_maximum_fusion.refs_0_), channel_id=1, source_target_pairs={{0,7},{1,0},{2,1},{3,2},{4,3},{5,4},{6,5},{7,6},{8,15},{9,8},{10,9... | collective-permute-start | bytes 786440 | tf_op jit(solution)/shard_map/ppermute | solution.py:256
  22.1 4.4 %collective-permute-done.6.refs_7_ = bf16[256,512]{1,0:T(8,128)(2,1)S(1)} collective-permute-done((bf16[256,512]{1,0:T(8,128)(2,1)S(1)}, bf16[256,512]{1,0:T(8,128)(2,1)S(1)}, u32[]{:S(2)}, u32[]{:S(2)}) %collective-permute-start.6) | collective-permute-done | bytes 262176 | tf_op jit(solution)/shard_map/ppermute | solution.py:256
  26.5 1.9 %collective-permute-start.7 = (bf16[256,512]{1,0:T(8,128)(2,1)S(1)}, bf16[256,512]{1,0:T(8,128)(2,1)S(1)}, u32[]{:S(2)}, u32[]{:S(2)}) collective-permute-start(bf16[256,512]{1,0:T(8,128)(2,1)S(1)} %collective-permute-done.6.refs_7_), channel_id=1, source_target_pairs={{0,1},{1,2},{2,3},{3,4},{4,5},{5,6},{6,7},{7,0},{8,9},{9,10},{10,1... | collective-permute-start | bytes 786440 | tf_op jit(solution)/shard_map/ppermute | solution.py:256
  28.4 5.1 %collective-permute-start.4 = (bf16[256,512]{1,0:T(8,128)(2,1)S(1)}, bf16[256,512]{1,0:T(8,128)(2,1)S(1)}, u32[]{:S(2)}, u32[]{:S(2)}) collective-permute-start(bf16[256,512]{1,0:T(8,128)(2,1)S(1)} %collective-permute-done.3.refs_1_), channel_id=1, source_target_pairs={{0,7},{1,0},{2,1},{3,2},{4,3},{5,4},{6,5},{7,6},{8,15},{9,8},{10,9... | collective-permute-start | bytes 786440 | tf_op jit(solution)/shard_map/ppermute | solution.py:256
  33.5 9.2 %collective-permute-done.7.refs_6_ = bf16[256,512]{1,0:T(8,128)(2,1)S(1)} collective-permute-done((bf16[256,512]{1,0:T(8,128)(2,1)S(1)}, bf16[256,512]{1,0:T(8,128)(2,1)S(1)}, u32[]{:S(2)}, u32[]{:S(2)}) %collective-permute-start.7) | collective-permute-done | bytes 262176 | tf_op jit(solution)/shard_map/ppermute | solution.py:256
  42.7 1.9 %collective-permute-start.8 = (bf16[256,512]{1,0:T(8,128)(2,1)S(1)}, bf16[256,512]{1,0:T(8,128)(2,1)}, u32[]{:S(2)}, u32[]{:S(2)}) collective-permute-start(bf16[256,512]{1,0:T(8,128)(2,1)S(1)} %collective-permute-done.7.refs_6_), channel_id=1, source_target_pairs={{0,1},{1,2},{2,3},{3,4},{4,5},{5,6},{6,7},{7,0},{8,9},{9,10},{10,1... | collective-permute-start | bytes 786440 | tf_op jit(solution)/shard_map/ppermute | solution.py:256
  44.7 4.8 %collective-permute-start.2 = (bf16[288,512]{1,0:T(8,128)(2,1)S(1)}, bf16[288,512]{1,0:T(8,128)(2,1)S(1)}, u32[]{:S(2)}, u32[]{:S(2)}) collective-permute-start(bf16[288,512]{1,0:T(8,128)(2,1)S(1)} %constant_dynamic-update-slice_fusion.q0), channel_id=1, source_target_pairs={{0,8},{8,16},{16,24},{24,0},{1,9},{9,17},{17,25},{25,1},{2,10},{10... | collective-permute-start | bytes 884744 | tf_op jit(solution)/shard_map/ppermute | solution.py:256
  49.5 1.9 %collective-permute-start.1 = (bf16[288,512]{1,0:T(8,128)(2,1)S(1)}, bf16[288,512]{1,0:T(8,128)(2,1)S(1)}, u32[]{:S(2)}, u32[]{:S(2)}) collective-permute-start(bf16[288,512]{1,0:T(8,128)(2,1)S(1)} %constant_dynamic-update-slice_fusion.q0), channel_id=1, source_target_pairs={{0,16},{8,24},{16,0},{24,8},{1,17},{9,25},{17,1},{25,9},{2,18},{10... | collective-permute-start | bytes 884744 | tf_op jit(solution)/shard_map/ppermute | solution.py:256
  51.4 3.1 %collective-permute-start = (bf16[288,512]{1,0:T(8,128)(2,1)S(1)}, bf16[288,512]{1,0:T(8,128)(2,1)S(1)}, u32[]{:S(2)}, u32[]{:S(2)}) collective-permute-start(bf16[288,512]{1,0:T(8,128)(2,1)S(1)} %constant_dynamic-update-slice_fusion.q0), channel_id=1, source_target_pairs={{0,24},{8,0},{16,8},{24,16},{1,25},{9,1},{17,9},{25,17},{2,26},{10... | collective-permute-start | bytes 884744 | tf_op jit(solution)/shard_map/ppermute | solution.py:256
  54.6 5.1 %collective-permute-start.5 = (bf16[256,512]{1,0:T(8,128)(2,1)S(1)}, bf16[256,512]{1,0:T(8,128)(2,1)}, u32[]{:S(2)}, u32[]{:S(2)}) collective-permute-start(bf16[256,512]{1,0:T(8,128)(2,1)S(1)} %collective-permute-done.4.refs_2_), channel_id=1, source_target_pairs={{0,7},{1,0},{2,1},{3,2},{4,3},{5,4},{6,5},{7,6},{8,15},{9,8},{10,9... | collective-permute-start | bytes 786440 | tf_op jit(solution)/shard_map/ppermute | solution.py:256
  59.7 1.9 %collective-permute-start.9 = (bf16[256,512]{1,0:T(8,128)(2,1)}, bf16[256,512]{1,0:T(8,128)(2,1)}, u32[]{:S(2)}, u32[]{:S(2)}) collective-permute-start(bf16[256,512]{1,0:T(8,128)(2,1)} %collective-permute-done.8.refs_5_), channel_id=1, source_target_pairs={{0,1},{1,2},{2,3},{3,4},{4,5},{5,6},{6,7},{7,0},{8,9},{9,10},{10,1... | collective-permute-start | bytes 786440 | tf_op jit(solution)/shard_map/ppermute | solution.py:256
  62.0 10.5 %collective-permute-done.1.q2 = bf16[288,512]{1,0:T(8,128)(2,1)S(1)} collective-permute-done((bf16[288,512]{1,0:T(8,128)(2,1)S(1)}, bf16[288,512]{1,0:T(8,128)(2,1)S(1)}, u32[]{:S(2)}, u32[]{:S(2)}) %collective-permute-start.1) | collective-permute-done | bytes 294944 | tf_op jit(solution)/shard_map/ppermute | solution.py:256
  73.7 4.3 %attend.2 = (f32[288,256]{1,0:T(8,128)S(1)}, bf16[288,256]{1,0:T(8,128)(2,1)}, bf16[288,256]{1,0:T(8,128)(2,1)}, bf16[288,256]{1,0:T(8,128)(2,1)}) custom-call(s32[2]{0:T(128)S(1)} %pad_add_fusion.place_ref, s32[2]{0:T(128)S(1)} %copy-done.17, s32[2]{0:T(128)S(1)} %copy-done.19, bf16[288,512]{1,0:T(8,128)(2,1)S(1)} %constant_dynamic-update-slice_fusion.q0, ...), custom_call_target="tpu_custom_call" | custom-call | flops 2415919104 | bytes 4194304 | tf_op jit(solution)/shard_map/attend/pallas_call | solution.py:190
  78.0 3.2 %collective-permute-start.10 = (bf16[288,256]{1,0:T(8,128)(2,1)}, bf16[288,256]{1,0:T(8,128)(2,1)S(1)}, u32[]{:S(2)}, u32[]{:S(2)}) collective-permute-start(bf16[288,256]{1,0:T(8,128)(2,1)} %get-tuple-element.11), channel_id=1, source_target_pairs={{0,8},{8,16},{16,24},{24,0},{1,9},{9,17},{17,25},{25,1},{2,10},{10... | collective-permute-start | bytes 442376 | tf_op jit(solution)/shard_map/ppermute | solution.py:256
  81.2 6.0 %collective-permute-start.11 = (bf16[288,256]{1,0:T(8,128)(2,1)}, bf16[288,256]{1,0:T(8,128)(2,1)S(1)}, u32[]{:S(2)}, u32[]{:S(2)}) collective-permute-start(bf16[288,256]{1,0:T(8,128)(2,1)} %get-tuple-element.12), channel_id=1, source_target_pairs={{0,16},{8,24},{16,0},{24,8},{1,17},{9,25},{17,1},{25,9},{2,18},{10... | collective-permute-start | bytes 442376 | tf_op jit(solution)/shard_map/ppermute | solution.py:256
  87.3 4.1 %collective-permute-start.12 = (bf16[288,256]{1,0:T(8,128)(2,1)}, bf16[288,256]{1,0:T(8,128)(2,1)S(1)}, u32[]{:S(2)}, u32[]{:S(2)}) collective-permute-start(bf16[288,256]{1,0:T(8,128)(2,1)} %get-tuple-element.13), channel_id=1, source_target_pairs={{0,24},{8,0},{16,8},{24,16},{1,25},{9,1},{17,9},{25,17},{2,26},{10... | collective-permute-start | bytes 442376 | tf_op jit(solution)/shard_map/ppermute | solution.py:256
  91.4 1.6 %copy-done.8 = bf16[2048,512]{1,0:T(8,128)(2,1)S(1)} copy-done((bf16[2048,512]{1,0:T(8,128)(2,1)S(1)}, bf16[2048,512]{1,0:T(8,128)(2,1)}, u32[]{:S(2)}) %copy-start.8) | copy-done | bytes 2097176
  97.9 2.8 %attend.3 = (f32[288,256]{1,0:T(8,128)S(1)}, bf16[288,256]{1,0:T(8,128)(2,1)S(1)}, bf16[288,256]{1,0:T(8,128)(2,1)S(1)}, bf16[288,256]{1,0:T(8,128)(2,1)S(1)}) custom-call(s32[2]{0:T(128)S(1)} %copy-done.22, s32[2]{0:T(128)S(1)} %copy-done.18, s32[2]{0:T(128)S(1)} %copy-done.20, bf16[288,512]{1,0:T(8,128)(2,1)S(1)} %constant_dynamic-update-slice_fusion.q0, ...), custom_call_target="tpu_custom_call" | custom-call | flops 2415919104 | bytes 4194304 | tf_op jit(solution)/shard_map/attend/pallas_call | solution.py:190
  100.7 5.7 %collective-permute-start.13 = (bf16[288,256]{1,0:T(8,128)(2,1)S(1)}, bf16[288,256]{1,0:T(8,128)(2,1)S(1)}, u32[]{:S(2)}, u32[]{:S(2)}) collective-permute-start(bf16[288,256]{1,0:T(8,128)(2,1)S(1)} %get-tuple-element.15), channel_id=1, source_target_pairs={{0,8},{8,16},{16,24},{24,0},{1,9},{9,17},{17,25},{25,1},{2,10},{10... | collective-permute-start | bytes 442376 | tf_op jit(solution)/shard_map/ppermute | solution.py:256
  106.4 1.9 %collective-permute-start.14 = (bf16[288,256]{1,0:T(8,128)(2,1)S(1)}, bf16[288,256]{1,0:T(8,128)(2,1)S(1)}, u32[]{:S(2)}, u32[]{:S(2)}) collective-permute-start(bf16[288,256]{1,0:T(8,128)(2,1)S(1)} %get-tuple-element.16), channel_id=1, source_target_pairs={{0,16},{8,24},{16,0},{24,8},{1,17},{9,25},{17,1},{25,9},{2,18},{10... | collective-permute-start | bytes 442376 | tf_op jit(solution)/shard_map/ppermute | solution.py:256
  108.3 3.5 %collective-permute-start.15 = (bf16[288,256]{1,0:T(8,128)(2,1)S(1)}, bf16[288,256]{1,0:T(8,128)(2,1)S(1)}, u32[]{:S(2)}, u32[]{:S(2)}) collective-permute-start(bf16[288,256]{1,0:T(8,128)(2,1)S(1)} %get-tuple-element.17), channel_id=1, source_target_pairs={{0,24},{8,0},{16,8},{24,16},{1,25},{9,1},{17,9},{25,17},{2,26},{10... | collective-permute-start | bytes 442376 | tf_op jit(solution)/shard_map/ppermute | solution.py:256
  111.9 8.9 %collective-permute-done.14.refs_6_ = bf16[288,256]{1,0:T(8,128)(2,1)S(1)} collective-permute-done((bf16[288,256]{1,0:T(8,128)(2,1)S(1)}, bf16[288,256]{1,0:T(8,128)(2,1)S(1)}, u32[]{:S(2)}, u32[]{:S(2)}) %collective-permute-start.14) | collective-permute-done | bytes 147488 | tf_op jit(solution)/shard_map/ppermute | solution.py:256
  120.8 1.5 %finish.1 = (bf16[256,1024]{1,0:T(8,128)(2,1)}, bf16[32,1024]{1,0:T(8,128)(2,1)}) custom-call(f32[288,256]{1,0:T(8,128)S(1)} %get-tuple-element.10.refs_0_, bf16[288,256]{1,0:T(8,128)(2,1)S(1)} %collective-permute-done.10.refs_1_, bf16[288,256]{1,0:T(8,128)(2,1)S(1)} %collective-permute-done.11.refs_2_, ...), custom_call_target="tpu_custom_call" | custom-call | tf_op jit(solution)/shard_map/finish/pallas_call | solution.py:245
  (71 shorter events, 8.4 us)
Async XLA Ops:
  7.2 37.4 %copy-start.23 = (bf16[256,512]{1,0:T(8,128)(2,1)S(1)}, bf16[256,512]{1,0:T(8,128)(2,1)}, u32[]{:S(2)}) copy-start(bf16[256,512]{1,0:T(8,128)(2,1)} %param.14) | copy-start | bytes 786436
  7.2 37.5 %copy-start.3 = (bf16[32,512]{1,0:T(8,128)(2,1)S(1)}, bf16[32,512]{1,0:T(8,128)(2,1)}, u32[]{:S(2)}) copy-start(bf16[32,512]{1,0:T(8,128)(2,1)} %refs_10_.1) | copy-start | bytes 98308
  7.2 54.5 %copy-start.24 = (s32[1024]{0:T(1024)S(1)}, s32[1024]{0:T(1024)}, u32[]{:S(2)}) copy-start(s32[1024]{0:T(1024)} %param.24) | copy-start | bytes 12292
  7.2 65.3 %copy-start.17 = (s32[2]{0:T(128)S(1)}, s32[2]{0:T(128)}, u32[]{:S(2)}) copy-start(s32[2]{0:T(128)} %start_ref.3) | copy-start | bytes 28
  7.2 65.3 %copy-start.19 = (s32[2]{0:T(128)S(1)}, s32[2]{0:T(128)}, u32[]{:S(2)}) copy-start(s32[2]{0:T(128)} %len_ref.3) | copy-start | bytes 28
  7.2 84.2 %all-gather.2.cloned.1.call-start = ((), (), s32[]{:S(2)}) async-start(), calls=%async_computation | async-start | bytes 2359296 | tf_op jit(solution)/shard_map/all_gather | solution.py:268
  9.2 17.2 %collective-permute-start.6 = (bf16[256,512]{1,0:T(8,128)(2,1)S(1)}, bf16[256,512]{1,0:T(8,128)(2,1)S(1)}, u32[]{:S(2)}, u32[]{:S(2)}) collective-permute-start(bf16[256,512]{1,0:T(8,128)(2,1)S(1)} %pad_maximum_fusion.refs_0_), channel_id=1, source_target_pairs={{0,1},{1,2},{2,3},{3,4},{4,5},{5,6},{6,7},{7,0},{8,9},{9,10},{10,1... | collective-permute-start | bytes 786440 | tf_op jit(solution)/shard_map/ppermute | solution.py:256
  13.5 14.9 %collective-permute-start.3 = (bf16[256,512]{1,0:T(8,128)(2,1)S(1)}, bf16[256,512]{1,0:T(8,128)(2,1)S(1)}, u32[]{:S(2)}, u32[]{:S(2)}) collective-permute-start(bf16[256,512]{1,0:T(8,128)(2,1)S(1)} %pad_maximum_fusion.refs_0_), channel_id=1, source_target_pairs={{0,7},{1,0},{2,1},{3,2},{4,3},{5,4},{6,5},{7,6},{8,15},{9,8},{10,9... | collective-permute-start | bytes 786440 | tf_op jit(solution)/shard_map/ppermute | solution.py:256
  26.5 16.2 %collective-permute-start.7 = (bf16[256,512]{1,0:T(8,128)(2,1)S(1)}, bf16[256,512]{1,0:T(8,128)(2,1)S(1)}, u32[]{:S(2)}, u32[]{:S(2)}) collective-permute-start(bf16[256,512]{1,0:T(8,128)(2,1)S(1)} %collective-permute-done.6.refs_7_), channel_id=1, source_target_pairs={{0,1},{1,2},{2,3},{3,4},{4,5},{5,6},{6,7},{7,0},{8,9},{9,10},{10,1... | collective-permute-start | bytes 786440 | tf_op jit(solution)/shard_map/ppermute | solution.py:256
  28.4 26.2 %collective-permute-start.4 = (bf16[256,512]{1,0:T(8,128)(2,1)S(1)}, bf16[256,512]{1,0:T(8,128)(2,1)S(1)}, u32[]{:S(2)}, u32[]{:S(2)}) collective-permute-start(bf16[256,512]{1,0:T(8,128)(2,1)S(1)} %collective-permute-done.3.refs_1_), channel_id=1, source_target_pairs={{0,7},{1,0},{2,1},{3,2},{4,3},{5,4},{6,5},{7,6},{8,15},{9,8},{10,9... | collective-permute-start | bytes 786440 | tf_op jit(solution)/shard_map/ppermute | solution.py:256
  42.7 17.0 %collective-permute-start.8 = (bf16[256,512]{1,0:T(8,128)(2,1)S(1)}, bf16[256,512]{1,0:T(8,128)(2,1)}, u32[]{:S(2)}, u32[]{:S(2)}) collective-permute-start(bf16[256,512]{1,0:T(8,128)(2,1)S(1)} %collective-permute-done.7.refs_6_), channel_id=1, source_target_pairs={{0,1},{1,2},{2,3},{3,4},{4,5},{5,6},{6,7},{7,0},{8,9},{9,10},{10,1... | collective-permute-start | bytes 786440 | tf_op jit(solution)/shard_map/ppermute | solution.py:256
  44.7 17.3 %collective-permute-start.2 = (bf16[288,512]{1,0:T(8,128)(2,1)S(1)}, bf16[288,512]{1,0:T(8,128)(2,1)S(1)}, u32[]{:S(2)}, u32[]{:S(2)}) collective-permute-start(bf16[288,512]{1,0:T(8,128)(2,1)S(1)} %constant_dynamic-update-slice_fusion.q0), channel_id=1, source_target_pairs={{0,8},{8,16},{16,24},{24,0},{1,9},{9,17},{17,25},{25,1},{2,10},{10... | collective-permute-start | bytes 884744 | tf_op jit(solution)/shard_map/ppermute | solution.py:256
  49.5 23.0 %collective-permute-start.1 = (bf16[288,512]{1,0:T(8,128)(2,1)S(1)}, bf16[288,512]{1,0:T(8,128)(2,1)S(1)}, u32[]{:S(2)}, u32[]{:S(2)}) collective-permute-start(bf16[288,512]{1,0:T(8,128)(2,1)S(1)} %constant_dynamic-update-slice_fusion.q0), channel_id=1, source_target_pairs={{0,16},{8,24},{16,0},{24,8},{1,17},{9,25},{17,1},{25,9},{2,18},{10... | collective-permute-start | bytes 884744 | tf_op jit(solution)/shard_map/ppermute | solution.py:256
  51.4 21.1 %collective-permute-start = (bf16[288,512]{1,0:T(8,128)(2,1)S(1)}, bf16[288,512]{1,0:T(8,128)(2,1)S(1)}, u32[]{:S(2)}, u32[]{:S(2)}) collective-permute-start(bf16[288,512]{1,0:T(8,128)(2,1)S(1)} %constant_dynamic-update-slice_fusion.q0), channel_id=1, source_target_pairs={{0,24},{8,0},{16,8},{24,16},{1,25},{9,1},{17,9},{25,17},{2,26},{10... | collective-permute-start | bytes 884744 | tf_op jit(solution)/shard_map/ppermute | solution.py:256
  54.6 17.9 %collective-permute-start.5 = (bf16[256,512]{1,0:T(8,128)(2,1)S(1)}, bf16[256,512]{1,0:T(8,128)(2,1)}, u32[]{:S(2)}, u32[]{:S(2)}) collective-permute-start(bf16[256,512]{1,0:T(8,128)(2,1)S(1)} %collective-permute-done.4.refs_2_), channel_id=1, source_target_pairs={{0,7},{1,0},{2,1},{3,2},{4,3},{5,4},{6,5},{7,6},{8,15},{9,8},{10,9... | collective-permute-start | bytes 786440 | tf_op jit(solution)/shard_map/ppermute | solution.py:256
  59.7 12.8 %collective-permute-start.9 = (bf16[256,512]{1,0:T(8,128)(2,1)}, bf16[256,512]{1,0:T(8,128)(2,1)}, u32[]{:S(2)}, u32[]{:S(2)}) collective-permute-start(bf16[256,512]{1,0:T(8,128)(2,1)} %collective-permute-done.8.refs_5_), channel_id=1, source_target_pairs={{0,1},{1,2},{2,3},{3,4},{4,5},{5,6},{6,7},{7,0},{8,9},{9,10},{10,1... | collective-permute-start | bytes 786440 | tf_op jit(solution)/shard_map/ppermute | solution.py:256
  78.0 30.3 %collective-permute-start.10 = (bf16[288,256]{1,0:T(8,128)(2,1)}, bf16[288,256]{1,0:T(8,128)(2,1)S(1)}, u32[]{:S(2)}, u32[]{:S(2)}) collective-permute-start(bf16[288,256]{1,0:T(8,128)(2,1)} %get-tuple-element.11), channel_id=1, source_target_pairs={{0,8},{8,16},{16,24},{24,0},{1,9},{9,17},{17,25},{25,1},{2,10},{10... | collective-permute-start | bytes 442376 | tf_op jit(solution)/shard_map/ppermute | solution.py:256
  81.2 30.6 %collective-permute-start.11 = (bf16[288,256]{1,0:T(8,128)(2,1)}, bf16[288,256]{1,0:T(8,128)(2,1)S(1)}, u32[]{:S(2)}, u32[]{:S(2)}) collective-permute-start(bf16[288,256]{1,0:T(8,128)(2,1)} %get-tuple-element.12), channel_id=1, source_target_pairs={{0,16},{8,24},{16,0},{24,8},{1,17},{9,25},{17,1},{25,9},{2,18},{10... | collective-permute-start | bytes 442376 | tf_op jit(solution)/shard_map/ppermute | solution.py:256
  87.3 33.5 %copy-start = (bf16[512,1024]{1,0:T(8,128)(2,1)S(1)}, bf16[512,1024]{1,0:T(8,128)(2,1)}, u32[]{:S(2)}) copy-start(bf16[512,1024]{1,0:T(8,128)(2,1)} %refs_15_.1) | copy-start | bytes 3145732
  87.3 33.5 %copy-start.1 = (bf16[256,1024]{1,0:T(8,128)(2,1)S(1)}, bf16[256,1024]{1,0:T(8,128)(2,1)}, u32[]{:S(2)}) copy-start(bf16[256,1024]{1,0:T(8,128)(2,1)} %refs_9_.1) | copy-start | bytes 1572868
  87.3 24.5 %collective-permute-start.12 = (bf16[288,256]{1,0:T(8,128)(2,1)}, bf16[288,256]{1,0:T(8,128)(2,1)S(1)}, u32[]{:S(2)}, u32[]{:S(2)}) collective-permute-start(bf16[288,256]{1,0:T(8,128)(2,1)} %get-tuple-element.13), channel_id=1, source_target_pairs={{0,24},{8,0},{16,8},{24,16},{1,25},{9,1},{17,9},{25,17},{2,26},{10... | collective-permute-start | bytes 442376 | tf_op jit(solution)/shard_map/ppermute | solution.py:256
  100.7 11.2 %collective-permute-start.13 = (bf16[288,256]{1,0:T(8,128)(2,1)S(1)}, bf16[288,256]{1,0:T(8,128)(2,1)S(1)}, u32[]{:S(2)}, u32[]{:S(2)}) collective-permute-start(bf16[288,256]{1,0:T(8,128)(2,1)S(1)} %get-tuple-element.15), channel_id=1, source_target_pairs={{0,8},{8,16},{16,24},{24,0},{1,9},{9,17},{17,25},{25,1},{2,10},{10... | collective-permute-start | bytes 442376 | tf_op jit(solution)/shard_map/ppermute | solution.py:256
  106.4 14.4 %collective-permute-start.14 = (bf16[288,256]{1,0:T(8,128)(2,1)S(1)}, bf16[288,256]{1,0:T(8,128)(2,1)S(1)}, u32[]{:S(2)}, u32[]{:S(2)}) collective-permute-start(bf16[288,256]{1,0:T(8,128)(2,1)S(1)} %get-tuple-element.16), channel_id=1, source_target_pairs={{0,16},{8,24},{16,0},{24,8},{1,17},{9,25},{17,1},{25,9},{2,18},{10... | collective-permute-start | bytes 442376 | tf_op jit(solution)/shard_map/ppermute | solution.py:256
  108.3 12.4 %collective-permute-start.15 = (bf16[288,256]{1,0:T(8,128)(2,1)S(1)}, bf16[288,256]{1,0:T(8,128)(2,1)S(1)}, u32[]{:S(2)}, u32[]{:S(2)}) collective-permute-start(bf16[288,256]{1,0:T(8,128)(2,1)S(1)} %get-tuple-element.17), channel_id=1, source_target_pairs={{0,24},{8,0},{16,8},{24,16},{1,25},{9,1},{17,9},{25,17},{2,26},{10... | collective-permute-start | bytes 442376 | tf_op jit(solution)/shard_map/ppermute | solution.py:256
  (18 other events, 225.1 us)
Sparse Core Ops, SparseCore 0:
  10.1 55.5 all-gather.1

commit v3 on v0

v3 whole, which is shorter than its diff:
```python
import functools
import math

import jax
import jax.numpy as jnp
from jax import lax
from jax.experimental import pallas as pl
from jax.experimental.pallas import tpu as pltpu
from jax.sharding import Mesh, PartitionSpec as P

HEADS = 4
DH = 128
NY = 4
NZ = 8
ROWS = 256
CROWS = 32
QROWS = ROWS + CROWS
FOLD = QROWS // 2
REST = ROWS - FOLD
BLOCK = 128
KEYS = NY * ROWS
TOTAL = KEYS + NY * CROWS
NOBODY = 1 << 30
HALF = 1.0 / (2.0 * math.sqrt(DH))
VMEM_LIMIT = 60 * 1024 * 1024
VMEM = pl.BlockSpec(memory_space=pltpu.VMEM)
SMEM = pl.BlockSpec(memory_space=pltpu.SMEM)
PARAMS = pltpu.CompilerParams(vmem_limit_bytes=VMEM_LIMIT)


def contract_lanes(a, b):
    return lax.dot_general(a, b, (((1,), (1,)), ((), ())), preferred_element_type=jnp.float32)


def silu_weight(scores):
    half = scores * HALF
    return (half * jnp.tanh(half) + half).astype(jnp.bfloat16)


def split_kernel(k_ref, v_ref, kv_ref):
    for h in range(HEADS):
        at = slice(h * DH, (h + 1) * DH)
        kv_ref[h * ROWS : (h + 1) * ROWS, 0:DH] = k_ref[:, at]
        kv_ref[h * ROWS : (h + 1) * ROWS, DH : 2 * DH] = v_ref[:, at]


def fold_kernel(q_ref, c_ref, out_ref):
    for h in range(HEADS):
        at = slice(h * DH, (h + 1) * DH)
        out_ref[h * FOLD : (h + 1) * FOLD, 0:DH] = q_ref[0:FOLD, at]
        out_ref[h * FOLD : h * FOLD + REST, DH : 2 * DH] = q_ref[FOLD:ROWS, at]
        out_ref[h * FOLD + REST : (h + 1) * FOLD, DH : 2 * DH] = c_ref[:, at]


def attend_kernel(offsets, first, last, place_ref, start_ref, len_ref, q_ref, user_ref, *refs):
    blocks = 2 if last else len(offsets)
    kv_refs = refs[:blocks]
    refs = refs[blocks:]
    if not first:
        in_ref, *refs = refs
    out_ref, kv, qs, acc = refs
    z = place_ref[1]
    starts = [start_ref[u] for u in range(2)]
    ends = [start_ref[u] + len_ref[u] for u in range(2)]

    size = kv_refs[0].shape[0]
    for i, ref in enumerate(kv_refs):
        kv[i * size : (i + 1) * size, :] = ref[...]
    for s in range(NY):
        qs[s * ROWS : s * ROWS + FOLD, :] = q_ref[s * FOLD : (s + 1) * FOLD, 0:DH]
        qs[s * ROWS + FOLD : (s + 1) * ROWS, :] = q_ref[s * FOLD : s * FOLD + REST, DH : 2 * DH]
        qs[KEYS + s * CROWS : KEYS + (s + 1) * CROWS, :] = q_ref[s * FOLD + REST : (s + 1) * FOLD, DH : 2 * DH]
    if first:
        acc[...] = jnp.zeros_like(acc)
    else:
        acc[...] = in_ref[...]

    lows, stops = [], []
    for half in range(2 * NY):
        event = (half // 2 * NZ + z) * ROWS + half % 2 * BLOCK
        low, stop = jnp.int32(NOBODY), jnp.int32(0)
        for s, t in zip(starts, ends):
            inside = (s <= event) & (event < t)
            low = jnp.where(inside, s, low)
            stop = jnp.where(inside, t, stop)
        lows.append(low)
        stops.append(stop)
    user = user_ref[...]
    cand_low = jnp.where(user == 0, starts[0], starts[1])
    cand_stop = jnp.where(user == 0, ends[0], ends[1])
    column = lax.broadcasted_iota(jnp.int32, (1, ROWS), 1)

    def block_step(part, slots):
        block = z + offsets[-1]
        for n, offset in enumerate(offsets[:-1]):
            block = jnp.where(part == n, z + offset, block)
        block = lax.rem(block, NZ)
        for strip, slot in enumerate(slots):
            row = slot * ROWS
            key = pl.multiple_of(part * KEYS + strip * ROWS, ROWS)
            events = (strip * NZ + block) * ROWS + column
            w = silu_weight(contract_lanes(qs[row:TOTAL, :], kv[pl.ds(key, ROWS), 0:DH]))
            parts = []
            for half in range(2 * slot, 2 * NY):
                at = half * BLOCK - row
                keep = jnp.where(events >= lows[half], 1.0, 0.0).astype(jnp.bfloat16)
                parts.append(w[at : at + BLOCK] * keep)
            keep = jnp.where((events >= cand_low) & (events < cand_stop), 1.0, 0.0).astype(jnp.bfloat16)
            parts.append(w[KEYS - row :] * keep)
            w = parts[0] if len(parts) == 1 else jnp.concatenate(parts, axis=0)
            acc[row:TOTAL, :] += jnp.dot(w, kv[pl.ds(key, ROWS), DH : 2 * DH], preferred_element_type=jnp.float32)

    def step(part, carry):
        block = z + offsets[-1]
        for n, offset in enumerate(offsets[:-1]):
            block = jnp.where(part == n, z + offset, block)
        before = lax.rem(block, NZ) < z

        @pl.when(before)
        def _():
            block_step(part, range(0, NY))

        @pl.when(jnp.logical_not(before))
        def _():
            block_step(part, range(1, NY + 1))

        return carry

    lax.fori_loop(0, len(offsets), step, 0)

    if offsets[0] == 0:
        at = lax.broadcasted_iota(jnp.int32, (BLOCK, ROWS), 0)
        to = lax.broadcasted_iota(jnp.int32, (BLOCK, ROWS), 1)
        for s in range(NY):
            rows = slice(s * ROWS, (s + 1) * ROWS)
            w = silu_weight(contract_lanes(qs[rows, :], kv[rows, 0:DH]))
            event = (s * NZ + z) * ROWS
            parts = []
            for half in range(2):
                mask = (to <= at + half * BLOCK) & (event + to >= lows[2 * s + half])
                parts.append(w[half * BLOCK : (half + 1) * BLOCK] * jnp.where(mask, 1.0, 0.0).astype(jnp.bfloat16))
            w = jnp.concatenate(parts, axis=0)
            acc[rows, :] += jnp.dot(w, kv[rows, DH : 2 * DH], preferred_element_type=jnp.float32)

    if not last:
        out_ref[...] = acc[...]
    else:
        for s in range(NY):
            event = (s * NZ + z) * ROWS
            at = lax.broadcasted_iota(jnp.int32, (ROWS, DH), 0)
            stop = jnp.where(at < BLOCK, stops[2 * s], stops[2 * s + 1])
            rows = jnp.where(event + at < stop, acc[s * ROWS : (s + 1) * ROWS, :], 0.0).astype(jnp.bfloat16)
            out_ref[s * FOLD : (s + 1) * FOLD, 0:DH] = rows[0:FOLD]
            out_ref[s * FOLD : s * FOLD + REST, DH : 2 * DH] = rows[FOLD:ROWS]
            cands = acc[KEYS + s * CROWS : KEYS + (s + 1) * CROWS, :].astype(jnp.bfloat16)
            out_ref[s * FOLD + REST : (s + 1) * FOLD, DH : 2 * DH] = cands


def attend(offsets, where, queries, users, blocks, total, last):
    first = total is None
    shape = jax.ShapeDtypeStruct((NY * FOLD, 2 * DH), jnp.bfloat16) if last else jax.ShapeDtypeStruct((TOTAL, DH), jnp.float32)
    state = [] if first else [total]
    return pl.pallas_call(
        functools.partial(attend_kernel, offsets, first, last),
        in_specs=[SMEM] * 3 + [VMEM] * (2 + len(blocks) + len(state)),
        out_specs=VMEM,
        out_shape=shape,
        scratch_shapes=[
            pltpu.VMEM((len(offsets) * KEYS, 2 * DH), jnp.bfloat16),
            pltpu.VMEM((TOTAL, DH), jnp.bfloat16),
            pltpu.VMEM((TOTAL, DH), jnp.float32),
        ],
        compiler_params=PARAMS,
        cost_estimate=pl.CostEstimate(
            flops=len(offsets) * 4 * TOTAL * KEYS * DH, bytes_accessed=len(offsets) << 20, transcendentals=0
        ),
        name="attend",
    )(*where, queries, users, *blocks, *state)


def finish_kernel(t_ref, hg, hx, cq, ck, cv, cg, cx, w_ref, ho, co):
    hist, cand = [], []
    for h in range(HEADS):
        at = slice(h * DH, (h + 1) * DH)
        rows = t_ref[h * FOLD : (h + 1) * FOLD, :].astype(jnp.float32)
        hist.append(jnp.concatenate([rows[:, 0:DH], rows[0:REST, DH : 2 * DH]], axis=0))
        scores = jnp.sum(cq[:, at].astype(jnp.float32) * ck[:, at].astype(jnp.float32), axis=-1, keepdims=True)
        weight = silu_weight(scores).astype(jnp.float32)
        cand.append(rows[REST:FOLD, DH : 2 * DH] + weight * cv[:, at].astype(jnp.float32))

    def tail(total, gate, inputs, out):
        mean = jnp.mean(total, axis=-1, keepdims=True)
        centered = total - mean
        spread = jnp.mean(centered * centered, axis=-1, keepdims=True)
        normed = centered * lax.rsqrt(spread + 1e-05)
        gated = (normed * gate[...].astype(jnp.float32)).astype(jnp.bfloat16)
        mixed = jnp.dot(gated, w_ref[...], preferred_element_type=jnp.float32)
        out[...] = (inputs[...].astype(jnp.float32) + mixed).astype(jnp.bfloat16)

    tail(jnp.concatenate(hist, axis=1), hg, hx, ho)
    tail(jnp.concatenate(cand, axis=1), cg, cx, co)


def call(kernel, shapes, *args):
    return pl.pallas_call(
        kernel,
        in_specs=[VMEM] * len(args),
        out_specs=[VMEM] * len(shapes),
        out_shape=[jax.ShapeDtypeStruct(s, jnp.bfloat16) for s in shapes],
        compiler_params=PARAMS,
    )(*args)


def turn(array, step):
    return lax.ppermute(array, "z", [(i, (i + step) % NZ) for i in range(NZ)])


def spread(array):
    return lax.all_to_all(array, "y", 0, 0, tiled=True)


def on_device(
    hist_query, hist_key, hist_value, hist_gate, hist_input,
    cand_query, cand_key, cand_value, cand_gate, cand_input,
    cand_user, hist_len, hist_start, out_weight,
):
    z = lax.axis_index("z")
    where = (jnp.stack([lax.axis_index("y"), z]).astype(jnp.int32), hist_start, hist_len)
    users = lax.dynamic_index_in_dim(cand_user.reshape(NY, NZ, CROWS), z, axis=1).reshape(NY * CROWS, 1)
    (own,) = call(split_kernel, [(KEYS, 2 * DH)], hist_key, hist_value)
    own = spread(own)
    (folded,) = call(fold_kernel, [(HEADS * FOLD, 2 * DH)], hist_query, cand_query)
    up1, down1 = turn(own, 1), turn(own, -1)
    queries = spread(folded)
    up1, down1, queries = lax.optimization_barrier((up1, down1, queries))
    up2, down2 = turn(up1, 1), turn(down1, -1)
    total = attend((0, 7, 1), where, queries, users, (own, up1, down1), None, False)
    up2, down2, total = lax.optimization_barrier((up2, down2, total))
    up3, down3 = turn(up2, 1), turn(down2, -1)
    total = attend((6, 2), where, queries, users, (up2, down2), total, False)
    up3, down3, total = lax.optimization_barrier((up3, down3, total))
    low, high = turn(up3[: KEYS // 2], 1), turn(down3[KEYS // 2 :], -1)
    total = attend((5, 3), where, queries, users, (up3, down3), total, False)
    total = attend((4,), where, queries, users, (low, high), total, True)
    return tuple(
        call(
            finish_kernel, [hist_input.shape, cand_input.shape],
            spread(total), hist_gate, hist_input, cand_query, cand_key, cand_value, cand_gate, cand_input, out_weight,
        )
    )


def solution(mesh):
    grid = Mesh(mesh.devices.reshape(-1, NY, NZ), ("batch", "y", "z"))
    rows = P(("batch", "y", "z"), None)
    return jax.shard_map(
        on_device,
        mesh=grid,
        in_specs=(rows,) * 10 + (P("batch"), P("batch"), P("batch"), P()),
        out_specs=(rows, rows),
        check_vma=False,
    )
```

time: 399 us -> 115 us (0.29)
  waiting for transfers between devices: 322 us -> 7.33 us
  blocking collectives: 0 us -> 42.2 us
  starting transfers between devices: 0.08 us -> 34.9 us
  matrix products: 31.2 us -> 0 us
  Pallas kernels: 0 us -> 24.2 us
  local copies, waits for them, and re-layouts: 20.3 us -> 3.71 us
  between operations: 16.8 us -> 0.78 us
  other arithmetic: 6.82 us -> 0.64 us
    all_gather x2 -> x0, waiting for transfers between devices: 321 us -> none  [the longest x1 168 us: on_device(): lax.all_gather(hist_key, 'ctx', axis=0, tiled=True)]
    all_to_all x0 -> x3, blocking collectives: none -> 42.2 us  [spread(): return lax.all_to_all(array, 'y', 0, 0, tiled=True)]
    ppermute x0 -> x8, starting transfers between devices: none -> 34.9 us  [turn(): return lax.ppermute(array, 'z', [(i, (i + step) % NZ) for i in range(NZ)])]
    dot_general x4 -> x0, matrix products: 31.2 us -> none  [the longest x2 29 us: pointwise(): jnp.einsum('hqk,khd->qhd', weights, v_heads, preferred_element_type=jnp.f...]
    pallas_call x0 -> x7, Pallas kernels: none -> 24.2 us  [the longest x4 17.4 us: attend(): pl.pallas_call(functools.partial(attend_kernel, offsets, first, last), in...]
    all_gather x1 -> x0, local copies, waits for them, and re-layouts: 12 us -> none  [on_device(): lax.all_gather(hist_value, 'ctx', axis=0, tiled=True)]
    ppermute x0 -> x8, waiting for transfers between devices: none -> 7.33 us  [turn(): return lax.ppermute(array, 'z', [(i, (i + step) % NZ) for i in range(NZ)])]
  transfers between devices with their start and end apart: 2 -> 8, of which waited for: 2 -> 4; matrix products, arithmetic and copies ran while one was open for 6% -> 1% of each run, Pallas kernels for 0% -> 14%
where the time goes in v3:
time: 115 us; the launch traced here: 114 us
  blocking collectives  42.2 us (37%)
  starting transfers between devices  34.9 us (30%)
  Pallas kernels  24.2 us (21%)
  waiting for transfers between devices  7.33 us (6%)
  local copies, waits for them, and re-layouts  3.71 us (3%)
    all_to_all x3, blocking collectives, spread(): return lax.all_to_all(array, 'y', 0, 0, tiled=True)  42.2 us
    ppermute x8, starting transfers between devices, turn(): return lax.ppermute(array, 'z', [(i, (i + step) % NZ) for i in range(NZ)])  34.9 us
    pallas_call x4, Pallas kernels, attend(): pl.pallas_call(functools.partial(attend_kernel, offsets, first, last), in...  17.4 us
    ppermute x8, waiting for transfers between devices, turn(): return lax.ppermute(array, 'z', [(i, (i + step) % NZ) for i in range(NZ)])  7.33 us
    pallas_call x3, Pallas kernels, call(): pl.pallas_call(kernel, in_specs=[VMEM] * len(args), out_specs=[VMEM] * le...  6.77 us
    unnamed x20, local copies, waits for them, and re-layouts  2.83 us
  transfers between devices with their start and end apart: 8, of which 4 were waited for; matrix products, arithmetic and copies ran while one was open for 1% of the time, Pallas kernels for 14%

profile of v3, /device:TPU:56, one launch (start us, length us, event | category | flops | bytes accessed | tf_op | source)
XLA Modules:
  0.0 113.8 jit_solution(3445037289246511241)
XLA Ops:
  0.6 1.9 %shard_map.149 = bf16[1024,256]{1,0:T(8,128)(2,1)} custom-call(bf16[256,512]{1,0:T(8,128)(2,1)} %k_ref.1, bf16[256,512]{1,0:T(8,128)(2,1)} %v_ref.1), custom_call_target="tpu_custom_call" | custom-call | tf_op jit(solution)/shard_map/pallas_call | solution.py:205
  2.5 18.8 %all_to_all.34 = bf16[4,256,256]{2,1,0:T(8,128)(2,1)S(1)} all-to-all(bf16[4,256,256]{2,1,0:T(8,128)(2,1)} %bitcast.8), channel_id=1, replica_groups=mesh['batch'=16,'y'=4,'z'=8] {'y'}, dimensions={0} | all-to-all | bytes 1048576 | tf_op jit(solution)/shard_map/all_to_all | solution.py:219
  21.3 10.9 %collective-permute-start.1 = (bf16[1024,256]{1,0:T(8,128)(2,1)S(1)}, bf16[1024,256]{1,0:T(8,128)(2,1)S(1)}, u32[]{:S(2)}, u32[]{:S(2)}) collective-permute-start(bf16[1024,256]{1,0:T(8,128)(2,1)S(1)} %bitcast.11), channel_id=1, source_target_pairs={{0,7},{1,0},{2,1},{3,2},{4,3},{5,4},{6,5},{7,6},{8,15},{9,8},{10,9... | collective-permute-start | bytes 1572872 | tf_op jit(solution)/shard_map/ppermute | solution.py:215
  32.2 1.9 %collective-permute-start = (bf16[1024,256]{1,0:T(8,128)(2,1)S(1)}, bf16[1024,256]{1,0:T(8,128)(2,1)S(1)}, u32[]{:S(2)}, u32[]{:S(2)}) collective-permute-start(bf16[1024,256]{1,0:T(8,128)(2,1)S(1)} %bitcast.12), channel_id=1, source_target_pairs={{0,1},{1,2},{2,3},{3,4},{4,5},{5,6},{6,7},{7,0},{8,9},{9,10},{10,1... | collective-permute-start | bytes 1572872 | tf_op jit(solution)/shard_map/ppermute | solution.py:215
  34.2 1.7 %shard_map.150 = bf16[576,256]{1,0:T(8,128)(2,1)} custom-call(bf16[256,512]{1,0:T(8,128)(2,1)} %q_ref.1, bf16[32,512]{1,0:T(8,128)(2,1)} %cq.1), custom_call_target="tpu_custom_call" | custom-call | tf_op jit(solution)/shard_map/pallas_call | solution.py:205
  35.9 13.0 %all_to_all.35 = bf16[4,144,256]{2,1,0:T(8,128)(2,1)} all-to-all(bf16[4,144,256]{2,1,0:T(8,128)(2,1)} %bitcast.10), channel_id=1, replica_groups=mesh['batch'=16,'y'=4,'z'=8] {'y'}, dimensions={0} | all-to-all | bytes 589824 | tf_op jit(solution)/shard_map/all_to_all | solution.py:219
  48.9 1.9 %collective-permute-start.2 = (bf16[1024,256]{1,0:T(8,128)(2,1)S(1)}, bf16[1024,256]{1,0:T(8,128)(2,1)S(1)}, u32[]{:S(2)}, u32[]{:S(2)}) collective-permute-start(bf16[1024,256]{1,0:T(8,128)(2,1)S(1)} %collective-permute-done.refs_1_), channel_id=1, source_target_pairs={{0,1},{1,2},{2,3},{3,4},{4,5},{5,6},{6,7},{7,0},{8,9},{9,10},{10,1... | collective-permute-start | bytes 1572872 | tf_op jit(solution)/shard_map/ppermute | solution.py:215
  50.8 5.1 %collective-permute-start.3 = (bf16[1024,256]{1,0:T(8,128)(2,1)S(1)}, bf16[1024,256]{1,0:T(8,128)(2,1)S(1)}, u32[]{:S(2)}, u32[]{:S(2)}) collective-permute-start(bf16[1024,256]{1,0:T(8,128)(2,1)S(1)} %collective-permute-done.1.refs_2_), channel_id=1, source_target_pairs={{0,7},{1,0},{2,1},{3,2},{4,3},{5,4},{6,5},{7,6},{8,15},{9,8},{10,9... | collective-permute-start | bytes 1572872 | tf_op jit(solution)/shard_map/ppermute | solution.py:215
  56.8 0.7 reshape.18.user_ref
  58.1 5.8 %attend.4.refs_2_ = f32[1152,128]{1,0:T(8,128)} custom-call(s32[2]{0:T(128)} %pad_add_fusion.place_ref, s32[2]{0:T(128)} %start_ref.7, s32[2]{0:T(128)} %len_ref.7, bf16[576,256]{1,0:T(8,128)(2,1)} %bitcast.14, s32[128,1]{1,0:T(8,128)} %reshape.18.user_ref, bf16[1024,256]{1,0:T(8,128)(2,1)} %bitcast.13, bf16[1024,256]{1,0:T(8,128)(2,1)} %copy-done.7, ...), custom_call_target="tpu_custom_call" | custom-call | flops 1811939328 | bytes 3145728 | tf_op jit(solution)/shard_map/attend/pallas_call | solution.py:163
  63.9 1.1 collective-permute-done.2.refs_0_
  65.0 1.2 %collective-permute-done.3.refs_1_ = bf16[1024,256]{1,0:T(8,128)(2,1)S(1)} collective-permute-done((bf16[1024,256]{1,0:T(8,128)(2,1)S(1)}, bf16[1024,256]{1,0:T(8,128)(2,1)S(1)}, u32[]{:S(2)}, u32[]{:S(2)}) %collective-permute-start.3) | collective-permute-done | bytes 524320 | tf_op jit(solution)/shard_map/ppermute | solution.py:215
  66.2 1.9 %collective-permute-start.4 = (bf16[1024,256]{1,0:T(8,128)(2,1)S(1)}, bf16[1024,256]{1,0:T(8,128)(2,1)S(1)}, u32[]{:S(2)}, u32[]{:S(2)}) collective-permute-start(bf16[1024,256]{1,0:T(8,128)(2,1)S(1)} %collective-permute-done.2.refs_0_), channel_id=1, source_target_pairs={{0,1},{1,2},{2,3},{3,4},{4,5},{5,6},{6,7},{7,0},{8,9},{9,10},{10,1... | collective-permute-start | bytes 1572872 | tf_op jit(solution)/shard_map/ppermute | solution.py:215
  68.1 5.6 %collective-permute-start.5 = (bf16[1024,256]{1,0:T(8,128)(2,1)S(1)}, bf16[1024,256]{1,0:T(8,128)(2,1)S(1)}, u32[]{:S(2)}, u32[]{:S(2)}) collective-permute-start(bf16[1024,256]{1,0:T(8,128)(2,1)S(1)} %collective-permute-done.3.refs_1_), channel_id=1, source_target_pairs={{0,7},{1,0},{2,1},{3,2},{4,3},{5,4},{6,5},{7,6},{8,15},{9,8},{10,9... | collective-permute-start | bytes 1572872 | tf_op jit(solution)/shard_map/ppermute | solution.py:215
  73.8 4.3 %attend.5.refs_2_ = f32[1152,128]{1,0:T(8,128)} custom-call(s32[2]{0:T(128)} %pad_add_fusion.place_ref, s32[2]{0:T(128)} %start_ref.7, s32[2]{0:T(128)} %len_ref.7, bf16[576,256]{1,0:T(8,128)(2,1)} %bitcast.15, s32[128,1]{1,0:T(8,128)} %reshape.18.user_ref, bf16[1024,256]{1,0:T(8,128)(2,1)} %copy-done.5, bf16[1024,256]{1,0:T(8,128)(2,1)} %copy-done.6, ...), custom_call_target="tpu_custom_call" | custom-call | flops 1207959552 | bytes 2097152 | tf_op jit(solution)/shard_map/attend/pallas_call | solution.py:163
  78.0 3.9 %collective-permute-done.4.refs_0_ = bf16[1024,256]{1,0:T(8,128)(2,1)S(1)} collective-permute-done((bf16[1024,256]{1,0:T(8,128)(2,1)S(1)}, bf16[1024,256]{1,0:T(8,128)(2,1)S(1)}, u32[]{:S(2)}, u32[]{:S(2)}) %collective-permute-start.4) | collective-permute-done | bytes 524320 | tf_op jit(solution)/shard_map/ppermute | solution.py:215
  81.9 1.2 %collective-permute-done.5.refs_1_ = bf16[1024,256]{1,0:T(8,128)(2,1)S(1)} collective-permute-done((bf16[1024,256]{1,0:T(8,128)(2,1)S(1)}, bf16[1024,256]{1,0:T(8,128)(2,1)S(1)}, u32[]{:S(2)}, u32[]{:S(2)}) %collective-permute-start.5) | collective-permute-done | bytes 524320 | tf_op jit(solution)/shard_map/ppermute | solution.py:215
  83.1 0.7 copy-done.2
  83.9 2.5 %collective-permute-start.6 = (bf16[512,256]{1,0:T(8,128)(2,1)S(1)}, bf16[512,256]{1,0:T(8,128)(2,1)S(1)}, u32[]{:S(2)}, u32[]{:S(2)}) collective-permute-start(bf16[512,256]{1,0:T(8,128)(2,1)S(1)} %slice.6), channel_id=1, source_target_pairs={{0,1},{1,2},{2,3},{3,4},{4,5},{5,6},{6,7},{7,0},{8,9},{9,10},{10,1... | collective-permute-start | bytes 786440 | tf_op jit(solution)/shard_map/ppermute | solution.py:215
  86.4 5.0 %collective-permute-start.7 = (bf16[512,256]{1,0:T(8,128)(2,1)S(1)}, bf16[512,256]{1,0:T(8,128)(2,1)S(1)}, u32[]{:S(2)}, u32[]{:S(2)}) collective-permute-start(bf16[512,256]{1,0:T(8,128)(2,1)S(1)} %slice.7), channel_id=1, source_target_pairs={{0,7},{1,0},{2,1},{3,2},{4,3},{5,4},{6,5},{7,6},{8,15},{9,8},{10,9... | collective-permute-start | bytes 786440 | tf_op jit(solution)/shard_map/ppermute | solution.py:215
  91.4 4.3 %attend.6.refs_2_ = f32[1152,128]{1,0:T(8,128)} custom-call(s32[2]{0:T(128)} %pad_add_fusion.place_ref, s32[2]{0:T(128)} %start_ref.7, s32[2]{0:T(128)} %len_ref.7, bf16[576,256]{1,0:T(8,128)(2,1)} %bitcast.16, s32[128,1]{1,0:T(8,128)} %reshape.18.user_ref, bf16[1024,256]{1,0:T(8,128)(2,1)} %copy-done.1, bf16[1024,256]{1,0:T(8,128)(2,1)} %copy-done.2, ...), custom_call_target="tpu_custom_call" | custom-call | flops 1207959552 | bytes 2097152 | tf_op jit(solution)/shard_map/attend/pallas_call | solution.py:163
  97.0 3.1 %attend.7 = bf16[576,256]{1,0:T(8,128)(2,1)} custom-call(s32[2]{0:T(128)} %pad_add_fusion.place_ref, s32[2]{0:T(128)} %start_ref.7, s32[2]{0:T(128)} %len_ref.7, bf16[576,256]{1,0:T(8,128)(2,1)} %bitcast.17, s32[128,1]{1,0:T(8,128)} %reshape.18.user_ref, bf16[512,256]{1,0:T(8,128)(2,1)} %copy-done.8, bf16[512,256]{1,0:T(8,128)(2,1)} %copy-done.9, ...), custom_call_target="tpu_custom_call" | custom-call | flops 603979776 | bytes 1048576 | tf_op jit(solution)/shard_map/attend/pallas_call | solution.py:163
  100.2 10.5 %all_to_all.36 = bf16[4,144,256]{2,1,0:T(8,128)(2,1)} all-to-all(bf16[4,144,256]{2,1,0:T(8,128)(2,1)} %bitcast.18), channel_id=1, replica_groups=mesh['batch'=16,'y'=4,'z'=8] {'y'}, dimensions={0} | all-to-all | bytes 589824 | tf_op jit(solution)/shard_map/all_to_all | solution.py:219
  110.6 3.2 %shard_map.151 = (bf16[256,1024]{1,0:T(8,128)(2,1)}, bf16[32,1024]{1,0:T(8,128)(2,1)}) custom-call(bf16[576,256]{1,0:T(8,128)(2,1)} %bitcast.9, bf16[256,512]{1,0:T(8,128)(2,1)} %hg.1, bf16[256,1024]{1,0:T(8,128)(2,1)} %hx.1, bf16[32,512]{1,0:T(8,128)(2,1)} %cq.1, bf16[32,512]{1,0:T(8,128)(2,1)} %ck.1, bf16[32,512]{1,0:T(8,128)(2,1)} %cv.1, ...), custom_call_target="tpu_custom_call" | custom-call | tf_op jit(solution)/shard_map/pallas_call | solution.py:205
  (28 shorter events, 2.9 us)
Async XLA Ops:
  21.3 27.6 %copy-start = (bf16[4,256,256]{2,1,0:T(8,128)(2,1)}, bf16[4,256,256]{2,1,0:T(8,128)(2,1)S(1)}, u32[]{:S(2)}) copy-start(bf16[4,256,256]{2,1,0:T(8,128)(2,1)S(1)} %all_to_all.34) | copy-start | bytes 1572868
  21.3 27.6 %collective-permute-start.1 = (bf16[1024,256]{1,0:T(8,128)(2,1)S(1)}, bf16[1024,256]{1,0:T(8,128)(2,1)S(1)}, u32[]{:S(2)}, u32[]{:S(2)}) collective-permute-start(bf16[1024,256]{1,0:T(8,128)(2,1)S(1)} %bitcast.11), channel_id=1, source_target_pairs={{0,7},{1,0},{2,1},{3,2},{4,3},{5,4},{6,5},{7,6},{8,15},{9,8},{10,9... | collective-permute-start | bytes 1572872 | tf_op jit(solution)/shard_map/ppermute | solution.py:215
  32.2 16.6 %collective-permute-start = (bf16[1024,256]{1,0:T(8,128)(2,1)S(1)}, bf16[1024,256]{1,0:T(8,128)(2,1)S(1)}, u32[]{:S(2)}, u32[]{:S(2)}) collective-permute-start(bf16[1024,256]{1,0:T(8,128)(2,1)S(1)} %bitcast.12), channel_id=1, source_target_pairs={{0,1},{1,2},{2,3},{3,4},{4,5},{5,6},{6,7},{7,0},{8,9},{9,10},{10,1... | collective-permute-start | bytes 1572872 | tf_op jit(solution)/shard_map/ppermute | solution.py:215
  48.9 9.3 %copy-start.4 = (bf16[1024,256]{1,0:T(8,128)(2,1)}, bf16[1024,256]{1,0:T(8,128)(2,1)S(1)}, u32[]{:S(2)}) copy-start(bf16[1024,256]{1,0:T(8,128)(2,1)S(1)} %collective-permute-done.1.refs_2_) | copy-start | bytes 1572868
  48.9 9.3 %copy-start.7 = (bf16[1024,256]{1,0:T(8,128)(2,1)}, bf16[1024,256]{1,0:T(8,128)(2,1)S(1)}, u32[]{:S(2)}) copy-start(bf16[1024,256]{1,0:T(8,128)(2,1)S(1)} %collective-permute-done.refs_1_) | copy-start | bytes 1572868
  48.9 16.1 %collective-permute-start.2 = (bf16[1024,256]{1,0:T(8,128)(2,1)S(1)}, bf16[1024,256]{1,0:T(8,128)(2,1)S(1)}, u32[]{:S(2)}, u32[]{:S(2)}) collective-permute-start(bf16[1024,256]{1,0:T(8,128)(2,1)S(1)} %collective-permute-done.refs_1_), channel_id=1, source_target_pairs={{0,1},{1,2},{2,3},{3,4},{4,5},{5,6},{6,7},{7,0},{8,9},{9,10},{10,1... | collective-permute-start | bytes 1572872 | tf_op jit(solution)/shard_map/ppermute | solution.py:215
  50.8 15.4 %collective-permute-start.3 = (bf16[1024,256]{1,0:T(8,128)(2,1)S(1)}, bf16[1024,256]{1,0:T(8,128)(2,1)S(1)}, u32[]{:S(2)}, u32[]{:S(2)}) collective-permute-start(bf16[1024,256]{1,0:T(8,128)(2,1)S(1)} %collective-permute-done.1.refs_2_), channel_id=1, source_target_pairs={{0,7},{1,0},{2,1},{3,2},{4,3},{5,4},{6,5},{7,6},{8,15},{9,8},{10,9... | collective-permute-start | bytes 1572872 | tf_op jit(solution)/shard_map/ppermute | solution.py:215
  56.0 0.7 copy-start.3
  65.0 8.7 %copy-start.5 = (bf16[1024,256]{1,0:T(8,128)(2,1)}, bf16[1024,256]{1,0:T(8,128)(2,1)S(1)}, u32[]{:S(2)}) copy-start(bf16[1024,256]{1,0:T(8,128)(2,1)S(1)} %collective-permute-done.2.refs_0_) | copy-start | bytes 1572868
  66.2 7.5 %copy-start.6 = (bf16[1024,256]{1,0:T(8,128)(2,1)}, bf16[1024,256]{1,0:T(8,128)(2,1)S(1)}, u32[]{:S(2)}) copy-start(bf16[1024,256]{1,0:T(8,128)(2,1)S(1)} %collective-permute-done.3.refs_1_) | copy-start | bytes 1572868
  66.2 15.7 %collective-permute-start.4 = (bf16[1024,256]{1,0:T(8,128)(2,1)S(1)}, bf16[1024,256]{1,0:T(8,128)(2,1)S(1)}, u32[]{:S(2)}, u32[]{:S(2)}) collective-permute-start(bf16[1024,256]{1,0:T(8,128)(2,1)S(1)} %collective-permute-done.2.refs_0_), channel_id=1, source_target_pairs={{0,1},{1,2},{2,3},{3,4},{4,5},{5,6},{6,7},{7,0},{8,9},{9,10},{10,1... | collective-permute-start | bytes 1572872 | tf_op jit(solution)/shard_map/ppermute | solution.py:215
  68.1 14.9 %collective-permute-start.5 = (bf16[1024,256]{1,0:T(8,128)(2,1)S(1)}, bf16[1024,256]{1,0:T(8,128)(2,1)S(1)}, u32[]{:S(2)}, u32[]{:S(2)}) collective-permute-start(bf16[1024,256]{1,0:T(8,128)(2,1)S(1)} %collective-permute-done.3.refs_1_), channel_id=1, source_target_pairs={{0,7},{1,0},{2,1},{3,2},{4,3},{5,4},{6,5},{7,6},{8,15},{9,8},{10,9... | collective-permute-start | bytes 1572872 | tf_op jit(solution)/shard_map/ppermute | solution.py:215
  81.9 1.2 %copy-start.1 = (bf16[1024,256]{1,0:T(8,128)(2,1)}, bf16[1024,256]{1,0:T(8,128)(2,1)S(1)}, u32[]{:S(2)}) copy-start(bf16[1024,256]{1,0:T(8,128)(2,1)S(1)} %collective-permute-done.4.refs_0_) | copy-start | bytes 1572868
  83.1 0.8 copy-start.2
  83.9 11.8 %collective-permute-start.6 = (bf16[512,256]{1,0:T(8,128)(2,1)S(1)}, bf16[512,256]{1,0:T(8,128)(2,1)S(1)}, u32[]{:S(2)}, u32[]{:S(2)}) collective-permute-start(bf16[512,256]{1,0:T(8,128)(2,1)S(1)} %slice.6), channel_id=1, source_target_pairs={{0,1},{1,2},{2,3},{3,4},{4,5},{5,6},{6,7},{7,0},{8,9},{9,10},{10,1... | collective-permute-start | bytes 786440 | tf_op jit(solution)/shard_map/ppermute | solution.py:215
  86.4 9.3 %collective-permute-start.7 = (bf16[512,256]{1,0:T(8,128)(2,1)S(1)}, bf16[512,256]{1,0:T(8,128)(2,1)S(1)}, u32[]{:S(2)}, u32[]{:S(2)}) collective-permute-start(bf16[512,256]{1,0:T(8,128)(2,1)S(1)} %slice.7), channel_id=1, source_target_pairs={{0,7},{1,0},{2,1},{3,2},{4,3},{5,4},{6,5},{7,6},{8,15},{9,8},{10,9... | collective-permute-start | bytes 786440 | tf_op jit(solution)/shard_map/ppermute | solution.py:215
  95.7 0.7 copy-start.8
  96.3 0.7 copy-start.9

commit v4 on v3

--- a/solution.py
+++ b/solution.py
@@ -17,12 +17,13 @@
 QROWS = ROWS + CROWS
 FOLD = QROWS // 2
 REST = ROWS - FOLD
+PART = ROWS + FOLD
 BLOCK = 128
 KEYS = NY * ROWS
 TOTAL = KEYS + NY * CROWS
 NOBODY = 1 << 30
 HALF = 1.0 / (2.0 * math.sqrt(DH))
-VMEM_LIMIT = 60 * 1024 * 1024
+VMEM_LIMIT = 16 * 1024 * 1024
 VMEM = pl.BlockSpec(memory_space=pltpu.VMEM)
 SMEM = pl.BlockSpec(memory_space=pltpu.SMEM)
 PARAMS = pltpu.CompilerParams(vmem_limit_bytes=VMEM_LIMIT)
@@ -37,19 +38,16 @@
     return (half * jnp.tanh(half) + half).astype(jnp.bfloat16)
 
 
-def split_kernel(k_ref, v_ref, kv_ref):
+def split_kernel(k_ref, v_ref, q_ref, c_ref, out_ref):
     for h in range(HEADS):
         at = slice(h * DH, (h + 1) * DH)
-        kv_ref[h * ROWS : (h + 1) * ROWS, 0:DH] = k_ref[:, at]
-        kv_ref[h * ROWS : (h + 1) * ROWS, DH : 2 * DH] = v_ref[:, at]
-
-
-def fold_kernel(q_ref, c_ref, out_ref):
-    for h in range(HEADS):
-        at = slice(h * DH, (h + 1) * DH)
-        out_ref[h * FOLD : (h + 1) * FOLD, 0:DH] = q_ref[0:FOLD, at]
-        out_ref[h * FOLD : h * FOLD + REST, DH : 2 * DH] = q_ref[FOLD:ROWS, at]
-        out_ref[h * FOLD + REST : (h + 1) * FOLD, DH : 2 * DH] = c_ref[:, at]
+        row = h * PART
+        out_ref[row : row + ROWS, 0:DH] = k_ref[:, at]
+        out_ref[row : row + ROWS, DH : 2 * DH] = v_ref[:, at]
+        row += ROWS
+        out_ref[row : row + FOLD, 0:DH] = q_ref[0:FOLD, at]
+        out_ref[row : row + REST, DH : 2 * DH] = q_ref[FOLD:ROWS, at]
+        out_ref[row + REST : row + FOLD, DH : 2 * DH] = c_ref[:, at]
 
 
 def attend_kernel(offsets, first, last, place_ref, start_ref, len_ref, q_ref, user_ref, *refs):
@@ -59,7 +57,7 @@
     if not first:
         in_ref, *refs = refs
     out_ref, kv, qs, acc = refs
-    z = place_ref[1]
+    z = place_ref[0]
     starts = [start_ref[u] for u in range(2)]
     ends = [start_ref[u] + len_ref[u] for u in range(2)]
 
@@ -67,9 +65,10 @@
     for i, ref in enumerate(kv_refs):
         kv[i * size : (i + 1) * size, :] = ref[...]
     for s in range(NY):
-        qs[s * ROWS : s * ROWS + FOLD, :] = q_ref[s * FOLD : (s + 1) * FOLD, 0:DH]
-        qs[s * ROWS + FOLD : (s + 1) * ROWS, :] = q_ref[s * FOLD : s * FOLD + REST, DH : 2 * DH]
-        qs[KEYS + s * CROWS : KEYS + (s + 1) * CROWS, :] = q_ref[s * FOLD + REST : (s + 1) * FOLD, DH : 2 * DH]
+        row = s * PART + ROWS
+        qs[s * ROWS : s * ROWS + FOLD, :] = q_ref[row : row + FOLD, 0:DH]
+        qs[s * ROWS + FOLD : (s + 1) * ROWS, :] = q_ref[row : row + REST, DH : 2 * DH]
+        qs[KEYS + s * CROWS : KEYS + (s + 1) * CROWS, :] = q_ref[row + REST : row + FOLD, DH : 2 * DH]
     if first:
         acc[...] = jnp.zeros_like(acc)
     else:
@@ -128,7 +127,7 @@
 
     lax.fori_loop(0, len(offsets), step, 0)
 
-    if offsets[0] == 0:
+    if first:
         at = lax.broadcasted_iota(jnp.int32, (BLOCK, ROWS), 0)
         to = lax.broadcasted_iota(jnp.int32, (BLOCK, ROWS), 1)
         for s in range(NY):
@@ -225,22 +224,23 @@
     cand_user, hist_len, hist_start, out_weight,
 ):
     z = lax.axis_index("z")
-    where = (jnp.stack([lax.axis_index("y"), z]).astype(jnp.int32), hist_start, hist_len)
+    where = (z.astype(jnp.int32).reshape(1), hist_start, hist_len)
     users = lax.dynamic_index_in_dim(cand_user.reshape(NY, NZ, CROWS), z, axis=1).reshape(NY * CROWS, 1)
-    (own,) = call(split_kernel, [(KEYS, 2 * DH)], hist_key, hist_value)
-    own = spread(own)
-    (folded,) = call(fold_kernel, [(HEADS * FOLD, 2 * DH)], hist_query, cand_query)
-    up1, down1 = turn(own, 1), turn(own, -1)
-    queries = spread(folded)
-    up1, down1, queries = lax.optimization_barrier((up1, down1, queries))
-    up2, down2 = turn(up1, 1), turn(down1, -1)
-    total = attend((0, 7, 1), where, queries, users, (own, up1, down1), None, False)
-    up2, down2, total = lax.optimization_barrier((up2, down2, total))
-    up3, down3 = turn(up2, 1), turn(down2, -1)
-    total = attend((6, 2), where, queries, users, (up2, down2), total, False)
-    up3, down3, total = lax.optimization_barrier((up3, down3, total))
-    low, high = turn(up3[: KEYS // 2], 1), turn(down3[KEYS // 2 :], -1)
-    total = attend((5, 3), where, queries, users, (up3, down3), total, False)
+    (parts,) = call(split_kernel, [(HEADS * PART, 2 * DH)], hist_key, hist_value, hist_query, cand_query)
+    queries = spread(parts)
+    own = queries.reshape(NY, PART, 2 * DH)[:, :ROWS].reshape(KEYS, 2 * DH)
+    up, down = turn(own, 1), turn(own, -1)
+    total = attend((0,), where, queries, users, (own,), None, False)
+    for step in (1, 2):
+        up, held = lax.optimization_barrier((up, total))
+        down, total = lax.optimization_barrier((down, held))
+        blocks = (up, down)
+        up, down = turn(up, 1), turn(down, -1)
+        total = attend((NZ - step, step), where, queries, users, blocks, total, False)
+    up, held = lax.optimization_barrier((up, total))
+    down, total = lax.optimization_barrier((down, held))
+    low, high = turn(up[: KEYS // 2], 1), turn(down[KEYS // 2 :], -1)
+    total = attend((NZ - 3, 3), where, queries, users, (up, down), total, False)
     total = attend((4,), where, queries, users, (low, high), total, True)
     return tuple(
         call(

time: 115 us -> 109 us (0.948)
  waiting for transfers between devices: 7.33 us -> 20.6 us
  Pallas kernels: 24.2 us -> 12.8 us
  blocking collectives: 42.2 us -> 34.3 us
  local copies, waits for them, and re-layouts: 3.71 us -> 5.25 us
    ppermute x8, waiting for transfers between devices: 7.33 us -> 20.6 us  [turn(): return lax.ppermute(array, 'z', [(i, (i + step) % NZ) for i in range(NZ)])]
    all_to_all x3 -> x2, blocking collectives: 42.2 us -> 34.3 us  [spread(): return lax.all_to_all(array, 'y', 0, 0, tiled=True)]
    pallas_call x4 -> x5, Pallas kernels: 17.4 us -> 11.2 us  [attend(): pl.pallas_call(functools.partial(attend_kernel, offsets, first, last), in...]
    pallas_call x3 -> x2, Pallas kernels: 6.77 us -> 1.64 us  [call(): pl.pallas_call(kernel, in_specs=[VMEM] * len(args), out_specs=[VMEM] * le...]
    unnamed x20 -> x30, local copies, waits for them, and re-layouts: 2.83 us -> 4.98 us
  transfers between devices with their start and end apart: 8 -> 8, of which waited for: 4 -> 5; matrix products, arithmetic and copies ran while one was open for 1% -> 0% of each run, Pallas kernels for 14% -> 9%
where the time goes in v4:
time: 109 us; the launch traced here: 108 us
  starting transfers between devices  34.5 us (32%)
  blocking collectives  34.3 us (31%)
  waiting for transfers between devices  20.6 us (19%)
  Pallas kernels  12.8 us (12%)
  local copies, waits for them, and re-layouts  5.25 us (5%)
    ppermute x8, starting transfers between devices, turn(): return lax.ppermute(array, 'z', [(i, (i + step) % NZ) for i in range(NZ)])  34.5 us
    all_to_all x2, blocking collectives, spread(): return lax.all_to_all(array, 'y', 0, 0, tiled=True)  34.3 us
    ppermute x8, waiting for transfers between devices, turn(): return lax.ppermute(array, 'z', [(i, (i + step) % NZ) for i in range(NZ)])  20.6 us
    pallas_call x5, Pallas kernels, attend(): pl.pallas_call(functools.partial(attend_kernel, offsets, first, last), in...  11.2 us
    unnamed x30, local copies, waits for them, and re-layouts  4.98 us
  transfers between devices with their start and end apart: 8, of which 5 were waited for; matrix products, arithmetic and copies ran while one was open for 0% of the time, Pallas kernels for 9%

profile of v4, /device:TPU:56, one launch (start us, length us, event | category | flops | bytes accessed | tf_op | source)
XLA Modules:
  0.0 108.4 jit_solution(9705591030255661405)
XLA Ops:
  0.6 0.9 copy-done.2
  1.6 0.9 copy-done.3
  2.5 0.9 copy-done.4
  4.4 24.0 %all_to_all.22 = bf16[4,400,256]{2,1,0:T(8,128)(2,1)S(1)} all-to-all(bf16[4,400,256]{2,1,0:T(8,128)(2,1)S(1)} %bitcast.11), channel_id=1, replica_groups=mesh['batch'=16,'y'=4,'z'=8] {'y'}, dimensions={0} | all-to-all | bytes 1638400 | tf_op jit(solution)/shard_map/all_to_all | solution.py:218
  28.5 4.3 %collective-permute-start = (bf16[1024,256]{1,0:T(8,128)(2,1)S(1)}, bf16[1024,256]{1,0:T(8,128)(2,1)S(1)}, u32[]{:S(2)}, u32[]{:S(2)}) collective-permute-start(bf16[1024,256]{1,0:T(8,128)(2,1)S(1)} %bitcast.14), channel_id=1, source_target_pairs={{0,1},{1,2},{2,3},{3,4},{4,5},{5,6},{6,7},{7,0},{8,9},{9,10},{10,1... | collective-permute-start | bytes 1572872 | tf_op jit(solution)/shard_map/ppermute | solution.py:214
  32.7 8.6 %collective-permute-start.2 = (bf16[1024,256]{1,0:T(8,128)(2,1)S(1)}, bf16[1024,256]{1,0:T(8,128)(2,1)S(1)}, u32[]{:S(2)}, u32[]{:S(2)}) collective-permute-start(bf16[1024,256]{1,0:T(8,128)(2,1)S(1)} %bitcast.15), channel_id=1, source_target_pairs={{0,7},{1,0},{2,1},{3,2},{4,3},{5,4},{6,5},{7,6},{8,15},{9,8},{10,9... | collective-permute-start | bytes 1572872 | tf_op jit(solution)/shard_map/ppermute | solution.py:214
  42.9 2.2 %attend.5.refs_2_ = f32[1152,128]{1,0:T(8,128)S(1)} custom-call(s32[1]{0:T(128)} %bitcast.place_ref, s32[2]{0:T(128)S(1)} %copy-done.12, s32[2]{0:T(128)S(1)} %copy-done.13, bf16[1600,256]{1,0:T(8,128)(2,1)S(1)} %bitcast.6, s32[128,1]{1,0:T(8,128)S(1)} %reshape.26.user_ref, bf16[1024,256]{1,0:T(8,128)(2,1)S(1)} %bitcast.16), custom_call_target="tpu_custom_call" | custom-call | flops 603979776 | bytes 1048576 | tf_op jit(solution)/shard_map/attend/pallas_call | solution.py:162
  45.1 6.0 %collective-permute-done.refs_0_ = bf16[1024,256]{1,0:T(8,128)(2,1)S(1)} collective-permute-done((bf16[1024,256]{1,0:T(8,128)(2,1)S(1)}, bf16[1024,256]{1,0:T(8,128)(2,1)S(1)}, u32[]{:S(2)}, u32[]{:S(2)}) %collective-permute-start) | collective-permute-done | bytes 524320 | tf_op jit(solution)/shard_map/ppermute | solution.py:214
  51.1 1.9 %collective-permute-start.1 = (bf16[1024,256]{1,0:T(8,128)(2,1)S(1)}, bf16[1024,256]{1,0:T(8,128)(2,1)S(1)}, u32[]{:S(2)}, u32[]{:S(2)}) collective-permute-start(bf16[1024,256]{1,0:T(8,128)(2,1)S(1)} %collective-permute-done.refs_0_), channel_id=1, source_target_pairs={{0,1},{1,2},{2,3},{3,4},{4,5},{5,6},{6,7},{7,0},{8,9},{9,10},{10,1... | collective-permute-start | bytes 1572872 | tf_op jit(solution)/shard_map/ppermute | solution.py:214
  53.1 5.1 %collective-permute-start.4 = (bf16[1024,256]{1,0:T(8,128)(2,1)S(1)}, bf16[1024,256]{1,0:T(8,128)(2,1)S(1)}, u32[]{:S(2)}, u32[]{:S(2)}) collective-permute-start(bf16[1024,256]{1,0:T(8,128)(2,1)S(1)} %collective-permute-done.2.refs_1_), channel_id=1, source_target_pairs={{0,7},{1,0},{2,1},{3,2},{4,3},{5,4},{6,5},{7,6},{8,15},{9,8},{10,9... | collective-permute-start | bytes 1572872 | tf_op jit(solution)/shard_map/ppermute | solution.py:214
  58.2 2.5 %attend.6.refs_2_ = f32[1152,128]{1,0:T(8,128)S(1)} custom-call(s32[1]{0:T(128)} %bitcast.place_ref, s32[2]{0:T(128)S(1)} %copy-done.12, s32[2]{0:T(128)S(1)} %copy-done.13, bf16[1600,256]{1,0:T(8,128)(2,1)S(1)} %bitcast.7, s32[128,1]{1,0:T(8,128)S(1)} %reshape.26.user_ref, bf16[1024,256]{1,0:T(8,128)(2,1)S(1)} %collective-permute-done.refs_0_, ...), custom_call_target="tpu_custom_call" | custom-call | flops 1207959552 | bytes 2097152 | tf_op jit(solution)/shard_map/attend/pallas_call | solution.py:162
  60.7 6.5 %collective-permute-done.1.refs_0_ = bf16[1024,256]{1,0:T(8,128)(2,1)S(1)} collective-permute-done((bf16[1024,256]{1,0:T(8,128)(2,1)S(1)}, bf16[1024,256]{1,0:T(8,128)(2,1)S(1)}, u32[]{:S(2)}, u32[]{:S(2)}) %collective-permute-start.1) | collective-permute-done | bytes 524320 | tf_op jit(solution)/shard_map/ppermute | solution.py:214
  67.2 1.9 %collective-permute-start.3 = (bf16[1024,256]{1,0:T(8,128)(2,1)S(1)}, bf16[1024,256]{1,0:T(8,128)(2,1)S(1)}, u32[]{:S(2)}, u32[]{:S(2)}) collective-permute-start(bf16[1024,256]{1,0:T(8,128)(2,1)S(1)} %collective-permute-done.1.refs_0_), channel_id=1, source_target_pairs={{0,1},{1,2},{2,3},{3,4},{4,5},{5,6},{6,7},{7,0},{8,9},{9,10},{10,1... | collective-permute-start | bytes 1572872 | tf_op jit(solution)/shard_map/ppermute | solution.py:214
  69.1 5.1 %collective-permute-start.6 = (bf16[1024,256]{1,0:T(8,128)(2,1)S(1)}, bf16[1024,256]{1,0:T(8,128)(2,1)S(1)}, u32[]{:S(2)}, u32[]{:S(2)}) collective-permute-start(bf16[1024,256]{1,0:T(8,128)(2,1)S(1)} %collective-permute-done.4.refs_1_), channel_id=1, source_target_pairs={{0,7},{1,0},{2,1},{3,2},{4,3},{5,4},{6,5},{7,6},{8,15},{9,8},{10,9... | collective-permute-start | bytes 1572872 | tf_op jit(solution)/shard_map/ppermute | solution.py:214
  74.2 2.5 %attend.7.refs_2_ = f32[1152,128]{1,0:T(8,128)S(1)} custom-call(s32[1]{0:T(128)} %bitcast.place_ref, s32[2]{0:T(128)S(1)} %copy-done.12, s32[2]{0:T(128)S(1)} %copy-done.13, bf16[1600,256]{1,0:T(8,128)(2,1)S(1)} %bitcast.8, s32[128,1]{1,0:T(8,128)S(1)} %reshape.26.user_ref, bf16[1024,256]{1,0:T(8,128)(2,1)S(1)} %collective-permute-done.1.refs_0_, ...), custom_call_target="tpu_custom_call" | custom-call | flops 1207959552 | bytes 2097152 | tf_op jit(solution)/shard_map/attend/pallas_call | solution.py:162
  76.7 5.5 %collective-permute-done.3.refs_0_ = bf16[1024,256]{1,0:T(8,128)(2,1)S(1)} collective-permute-done((bf16[1024,256]{1,0:T(8,128)(2,1)S(1)}, bf16[1024,256]{1,0:T(8,128)(2,1)S(1)}, u32[]{:S(2)}, u32[]{:S(2)}) %collective-permute-start.3) | collective-permute-done | bytes 524320 | tf_op jit(solution)/shard_map/ppermute | solution.py:214
  82.2 1.2 %collective-permute-done.6.refs_1_ = bf16[1024,256]{1,0:T(8,128)(2,1)S(1)} collective-permute-done((bf16[1024,256]{1,0:T(8,128)(2,1)S(1)}, bf16[1024,256]{1,0:T(8,128)(2,1)S(1)}, u32[]{:S(2)}, u32[]{:S(2)}) %collective-permute-start.6) | collective-permute-done | bytes 524320 | tf_op jit(solution)/shard_map/ppermute | solution.py:214
  83.5 1.9 %collective-permute-start.5 = (bf16[512,256]{1,0:T(8,128)(2,1)S(1)}, bf16[512,256]{1,0:T(8,128)(2,1)S(1)}, u32[]{:S(2)}, u32[]{:S(2)}) collective-permute-start(bf16[512,256]{1,0:T(8,128)(2,1)S(1)} %slice.10), channel_id=1, source_target_pairs={{0,1},{1,2},{2,3},{3,4},{4,5},{5,6},{6,7},{7,0},{8,9},{9,10},{10,1... | collective-permute-start | bytes 786440 | tf_op jit(solution)/shard_map/ppermute | solution.py:214
  85.4 5.6 %collective-permute-start.7 = (bf16[512,256]{1,0:T(8,128)(2,1)S(1)}, bf16[512,256]{1,0:T(8,128)(2,1)S(1)}, u32[]{:S(2)}, u32[]{:S(2)}) collective-permute-start(bf16[512,256]{1,0:T(8,128)(2,1)S(1)} %slice.11), channel_id=1, source_target_pairs={{0,7},{1,0},{2,1},{3,2},{4,3},{5,4},{6,5},{7,6},{8,15},{9,8},{10,9... | collective-permute-start | bytes 786440 | tf_op jit(solution)/shard_map/ppermute | solution.py:214
  91.0 2.5 %attend.8.refs_2_ = f32[1152,128]{1,0:T(8,128)S(1)} custom-call(s32[1]{0:T(128)} %bitcast.place_ref, s32[2]{0:T(128)S(1)} %copy-done.12, s32[2]{0:T(128)S(1)} %copy-done.13, bf16[1600,256]{1,0:T(8,128)(2,1)S(1)} %bitcast.9, s32[128,1]{1,0:T(8,128)S(1)} %reshape.26.user_ref, bf16[1024,256]{1,0:T(8,128)(2,1)S(1)} %collective-permute-done.3.refs_0_, ...), custom_call_target="tpu_custom_call" | custom-call | flops 1207959552 | bytes 2097152 | tf_op jit(solution)/shard_map/attend/pallas_call | solution.py:162
  93.5 1.4 %collective-permute-done.7.refs_1_ = bf16[512,256]{1,0:T(8,128)(2,1)S(1)} collective-permute-done((bf16[512,256]{1,0:T(8,128)(2,1)S(1)}, bf16[512,256]{1,0:T(8,128)(2,1)S(1)}, u32[]{:S(2)}, u32[]{:S(2)}) %collective-permute-start.7) | collective-permute-done | bytes 262176 | tf_op jit(solution)/shard_map/ppermute | solution.py:214
  94.9 1.6 %attend.9 = bf16[576,256]{1,0:T(8,128)(2,1)S(1)} custom-call(s32[1]{0:T(128)} %bitcast.place_ref, s32[2]{0:T(128)S(1)} %copy-done.12, s32[2]{0:T(128)S(1)} %copy-done.13, bf16[1600,256]{1,0:T(8,128)(2,1)S(1)} %bitcast.10, s32[128,1]{1,0:T(8,128)S(1)} %reshape.26.user_ref, bf16[512,256]{1,0:T(8,128)(2,1)S(1)} %collective-permute-done.5.refs_0_, ...), custom_call_target="tpu_custom_call" | custom-call | flops 603979776 | bytes 1048576 | tf_op jit(solution)/shard_map/attend/pallas_call | solution.py:162
  96.6 10.3 %all_to_all.23 = bf16[4,144,256]{2,1,0:T(8,128)(2,1)S(1)} all-to-all(bf16[4,144,256]{2,1,0:T(8,128)(2,1)S(1)} %bitcast.12), channel_id=1, replica_groups=mesh['batch'=16,'y'=4,'z'=8] {'y'}, dimensions={0} | all-to-all | bytes 589824 | tf_op jit(solution)/shard_map/all_to_all | solution.py:218
  106.9 1.5 %shard_map.150 = (bf16[256,1024]{1,0:T(8,128)(2,1)}, bf16[32,1024]{1,0:T(8,128)(2,1)}) custom-call(bf16[576,256]{1,0:T(8,128)(2,1)S(1)} %bitcast.13, bf16[256,512]{1,0:T(8,128)(2,1)S(1)} %copy-done.5, bf16[256,1024]{1,0:T(8,128)(2,1)S(1)} %copy-done.1, bf16[32,512]{1,0:T(8,128)(2,1)S(1)} %copy-done.7, bf16[32,512]{1,0:T(8,128)(2,1)S(1)} %copy-done.9, ...), custom_call_target="tpu_custom_call" | custom-call | tf_op jit(solution)/shard_map/pallas_call | solution.py:204
  (37 shorter events, 2.6 us)
Async XLA Ops:
  0.6 1.0 copy-start.2
  1.6 0.9 copy-start.3
  2.5 0.9 copy-start.4
  3.5 0.8 copy-start.6
  28.5 22.7 %collective-permute-start = (bf16[1024,256]{1,0:T(8,128)(2,1)S(1)}, bf16[1024,256]{1,0:T(8,128)(2,1)S(1)}, u32[]{:S(2)}, u32[]{:S(2)}) collective-permute-start(bf16[1024,256]{1,0:T(8,128)(2,1)S(1)} %bitcast.14), channel_id=1, source_target_pairs={{0,1},{1,2},{2,3},{3,4},{4,5},{5,6},{6,7},{7,0},{8,9},{9,10},{10,1... | collective-permute-start | bytes 1572872 | tf_op jit(solution)/shard_map/ppermute | solution.py:214
  32.7 20.3 %collective-permute-start.2 = (bf16[1024,256]{1,0:T(8,128)(2,1)S(1)}, bf16[1024,256]{1,0:T(8,128)(2,1)S(1)}, u32[]{:S(2)}, u32[]{:S(2)}) collective-permute-start(bf16[1024,256]{1,0:T(8,128)(2,1)S(1)} %bitcast.15), channel_id=1, source_target_pairs={{0,7},{1,0},{2,1},{3,2},{4,3},{5,4},{6,5},{7,6},{8,15},{9,8},{10,9... | collective-permute-start | bytes 1572872 | tf_op jit(solution)/shard_map/ppermute | solution.py:214
  41.3 0.7 copy-start.14
  42.2 0.7 copy-start.12
  42.3 0.7 copy-start.13
  51.1 16.0 %collective-permute-start.1 = (bf16[1024,256]{1,0:T(8,128)(2,1)S(1)}, bf16[1024,256]{1,0:T(8,128)(2,1)S(1)}, u32[]{:S(2)}, u32[]{:S(2)}) collective-permute-start(bf16[1024,256]{1,0:T(8,128)(2,1)S(1)} %collective-permute-done.refs_0_), channel_id=1, source_target_pairs={{0,1},{1,2},{2,3},{3,4},{4,5},{5,6},{6,7},{7,0},{8,9},{9,10},{10,1... | collective-permute-start | bytes 1572872 | tf_op jit(solution)/shard_map/ppermute | solution.py:214
  53.1 16.0 %collective-permute-start.4 = (bf16[1024,256]{1,0:T(8,128)(2,1)S(1)}, bf16[1024,256]{1,0:T(8,128)(2,1)S(1)}, u32[]{:S(2)}, u32[]{:S(2)}) collective-permute-start(bf16[1024,256]{1,0:T(8,128)(2,1)S(1)} %collective-permute-done.2.refs_1_), channel_id=1, source_target_pairs={{0,7},{1,0},{2,1},{3,2},{4,3},{5,4},{6,5},{7,6},{8,15},{9,8},{10,9... | collective-permute-start | bytes 1572872 | tf_op jit(solution)/shard_map/ppermute | solution.py:214
  67.2 15.1 %collective-permute-start.3 = (bf16[1024,256]{1,0:T(8,128)(2,1)S(1)}, bf16[1024,256]{1,0:T(8,128)(2,1)S(1)}, u32[]{:S(2)}, u32[]{:S(2)}) collective-permute-start(bf16[1024,256]{1,0:T(8,128)(2,1)S(1)} %collective-permute-done.1.refs_0_), channel_id=1, source_target_pairs={{0,1},{1,2},{2,3},{3,4},{4,5},{5,6},{6,7},{7,0},{8,9},{9,10},{10,1... | collective-permute-start | bytes 1572872 | tf_op jit(solution)/shard_map/ppermute | solution.py:214
  69.1 14.4 %collective-permute-start.6 = (bf16[1024,256]{1,0:T(8,128)(2,1)S(1)}, bf16[1024,256]{1,0:T(8,128)(2,1)S(1)}, u32[]{:S(2)}, u32[]{:S(2)}) collective-permute-start(bf16[1024,256]{1,0:T(8,128)(2,1)S(1)} %collective-permute-done.4.refs_1_), channel_id=1, source_target_pairs={{0,7},{1,0},{2,1},{3,2},{4,3},{5,4},{6,5},{7,6},{8,15},{9,8},{10,9... | collective-permute-start | bytes 1572872 | tf_op jit(solution)/shard_map/ppermute | solution.py:214
  83.5 10.0 %collective-permute-start.5 = (bf16[512,256]{1,0:T(8,128)(2,1)S(1)}, bf16[512,256]{1,0:T(8,128)(2,1)S(1)}, u32[]{:S(2)}, u32[]{:S(2)}) collective-permute-start(bf16[512,256]{1,0:T(8,128)(2,1)S(1)} %slice.10), channel_id=1, source_target_pairs={{0,1},{1,2},{2,3},{3,4},{4,5},{5,6},{6,7},{7,0},{8,9},{9,10},{10,1... | collective-permute-start | bytes 786440 | tf_op jit(solution)/shard_map/ppermute | solution.py:214
  85.4 9.5 %collective-permute-start.7 = (bf16[512,256]{1,0:T(8,128)(2,1)S(1)}, bf16[512,256]{1,0:T(8,128)(2,1)S(1)}, u32[]{:S(2)}, u32[]{:S(2)}) collective-permute-start(bf16[512,256]{1,0:T(8,128)(2,1)S(1)} %slice.11), channel_id=1, source_target_pairs={{0,7},{1,0},{2,1},{3,2},{4,3},{5,4},{6,5},{7,6},{8,15},{9,8},{10,9... | collective-permute-start | bytes 786440 | tf_op jit(solution)/shard_map/ppermute | solution.py:214
  93.5 13.3 %copy-start = (bf16[512,1024]{1,0:T(8,128)(2,1)S(1)}, bf16[512,1024]{1,0:T(8,128)(2,1)}, u32[]{:S(2)}) copy-start(bf16[512,1024]{1,0:T(8,128)(2,1)} %w_ref.1) | copy-start | bytes 3145732
  94.9 11.9 %copy-start.5 = (bf16[256,512]{1,0:T(8,128)(2,1)S(1)}, bf16[256,512]{1,0:T(8,128)(2,1)}, u32[]{:S(2)}) copy-start(bf16[256,512]{1,0:T(8,128)(2,1)} %hg.1) | copy-start | bytes 786436
  94.9 11.9 %copy-start.8 = (bf16[32,1024]{1,0:T(8,128)(2,1)S(1)}, bf16[32,1024]{1,0:T(8,128)(2,1)}, u32[]{:S(2)}) copy-start(bf16[32,1024]{1,0:T(8,128)(2,1)} %cx.1) | copy-start | bytes 196612
  94.9 12.0 %copy-start.10 = (bf16[32,512]{1,0:T(8,128)(2,1)S(1)}, bf16[32,512]{1,0:T(8,128)(2,1)}, u32[]{:S(2)}) copy-start(bf16[32,512]{1,0:T(8,128)(2,1)} %cv.1) | copy-start | bytes 98308
  94.9 12.0 %copy-start.11 = (bf16[32,512]{1,0:T(8,128)(2,1)S(1)}, bf16[32,512]{1,0:T(8,128)(2,1)}, u32[]{:S(2)}) copy-start(bf16[32,512]{1,0:T(8,128)(2,1)} %cg.1) | copy-start | bytes 98308
  96.5 10.4 %copy-start.1 = (bf16[256,1024]{1,0:T(8,128)(2,1)S(1)}, bf16[256,1024]{1,0:T(8,128)(2,1)}, u32[]{:S(2)}) copy-start(bf16[256,1024]{1,0:T(8,128)(2,1)} %hx.1) | copy-start | bytes 1572868
  96.5 10.4 %copy-start.7 = (bf16[32,512]{1,0:T(8,128)(2,1)S(1)}, bf16[32,512]{1,0:T(8,128)(2,1)}, u32[]{:S(2)}) copy-start(bf16[32,512]{1,0:T(8,128)(2,1)} %cq.1) | copy-start | bytes 98308
  96.5 10.3 %copy-start.9 = (bf16[32,512]{1,0:T(8,128)(2,1)S(1)}, bf16[32,512]{1,0:T(8,128)(2,1)}, u32[]{:S(2)}) copy-start(bf16[32,512]{1,0:T(8,128)(2,1)} %ck.1) | copy-start | bytes 98308

commit v5 on v4

--- a/solution.py
+++ b/solution.py
@@ -17,13 +17,13 @@
 QROWS = ROWS + CROWS
 FOLD = QROWS // 2
 REST = ROWS - FOLD
-PART = ROWS + FOLD
 BLOCK = 128
 KEYS = NY * ROWS
 TOTAL = KEYS + NY * CROWS
 NOBODY = 1 << 30
 HALF = 1.0 / (2.0 * math.sqrt(DH))
 VMEM_LIMIT = 16 * 1024 * 1024
+WIDE_LIMIT = 60 * 1024 * 1024
 VMEM = pl.BlockSpec(memory_space=pltpu.VMEM)
 SMEM = pl.BlockSpec(memory_space=pltpu.SMEM)
 PARAMS = pltpu.CompilerParams(vmem_limit_bytes=VMEM_LIMIT)
@@ -38,37 +38,51 @@
     return (half * jnp.tanh(half) + half).astype(jnp.bfloat16)
 
 
-def split_kernel(k_ref, v_ref, q_ref, c_ref, out_ref):
-    for h in range(HEADS):
-        at = slice(h * DH, (h + 1) * DH)
-        row = h * PART
-        out_ref[row : row + ROWS, 0:DH] = k_ref[:, at]
-        out_ref[row : row + ROWS, DH : 2 * DH] = v_ref[:, at]
-        row += ROWS
-        out_ref[row : row + FOLD, 0:DH] = q_ref[0:FOLD, at]
-        out_ref[row : row + REST, DH : 2 * DH] = q_ref[FOLD:ROWS, at]
-        out_ref[row + REST : row + FOLD, DH : 2 * DH] = c_ref[:, at]
-
-
-def attend_kernel(offsets, first, last, place_ref, start_ref, len_ref, q_ref, user_ref, *refs):
-    blocks = 2 if last else len(offsets)
-    kv_refs = refs[:blocks]
-    refs = refs[blocks:]
-    if not first:
-        in_ref, *refs = refs
-    out_ref, kv, qs, acc = refs
-    z = place_ref[0]
+def split_kernel(y_ref, k_ref, v_ref, q_ref, c_ref, *outs):
+    for i in range(HEADS):
+        at = pl.ds(pl.multiple_of(lax.rem(y_ref[0] + i, HEADS) * DH, DH), DH)
+        kv, q = outs[i], outs[HEADS + i]
+        kv[:, 0:DH] = k_ref[:, at]
+        kv[:, DH : 2 * DH] = v_ref[:, at]
+        q[:, 0:DH] = q_ref[0:FOLD, at]
+        q[0:REST, DH : 2 * DH] = q_ref[FOLD:ROWS, at]
+        q[REST:FOLD, DH : 2 * DH] = c_ref[:, at]
+
+
+def join_kernel(y_ref, *refs):
+    *pieces, low, high, whole = refs
+    for i, piece in enumerate(pieces):
+        strip = lax.rem(y_ref[0] + NY - i, NY)
+        whole[pl.ds(pl.multiple_of(strip * ROWS, ROWS), ROWS), :] = piece[...]
+    low[...] = whole[0 : 2 * ROWS, :]
+    high[...] = whole[2 * ROWS : KEYS, :]
+
+
+def unfold_kernel(y_ref, *refs):
+    *pieces, out = refs
+    for i, piece in enumerate(pieces):
+        strip = lax.rem(y_ref[0] + NY - i, NY)
+        row = pl.multiple_of(strip * ROWS, ROWS)
+        out[pl.ds(row, FOLD), :] = piece[:, 0:DH]
+        out[pl.ds(pl.multiple_of(row + FOLD, 16), REST), :] = piece[0:REST, DH : 2 * DH]
+        out[pl.ds(pl.multiple_of(KEYS + strip * CROWS, CROWS), CROWS), :] = piece[REST:FOLD, DH : 2 * DH]
+
+
+def attend_kernel(offsets, strips, first, last, z_ref, start_ref, len_ref, qs, user_ref, *refs):
+    *kv_refs, in_ref = refs[: len(refs) - (2 if last else 3)] if not first else (*refs[:-3], None)
+    out_ref, acc = (refs[-2], refs[-1]) if last else (refs[-3], refs[-1])
+    z = z_ref[0]
     starts = [start_ref[u] for u in range(2)]
     ends = [start_ref[u] + len_ref[u] for u in range(2)]
-
-    size = kv_refs[0].shape[0]
-    for i, ref in enumerate(kv_refs):
-        kv[i * size : (i + 1) * size, :] = ref[...]
-    for s in range(NY):
-        row = s * PART + ROWS
-        qs[s * ROWS : s * ROWS + FOLD, :] = q_ref[row : row + FOLD, 0:DH]
-        qs[s * ROWS + FOLD : (s + 1) * ROWS, :] = q_ref[row : row + REST, DH : 2 * DH]
-        qs[KEYS + s * CROWS : KEYS + (s + 1) * CROWS, :] = q_ref[row + REST : row + FOLD, DH : 2 * DH]
+    span = len(strips) * ROWS
+
+    if last:
+        (kv,) = kv_refs
+    else:
+        kv = refs[-2]
+        size = kv_refs[0].shape[0]
+        for i, ref in enumerate(kv_refs):
+            kv[i * size : (i + 1) * size, :] = ref[...]
     if first:
         acc[...] = jnp.zeros_like(acc)
     else:
@@ -89,14 +103,11 @@
     cand_stop = jnp.where(user == 0, ends[0], ends[1])
     column = lax.broadcasted_iota(jnp.int32, (1, ROWS), 1)
 
-    def block_step(part, slots):
-        block = z + offsets[-1]
-        for n, offset in enumerate(offsets[:-1]):
-            block = jnp.where(part == n, z + offset, block)
-        block = lax.rem(block, NZ)
-        for strip, slot in enumerate(slots):
+    def block_step(block, base, shift):
+        for i, strip in enumerate(strips):
+            slot = strip + shift
             row = slot * ROWS
-            key = pl.multiple_of(part * KEYS + strip * ROWS, ROWS)
+            key = pl.multiple_of(base + i * ROWS, ROWS)
             events = (strip * NZ + block) * ROWS + column
             w = silu_weight(contract_lanes(qs[row:TOTAL, :], kv[pl.ds(key, ROWS), 0:DH]))
             parts = []
@@ -113,15 +124,16 @@
         block = z + offsets[-1]
         for n, offset in enumerate(offsets[:-1]):
             block = jnp.where(part == n, z + offset, block)
-        before = lax.rem(block, NZ) < z
-
-        @pl.when(before)
+        block = lax.rem(block, NZ)
+        base = (block if last else part) * span
+
+        @pl.when(block < z)
         def _():
-            block_step(part, range(0, NY))
-
-        @pl.when(jnp.logical_not(before))
+            block_step(block, base, 0)
+
+        @pl.when(block >= z)
         def _():
-            block_step(part, range(1, NY + 1))
+            block_step(block, base, 1)
 
         return carry
 
@@ -155,24 +167,19 @@
             out_ref[s * FOLD + REST : (s + 1) * FOLD, DH : 2 * DH] = cands
 
 
-def attend(offsets, where, queries, users, blocks, total, last):
+def attend(offsets, strips, where, queries, users, blocks, total, last=False):
     first = total is None
     shape = jax.ShapeDtypeStruct((NY * FOLD, 2 * DH), jnp.bfloat16) if last else jax.ShapeDtypeStruct((TOTAL, DH), jnp.float32)
     state = [] if first else [total]
+    keys = len(offsets) * len(strips) * ROWS
     return pl.pallas_call(
-        functools.partial(attend_kernel, offsets, first, last),
+        functools.partial(attend_kernel, offsets, strips, first, last),
         in_specs=[SMEM] * 3 + [VMEM] * (2 + len(blocks) + len(state)),
         out_specs=VMEM,
         out_shape=shape,
-        scratch_shapes=[
-            pltpu.VMEM((len(offsets) * KEYS, 2 * DH), jnp.bfloat16),
-            pltpu.VMEM((TOTAL, DH), jnp.bfloat16),
-            pltpu.VMEM((TOTAL, DH), jnp.float32),
-        ],
+        scratch_shapes=([] if last else [pltpu.VMEM((keys, 2 * DH), jnp.bfloat16)]) + [pltpu.VMEM((TOTAL, DH), jnp.float32)],
         compiler_params=PARAMS,
-        cost_estimate=pl.CostEstimate(
-            flops=len(offsets) * 4 * TOTAL * KEYS * DH, bytes_accessed=len(offsets) << 20, transcendentals=0
-        ),
+        cost_estimate=pl.CostEstimate(flops=4 * TOTAL * keys * DH, bytes_accessed=1 << 20, transcendentals=0),
         name="attend",
     )(*where, queries, users, *blocks, *state)
 
@@ -200,22 +207,21 @@
     tail(jnp.concatenate(cand, axis=1), cg, cx, co)
 
 
-def call(kernel, shapes, *args):
+def call(kernel, shapes, *args, place=None, scratch=(), limit=VMEM_LIMIT):
+    args = args if place is None else (place, *args)
     return pl.pallas_call(
         kernel,
-        in_specs=[VMEM] * len(args),
+        in_specs=[SMEM] * (place is not None) + [VMEM] * (len(args) - (place is not None)),
         out_specs=[VMEM] * len(shapes),
         out_shape=[jax.ShapeDtypeStruct(s, jnp.bfloat16) for s in shapes],
-        compiler_params=PARAMS,
+        scratch_shapes=scratch,
+        compiler_params=pltpu.CompilerParams(vmem_limit_bytes=limit),
     )(*args)
 
 
-def turn(array, step):
-    return lax.ppermute(array, "z", [(i, (i + step) % NZ) for i in range(NZ)])
-
-
-def spread(array):
-    return lax.all_to_all(array, "y", 0, 0, tiled=True)
+def turn(array, axis, step):
+    count = NY if axis == "y" else NZ
+    return lax.ppermute(array, axis, [(i, (i + step) % count) for i in range(count)])
 
 
 def on_device(
@@ -224,28 +230,39 @@
     cand_user, hist_len, hist_start, out_weight,
 ):
     z = lax.axis_index("z")
+    y = lax.axis_index("y").astype(jnp.int32).reshape(1)
     where = (z.astype(jnp.int32).reshape(1), hist_start, hist_len)
     users = lax.dynamic_index_in_dim(cand_user.reshape(NY, NZ, CROWS), z, axis=1).reshape(NY * CROWS, 1)
-    (parts,) = call(split_kernel, [(HEADS * PART, 2 * DH)], hist_key, hist_value, hist_query, cand_query)
-    queries = spread(parts)
-    own = queries.reshape(NY, PART, 2 * DH)[:, :ROWS].reshape(KEYS, 2 * DH)
-    up, down = turn(own, 1), turn(own, -1)
-    total = attend((0,), where, queries, users, (own,), None, False)
+    parts = call(
+        split_kernel, [(ROWS, 2 * DH)] * HEADS + [(FOLD, 2 * DH)] * HEADS,
+        hist_key, hist_value, hist_query, cand_query, place=y, limit=WIDE_LIMIT,
+    )
+    pieces = [parts[0]] + [turn(parts[i], "y", i) for i in (1, 2, 3)]
+    folds = [parts[HEADS]] + [turn(parts[HEADS + i], "y", i) for i in (1, 2, 3)]
+    near, far = call(
+        join_kernel, [(2 * ROWS, 2 * DH)] * 2, *pieces, place=y, scratch=[pltpu.VMEM((KEYS, 2 * DH), jnp.bfloat16)]
+    )
+    gathered = lax.all_gather(far, "z", axis=0, tiled=True)
+    up, down = turn(near, "z", 1), turn(near, "z", -1)
+    (queries,) = call(unfold_kernel, [(TOTAL, DH)], *folds, place=y)
+    total = attend((0,), (0, 1, 2, 3), where, queries, users, (near, far), None)
     for step in (1, 2):
         up, held = lax.optimization_barrier((up, total))
         down, total = lax.optimization_barrier((down, held))
         blocks = (up, down)
-        up, down = turn(up, 1), turn(down, -1)
-        total = attend((NZ - step, step), where, queries, users, blocks, total, False)
+        up, down = turn(up, "z", 1), turn(down, "z", -1)
+        total = attend((NZ - step, step), (0, 1), where, queries, users, blocks, total)
     up, held = lax.optimization_barrier((up, total))
     down, total = lax.optimization_barrier((down, held))
-    low, high = turn(up[: KEYS // 2], 1), turn(down[KEYS // 2 :], -1)
-    total = attend((NZ - 3, 3), where, queries, users, (up, down), total, False)
-    total = attend((4,), where, queries, users, (low, high), total, True)
+    low, high = turn(up[:ROWS], "z", 1), turn(down[ROWS:], "z", -1)
+    total = attend((NZ - 3, 3), (0, 1), where, queries, users, (up, down), total)
+    total = attend((4,), (0, 1), where, queries, users, (low, high), total)
+    total = attend(tuple(range(1, NZ)), (2, 3), where, queries, users, (gathered,), total, last=True)
+    total = lax.all_to_all(total, "y", 0, 0, tiled=True)
     return tuple(
         call(
             finish_kernel, [hist_input.shape, cand_input.shape],
-            spread(total), hist_gate, hist_input, cand_query, cand_key, cand_value, cand_gate, cand_input, out_weight,
+            total, hist_gate, hist_input, cand_query, cand_key, cand_value, cand_gate, cand_input, out_weight,
         )
     )
 

time: 109 us -> 127 us (1.17)
  blocking collectives: 34.3 us -> 10.2 us
  starting transfers between devices: 34.5 us -> 54.4 us
  between operations: 0.9 us -> 14.4 us
  Pallas kernels: 12.8 us -> 18.3 us
  waiting for transfers between devices: 20.6 us -> 24.5 us
    all_to_all x2 -> x1, blocking collectives: 34.3 us -> 10.2 us  [on_device(): total = lax.all_to_all(total, 'y', 0, 0, tiled=True)]
    ppermute x8 -> x14, starting transfers between devices: 34.5 us -> 54.4 us  [turn(): lax.ppermute(array, axis, [(i, (i + step) % count) for i in range(count)])]
    pallas_call x7 -> x10, Pallas kernels: 12.8 us -> 18.3 us  [the longest x6 13.9 us: attend(): pl.pallas_call(functools.partial(attend_kernel, offsets, strips, first, l...]
    ppermute x8 -> x14, waiting for transfers between devices: 20.6 us -> 24.5 us  [turn(): lax.ppermute(array, axis, [(i, (i + step) % count) for i in range(count)])]
    unnamed x30 -> x26, local copies, waits for them, and re-layouts: 4.98 us -> 3.55 us
  transfers between devices with their start and end apart: 8 -> 15, of which waited for: 5 -> 7; matrix products, arithmetic and copies ran while one was open for 0% -> 1% of each run, Pallas kernels for 9% -> 8%
where the time goes in v5:
time: 127 us; the launch traced here: 126 us
  starting transfers between devices  54.4 us (43%)
  waiting for transfers between devices  24.5 us (19%)
  Pallas kernels  18.3 us (14%)
  between operations  14.4 us (11%)
  blocking collectives  10.2 us (8%)
  local copies, waits for them, and re-layouts  4.46 us (4%)
    ppermute x14, starting transfers between devices, turn(): lax.ppermute(array, axis, [(i, (i + step) % count) for i in range(count)])  54.4 us
    ppermute x14, waiting for transfers between devices, turn(): lax.ppermute(array, axis, [(i, (i + step) % count) for i in range(count)])  24.5 us
    pallas_call x6, Pallas kernels, attend(): pl.pallas_call(functools.partial(attend_kernel, offsets, strips, first, l...  13.9 us
    all_to_all x1, blocking collectives, on_device(): total = lax.all_to_all(total, 'y', 0, 0, tiled=True)  10.2 us
    pallas_call x4, Pallas kernels, call(): pl.pallas_call(kernel, in_specs=[SMEM] * (place is not None) + [VMEM] * (...  4.46 us
    unnamed x26, local copies, waits for them, and re-layouts  3.55 us
  transfers between devices with their start and end apart: 15, of which 7 were waited for; matrix products, arithmetic and copies ran while one was open for 1% of the time, Pallas kernels for 8%

profile of v5, /device:TPU:56, one launch (start us, length us, event | category | flops | bytes accessed | tf_op | source)
XLA Modules:
  0.0 126.3 jit_solution(2000908620378726281)
XLA Ops:
  7.2 2.1 %shard_map.149 = (bf16[256,256]{1,0:T(8,128)(2,1)}, bf16[256,256]{1,0:T(8,128)(2,1)}, bf16[256,256]{1,0:T(8,128)(2,1)}, bf16[256,256]{1,0:T(8,128)(2,1)}, bf16[1...) custom-call(s32[1]{0:T(128)} %bitcast.1.y_ref, ...), custom_call_target="tpu_custom_call" | custom-call | tf_op jit(solution)/shard_map/pallas_call | solution.py:212
  9.4 4.8 %collective-permute-start.3 = (bf16[256,256]{1,0:T(8,128)(2,1)}, bf16[256,256]{1,0:T(8,128)(2,1)S(1)}, u32[]{:S(2)}, u32[]{:S(2)}) collective-permute-start(bf16[256,256]{1,0:T(8,128)(2,1)} %get-tuple-element.29), channel_id=1, source_target_pairs={{0,8},{8,16},{16,24},{24,0},{1,9},{9,17},{17,25},{25,1},{2,10},{10... | collective-permute-start | bytes 393224 | tf_op jit(solution)/shard_map/ppermute | solution.py:224
  14.2 1.9 %collective-permute-start.4 = (bf16[256,256]{1,0:T(8,128)(2,1)}, bf16[256,256]{1,0:T(8,128)(2,1)S(1)}, u32[]{:S(2)}, u32[]{:S(2)}) collective-permute-start(bf16[256,256]{1,0:T(8,128)(2,1)} %get-tuple-element.30), channel_id=1, source_target_pairs={{0,16},{8,24},{16,0},{24,8},{1,17},{9,25},{17,1},{25,9},{2,18},{10... | collective-permute-start | bytes 393224 | tf_op jit(solution)/shard_map/ppermute | solution.py:224
  16.1 3.1 %collective-permute-start.5 = (bf16[256,256]{1,0:T(8,128)(2,1)}, bf16[256,256]{1,0:T(8,128)(2,1)S(1)}, u32[]{:S(2)}, u32[]{:S(2)}) collective-permute-start(bf16[256,256]{1,0:T(8,128)(2,1)} %get-tuple-element.31), channel_id=1, source_target_pairs={{0,24},{8,0},{16,8},{24,16},{1,25},{9,1},{17,9},{25,17},{2,26},{10... | collective-permute-start | bytes 393224 | tf_op jit(solution)/shard_map/ppermute | solution.py:224
  19.3 7.4 %collective-permute-done.4.refs_2_ = bf16[256,256]{1,0:T(8,128)(2,1)S(1)} collective-permute-done((bf16[256,256]{1,0:T(8,128)(2,1)}, bf16[256,256]{1,0:T(8,128)(2,1)S(1)}, u32[]{:S(2)}, u32[]{:S(2)}) %collective-permute-start.4) | collective-permute-done | bytes 131104 | tf_op jit(solution)/shard_map/ppermute | solution.py:224
  28.4 4.3 %collective-permute-start.6 = (bf16[512,256]{1,0:T(8,128)(2,1)S(1)}, bf16[512,256]{1,0:T(8,128)(2,1)S(1)}, u32[]{:S(2)}, u32[]{:S(2)}) collective-permute-start(bf16[512,256]{1,0:T(8,128)(2,1)S(1)} %get-tuple-element.33.refs_0_), channel_id=1, source_target_pairs={{0,1},{1,2},{2,3},{3,4},{4,5},{5,6},{6,7},{7,0},{8,9},{9,10},{10,1... | collective-permute-start | bytes 786440 | tf_op jit(solution)/shard_map/ppermute | solution.py:224
  32.7 8.6 %collective-permute-start.8 = (bf16[512,256]{1,0:T(8,128)(2,1)S(1)}, bf16[512,256]{1,0:T(8,128)(2,1)S(1)}, u32[]{:S(2)}, u32[]{:S(2)}) collective-permute-start(bf16[512,256]{1,0:T(8,128)(2,1)S(1)} %get-tuple-element.33.refs_0_), channel_id=1, source_target_pairs={{0,7},{1,0},{2,1},{3,2},{4,3},{5,4},{6,5},{7,6},{8,15},{9,8},{10,9... | collective-permute-start | bytes 786440 | tf_op jit(solution)/shard_map/ppermute | solution.py:224
  41.3 3.5 %collective-permute-start = (bf16[144,256]{1,0:T(8,128)(2,1)}, bf16[144,256]{1,0:T(8,128)(2,1)S(1)}, u32[]{:S(2)}, u32[]{:S(2)}) collective-permute-start(bf16[144,256]{1,0:T(8,128)(2,1)} %get-tuple-element.25), channel_id=1, source_target_pairs={{0,8},{8,16},{16,24},{24,0},{1,9},{9,17},{17,25},{25,1},{2,10},{10... | collective-permute-start | bytes 221192 | tf_op jit(solution)/shard_map/ppermute | solution.py:224
  44.8 2.7 %collective-permute-start.1 = (bf16[144,256]{1,0:T(8,128)(2,1)}, bf16[144,256]{1,0:T(8,128)(2,1)S(1)}, u32[]{:S(2)}, u32[]{:S(2)}) collective-permute-start(bf16[144,256]{1,0:T(8,128)(2,1)} %get-tuple-element.26), channel_id=1, source_target_pairs={{0,16},{8,24},{16,0},{24,8},{1,17},{9,25},{17,1},{25,9},{2,18},{10... | collective-permute-start | bytes 221192 | tf_op jit(solution)/shard_map/ppermute | solution.py:224
  47.4 3.9 %collective-permute-start.2 = (bf16[144,256]{1,0:T(8,128)(2,1)}, bf16[144,256]{1,0:T(8,128)(2,1)S(1)}, u32[]{:S(2)}, u32[]{:S(2)}) collective-permute-start(bf16[144,256]{1,0:T(8,128)(2,1)} %get-tuple-element.27), channel_id=1, source_target_pairs={{0,24},{8,0},{16,8},{24,16},{1,25},{9,1},{17,9},{25,17},{2,26},{10... | collective-permute-start | bytes 221192 | tf_op jit(solution)/shard_map/ppermute | solution.py:224
  52.8 2.9 %collective-permute-done.2.refs_3_ = bf16[144,256]{1,0:T(8,128)(2,1)S(1)} collective-permute-done((bf16[144,256]{1,0:T(8,128)(2,1)}, bf16[144,256]{1,0:T(8,128)(2,1)S(1)}, u32[]{:S(2)}, u32[]{:S(2)}) %collective-permute-start.2) | collective-permute-done | bytes 73760 | tf_op jit(solution)/shard_map/ppermute | solution.py:224
  56.6 2.6 %attend.6.refs_2_ = f32[1152,128]{1,0:T(8,128)S(1)} custom-call(s32[1]{0:T(128)} %bitcast.z_ref, s32[2]{0:T(128)S(1)} %copy-done.10, s32[2]{0:T(128)S(1)} %copy-done.11, bf16[1152,128]{1,0:T(8,128)(2,1)S(1)} %shard_map.150.qs, s32[128,1]{1,0:T(8,128)S(1)} %reshape.22.user_ref, bf16[512,256]{1,0:T(8,128)(2,1)S(1)} %get-tuple-element.33.refs_0_, ...), custom_call_target="tpu_custom_call" | custom-call | flops 603979776 | bytes 1048576 | tf_op jit(solution)/shard_map/attend/pallas_call | solution.py:175
  59.2 1.9 %collective-permute-start.7 = (bf16[512,256]{1,0:T(8,128)(2,1)S(1)}, bf16[512,256]{1,0:T(8,128)(2,1)S(1)}, u32[]{:S(2)}, u32[]{:S(2)}) collective-permute-start(bf16[512,256]{1,0:T(8,128)(2,1)S(1)} %collective-permute-done.6.refs_0_), channel_id=1, source_target_pairs={{0,1},{1,2},{2,3},{3,4},{4,5},{5,6},{6,7},{7,0},{8,9},{9,10},{10,1... | collective-permute-start | bytes 786440 | tf_op jit(solution)/shard_map/ppermute | solution.py:224
  61.2 5.1 %collective-permute-start.10 = (bf16[512,256]{1,0:T(8,128)(2,1)S(1)}, bf16[512,256]{1,0:T(8,128)(2,1)S(1)}, u32[]{:S(2)}, u32[]{:S(2)}) collective-permute-start(bf16[512,256]{1,0:T(8,128)(2,1)S(1)} %collective-permute-done.8.refs_1_), channel_id=1, source_target_pairs={{0,7},{1,0},{2,1},{3,2},{4,3},{5,4},{6,5},{7,6},{8,15},{9,8},{10,9... | collective-permute-start | bytes 786440 | tf_op jit(solution)/shard_map/ppermute | solution.py:224
  66.3 2.1 %attend.7.refs_2_ = f32[1152,128]{1,0:T(8,128)S(1)} custom-call(s32[1]{0:T(128)} %bitcast.z_ref, s32[2]{0:T(128)S(1)} %copy-done.10, s32[2]{0:T(128)S(1)} %copy-done.11, bf16[1152,128]{1,0:T(8,128)(2,1)S(1)} %shard_map.150.qs, s32[128,1]{1,0:T(8,128)S(1)} %reshape.22.user_ref, bf16[512,256]{1,0:T(8,128)(2,1)S(1)} %collective-permute-done.6.refs_0_, ...), custom_call_target="tpu_custom_call" | custom-call | flops 603979776 | bytes 1048576 | tf_op jit(solution)/shard_map/attend/pallas_call | solution.py:175
  68.4 7.8 %collective-permute-done.7.refs_0_ = bf16[512,256]{1,0:T(8,128)(2,1)S(1)} collective-permute-done((bf16[512,256]{1,0:T(8,128)(2,1)S(1)}, bf16[512,256]{1,0:T(8,128)(2,1)S(1)}, u32[]{:S(2)}, u32[]{:S(2)}) %collective-permute-start.7) | collective-permute-done | bytes 262176 | tf_op jit(solution)/shard_map/ppermute | solution.py:224
  78.1 5.1 %collective-permute-start.12 = (bf16[512,256]{1,0:T(8,128)(2,1)S(1)}, bf16[512,256]{1,0:T(8,128)(2,1)S(1)}, u32[]{:S(2)}, u32[]{:S(2)}) collective-permute-start(bf16[512,256]{1,0:T(8,128)(2,1)S(1)} %collective-permute-done.10.refs_1_), channel_id=1, source_target_pairs={{0,7},{1,0},{2,1},{3,2},{4,3},{5,4},{6,5},{7,6},{8,15},{9,8},{10,9... | collective-permute-start | bytes 786440 | tf_op jit(solution)/shard_map/ppermute | solution.py:224
  83.3 2.1 %attend.8.refs_2_ = f32[1152,128]{1,0:T(8,128)S(1)} custom-call(s32[1]{0:T(128)} %bitcast.z_ref, s32[2]{0:T(128)S(1)} %copy-done.10, s32[2]{0:T(128)S(1)} %copy-done.11, bf16[1152,128]{1,0:T(8,128)(2,1)S(1)} %shard_map.150.qs, s32[128,1]{1,0:T(8,128)S(1)} %reshape.22.user_ref, bf16[512,256]{1,0:T(8,128)(2,1)S(1)} %collective-permute-done.7.refs_0_, ...), custom_call_target="tpu_custom_call" | custom-call | flops 603979776 | bytes 1048576 | tf_op jit(solution)/shard_map/attend/pallas_call | solution.py:175
  87.2 5.6 %collective-permute-start.13 = (bf16[256,256]{1,0:T(8,128)(2,1)S(1)}, bf16[256,256]{1,0:T(8,128)(2,1)S(1)}, u32[]{:S(2)}, u32[]{:S(2)}) collective-permute-start(bf16[256,256]{1,0:T(8,128)(2,1)S(1)} %slice.7), channel_id=1, source_target_pairs={{0,7},{1,0},{2,1},{3,2},{4,3},{5,4},{6,5},{7,6},{8,15},{9,8},{10,9... | collective-permute-start | bytes 393224 | tf_op jit(solution)/shard_map/ppermute | solution.py:224
  92.8 1.9 %collective-permute-start.11 = (bf16[256,256]{1,0:T(8,128)(2,1)S(1)}, bf16[256,256]{1,0:T(8,128)(2,1)S(1)}, u32[]{:S(2)}, u32[]{:S(2)}) collective-permute-start(bf16[256,256]{1,0:T(8,128)(2,1)S(1)} %slice.6), channel_id=1, source_target_pairs={{0,1},{1,2},{2,3},{3,4},{4,5},{5,6},{6,7},{7,0},{8,9},{9,10},{10,1... | collective-permute-start | bytes 393224 | tf_op jit(solution)/shard_map/ppermute | solution.py:224
  94.7 2.1 %attend.9.refs_2_ = f32[1152,128]{1,0:T(8,128)S(1)} custom-call(s32[1]{0:T(128)} %bitcast.z_ref, s32[2]{0:T(128)S(1)} %copy-done.10, s32[2]{0:T(128)S(1)} %copy-done.11, bf16[1152,128]{1,0:T(8,128)(2,1)S(1)} %shard_map.150.qs, s32[128,1]{1,0:T(8,128)S(1)} %reshape.22.user_ref, bf16[512,256]{1,0:T(8,128)(2,1)S(1)} %collective-permute-done.9.refs_0_, ...), custom_call_target="tpu_custom_call" | custom-call | flops 603979776 | bytes 1048576 | tf_op jit(solution)/shard_map/attend/pallas_call | solution.py:175
  96.8 4.0 %collective-permute-done.11.refs_0_ = bf16[256,256]{1,0:T(8,128)(2,1)S(1)} collective-permute-done((bf16[256,256]{1,0:T(8,128)(2,1)S(1)}, bf16[256,256]{1,0:T(8,128)(2,1)S(1)}, u32[]{:S(2)}, u32[]{:S(2)}) %collective-permute-start.11) | collective-permute-done | bytes 131104 | tf_op jit(solution)/shard_map/ppermute | solution.py:224
  104.0 3.7 %attend.11 = bf16[576,256]{1,0:T(8,128)(2,1)S(1)} custom-call(s32[1]{0:T(128)} %bitcast.z_ref, s32[2]{0:T(128)S(1)} %copy-done.10, s32[2]{0:T(128)S(1)} %copy-done.11, bf16[1152,128]{1,0:T(8,128)(2,1)S(1)} %shard_map.150.qs, s32[128,1]{1,0:T(8,128)S(1)} %reshape.22.user_ref, bf16[4096,256]{1,0:T(8,128)(2,1)S(1)} %copy-done.12, f32[1152,128]{1,0:T(8,128)S(1)} %attend.10.refs_1_), custom_call_target="tpu_custom_call" | custom-call | flops 2113929216 | bytes 1048576 | tf_op jit(solution)/shard_map/attend/pallas_call | solution.py:175
  107.8 10.2 %all_to_all.11 = bf16[4,144,256]{2,1,0:T(8,128)(2,1)S(1)} all-to-all(bf16[4,144,256]{2,1,0:T(8,128)(2,1)S(1)} %bitcast.5), channel_id=1, replica_groups=mesh['batch'=16,'y'=4,'z'=8] {'y'}, dimensions={0} | all-to-all | bytes 589824 | tf_op jit(solution)/shard_map/all_to_all | solution.py:261
  (49 shorter events, 12.5 us)
Async XLA Ops:
  7.2 49.5 %copy-start.11 = (s32[2]{0:T(128)S(1)}, s32[2]{0:T(128)}, u32[]{:S(2)}) copy-start(s32[2]{0:T(128)} %len_ref.11) | copy-start | bytes 28
  7.2 49.5 %copy-start.10 = (s32[2]{0:T(128)S(1)}, s32[2]{0:T(128)}, u32[]{:S(2)}) copy-start(s32[2]{0:T(128)} %start_ref.11) | copy-start | bytes 28
  7.2 95.1 %all-gather.2.cloned.1.call-start = ((), (), s32[]{:S(2)}) async-start(), calls=%async_computation.1 | async-start | bytes 2359296 | tf_op jit(solution)/shard_map/all_gather | solution.py:245
  9.4 9.9 %collective-permute-start.3 = (bf16[256,256]{1,0:T(8,128)(2,1)}, bf16[256,256]{1,0:T(8,128)(2,1)S(1)}, u32[]{:S(2)}, u32[]{:S(2)}) collective-permute-start(bf16[256,256]{1,0:T(8,128)(2,1)} %get-tuple-element.29), channel_id=1, source_target_pairs={{0,8},{8,16},{16,24},{24,0},{1,9},{9,17},{17,25},{25,1},{2,10},{10... | collective-permute-start | bytes 393224 | tf_op jit(solution)/shard_map/ppermute | solution.py:224
  14.2 12.5 %collective-permute-start.4 = (bf16[256,256]{1,0:T(8,128)(2,1)}, bf16[256,256]{1,0:T(8,128)(2,1)S(1)}, u32[]{:S(2)}, u32[]{:S(2)}) collective-permute-start(bf16[256,256]{1,0:T(8,128)(2,1)} %get-tuple-element.30), channel_id=1, source_target_pairs={{0,16},{8,24},{16,0},{24,8},{1,17},{9,25},{17,1},{25,9},{2,18},{10... | collective-permute-start | bytes 393224 | tf_op jit(solution)/shard_map/ppermute | solution.py:224
  16.1 10.6 %collective-permute-start.5 = (bf16[256,256]{1,0:T(8,128)(2,1)}, bf16[256,256]{1,0:T(8,128)(2,1)S(1)}, u32[]{:S(2)}, u32[]{:S(2)}) collective-permute-start(bf16[256,256]{1,0:T(8,128)(2,1)} %get-tuple-element.31), channel_id=1, source_target_pairs={{0,24},{8,0},{16,8},{24,16},{1,25},{9,1},{17,9},{25,17},{2,26},{10... | collective-permute-start | bytes 393224 | tf_op jit(solution)/shard_map/ppermute | solution.py:224
  28.4 30.8 %collective-permute-start.6 = (bf16[512,256]{1,0:T(8,128)(2,1)S(1)}, bf16[512,256]{1,0:T(8,128)(2,1)S(1)}, u32[]{:S(2)}, u32[]{:S(2)}) collective-permute-start(bf16[512,256]{1,0:T(8,128)(2,1)S(1)} %get-tuple-element.33.refs_0_), channel_id=1, source_target_pairs={{0,1},{1,2},{2,3},{3,4},{4,5},{5,6},{6,7},{7,0},{8,9},{9,10},{10,1... | collective-permute-start | bytes 786440 | tf_op jit(solution)/shard_map/ppermute | solution.py:224
  32.7 28.5 %collective-permute-start.8 = (bf16[512,256]{1,0:T(8,128)(2,1)S(1)}, bf16[512,256]{1,0:T(8,128)(2,1)S(1)}, u32[]{:S(2)}, u32[]{:S(2)}) collective-permute-start(bf16[512,256]{1,0:T(8,128)(2,1)S(1)} %get-tuple-element.33.refs_0_), channel_id=1, source_target_pairs={{0,7},{1,0},{2,1},{3,2},{4,3},{5,4},{6,5},{7,6},{8,15},{9,8},{10,9... | collective-permute-start | bytes 786440 | tf_op jit(solution)/shard_map/ppermute | solution.py:224
  41.3 11.0 %collective-permute-start = (bf16[144,256]{1,0:T(8,128)(2,1)}, bf16[144,256]{1,0:T(8,128)(2,1)S(1)}, u32[]{:S(2)}, u32[]{:S(2)}) collective-permute-start(bf16[144,256]{1,0:T(8,128)(2,1)} %get-tuple-element.25), channel_id=1, source_target_pairs={{0,8},{8,16},{16,24},{24,0},{1,9},{9,17},{17,25},{25,1},{2,10},{10... | collective-permute-start | bytes 221192 | tf_op jit(solution)/shard_map/ppermute | solution.py:224
  44.8 8.1 %collective-permute-start.1 = (bf16[144,256]{1,0:T(8,128)(2,1)}, bf16[144,256]{1,0:T(8,128)(2,1)S(1)}, u32[]{:S(2)}, u32[]{:S(2)}) collective-permute-start(bf16[144,256]{1,0:T(8,128)(2,1)} %get-tuple-element.26), channel_id=1, source_target_pairs={{0,16},{8,24},{16,0},{24,8},{1,17},{9,25},{17,1},{25,9},{2,18},{10... | collective-permute-start | bytes 221192 | tf_op jit(solution)/shard_map/ppermute | solution.py:224
  47.4 8.3 %collective-permute-start.2 = (bf16[144,256]{1,0:T(8,128)(2,1)}, bf16[144,256]{1,0:T(8,128)(2,1)S(1)}, u32[]{:S(2)}, u32[]{:S(2)}) collective-permute-start(bf16[144,256]{1,0:T(8,128)(2,1)} %get-tuple-element.27), channel_id=1, source_target_pairs={{0,24},{8,0},{16,8},{24,16},{1,25},{9,1},{17,9},{25,17},{2,26},{10... | collective-permute-start | bytes 221192 | tf_op jit(solution)/shard_map/ppermute | solution.py:224
  59.2 17.0 %collective-permute-start.7 = (bf16[512,256]{1,0:T(8,128)(2,1)S(1)}, bf16[512,256]{1,0:T(8,128)(2,1)S(1)}, u32[]{:S(2)}, u32[]{:S(2)}) collective-permute-start(bf16[512,256]{1,0:T(8,128)(2,1)S(1)} %collective-permute-done.6.refs_0_), channel_id=1, source_target_pairs={{0,1},{1,2},{2,3},{3,4},{4,5},{5,6},{6,7},{7,0},{8,9},{9,10},{10,1... | collective-permute-start | bytes 786440 | tf_op jit(solution)/shard_map/ppermute | solution.py:224
  61.2 17.0 %collective-permute-start.10 = (bf16[512,256]{1,0:T(8,128)(2,1)S(1)}, bf16[512,256]{1,0:T(8,128)(2,1)S(1)}, u32[]{:S(2)}, u32[]{:S(2)}) collective-permute-start(bf16[512,256]{1,0:T(8,128)(2,1)S(1)} %collective-permute-done.8.refs_1_), channel_id=1, source_target_pairs={{0,7},{1,0},{2,1},{3,2},{4,3},{5,4},{6,5},{7,6},{8,15},{9,8},{10,9... | collective-permute-start | bytes 786440 | tf_op jit(solution)/shard_map/ppermute | solution.py:224
  76.2 9.5 %collective-permute-start.9 = (bf16[512,256]{1,0:T(8,128)(2,1)S(1)}, bf16[512,256]{1,0:T(8,128)(2,1)S(1)}, u32[]{:S(2)}, u32[]{:S(2)}) collective-permute-start(bf16[512,256]{1,0:T(8,128)(2,1)S(1)} %collective-permute-done.7.refs_0_), channel_id=1, source_target_pairs={{0,1},{1,2},{2,3},{3,4},{4,5},{5,6},{6,7},{7,0},{8,9},{9,10},{10,1... | collective-permute-start | bytes 786440 | tf_op jit(solution)/shard_map/ppermute | solution.py:224
  78.1 9.0 %collective-permute-start.12 = (bf16[512,256]{1,0:T(8,128)(2,1)S(1)}, bf16[512,256]{1,0:T(8,128)(2,1)S(1)}, u32[]{:S(2)}, u32[]{:S(2)}) collective-permute-start(bf16[512,256]{1,0:T(8,128)(2,1)S(1)} %collective-permute-done.10.refs_1_), channel_id=1, source_target_pairs={{0,7},{1,0},{2,1},{3,2},{4,3},{5,4},{6,5},{7,6},{8,15},{9,8},{10,9... | collective-permute-start | bytes 786440 | tf_op jit(solution)/shard_map/ppermute | solution.py:224
  87.2 9.6 %collective-permute-start.13 = (bf16[256,256]{1,0:T(8,128)(2,1)S(1)}, bf16[256,256]{1,0:T(8,128)(2,1)S(1)}, u32[]{:S(2)}, u32[]{:S(2)}) collective-permute-start(bf16[256,256]{1,0:T(8,128)(2,1)S(1)} %slice.7), channel_id=1, source_target_pairs={{0,7},{1,0},{2,1},{3,2},{4,3},{5,4},{6,5},{7,6},{8,15},{9,8},{10,9... | collective-permute-start | bytes 393224 | tf_op jit(solution)/shard_map/ppermute | solution.py:224
  92.8 8.1 %collective-permute-start.11 = (bf16[256,256]{1,0:T(8,128)(2,1)S(1)}, bf16[256,256]{1,0:T(8,128)(2,1)S(1)}, u32[]{:S(2)}, u32[]{:S(2)}) collective-permute-start(bf16[256,256]{1,0:T(8,128)(2,1)S(1)} %slice.6), channel_id=1, source_target_pairs={{0,1},{1,2},{2,3},{3,4},{4,5},{5,6},{6,7},{7,0},{8,9},{9,10},{10,1... | collective-permute-start | bytes 393224 | tf_op jit(solution)/shard_map/ppermute | solution.py:224
  102.2 15.7 %copy-start = (bf16[512,1024]{1,0:T(8,128)(2,1)S(1)}, bf16[512,1024]{1,0:T(8,128)(2,1)}, u32[]{:S(2)}) copy-start(bf16[512,1024]{1,0:T(8,128)(2,1)} %w_ref.1) | copy-start | bytes 3145732
  102.2 15.7 %copy-start.1 = (bf16[256,1024]{1,0:T(8,128)(2,1)S(1)}, bf16[256,1024]{1,0:T(8,128)(2,1)}, u32[]{:S(2)}) copy-start(bf16[256,1024]{1,0:T(8,128)(2,1)} %hx.1) | copy-start | bytes 1572868
  102.2 15.7 %copy-start.2 = (bf16[256,512]{1,0:T(8,128)(2,1)S(1)}, bf16[256,512]{1,0:T(8,128)(2,1)}, u32[]{:S(2)}) copy-start(bf16[256,512]{1,0:T(8,128)(2,1)} %hg.1) | copy-start | bytes 786436
  102.2 15.7 %copy-start.3 = (bf16[32,512]{1,0:T(8,128)(2,1)S(1)}, bf16[32,512]{1,0:T(8,128)(2,1)}, u32[]{:S(2)}) copy-start(bf16[32,512]{1,0:T(8,128)(2,1)} %cq.1) | copy-start | bytes 98308
  102.3 15.7 %copy-start.6 = (bf16[32,1024]{1,0:T(8,128)(2,1)S(1)}, bf16[32,1024]{1,0:T(8,128)(2,1)}, u32[]{:S(2)}) copy-start(bf16[32,1024]{1,0:T(8,128)(2,1)} %cx.1) | copy-start | bytes 196612
  102.3 15.7 %copy-start.7 = (bf16[32,512]{1,0:T(8,128)(2,1)S(1)}, bf16[32,512]{1,0:T(8,128)(2,1)}, u32[]{:S(2)}) copy-start(bf16[32,512]{1,0:T(8,128)(2,1)} %ck.1) | copy-start | bytes 98308
  102.3 15.7 %copy-start.8 = (bf16[32,512]{1,0:T(8,128)(2,1)S(1)}, bf16[32,512]{1,0:T(8,128)(2,1)}, u32[]{:S(2)}) copy-start(bf16[32,512]{1,0:T(8,128)(2,1)} %cv.1) | copy-start | bytes 98308
  (4 other events, 19.2 us)
Sparse Core Ops, SparseCore 0:
  28.5 50.9 all-gather.1

commit v6 on v4

v6 whole, which is shorter than its diff:
```python
import functools
import math

import jax
import jax.numpy as jnp
from jax import lax
from jax.experimental import pallas as pl
from jax.experimental.pallas import tpu as pltpu
from jax.sharding import Mesh, PartitionSpec as P

HEADS = 4
DH = 128
HD = HEADS * DH
NY = 4
NZ = 8
ROWS = 256
CROWS = 32
QROWS = ROWS + CROWS
BLOCK = 128
HISTS = NY * ROWS
TOTAL = HISTS + NY * CROWS
NOBODY = 1 << 30
HALF = 1.0 / (2.0 * math.sqrt(DH))
VMEM_LIMIT = 20 * 1024 * 1024
WIDE_LIMIT = 60 * 1024 * 1024
VMEM = pl.BlockSpec(memory_space=pltpu.VMEM)
SMEM = pl.BlockSpec(memory_space=pltpu.SMEM)


def contract_lanes(a, b):
    return lax.dot_general(a, b, (((1,), (1,)), ((), ())), preferred_element_type=jnp.float32)


def silu_weight(scores):
    half = scores * HALF
    return (half * jnp.tanh(half) + half).astype(jnp.bfloat16)


def flag(mask):
    return jnp.where(mask, 1.0, 0.0).astype(jnp.bfloat16)


def head(h):
    return slice(h * DH, (h + 1) * DH)


def stack_kernel(k_ref, v_ref, q_ref, c_ref, kv, qc):
    kv[0:ROWS, :] = k_ref[...]
    kv[ROWS : 2 * ROWS, :] = v_ref[...]
    qc[0:ROWS, :] = q_ref[...]
    qc[ROWS:QROWS, :] = c_ref[...]


def attend_kernel(offsets, first, last, place_ref, start_ref, len_ref, user_ref, *refs):
    refs = list(refs)
    if last:
        k_refs, v_refs, kv_row = [refs.pop(0)], [refs.pop(0)], 0
    else:
        k_refs = v_refs = [refs.pop(0) for _ in offsets]
        kv_row = ROWS
    if first:
        pieces = [refs.pop(0) for _ in range(NY)]
        acc, qs = refs
    else:
        qs, in_ref = refs.pop(0), refs.pop(0)
        if last:
            own, *away, acc = refs
        else:
            (acc,) = refs
    y = place_ref[0]
    z = place_ref[1]
    starts = [start_ref[u] for u in range(2)]
    ends = [start_ref[u] + len_ref[u] for u in range(2)]

    if first:
        for slot, piece in enumerate(pieces):
            qs[slot * ROWS : (slot + 1) * ROWS, :] = piece[0:ROWS, :]
            qs[HISTS + slot * CROWS : HISTS + (slot + 1) * CROWS, :] = piece[ROWS:QROWS, :]
        acc[...] = jnp.zeros_like(acc)
    else:
        acc[...] = in_ref[...]

    def owner_of(event):
        low, stop = jnp.int32(NOBODY), jnp.int32(0)
        for s, t in zip(starts, ends):
            inside = (s <= event) & (event < t)
            low = jnp.where(inside, s, low)
            stop = jnp.where(inside, t, stop)
        return low, stop

    column = lax.broadcasted_iota(jnp.int32, (1, ROWS), 1)
    blocks = [lax.rem(z + offset, NZ) for offset in offsets]
    events = [(y * NZ + block) * ROWS + column for block in blocks]

    def weights(rows, i, h):
        return silu_weight(contract_lanes(rows, k_refs[i][0:ROWS, head(h)]))

    def values(i, h):
        return v_refs[i][kv_row : kv_row + ROWS, head(h)]

    def slot_step(slot, carry):
        event = ((y + slot) * NZ + z) * ROWS
        row = pl.multiple_of(slot * ROWS, ROWS)
        low0, _ = owner_of(event)
        low1, _ = owner_of(event + BLOCK)
        keeps = []
        for block, keys in zip(blocks, events):
            late = jnp.where((slot == 0) & (block >= z), NOBODY, 0)
            keeps.append([flag(keys >= jnp.maximum(low, late)) for low in (low0, low1)])
        for h in range(HEADS):
            out = None
            for i in range(len(blocks)):
                w = weights(qs[pl.ds(row, ROWS), head(h)], i, h)
                w = jnp.concatenate([w[0:BLOCK] * keeps[i][0], w[BLOCK:ROWS] * keeps[i][1]], axis=0)
                term = jnp.dot(w, values(i, h), preferred_element_type=jnp.float32)
                out = term if out is None else out + term
            acc[pl.ds(row, ROWS), head(h)] += out
        return carry

    lax.fori_loop(0, NY - y, slot_step, 0)

    user = user_ref[...]
    cand_low = jnp.where(user == 0, starts[0], starts[1])
    cand_stop = jnp.where(user == 0, ends[0], ends[1])
    keeps = [flag((keys >= cand_low) & (keys < cand_stop)) for keys in events]
    for h in range(HEADS):
        out = None
        for i in range(len(blocks)):
            w = weights(qs[HISTS:TOTAL, head(h)], i, h) * keeps[i]
            term = jnp.dot(w, values(i, h), preferred_element_type=jnp.float32)
            out = term if out is None else out + term
        acc[HISTS:TOTAL, head(h)] += out

    if first:
        at = lax.broadcasted_iota(jnp.int32, (ROWS, ROWS), 0)
        to = lax.broadcasted_iota(jnp.int32, (ROWS, ROWS), 1)
        event = (y * NZ + z) * ROWS
        low0, _ = owner_of(event)
        low1, _ = owner_of(event + BLOCK)
        keep = flag((to <= at) & (event + to >= jnp.where(at < BLOCK, low0, low1)))
        for h in range(HEADS):
            w = weights(qs[0:ROWS, head(h)], 0, h) * keep
            acc[0:ROWS, head(h)] += jnp.dot(w, values(0, h), preferred_element_type=jnp.float32)

    if last:
        at = lax.broadcasted_iota(jnp.int32, (ROWS, HD), 0)
        for slot in range(NY):
            event = ((y + slot) * NZ + z) * ROWS
            _, stop0 = owner_of(event)
            _, stop1 = owner_of(event + BLOCK)
            stop = jnp.where(at < BLOCK, stop0, stop1)
            out = own if slot == 0 else away[slot - 1]
            rows = jnp.where(event + at < stop, acc[slot * ROWS : (slot + 1) * ROWS, :], 0.0)
            out[0:ROWS, :] = rows.astype(out.dtype)
            out[ROWS:QROWS, :] = acc[HISTS + slot * CROWS : HISTS + (slot + 1) * CROWS, :].astype(out.dtype)


def attend(offsets, where, users, blocks, queries, total, last=False):
    first = total is None
    state = jax.ShapeDtypeStruct((TOTAL, HD), jnp.float32)
    if last:
        shapes = [jax.ShapeDtypeStruct((QROWS, HD), jnp.float32)] + [jax.ShapeDtypeStruct((QROWS, HD), jnp.bfloat16)] * 3
    elif first:
        shapes = [state, jax.ShapeDtypeStruct((TOTAL, HD), jnp.bfloat16)]
    else:
        shapes = [state]
    args = [*blocks, *queries] if first else [*blocks, queries, total]
    return pl.pallas_call(
        functools.partial(attend_kernel, offsets, first, last),
        in_specs=[SMEM] * 3 + [VMEM] * (1 + len(args)),
        out_specs=[VMEM] * len(shapes),
        out_shape=shapes,
        scratch_shapes=[pltpu.VMEM((TOTAL, HD), jnp.float32)] * last,
        compiler_params=pltpu.CompilerParams(vmem_limit_bytes=VMEM_LIMIT),
        cost_estimate=pl.CostEstimate(
            flops=4 * TOTAL * len(offsets) * ROWS * HD, bytes_accessed=1 << 20, transcendentals=0
        ),
        name="attend",
    )(*where, users, *args)


def finish_kernel(t0, t1, t2, t3, hg, hx, cq, ck, cv, cg, cx, w_ref, ho, co):
    total = t0[...]
    for part in (t1, t2, t3):
        total = total + part[...].astype(jnp.float32)
    own = []
    for h in range(HEADS):
        scores = jnp.sum(cq[:, head(h)].astype(jnp.float32) * ck[:, head(h)].astype(jnp.float32), axis=-1, keepdims=True)
        own.append(silu_weight(scores).astype(jnp.float32) * cv[:, head(h)].astype(jnp.float32))

    def tail(rows, gate, inputs, out):
        mean = jnp.mean(rows, axis=-1, keepdims=True)
        centered = rows - mean
        spread = jnp.mean(centered * centered, axis=-1, keepdims=True)
        normed = centered * lax.rsqrt(spread + 1e-05)
        gated = (normed * gate[...].astype(jnp.float32)).astype(jnp.bfloat16)
        mixed = jnp.dot(gated, w_ref[...], preferred_element_type=jnp.float32)
        out[...] = (inputs[...].astype(jnp.float32) + mixed).astype(jnp.bfloat16)

    tail(total[0:ROWS], hg, hx, ho)
    tail(total[ROWS:QROWS] + jnp.concatenate(own, axis=1), cg, cx, co)


def call(kernel, shapes, *args, limit=VMEM_LIMIT):
    return pl.pallas_call(
        kernel,
        in_specs=[VMEM] * len(args),
        out_specs=[VMEM] * len(shapes),
        out_shape=[jax.ShapeDtypeStruct(s, jnp.bfloat16) for s in shapes],
        compiler_params=pltpu.CompilerParams(vmem_limit_bytes=limit),
    )(*args)


def turn(array, axis, step):
    count = NY if axis == "y" else NZ
    return lax.ppermute(array, axis, [(i, (i + step) % count) for i in range(count)])


def on_device(
    hist_query, hist_key, hist_value, hist_gate, hist_input,
    cand_query, cand_key, cand_value, cand_gate, cand_input,
    cand_user, hist_len, hist_start, out_weight,
):
    y, z = lax.axis_index("y"), lax.axis_index("z")
    where = (jnp.stack([y, z]).astype(jnp.int32), hist_start, hist_len)
    users = lax.dynamic_index_in_dim(cand_user.reshape(NY, NZ, CROWS), z, axis=1, keepdims=False)
    users = lax.dynamic_slice_in_dim(jnp.concatenate([users, users]), y, NY).reshape(NY * CROWS, 1)
    kv, mine = call(
        stack_kernel, [(2 * ROWS, HD), (QROWS, HD)], hist_key, hist_value, hist_query, cand_query, limit=WIDE_LIMIT
    )
    up, down = turn(kv, "z", 1), turn(kv, "z", -1)
    queries = [mine] + [turn(mine, "y", -k) for k in (1, 2, 3)]
    up, *queries = lax.optimization_barrier((up, *queries))
    blocks = (kv, up, down)
    up, down = turn(up, "z", 1), turn(down, "z", -1)
    total, queries = attend((0, NZ - 1, 1), where, users, blocks, queries, None)
    up, held = lax.optimization_barrier((up, total))
    down, total = lax.optimization_barrier((down, held))
    blocks = (up, down)
    up, down = turn(up, "z", 1), turn(down, "z", -1)
    (total,) = attend((NZ - 2, 2), where, users, blocks, queries, total)
    up, held = lax.optimization_barrier((up, total))
    down, total = lax.optimization_barrier((down, held))
    keys, values = turn(up[:ROWS], "z", 1), turn(down[ROWS:], "z", -1)
    (total,) = attend((NZ - 3, 3), where, users, (up, down), queries, total)
    own, *away = attend((4,), where, users, (keys, values), queries, total, last=True)
    back = [turn(a, "y", k) for k, a in zip((1, 2, 3), away)]
    return tuple(
        call(
            finish_kernel, [hist_input.shape, cand_input.shape],
            own, *back, hist_gate, hist_input, cand_query, cand_key, cand_value, cand_gate, cand_input, out_weight,
        )
    )


def solution(mesh):
    grid = Mesh(mesh.devices.reshape(-1, NY, NZ), ("batch", "y", "z"))
    rows = P(("batch", "y", "z"), None)
    return jax.shard_map(
        on_device,
        mesh=grid,
        in_specs=(rows,) * 10 + (P("batch"), P("batch"), P("batch"), P()),
        out_specs=(rows, rows),
        check_vma=False,
    )
```

time: 109 us -> 131 us (1.20)
  the two profiles are of different devices: /device:TPU:56 before, /device:TPU:13 now
where the time goes in v6:
time: 131 us
  starting transfers between devices  51.6 us (39%)
  waiting for transfers between devices  48.3 us (37%)
  Pallas kernels  25.5 us (19%)
  local copies, waits for them, and re-layouts  4.3 us (3%)
    ppermute x14, starting transfers between devices, turn(): lax.ppermute(array, axis, [(i, (i + step) % count) for i in range(count)])  51.6 us
    ppermute x14, waiting for transfers between devices, turn(): lax.ppermute(array, axis, [(i, (i + step) % count) for i in range(count)])  48.3 us
    pallas_call x4, Pallas kernels, attend(): pl.pallas_call(functools.partial(attend_kernel, offsets, first, last), in...  21.9 us
    pallas_call x2, Pallas kernels, call(): pl.pallas_call(kernel, in_specs=[VMEM] * len(args), out_specs=[VMEM] * le...  3.56 us
    unnamed x28, local copies, waits for them, and re-layouts  3.38 us
  transfers between devices with their start and end apart: 14, of which 7 were waited for; matrix products, arithmetic and copies ran while one was open for 1% of the time, Pallas kernels for 14%

profile of v6, /device:TPU:13, one launch (start us, length us, event | category | flops | bytes accessed | tf_op | source)
XLA Modules:
  0.0 130.8 jit_solution(5755444891616726150)
XLA Ops:
  0.6 2.0 %shard_map.149 = (bf16[512,512]{1,0:T(8,128)(2,1)}, bf16[288,512]{1,0:T(8,128)(2,1)}) custom-call(bf16[256,512]{1,0:T(8,128)(2,1)} %k_ref.1, bf16[256,512]{1,0:T(8,128)(2,1)} %v_ref.1, bf16[256,512]{1,0:T(8,128)(2,1)} %q_ref.1, bf16[32,512]{1,0:T(8,128)(2,1)} %cq.1), custom_call_target="tpu_custom_call" | custom-call | tf_op jit(solution)/shard_map/pallas_call | solution.py:205
  2.7 4.0 %collective-permute-start = (bf16[512,512]{1,0:T(8,128)(2,1)}, bf16[512,512]{1,0:T(8,128)(2,1)S(1)}, u32[]{:S(2)}, u32[]{:S(2)}) collective-permute-start(bf16[512,512]{1,0:T(8,128)(2,1)} %get-tuple-element.23.refs_0_), channel_id=1, source_target_pairs={{0,1},{1,2},{2,3},{3,4},{4,5},{5,6},{6,7},{7,0},{8,9},{9,10},{10,1... | collective-permute-start | bytes 1572872 | tf_op jit(solution)/shard_map/ppermute | solution.py:216
  6.7 8.6 %collective-permute-start.5 = (bf16[512,512]{1,0:T(8,128)(2,1)}, bf16[512,512]{1,0:T(8,128)(2,1)S(1)}, u32[]{:S(2)}, u32[]{:S(2)}) collective-permute-start(bf16[512,512]{1,0:T(8,128)(2,1)} %get-tuple-element.23.refs_0_), channel_id=1, source_target_pairs={{0,7},{1,0},{2,1},{3,2},{4,3},{5,4},{6,5},{7,6},{8,15},{9,8},{10,9... | collective-permute-start | bytes 1572872 | tf_op jit(solution)/shard_map/ppermute | solution.py:216
  15.2 2.1 %collective-permute-start.1 = (bf16[288,512]{1,0:T(8,128)(2,1)}, bf16[288,512]{1,0:T(8,128)(2,1)S(1)}, u32[]{:S(2)}, u32[]{:S(2)}) collective-permute-start(bf16[288,512]{1,0:T(8,128)(2,1)} %get-tuple-element.26.refs_3_), channel_id=1, source_target_pairs={{0,24},{8,0},{16,8},{24,16},{1,25},{9,1},{17,9},{25,17},{2,26},{10... | collective-permute-start | bytes 884744 | tf_op jit(solution)/shard_map/ppermute | solution.py:216
  17.3 4.2 %collective-permute-start.2 = (bf16[288,512]{1,0:T(8,128)(2,1)}, bf16[288,512]{1,0:T(8,128)(2,1)S(1)}, u32[]{:S(2)}, u32[]{:S(2)}) collective-permute-start(bf16[288,512]{1,0:T(8,128)(2,1)} %get-tuple-element.26.refs_3_), channel_id=1, source_target_pairs={{0,16},{8,24},{16,0},{24,8},{1,17},{9,25},{17,1},{25,9},{2,18},{10... | collective-permute-start | bytes 884744 | tf_op jit(solution)/shard_map/ppermute | solution.py:216
  21.6 4.1 %collective-permute-start.3 = (bf16[288,512]{1,0:T(8,128)(2,1)}, bf16[288,512]{1,0:T(8,128)(2,1)S(1)}, u32[]{:S(2)}, u32[]{:S(2)}) collective-permute-start(bf16[288,512]{1,0:T(8,128)(2,1)} %get-tuple-element.26.refs_3_), channel_id=1, source_target_pairs={{0,8},{8,16},{16,24},{24,0},{1,9},{9,17},{17,25},{25,1},{2,10},{10... | collective-permute-start | bytes 884744 | tf_op jit(solution)/shard_map/ppermute | solution.py:216
  26.4 13.6 %collective-permute-done.2.refs_5_ = bf16[288,512]{1,0:T(8,128)(2,1)S(1)} collective-permute-done((bf16[288,512]{1,0:T(8,128)(2,1)}, bf16[288,512]{1,0:T(8,128)(2,1)S(1)}, u32[]{:S(2)}, u32[]{:S(2)}) %collective-permute-start.2) | collective-permute-done | bytes 294944 | tf_op jit(solution)/shard_map/ppermute | solution.py:216
  40.0 6.3 %collective-permute-done.3.refs_6_ = bf16[288,512]{1,0:T(8,128)(2,1)S(1)} collective-permute-done((bf16[288,512]{1,0:T(8,128)(2,1)}, bf16[288,512]{1,0:T(8,128)(2,1)S(1)}, u32[]{:S(2)}, u32[]{:S(2)}) %collective-permute-start.3) | collective-permute-done | bytes 294944 | tf_op jit(solution)/shard_map/ppermute | solution.py:216
  46.4 1.9 %collective-permute-start.4 = (bf16[512,512]{1,0:T(8,128)(2,1)S(1)}, bf16[512,512]{1,0:T(8,128)(2,1)S(1)}, u32[]{:S(2)}, u32[]{:S(2)}) collective-permute-start(bf16[512,512]{1,0:T(8,128)(2,1)S(1)} %collective-permute-done.refs_1_), channel_id=1, source_target_pairs={{0,1},{1,2},{2,3},{3,4},{4,5},{5,6},{6,7},{7,0},{8,9},{9,10},{10,1... | collective-permute-start | bytes 1572872 | tf_op jit(solution)/shard_map/ppermute | solution.py:216
  48.3 4.6 %collective-permute-start.7 = (bf16[512,512]{1,0:T(8,128)(2,1)S(1)}, bf16[512,512]{1,0:T(8,128)(2,1)S(1)}, u32[]{:S(2)}, u32[]{:S(2)}) collective-permute-start(bf16[512,512]{1,0:T(8,128)(2,1)S(1)} %collective-permute-done.5.refs_2_), channel_id=1, source_target_pairs={{0,7},{1,0},{2,1},{3,2},{4,3},{5,4},{6,5},{7,6},{8,15},{9,8},{10,9... | collective-permute-start | bytes 1572872 | tf_op jit(solution)/shard_map/ppermute | solution.py:216
  56.4 8.1 %attend.4 = (f32[1152,512]{1,0:T(8,128)S(1)}, bf16[1152,512]{1,0:T(8,128)(2,1)S(1)}) custom-call(s32[2]{0:T(128)S(1)} %pad_add_fusion.1.place_ref, s32[2]{0:T(128)S(1)} %copy-done.8, s32[2]{0:T(128)S(1)} %copy-done.10, s32[128,1]{1,0:T(8,128)S(1)} %reshape.12.user_ref, bf16[512,512]{1,0:T(8,128)(2,1)S(1)} %copy-done.12, ...), custom_call_target="tpu_custom_call" | custom-call | flops 1811939328 | bytes 1048576 | tf_op jit(solution)/shard_map/attend/pallas_call | solution.py:168
  64.6 1.9 %collective-permute-start.6 = (bf16[512,512]{1,0:T(8,128)(2,1)S(1)}, bf16[512,512]{1,0:T(8,128)(2,1)S(1)}, u32[]{:S(2)}, u32[]{:S(2)}) collective-permute-start(bf16[512,512]{1,0:T(8,128)(2,1)S(1)} %collective-permute-done.4.refs_0_), channel_id=1, source_target_pairs={{0,1},{1,2},{2,3},{3,4},{4,5},{5,6},{6,7},{7,0},{8,9},{9,10},{10,1... | collective-permute-start | bytes 1572872 | tf_op jit(solution)/shard_map/ppermute | solution.py:216
  66.5 4.6 %collective-permute-start.9 = (bf16[512,512]{1,0:T(8,128)(2,1)S(1)}, bf16[512,512]{1,0:T(8,128)(2,1)S(1)}, u32[]{:S(2)}, u32[]{:S(2)}) collective-permute-start(bf16[512,512]{1,0:T(8,128)(2,1)S(1)} %collective-permute-done.7.refs_1_), channel_id=1, source_target_pairs={{0,7},{1,0},{2,1},{3,2},{4,3},{5,4},{6,5},{7,6},{8,15},{9,8},{10,9... | collective-permute-start | bytes 1572872 | tf_op jit(solution)/shard_map/ppermute | solution.py:216
  71.1 5.2 %attend.5.refs_3_ = f32[1152,512]{1,0:T(8,128)S(1)} custom-call(s32[2]{0:T(128)S(1)} %pad_add_fusion.1.place_ref, s32[2]{0:T(128)S(1)} %copy-done.8, s32[2]{0:T(128)S(1)} %copy-done.10, s32[128,1]{1,0:T(8,128)S(1)} %reshape.12.user_ref, bf16[512,512]{1,0:T(8,128)(2,1)S(1)} %collective-permute-done.4.refs_0_, ...), custom_call_target="tpu_custom_call" | custom-call | flops 1207959552 | bytes 1048576 | tf_op jit(solution)/shard_map/attend/pallas_call | solution.py:168
  76.3 3.8 %collective-permute-done.6.refs_0_ = bf16[512,512]{1,0:T(8,128)(2,1)S(1)} collective-permute-done((bf16[512,512]{1,0:T(8,128)(2,1)S(1)}, bf16[512,512]{1,0:T(8,128)(2,1)S(1)}, u32[]{:S(2)}, u32[]{:S(2)}) %collective-permute-start.6) | collective-permute-done | bytes 524320 | tf_op jit(solution)/shard_map/ppermute | solution.py:216
  81.0 5.3 %collective-permute-start.10 = (bf16[256,512]{1,0:T(8,128)(2,1)S(1)}, bf16[256,512]{1,0:T(8,128)(2,1)S(1)}, u32[]{:S(2)}, u32[]{:S(2)}) collective-permute-start(bf16[256,512]{1,0:T(8,128)(2,1)S(1)} %slice.7), channel_id=1, source_target_pairs={{0,7},{1,0},{2,1},{3,2},{4,3},{5,4},{6,5},{7,6},{8,15},{9,8},{10,9... | collective-permute-start | bytes 786440 | tf_op jit(solution)/shard_map/ppermute | solution.py:216
  86.3 1.9 %collective-permute-start.8 = (bf16[256,512]{1,0:T(8,128)(2,1)S(1)}, bf16[256,512]{1,0:T(8,128)(2,1)S(1)}, u32[]{:S(2)}, u32[]{:S(2)}) collective-permute-start(bf16[256,512]{1,0:T(8,128)(2,1)S(1)} %slice.6), channel_id=1, source_target_pairs={{0,1},{1,2},{2,3},{3,4},{4,5},{5,6},{6,7},{7,0},{8,9},{9,10},{10,1... | collective-permute-start | bytes 786440 | tf_op jit(solution)/shard_map/ppermute | solution.py:216
  88.3 5.2 %attend.6.refs_3_ = f32[1152,512]{1,0:T(8,128)S(1)} custom-call(s32[2]{0:T(128)S(1)} %pad_add_fusion.1.place_ref, s32[2]{0:T(128)S(1)} %copy-done.9, s32[2]{0:T(128)S(1)} %copy-done.11, s32[128,1]{1,0:T(8,128)S(1)} %reshape.12.user_ref, bf16[512,512]{1,0:T(8,128)(2,1)S(1)} %collective-permute-done.6.refs_0_, ...), custom_call_target="tpu_custom_call" | custom-call | flops 1207959552 | bytes 1048576 | tf_op jit(solution)/shard_map/attend/pallas_call | solution.py:168
  94.6 3.4 %attend.7 = (f32[288,512]{1,0:T(8,128)S(1)}, bf16[288,512]{1,0:T(8,128)(2,1)S(1)}, bf16[288,512]{1,0:T(8,128)(2,1)S(1)}, bf16[288,512]{1,0:T(8,128)(2,1)S(1)}) custom-call(s32[2]{0:T(128)S(1)} %pad_add_fusion.1.place_ref, s32[2]{0:T(128)S(1)} %copy-done.9, s32[2]{0:T(128)S(1)} %copy-done.11, s32[128,1]{1,0:T(8,128)S(1)} %reshape.12.user_ref, ...), custom_call_target="tpu_custom_call" | custom-call | flops 603979776 | bytes 1048576 | tf_op jit(solution)/shard_map/attend/pallas_call | solution.py:168
  98.1 1.9 %collective-permute-start.11 = (bf16[288,512]{1,0:T(8,128)(2,1)S(1)}, bf16[288,512]{1,0:T(8,128)(2,1)S(1)}, u32[]{:S(2)}, u32[]{:S(2)}) collective-permute-start(bf16[288,512]{1,0:T(8,128)(2,1)S(1)} %get-tuple-element.41), channel_id=1, source_target_pairs={{0,8},{8,16},{16,24},{24,0},{1,9},{9,17},{17,25},{25,1},{2,10},{10... | collective-permute-start | bytes 884744 | tf_op jit(solution)/shard_map/ppermute | solution.py:216
  100.0 4.6 %collective-permute-start.12 = (bf16[288,512]{1,0:T(8,128)(2,1)S(1)}, bf16[288,512]{1,0:T(8,128)(2,1)S(1)}, u32[]{:S(2)}, u32[]{:S(2)}) collective-permute-start(bf16[288,512]{1,0:T(8,128)(2,1)S(1)} %get-tuple-element.42), channel_id=1, source_target_pairs={{0,16},{8,24},{16,0},{24,8},{1,17},{9,25},{17,1},{25,9},{2,18},{10... | collective-permute-start | bytes 884744 | tf_op jit(solution)/shard_map/ppermute | solution.py:216
  104.6 1.9 %collective-permute-start.13 = (bf16[288,512]{1,0:T(8,128)(2,1)S(1)}, bf16[288,512]{1,0:T(8,128)(2,1)S(1)}, u32[]{:S(2)}, u32[]{:S(2)}) collective-permute-start(bf16[288,512]{1,0:T(8,128)(2,1)S(1)} %get-tuple-element.43), channel_id=1, source_target_pairs={{0,24},{8,0},{16,8},{24,16},{1,25},{9,1},{17,9},{25,17},{2,26},{10... | collective-permute-start | bytes 884744 | tf_op jit(solution)/shard_map/ppermute | solution.py:216
  106.6 17.3 %collective-permute-done.12.t2 = bf16[288,512]{1,0:T(8,128)(2,1)S(1)} collective-permute-done((bf16[288,512]{1,0:T(8,128)(2,1)S(1)}, bf16[288,512]{1,0:T(8,128)(2,1)S(1)}, u32[]{:S(2)}, u32[]{:S(2)}) %collective-permute-start.12) | collective-permute-done | bytes 294944 | tf_op jit(solution)/shard_map/ppermute | solution.py:216
  123.9 5.4 %collective-permute-done.13.t3 = bf16[288,512]{1,0:T(8,128)(2,1)S(1)} collective-permute-done((bf16[288,512]{1,0:T(8,128)(2,1)S(1)}, bf16[288,512]{1,0:T(8,128)(2,1)S(1)}, u32[]{:S(2)}, u32[]{:S(2)}) %collective-permute-start.13) | collective-permute-done | bytes 294944 | tf_op jit(solution)/shard_map/ppermute | solution.py:216
  (46 shorter events, 7.9 us)
Async XLA Ops:
  2.7 43.7 %collective-permute-start = (bf16[512,512]{1,0:T(8,128)(2,1)}, bf16[512,512]{1,0:T(8,128)(2,1)S(1)}, u32[]{:S(2)}, u32[]{:S(2)}) collective-permute-start(bf16[512,512]{1,0:T(8,128)(2,1)} %get-tuple-element.23.refs_0_), channel_id=1, source_target_pairs={{0,1},{1,2},{2,3},{3,4},{4,5},{5,6},{6,7},{7,0},{8,9},{9,10},{10,1... | collective-permute-start | bytes 1572872 | tf_op jit(solution)/shard_map/ppermute | solution.py:216
  6.7 41.6 %collective-permute-start.5 = (bf16[512,512]{1,0:T(8,128)(2,1)}, bf16[512,512]{1,0:T(8,128)(2,1)S(1)}, u32[]{:S(2)}, u32[]{:S(2)}) collective-permute-start(bf16[512,512]{1,0:T(8,128)(2,1)} %get-tuple-element.23.refs_0_), channel_id=1, source_target_pairs={{0,7},{1,0},{2,1},{3,2},{4,3},{5,4},{6,5},{7,6},{8,15},{9,8},{10,9... | collective-permute-start | bytes 1572872 | tf_op jit(solution)/shard_map/ppermute | solution.py:216
  15.2 11.2 %collective-permute-start.1 = (bf16[288,512]{1,0:T(8,128)(2,1)}, bf16[288,512]{1,0:T(8,128)(2,1)S(1)}, u32[]{:S(2)}, u32[]{:S(2)}) collective-permute-start(bf16[288,512]{1,0:T(8,128)(2,1)} %get-tuple-element.26.refs_3_), channel_id=1, source_target_pairs={{0,24},{8,0},{16,8},{24,16},{1,25},{9,1},{17,9},{25,17},{2,26},{10... | collective-permute-start | bytes 884744 | tf_op jit(solution)/shard_map/ppermute | solution.py:216
  17.3 22.7 %collective-permute-start.2 = (bf16[288,512]{1,0:T(8,128)(2,1)}, bf16[288,512]{1,0:T(8,128)(2,1)S(1)}, u32[]{:S(2)}, u32[]{:S(2)}) collective-permute-start(bf16[288,512]{1,0:T(8,128)(2,1)} %get-tuple-element.26.refs_3_), channel_id=1, source_target_pairs={{0,16},{8,24},{16,0},{24,8},{1,17},{9,25},{17,1},{25,9},{2,18},{10... | collective-permute-start | bytes 884744 | tf_op jit(solution)/shard_map/ppermute | solution.py:216
  21.6 24.8 %collective-permute-start.3 = (bf16[288,512]{1,0:T(8,128)(2,1)}, bf16[288,512]{1,0:T(8,128)(2,1)S(1)}, u32[]{:S(2)}, u32[]{:S(2)}) collective-permute-start(bf16[288,512]{1,0:T(8,128)(2,1)} %get-tuple-element.26.refs_3_), channel_id=1, source_target_pairs={{0,8},{8,16},{16,24},{24,0},{1,9},{9,17},{17,25},{25,1},{2,10},{10... | collective-permute-start | bytes 884744 | tf_op jit(solution)/shard_map/ppermute | solution.py:216
  46.4 18.2 %collective-permute-start.4 = (bf16[512,512]{1,0:T(8,128)(2,1)S(1)}, bf16[512,512]{1,0:T(8,128)(2,1)S(1)}, u32[]{:S(2)}, u32[]{:S(2)}) collective-permute-start(bf16[512,512]{1,0:T(8,128)(2,1)S(1)} %collective-permute-done.refs_1_), channel_id=1, source_target_pairs={{0,1},{1,2},{2,3},{3,4},{4,5},{5,6},{6,7},{7,0},{8,9},{9,10},{10,1... | collective-permute-start | bytes 1572872 | tf_op jit(solution)/shard_map/ppermute | solution.py:216
  48.3 18.2 %collective-permute-start.7 = (bf16[512,512]{1,0:T(8,128)(2,1)S(1)}, bf16[512,512]{1,0:T(8,128)(2,1)S(1)}, u32[]{:S(2)}, u32[]{:S(2)}) collective-permute-start(bf16[512,512]{1,0:T(8,128)(2,1)S(1)} %collective-permute-done.5.refs_2_), channel_id=1, source_target_pairs={{0,7},{1,0},{2,1},{3,2},{4,3},{5,4},{6,5},{7,6},{8,15},{9,8},{10,9... | collective-permute-start | bytes 1572872 | tf_op jit(solution)/shard_map/ppermute | solution.py:216
  64.6 15.5 %collective-permute-start.6 = (bf16[512,512]{1,0:T(8,128)(2,1)S(1)}, bf16[512,512]{1,0:T(8,128)(2,1)S(1)}, u32[]{:S(2)}, u32[]{:S(2)}) collective-permute-start(bf16[512,512]{1,0:T(8,128)(2,1)S(1)} %collective-permute-done.4.refs_0_), channel_id=1, source_target_pairs={{0,1},{1,2},{2,3},{3,4},{4,5},{5,6},{6,7},{7,0},{8,9},{9,10},{10,1... | collective-permute-start | bytes 1572872 | tf_op jit(solution)/shard_map/ppermute | solution.py:216
  66.5 14.4 %collective-permute-start.9 = (bf16[512,512]{1,0:T(8,128)(2,1)S(1)}, bf16[512,512]{1,0:T(8,128)(2,1)S(1)}, u32[]{:S(2)}, u32[]{:S(2)}) collective-permute-start(bf16[512,512]{1,0:T(8,128)(2,1)S(1)} %collective-permute-done.7.refs_1_), channel_id=1, source_target_pairs={{0,7},{1,0},{2,1},{3,2},{4,3},{5,4},{6,5},{7,6},{8,15},{9,8},{10,9... | collective-permute-start | bytes 1572872 | tf_op jit(solution)/shard_map/ppermute | solution.py:216
  71.1 17.2 %copy-start.9 = (s32[2]{0:T(128)S(1)}, s32[2]{0:T(128)}, u32[]{:S(2)}) copy-start(s32[2]{0:T(128)} %start_ref.7) | copy-start | bytes 28
  71.1 17.2 %copy-start.11 = (s32[2]{0:T(128)S(1)}, s32[2]{0:T(128)}, u32[]{:S(2)}) copy-start(s32[2]{0:T(128)} %len_ref.7) | copy-start | bytes 28
  81.0 12.6 %collective-permute-start.10 = (bf16[256,512]{1,0:T(8,128)(2,1)S(1)}, bf16[256,512]{1,0:T(8,128)(2,1)S(1)}, u32[]{:S(2)}, u32[]{:S(2)}) collective-permute-start(bf16[256,512]{1,0:T(8,128)(2,1)S(1)} %slice.7), channel_id=1, source_target_pairs={{0,7},{1,0},{2,1},{3,2},{4,3},{5,4},{6,5},{7,6},{8,15},{9,8},{10,9... | collective-permute-start | bytes 786440 | tf_op jit(solution)/shard_map/ppermute | solution.py:216
  86.3 8.3 %collective-permute-start.8 = (bf16[256,512]{1,0:T(8,128)(2,1)S(1)}, bf16[256,512]{1,0:T(8,128)(2,1)S(1)}, u32[]{:S(2)}, u32[]{:S(2)}) collective-permute-start(bf16[256,512]{1,0:T(8,128)(2,1)S(1)} %slice.6), channel_id=1, source_target_pairs={{0,1},{1,2},{2,3},{3,4},{4,5},{5,6},{6,7},{7,0},{8,9},{9,10},{10,1... | collective-permute-start | bytes 786440 | tf_op jit(solution)/shard_map/ppermute | solution.py:216
  93.4 35.8 %copy-start = (bf16[512,1024]{1,0:T(8,128)(2,1)S(1)}, bf16[512,1024]{1,0:T(8,128)(2,1)}, u32[]{:S(2)}) copy-start(bf16[512,1024]{1,0:T(8,128)(2,1)} %w_ref.1) | copy-start | bytes 3145732
  93.5 35.8 %copy-start.1 = (bf16[256,1024]{1,0:T(8,128)(2,1)S(1)}, bf16[256,1024]{1,0:T(8,128)(2,1)}, u32[]{:S(2)}) copy-start(bf16[256,1024]{1,0:T(8,128)(2,1)} %hx.1) | copy-start | bytes 1572868
  93.5 35.8 %copy-start.2 = (bf16[256,512]{1,0:T(8,128)(2,1)S(1)}, bf16[256,512]{1,0:T(8,128)(2,1)}, u32[]{:S(2)}) copy-start(bf16[256,512]{1,0:T(8,128)(2,1)} %hg.1) | copy-start | bytes 786436
  93.5 35.8 %copy-start.3 = (bf16[32,512]{1,0:T(8,128)(2,1)S(1)}, bf16[32,512]{1,0:T(8,128)(2,1)}, u32[]{:S(2)}) copy-start(bf16[32,512]{1,0:T(8,128)(2,1)} %cq.1) | copy-start | bytes 98308
  93.5 35.8 %copy-start.4 = (bf16[32,1024]{1,0:T(8,128)(2,1)S(1)}, bf16[32,1024]{1,0:T(8,128)(2,1)}, u32[]{:S(2)}) copy-start(bf16[32,1024]{1,0:T(8,128)(2,1)} %cx.1) | copy-start | bytes 196612
  93.5 35.7 %copy-start.5 = (bf16[32,512]{1,0:T(8,128)(2,1)S(1)}, bf16[32,512]{1,0:T(8,128)(2,1)}, u32[]{:S(2)}) copy-start(bf16[32,512]{1,0:T(8,128)(2,1)} %ck.1) | copy-start | bytes 98308
  93.5 35.7 %copy-start.6 = (bf16[32,512]{1,0:T(8,128)(2,1)S(1)}, bf16[32,512]{1,0:T(8,128)(2,1)}, u32[]{:S(2)}) copy-start(bf16[32,512]{1,0:T(8,128)(2,1)} %cv.1) | copy-start | bytes 98308
  93.5 35.7 %copy-start.7 = (bf16[32,512]{1,0:T(8,128)(2,1)S(1)}, bf16[32,512]{1,0:T(8,128)(2,1)}, u32[]{:S(2)}) copy-start(bf16[32,512]{1,0:T(8,128)(2,1)} %cg.1) | copy-start | bytes 98308
  98.1 8.5 %collective-permute-start.11 = (bf16[288,512]{1,0:T(8,128)(2,1)S(1)}, bf16[288,512]{1,0:T(8,128)(2,1)S(1)}, u32[]{:S(2)}, u32[]{:S(2)}) collective-permute-start(bf16[288,512]{1,0:T(8,128)(2,1)S(1)} %get-tuple-element.41), channel_id=1, source_target_pairs={{0,8},{8,16},{16,24},{24,0},{1,9},{9,17},{17,25},{25,1},{2,10},{10... | collective-permute-start | bytes 884744 | tf_op jit(solution)/shard_map/ppermute | solution.py:216
  100.0 23.8 %collective-permute-start.12 = (bf16[288,512]{1,0:T(8,128)(2,1)S(1)}, bf16[288,512]{1,0:T(8,128)(2,1)S(1)}, u32[]{:S(2)}, u32[]{:S(2)}) collective-permute-start(bf16[288,512]{1,0:T(8,128)(2,1)S(1)} %get-tuple-element.42), channel_id=1, source_target_pairs={{0,16},{8,24},{16,0},{24,8},{1,17},{9,25},{17,1},{25,9},{2,18},{10... | collective-permute-start | bytes 884744 | tf_op jit(solution)/shard_map/ppermute | solution.py:216
  104.6 24.6 %collective-permute-start.13 = (bf16[288,512]{1,0:T(8,128)(2,1)S(1)}, bf16[288,512]{1,0:T(8,128)(2,1)S(1)}, u32[]{:S(2)}, u32[]{:S(2)}) collective-permute-start(bf16[288,512]{1,0:T(8,128)(2,1)S(1)} %get-tuple-element.43), channel_id=1, source_target_pairs={{0,24},{8,0},{16,8},{24,16},{1,25},{9,1},{17,9},{25,17},{2,26},{10... | collective-permute-start | bytes 884744 | tf_op jit(solution)/shard_map/ppermute | solution.py:216
  (4 other events, 3.3 us)

commit v7 on v6

--- a/solution.py
+++ b/solution.py
@@ -53,105 +53,95 @@
 
 def attend_kernel(offsets, first, last, place_ref, start_ref, len_ref, user_ref, *refs):
     refs = list(refs)
-    if last:
-        k_refs, v_refs, kv_row = [refs.pop(0)], [refs.pop(0)], 0
-    else:
-        k_refs = v_refs = [refs.pop(0) for _ in offsets]
-        kv_row = ROWS
+    blocks = [refs.pop(0) for _ in offsets]
     if first:
         pieces = [refs.pop(0) for _ in range(NY)]
-        acc, qs = refs
+        acc, qs, kv = refs
     else:
         qs, in_ref = refs.pop(0), refs.pop(0)
         if last:
-            own, *away, acc = refs
+            own, *away, acc, kv = refs
         else:
-            (acc,) = refs
+            acc, kv = refs
     y = place_ref[0]
     z = place_ref[1]
     starts = [start_ref[u] for u in range(2)]
     ends = [start_ref[u] + len_ref[u] for u in range(2)]
 
+    for i, block in enumerate(blocks):
+        kv[i * 2 * ROWS : (i + 1) * 2 * ROWS, :] = block[...]
     if first:
         for slot, piece in enumerate(pieces):
-            qs[slot * ROWS : (slot + 1) * ROWS, :] = piece[0:ROWS, :]
+            at = (NY - 1 - slot) * ROWS
+            qs[at : at + ROWS, :] = piece[0:ROWS, :]
             qs[HISTS + slot * CROWS : HISTS + (slot + 1) * CROWS, :] = piece[ROWS:QROWS, :]
         acc[...] = jnp.zeros_like(acc)
     else:
         acc[...] = in_ref[...]
 
-    def owner_of(event):
+    lows, stops = [], []
+    for half in range(2 * NY):
+        event = ((y + NY - 1 - half // 2) * NZ + z) * ROWS + half % 2 * BLOCK
         low, stop = jnp.int32(NOBODY), jnp.int32(0)
         for s, t in zip(starts, ends):
             inside = (s <= event) & (event < t)
             low = jnp.where(inside, s, low)
             stop = jnp.where(inside, t, stop)
-        return low, stop
-
-    column = lax.broadcasted_iota(jnp.int32, (1, ROWS), 1)
-    blocks = [lax.rem(z + offset, NZ) for offset in offsets]
-    events = [(y * NZ + block) * ROWS + column for block in blocks]
-
-    def weights(rows, i, h):
-        return silu_weight(contract_lanes(rows, k_refs[i][0:ROWS, head(h)]))
-
-    def values(i, h):
-        return v_refs[i][kv_row : kv_row + ROWS, head(h)]
-
-    def slot_step(slot, carry):
-        event = ((y + slot) * NZ + z) * ROWS
-        row = pl.multiple_of(slot * ROWS, ROWS)
-        low0, _ = owner_of(event)
-        low1, _ = owner_of(event + BLOCK)
-        keeps = []
-        for block, keys in zip(blocks, events):
-            late = jnp.where((slot == 0) & (block >= z), NOBODY, 0)
-            keeps.append([flag(keys >= jnp.maximum(low, late)) for low in (low0, low1)])
-        for h in range(HEADS):
-            out = None
-            for i in range(len(blocks)):
-                w = weights(qs[pl.ds(row, ROWS), head(h)], i, h)
-                w = jnp.concatenate([w[0:BLOCK] * keeps[i][0], w[BLOCK:ROWS] * keeps[i][1]], axis=0)
-                term = jnp.dot(w, values(i, h), preferred_element_type=jnp.float32)
-                out = term if out is None else out + term
-            acc[pl.ds(row, ROWS), head(h)] += out
-        return carry
-
-    lax.fori_loop(0, NY - y, slot_step, 0)
-
+        lows.append(low)
+        stops.append(stop)
     user = user_ref[...]
     cand_low = jnp.where(user == 0, starts[0], starts[1])
     cand_stop = jnp.where(user == 0, ends[0], ends[1])
-    keeps = [flag((keys >= cand_low) & (keys < cand_stop)) for keys in events]
-    for h in range(HEADS):
-        out = None
-        for i in range(len(blocks)):
-            w = weights(qs[HISTS:TOTAL, head(h)], i, h) * keeps[i]
-            term = jnp.dot(w, values(i, h), preferred_element_type=jnp.float32)
-            out = term if out is None else out + term
-        acc[HISTS:TOTAL, head(h)] += out
+    column = lax.broadcasted_iota(jnp.int32, (1, ROWS), 1)
+
+    def block_step(skip, part):
+        block = z + offsets[-1]
+        for n, offset in enumerate(offsets[:-1]):
+            block = jnp.where(part == n, z + offset, block)
+        block = lax.rem(block, NZ)
+        late = jnp.where(block >= z, NOBODY, 0)
+        events = (y * NZ + block) * ROWS + column
+        keeps = []
+        for half in range(2 * skip, 2 * NY):
+            low = lows[half] if half < 2 * NY - 2 else jnp.maximum(lows[half], late)
+            keeps.append(flag(events >= low))
+        keeps.append(flag((events >= cand_low) & (events < cand_stop)))
+        key = pl.multiple_of(part * 2 * ROWS, ROWS)
+        for h in range(HEADS):
+            w = silu_weight(contract_lanes(qs[skip * ROWS : TOTAL, head(h)], kv[pl.ds(key, ROWS), head(h)]))
+            w = jnp.concatenate([w[i * BLOCK : (i + 1) * BLOCK] * keep for i, keep in enumerate(keeps)], axis=0)
+            v = kv[pl.ds(pl.multiple_of(key + ROWS, ROWS), ROWS), head(h)]
+            acc[skip * ROWS : TOTAL, head(h)] += jnp.dot(w, v, preferred_element_type=jnp.float32)
+
+    for skip in range(NY):
+
+        @pl.when(y == skip)
+        def _(skip=skip):
+            def step(part, carry):
+                block_step(skip, part)
+                return carry
+
+            lax.fori_loop(0, len(offsets), step, 0)
 
     if first:
         at = lax.broadcasted_iota(jnp.int32, (ROWS, ROWS), 0)
         to = lax.broadcasted_iota(jnp.int32, (ROWS, ROWS), 1)
         event = (y * NZ + z) * ROWS
-        low0, _ = owner_of(event)
-        low1, _ = owner_of(event + BLOCK)
-        keep = flag((to <= at) & (event + to >= jnp.where(at < BLOCK, low0, low1)))
+        keep = flag((to <= at) & (event + to >= jnp.where(at < BLOCK, lows[-2], lows[-1])))
+        rows = slice(HISTS - ROWS, HISTS)
         for h in range(HEADS):
-            w = weights(qs[0:ROWS, head(h)], 0, h) * keep
-            acc[0:ROWS, head(h)] += jnp.dot(w, values(0, h), preferred_element_type=jnp.float32)
+            w = silu_weight(contract_lanes(qs[rows, head(h)], kv[0:ROWS, head(h)])) * keep
+            acc[rows, head(h)] += jnp.dot(w, kv[ROWS : 2 * ROWS, head(h)], preferred_element_type=jnp.float32)
 
     if last:
         at = lax.broadcasted_iota(jnp.int32, (ROWS, HD), 0)
         for slot in range(NY):
             event = ((y + slot) * NZ + z) * ROWS
-            _, stop0 = owner_of(event)
-            _, stop1 = owner_of(event + BLOCK)
-            stop = jnp.where(at < BLOCK, stop0, stop1)
+            row = (NY - 1 - slot) * ROWS
+            half = 2 * (NY - 1 - slot)
+            stop = jnp.where(at < BLOCK, stops[half], stops[half + 1])
             out = own if slot == 0 else away[slot - 1]
-            rows = jnp.where(event + at < stop, acc[slot * ROWS : (slot + 1) * ROWS, :], 0.0)
-            out[0:ROWS, :] = rows.astype(out.dtype)
+            out[0:ROWS, :] = jnp.where(event + at < stop, acc[row : row + ROWS, :], 0.0).astype(out.dtype)
             out[ROWS:QROWS, :] = acc[HISTS + slot * CROWS : HISTS + (slot + 1) * CROWS, :].astype(out.dtype)
 
 
@@ -170,7 +160,8 @@
         in_specs=[SMEM] * 3 + [VMEM] * (1 + len(args)),
         out_specs=[VMEM] * len(shapes),
         out_shape=shapes,
-        scratch_shapes=[pltpu.VMEM((TOTAL, HD), jnp.float32)] * last,
+        scratch_shapes=[pltpu.VMEM((TOTAL, HD), jnp.float32)] * last
+        + [pltpu.VMEM((len(offsets) * 2 * ROWS, HD), jnp.bfloat16)],
         compiler_params=pltpu.CompilerParams(vmem_limit_bytes=VMEM_LIMIT),
         cost_estimate=pl.CostEstimate(
             flops=4 * TOTAL * len(offsets) * ROWS * HD, bytes_accessed=1 << 20, transcendentals=0
@@ -228,22 +219,19 @@
     kv, mine = call(
         stack_kernel, [(2 * ROWS, HD), (QROWS, HD)], hist_key, hist_value, hist_query, cand_query, limit=WIDE_LIMIT
     )
-    up, down = turn(kv, "z", 1), turn(kv, "z", -1)
-    queries = [mine] + [turn(mine, "y", -k) for k in (1, 2, 3)]
-    up, *queries = lax.optimization_barrier((up, *queries))
-    blocks = (kv, up, down)
-    up, down = turn(up, "z", 1), turn(down, "z", -1)
-    total, queries = attend((0, NZ - 1, 1), where, users, blocks, queries, None)
-    up, held = lax.optimization_barrier((up, total))
-    down, total = lax.optimization_barrier((down, held))
-    blocks = (up, down)
-    up, down = turn(up, "z", 1), turn(down, "z", -1)
-    (total,) = attend((NZ - 2, 2), where, users, blocks, queries, total)
-    up, held = lax.optimization_barrier((up, total))
-    down, total = lax.optimization_barrier((down, held))
-    keys, values = turn(up[:ROWS], "z", 1), turn(down[ROWS:], "z", -1)
-    (total,) = attend((NZ - 3, 3), where, users, (up, down), queries, total)
-    own, *away = attend((4,), where, users, (keys, values), queries, total, last=True)
+    blocks, queries = [(kv, kv)], [mine]
+    for step in range(3):
+        up, down = blocks[-1]
+        if step:
+            up, _ = lax.optimization_barrier((up, queries[-1]))
+            down, _ = lax.optimization_barrier((down, queries[-1]))
+        blocks.append((turn(up, "z", 1), turn(down, "z", -1)))
+        queries.append(turn(queries[-1], "y", -1))
+    across = turn(blocks[3][0], "z", 1)
+    total, stacked = attend((0, NZ - 1, 1), where, users, (kv, *blocks[1]), queries, None)
+    for step in (2, 3):
+        (total,) = attend((NZ - step, step), where, users, blocks[step], stacked, total)
+    own, *away = attend((4,), where, users, (across,), stacked, total, last=True)
     back = [turn(a, "y", k) for k, a in zip((1, 2, 3), away)]
     return tuple(
         call(

time: 131 us -> 112 us (0.85)
  the two profiles are of different devices: /device:TPU:13 before, /device:TPU:43 now
where the time goes in v7:
time: 112 us; the launch traced here: 111 us
  starting transfers between devices  47.6 us (42%)
  waiting for transfers between devices  38.5 us (34%)
  Pallas kernels  18.2 us (16%)
  local copies, waits for them, and re-layouts  6.09 us (5%)
    ppermute x13, starting transfers between devices, turn(): lax.ppermute(array, axis, [(i, (i + step) % count) for i in range(count)])  47.6 us
    ppermute x13, waiting for transfers between devices, turn(): lax.ppermute(array, axis, [(i, (i + step) % count) for i in range(count)])  38.5 us
    pallas_call x4, Pallas kernels, attend(): pl.pallas_call(functools.partial(attend_kernel, offsets, first, last), in...  14.7 us
    unnamed x28, local copies, waits for them, and re-layouts  5.21 us
    pallas_call x2, Pallas kernels, call(): pl.pallas_call(kernel, in_specs=[VMEM] * len(args), out_specs=[VMEM] * le...  3.54 us
  transfers between devices with their start and end apart: 13, of which 6 were waited for; matrix products, arithmetic and copies ran while one was open for 1% of the time, Pallas kernels for 11%

profile of v7, /device:TPU:43, one launch (start us, length us, event | category | flops | bytes accessed | tf_op | source)
XLA Modules:
  0.0 111.5 jit_solution(15861298356753744729)
XLA Ops:
  0.6 2.0 %shard_map.149 = (bf16[512,512]{1,0:T(8,128)(2,1)}, bf16[288,512]{1,0:T(8,128)(2,1)}) custom-call(bf16[256,512]{1,0:T(8,128)(2,1)} %k_ref.1, bf16[256,512]{1,0:T(8,128)(2,1)} %v_ref.1, bf16[256,512]{1,0:T(8,128)(2,1)} %q_ref.1, bf16[32,512]{1,0:T(8,128)(2,1)} %cq.1), custom_call_target="tpu_custom_call" | custom-call | tf_op jit(solution)/shard_map/pallas_call | solution.py:196
  2.7 4.0 %collective-permute-start = (bf16[512,512]{1,0:T(8,128)(2,1)}, bf16[512,512]{1,0:T(8,128)(2,1)S(1)}, u32[]{:S(2)}, u32[]{:S(2)}) collective-permute-start(bf16[512,512]{1,0:T(8,128)(2,1)} %get-tuple-element.14.refs_0_), channel_id=1, source_target_pairs={{0,1},{1,2},{2,3},{3,4},{4,5},{5,6},{6,7},{7,0},{8,9},{9,10},{10,1... | collective-permute-start | bytes 1572872 | tf_op jit(solution)/shard_map/ppermute | solution.py:207
  6.7 3.0 %collective-permute-start.1 = (bf16[288,512]{1,0:T(8,128)(2,1)}, bf16[288,512]{1,0:T(8,128)(2,1)S(1)}, u32[]{:S(2)}, u32[]{:S(2)}) collective-permute-start(bf16[288,512]{1,0:T(8,128)(2,1)} %get-tuple-element.15.refs_3_), channel_id=1, source_target_pairs={{0,24},{8,0},{16,8},{24,16},{1,25},{9,1},{17,9},{25,17},{2,26},{10... | collective-permute-start | bytes 884744 | tf_op jit(solution)/shard_map/ppermute | solution.py:207
  9.7 8.6 %collective-permute-start.6 = (bf16[512,512]{1,0:T(8,128)(2,1)}, bf16[512,512]{1,0:T(8,128)(2,1)S(1)}, u32[]{:S(2)}, u32[]{:S(2)}) collective-permute-start(bf16[512,512]{1,0:T(8,128)(2,1)} %get-tuple-element.14.refs_0_), channel_id=1, source_target_pairs={{0,7},{1,0},{2,1},{3,2},{4,3},{5,4},{6,5},{7,6},{8,15},{9,8},{10,9... | collective-permute-start | bytes 1572872 | tf_op jit(solution)/shard_map/ppermute | solution.py:207
  18.3 6.9 %collective-permute-done.refs_1_ = bf16[512,512]{1,0:T(8,128)(2,1)S(1)} collective-permute-done((bf16[512,512]{1,0:T(8,128)(2,1)}, bf16[512,512]{1,0:T(8,128)(2,1)S(1)}, u32[]{:S(2)}, u32[]{:S(2)}) %collective-permute-start) | collective-permute-done | bytes 524320 | tf_op jit(solution)/shard_map/ppermute | solution.py:207
  25.2 1.9 %collective-permute-start.2 = (bf16[512,512]{1,0:T(8,128)(2,1)S(1)}, bf16[512,512]{1,0:T(8,128)(2,1)S(1)}, u32[]{:S(2)}, u32[]{:S(2)}) collective-permute-start(bf16[512,512]{1,0:T(8,128)(2,1)S(1)} %collective-permute-done.refs_1_), channel_id=1, source_target_pairs={{0,1},{1,2},{2,3},{3,4},{4,5},{5,6},{6,7},{7,0},{8,9},{9,10},{10,1... | collective-permute-start | bytes 1572872 | tf_op jit(solution)/shard_map/ppermute | solution.py:207
  27.1 3.0 %collective-permute-start.3 = (bf16[288,512]{1,0:T(8,128)(2,1)S(1)}, bf16[288,512]{1,0:T(8,128)(2,1)}, u32[]{:S(2)}, u32[]{:S(2)}) collective-permute-start(bf16[288,512]{1,0:T(8,128)(2,1)S(1)} %collective-permute-done.1.refs_4_), channel_id=1, source_target_pairs={{0,24},{8,0},{16,8},{24,16},{1,25},{9,1},{17,9},{25,17},{2,26},{10... | collective-permute-start | bytes 884744 | tf_op jit(solution)/shard_map/ppermute | solution.py:207
  30.1 4.6 %collective-permute-start.8 = (bf16[512,512]{1,0:T(8,128)(2,1)S(1)}, bf16[512,512]{1,0:T(8,128)(2,1)S(1)}, u32[]{:S(2)}, u32[]{:S(2)}) collective-permute-start(bf16[512,512]{1,0:T(8,128)(2,1)S(1)} %collective-permute-done.6.refs_2_), channel_id=1, source_target_pairs={{0,7},{1,0},{2,1},{3,2},{4,3},{5,4},{6,5},{7,6},{8,15},{9,8},{10,9... | collective-permute-start | bytes 1572872 | tf_op jit(solution)/shard_map/ppermute | solution.py:207
  36.4 4.1 %collective-permute-done.2.refs_0_ = bf16[512,512]{1,0:T(8,128)(2,1)S(1)} collective-permute-done((bf16[512,512]{1,0:T(8,128)(2,1)S(1)}, bf16[512,512]{1,0:T(8,128)(2,1)S(1)}, u32[]{:S(2)}, u32[]{:S(2)}) %collective-permute-start.2) | collective-permute-done | bytes 524320 | tf_op jit(solution)/shard_map/ppermute | solution.py:207
  40.5 1.9 %collective-permute-start.4 = (bf16[512,512]{1,0:T(8,128)(2,1)S(1)}, bf16[512,512]{1,0:T(8,128)(2,1)S(1)}, u32[]{:S(2)}, u32[]{:S(2)}) collective-permute-start(bf16[512,512]{1,0:T(8,128)(2,1)S(1)} %collective-permute-done.2.refs_0_), channel_id=1, source_target_pairs={{0,1},{1,2},{2,3},{3,4},{4,5},{5,6},{6,7},{7,0},{8,9},{9,10},{10,1... | collective-permute-start | bytes 1572872 | tf_op jit(solution)/shard_map/ppermute | solution.py:207
  43.2 3.0 %collective-permute-start.7 = (bf16[288,512]{1,0:T(8,128)(2,1)}, bf16[288,512]{1,0:T(8,128)(2,1)}, u32[]{:S(2)}, u32[]{:S(2)}) collective-permute-start(bf16[288,512]{1,0:T(8,128)(2,1)} %collective-permute-done.3.refs_5_), channel_id=1, source_target_pairs={{0,24},{8,0},{16,8},{24,16},{1,25},{9,1},{17,9},{25,17},{2,26},{10... | collective-permute-start | bytes 884744 | tf_op jit(solution)/shard_map/ppermute | solution.py:207
  46.1 4.6 %collective-permute-start.9 = (bf16[512,512]{1,0:T(8,128)(2,1)S(1)}, bf16[512,512]{1,0:T(8,128)(2,1)S(1)}, u32[]{:S(2)}, u32[]{:S(2)}) collective-permute-start(bf16[512,512]{1,0:T(8,128)(2,1)S(1)} %collective-permute-done.8.refs_1_), channel_id=1, source_target_pairs={{0,7},{1,0},{2,1},{3,2},{4,3},{5,4},{6,5},{7,6},{8,15},{9,8},{10,9... | collective-permute-start | bytes 1572872 | tf_op jit(solution)/shard_map/ppermute | solution.py:207
  50.7 4.1 %collective-permute-done.4.refs_0_ = bf16[512,512]{1,0:T(8,128)(2,1)S(1)} collective-permute-done((bf16[512,512]{1,0:T(8,128)(2,1)S(1)}, bf16[512,512]{1,0:T(8,128)(2,1)S(1)}, u32[]{:S(2)}, u32[]{:S(2)}) %collective-permute-start.4) | collective-permute-done | bytes 524320 | tf_op jit(solution)/shard_map/ppermute | solution.py:207
  54.8 1.9 %collective-permute-start.5 = (bf16[512,512]{1,0:T(8,128)(2,1)S(1)}, bf16[512,512]{1,0:T(8,128)(2,1)S(1)}, u32[]{:S(2)}, u32[]{:S(2)}) collective-permute-start(bf16[512,512]{1,0:T(8,128)(2,1)S(1)} %collective-permute-done.4.refs_0_), channel_id=1, source_target_pairs={{0,1},{1,2},{2,3},{3,4},{4,5},{5,6},{6,7},{7,0},{8,9},{9,10},{10,1... | collective-permute-start | bytes 1572872 | tf_op jit(solution)/shard_map/ppermute | solution.py:207
  61.3 5.8 %attend.4 = (f32[1152,512]{1,0:T(8,128)S(1)}, bf16[1152,512]{1,0:T(8,128)(2,1)S(1)}) custom-call(s32[2]{0:T(128)S(1)} %pad_add_fusion.1.place_ref, s32[2]{0:T(128)S(1)} %copy-done.8, s32[2]{0:T(128)S(1)} %copy-done.9, s32[128,1]{1,0:T(8,128)S(1)} %reshape.12.user_ref, bf16[512,512]{1,0:T(8,128)(2,1)S(1)} %copy-done.10, ...), custom_call_target="tpu_custom_call" | custom-call | flops 1811939328 | bytes 1048576 | tf_op jit(solution)/shard_map/attend/pallas_call | solution.py:158
  67.1 3.3 %attend.5.refs_3_ = f32[1152,512]{1,0:T(8,128)S(1)} custom-call(s32[2]{0:T(128)S(1)} %pad_add_fusion.1.place_ref, s32[2]{0:T(128)S(1)} %copy-done.8, s32[2]{0:T(128)S(1)} %copy-done.9, s32[128,1]{1,0:T(8,128)S(1)} %reshape.12.user_ref, bf16[512,512]{1,0:T(8,128)(2,1)S(1)} %collective-permute-done.2.refs_0_, ...), custom_call_target="tpu_custom_call" | custom-call | flops 1207959552 | bytes 1048576 | tf_op jit(solution)/shard_map/attend/pallas_call | solution.py:158
  70.4 3.5 %attend.6.refs_2_ = f32[1152,512]{1,0:T(8,128)S(1)} custom-call(s32[2]{0:T(128)S(1)} %pad_add_fusion.1.place_ref, s32[2]{0:T(128)S(1)} %copy-done.8, s32[2]{0:T(128)S(1)} %copy-done.9, s32[128,1]{1,0:T(8,128)S(1)} %reshape.12.user_ref, bf16[512,512]{1,0:T(8,128)(2,1)S(1)} %collective-permute-done.4.refs_0_, ...), custom_call_target="tpu_custom_call" | custom-call | flops 1207959552 | bytes 1048576 | tf_op jit(solution)/shard_map/attend/pallas_call | solution.py:158
  74.0 2.1 %attend.7 = (f32[288,512]{1,0:T(8,128)S(1)}, bf16[288,512]{1,0:T(8,128)(2,1)S(1)}, bf16[288,512]{1,0:T(8,128)(2,1)S(1)}, bf16[288,512]{1,0:T(8,128)(2,1)S(1)}) custom-call(s32[2]{0:T(128)S(1)} %pad_add_fusion.1.place_ref, s32[2]{0:T(128)S(1)} %copy-done.8, s32[2]{0:T(128)S(1)} %copy-done.9, s32[128,1]{1,0:T(8,128)S(1)} %reshape.12.user_ref, ...), custom_call_target="tpu_custom_call" | custom-call | flops 603979776 | bytes 1048576 | tf_op jit(solution)/shard_map/attend/pallas_call | solution.py:158
  76.1 1.9 %collective-permute-start.10 = (bf16[288,512]{1,0:T(8,128)(2,1)S(1)}, bf16[288,512]{1,0:T(8,128)(2,1)S(1)}, u32[]{:S(2)}, u32[]{:S(2)}) collective-permute-start(bf16[288,512]{1,0:T(8,128)(2,1)S(1)} %get-tuple-element.23), channel_id=1, source_target_pairs={{0,8},{8,16},{16,24},{24,0},{1,9},{9,17},{17,25},{25,1},{2,10},{10... | collective-permute-start | bytes 884744 | tf_op jit(solution)/shard_map/ppermute | solution.py:207
  78.1 7.4 %collective-permute-start.11 = (bf16[288,512]{1,0:T(8,128)(2,1)S(1)}, bf16[288,512]{1,0:T(8,128)(2,1)S(1)}, u32[]{:S(2)}, u32[]{:S(2)}) collective-permute-start(bf16[288,512]{1,0:T(8,128)(2,1)S(1)} %get-tuple-element.24), channel_id=1, source_target_pairs={{0,16},{8,24},{16,0},{24,8},{1,17},{9,25},{17,1},{25,9},{2,18},{10... | collective-permute-start | bytes 884744 | tf_op jit(solution)/shard_map/ppermute | solution.py:207
  85.4 1.9 %collective-permute-start.12 = (bf16[288,512]{1,0:T(8,128)(2,1)S(1)}, bf16[288,512]{1,0:T(8,128)(2,1)S(1)}, u32[]{:S(2)}, u32[]{:S(2)}) collective-permute-start(bf16[288,512]{1,0:T(8,128)(2,1)S(1)} %get-tuple-element.25), channel_id=1, source_target_pairs={{0,24},{8,0},{16,8},{24,16},{1,25},{9,1},{17,9},{25,17},{2,26},{10... | collective-permute-start | bytes 884744 | tf_op jit(solution)/shard_map/ppermute | solution.py:207
  87.4 14.9 %collective-permute-done.11.t2 = bf16[288,512]{1,0:T(8,128)(2,1)S(1)} collective-permute-done((bf16[288,512]{1,0:T(8,128)(2,1)S(1)}, bf16[288,512]{1,0:T(8,128)(2,1)S(1)}, u32[]{:S(2)}, u32[]{:S(2)}) %collective-permute-start.11) | collective-permute-done | bytes 294944 | tf_op jit(solution)/shard_map/ppermute | solution.py:207
  102.3 7.6 %collective-permute-done.12.t3 = bf16[288,512]{1,0:T(8,128)(2,1)S(1)} collective-permute-done((bf16[288,512]{1,0:T(8,128)(2,1)S(1)}, bf16[288,512]{1,0:T(8,128)(2,1)S(1)}, u32[]{:S(2)}, u32[]{:S(2)}) %collective-permute-start.12) | collective-permute-done | bytes 294944 | tf_op jit(solution)/shard_map/ppermute | solution.py:207
  110.0 1.5 %shard_map.150 = (bf16[256,1024]{1,0:T(8,128)(2,1)}, bf16[32,1024]{1,0:T(8,128)(2,1)}) custom-call(f32[288,512]{1,0:T(8,128)S(1)} %get-tuple-element.22.t0, bf16[288,512]{1,0:T(8,128)(2,1)S(1)} %collective-permute-done.10.t1, bf16[288,512]{1,0:T(8,128)(2,1)S(1)} %collective-permute-done.11.t2, bf16[288,512]{1,0:T(8,128)(2,1)S(1)} %collective-permute-done.12.t3, ...), custom_call_target="tpu_custom_call" | custom-call | tf_op jit(solution)/shard_map/pallas_call | solution.py:196
  (42 shorter events, 7.1 us)
Async XLA Ops:
  2.7 22.5 %collective-permute-start = (bf16[512,512]{1,0:T(8,128)(2,1)}, bf16[512,512]{1,0:T(8,128)(2,1)S(1)}, u32[]{:S(2)}, u32[]{:S(2)}) collective-permute-start(bf16[512,512]{1,0:T(8,128)(2,1)} %get-tuple-element.14.refs_0_), channel_id=1, source_target_pairs={{0,1},{1,2},{2,3},{3,4},{4,5},{5,6},{6,7},{7,0},{8,9},{9,10},{10,1... | collective-permute-start | bytes 1572872 | tf_op jit(solution)/shard_map/ppermute | solution.py:207
  6.7 11.6 %collective-permute-start.1 = (bf16[288,512]{1,0:T(8,128)(2,1)}, bf16[288,512]{1,0:T(8,128)(2,1)S(1)}, u32[]{:S(2)}, u32[]{:S(2)}) collective-permute-start(bf16[288,512]{1,0:T(8,128)(2,1)} %get-tuple-element.15.refs_3_), channel_id=1, source_target_pairs={{0,24},{8,0},{16,8},{24,16},{1,25},{9,1},{17,9},{25,17},{2,26},{10... | collective-permute-start | bytes 884744 | tf_op jit(solution)/shard_map/ppermute | solution.py:207
  9.7 20.4 %collective-permute-start.6 = (bf16[512,512]{1,0:T(8,128)(2,1)}, bf16[512,512]{1,0:T(8,128)(2,1)S(1)}, u32[]{:S(2)}, u32[]{:S(2)}) collective-permute-start(bf16[512,512]{1,0:T(8,128)(2,1)} %get-tuple-element.14.refs_0_), channel_id=1, source_target_pairs={{0,7},{1,0},{2,1},{3,2},{4,3},{5,4},{6,5},{7,6},{8,15},{9,8},{10,9... | collective-permute-start | bytes 1572872 | tf_op jit(solution)/shard_map/ppermute | solution.py:207
  25.2 15.3 %collective-permute-start.2 = (bf16[512,512]{1,0:T(8,128)(2,1)S(1)}, bf16[512,512]{1,0:T(8,128)(2,1)S(1)}, u32[]{:S(2)}, u32[]{:S(2)}) collective-permute-start(bf16[512,512]{1,0:T(8,128)(2,1)S(1)} %collective-permute-done.refs_1_), channel_id=1, source_target_pairs={{0,1},{1,2},{2,3},{3,4},{4,5},{5,6},{6,7},{7,0},{8,9},{9,10},{10,1... | collective-permute-start | bytes 1572872 | tf_op jit(solution)/shard_map/ppermute | solution.py:207
  27.1 9.3 %collective-permute-start.3 = (bf16[288,512]{1,0:T(8,128)(2,1)S(1)}, bf16[288,512]{1,0:T(8,128)(2,1)}, u32[]{:S(2)}, u32[]{:S(2)}) collective-permute-start(bf16[288,512]{1,0:T(8,128)(2,1)S(1)} %collective-permute-done.1.refs_4_), channel_id=1, source_target_pairs={{0,24},{8,0},{16,8},{24,16},{1,25},{9,1},{17,9},{25,17},{2,26},{10... | collective-permute-start | bytes 884744 | tf_op jit(solution)/shard_map/ppermute | solution.py:207
  30.1 16.0 %collective-permute-start.8 = (bf16[512,512]{1,0:T(8,128)(2,1)S(1)}, bf16[512,512]{1,0:T(8,128)(2,1)S(1)}, u32[]{:S(2)}, u32[]{:S(2)}) collective-permute-start(bf16[512,512]{1,0:T(8,128)(2,1)S(1)} %collective-permute-done.6.refs_2_), channel_id=1, source_target_pairs={{0,7},{1,0},{2,1},{3,2},{4,3},{5,4},{6,5},{7,6},{8,15},{9,8},{10,9... | collective-permute-start | bytes 1572872 | tf_op jit(solution)/shard_map/ppermute | solution.py:207
  40.5 14.4 %collective-permute-start.4 = (bf16[512,512]{1,0:T(8,128)(2,1)S(1)}, bf16[512,512]{1,0:T(8,128)(2,1)S(1)}, u32[]{:S(2)}, u32[]{:S(2)}) collective-permute-start(bf16[512,512]{1,0:T(8,128)(2,1)S(1)} %collective-permute-done.2.refs_0_), channel_id=1, source_target_pairs={{0,1},{1,2},{2,3},{3,4},{4,5},{5,6},{6,7},{7,0},{8,9},{9,10},{10,1... | collective-permute-start | bytes 1572872 | tf_op jit(solution)/shard_map/ppermute | solution.py:207
  43.2 13.8 %collective-permute-start.7 = (bf16[288,512]{1,0:T(8,128)(2,1)}, bf16[288,512]{1,0:T(8,128)(2,1)}, u32[]{:S(2)}, u32[]{:S(2)}) collective-permute-start(bf16[288,512]{1,0:T(8,128)(2,1)} %collective-permute-done.3.refs_5_), channel_id=1, source_target_pairs={{0,24},{8,0},{16,8},{24,16},{1,25},{9,1},{17,9},{25,17},{2,26},{10... | collective-permute-start | bytes 884744 | tf_op jit(solution)/shard_map/ppermute | solution.py:207
  46.1 24.3 %collective-permute-start.9 = (bf16[512,512]{1,0:T(8,128)(2,1)S(1)}, bf16[512,512]{1,0:T(8,128)(2,1)S(1)}, u32[]{:S(2)}, u32[]{:S(2)}) collective-permute-start(bf16[512,512]{1,0:T(8,128)(2,1)S(1)} %collective-permute-done.8.refs_1_), channel_id=1, source_target_pairs={{0,7},{1,0},{2,1},{3,2},{4,3},{5,4},{6,5},{7,6},{8,15},{9,8},{10,9... | collective-permute-start | bytes 1572872 | tf_op jit(solution)/shard_map/ppermute | solution.py:207
  54.8 19.1 %collective-permute-start.5 = (bf16[512,512]{1,0:T(8,128)(2,1)S(1)}, bf16[512,512]{1,0:T(8,128)(2,1)S(1)}, u32[]{:S(2)}, u32[]{:S(2)}) collective-permute-start(bf16[512,512]{1,0:T(8,128)(2,1)S(1)} %collective-permute-done.4.refs_0_), channel_id=1, source_target_pairs={{0,1},{1,2},{2,3},{3,4},{4,5},{5,6},{6,7},{7,0},{8,9},{9,10},{10,1... | collective-permute-start | bytes 1572872 | tf_op jit(solution)/shard_map/ppermute | solution.py:207
  58.3 1.0 copy-start.10
  59.3 1.0 copy-start.12
  60.4 1.0 copy-start.13
  73.9 36.0 %copy-start = (bf16[512,1024]{1,0:T(8,128)(2,1)S(1)}, bf16[512,1024]{1,0:T(8,128)(2,1)}, u32[]{:S(2)}) copy-start(bf16[512,1024]{1,0:T(8,128)(2,1)} %w_ref.1) | copy-start | bytes 3145732
  73.9 36.0 %copy-start.1 = (bf16[256,1024]{1,0:T(8,128)(2,1)S(1)}, bf16[256,1024]{1,0:T(8,128)(2,1)}, u32[]{:S(2)}) copy-start(bf16[256,1024]{1,0:T(8,128)(2,1)} %hx.1) | copy-start | bytes 1572868
  73.9 36.0 %copy-start.2 = (bf16[256,512]{1,0:T(8,128)(2,1)S(1)}, bf16[256,512]{1,0:T(8,128)(2,1)}, u32[]{:S(2)}) copy-start(bf16[256,512]{1,0:T(8,128)(2,1)} %hg.1) | copy-start | bytes 786436
  73.9 36.0 %copy-start.3 = (bf16[32,512]{1,0:T(8,128)(2,1)S(1)}, bf16[32,512]{1,0:T(8,128)(2,1)}, u32[]{:S(2)}) copy-start(bf16[32,512]{1,0:T(8,128)(2,1)} %cq.1) | copy-start | bytes 98308
  73.9 36.0 %copy-start.4 = (bf16[32,1024]{1,0:T(8,128)(2,1)S(1)}, bf16[32,1024]{1,0:T(8,128)(2,1)}, u32[]{:S(2)}) copy-start(bf16[32,1024]{1,0:T(8,128)(2,1)} %cx.1) | copy-start | bytes 196612
  73.9 36.0 %copy-start.5 = (bf16[32,512]{1,0:T(8,128)(2,1)S(1)}, bf16[32,512]{1,0:T(8,128)(2,1)}, u32[]{:S(2)}) copy-start(bf16[32,512]{1,0:T(8,128)(2,1)} %ck.1) | copy-start | bytes 98308
  73.9 36.0 %copy-start.6 = (bf16[32,512]{1,0:T(8,128)(2,1)S(1)}, bf16[32,512]{1,0:T(8,128)(2,1)}, u32[]{:S(2)}) copy-start(bf16[32,512]{1,0:T(8,128)(2,1)} %cv.1) | copy-start | bytes 98308
  74.0 36.0 %copy-start.7 = (bf16[32,512]{1,0:T(8,128)(2,1)S(1)}, bf16[32,512]{1,0:T(8,128)(2,1)}, u32[]{:S(2)}) copy-start(bf16[32,512]{1,0:T(8,128)(2,1)} %cg.1) | copy-start | bytes 98308
  76.1 11.2 %collective-permute-start.10 = (bf16[288,512]{1,0:T(8,128)(2,1)S(1)}, bf16[288,512]{1,0:T(8,128)(2,1)S(1)}, u32[]{:S(2)}, u32[]{:S(2)}) collective-permute-start(bf16[288,512]{1,0:T(8,128)(2,1)S(1)} %get-tuple-element.23), channel_id=1, source_target_pairs={{0,8},{8,16},{16,24},{24,0},{1,9},{9,17},{17,25},{25,1},{2,10},{10... | collective-permute-start | bytes 884744 | tf_op jit(solution)/shard_map/ppermute | solution.py:207
  78.1 24.2 %collective-permute-start.11 = (bf16[288,512]{1,0:T(8,128)(2,1)S(1)}, bf16[288,512]{1,0:T(8,128)(2,1)S(1)}, u32[]{:S(2)}, u32[]{:S(2)}) collective-permute-start(bf16[288,512]{1,0:T(8,128)(2,1)S(1)} %get-tuple-element.24), channel_id=1, source_target_pairs={{0,16},{8,24},{16,0},{24,8},{1,17},{9,25},{17,1},{25,9},{2,18},{10... | collective-permute-start | bytes 884744 | tf_op jit(solution)/shard_map/ppermute | solution.py:207
  85.4 24.5 %collective-permute-start.12 = (bf16[288,512]{1,0:T(8,128)(2,1)S(1)}, bf16[288,512]{1,0:T(8,128)(2,1)S(1)}, u32[]{:S(2)}, u32[]{:S(2)}) collective-permute-start(bf16[288,512]{1,0:T(8,128)(2,1)S(1)} %get-tuple-element.25), channel_id=1, source_target_pairs={{0,24},{8,0},{16,8},{24,16},{1,25},{9,1},{17,9},{25,17},{2,26},{10... | collective-permute-start | bytes 884744 | tf_op jit(solution)/shard_map/ppermute | solution.py:207
  (3 other events, 2.1 us)

commit v8 on v4

--- a/solution.py
+++ b/solution.py
@@ -24,6 +24,7 @@
 NOBODY = 1 << 30
 HALF = 1.0 / (2.0 * math.sqrt(DH))
 VMEM_LIMIT = 16 * 1024 * 1024
+WIDE_LIMIT = 60 * 1024 * 1024
 VMEM = pl.BlockSpec(memory_space=pltpu.VMEM)
 SMEM = pl.BlockSpec(memory_space=pltpu.SMEM)
 PARAMS = pltpu.CompilerParams(vmem_limit_bytes=VMEM_LIMIT)
@@ -50,20 +51,18 @@
         out_ref[row + REST : row + FOLD, DH : 2 * DH] = c_ref[:, at]
 
 
-def attend_kernel(offsets, first, last, place_ref, start_ref, len_ref, q_ref, user_ref, *refs):
-    blocks = 2 if last else len(offsets)
-    kv_refs = refs[:blocks]
-    refs = refs[blocks:]
+def attend_kernel(offsets, first, last, info_ref, q_ref, user_ref, *refs):
+    kv_refs = refs[: len(offsets)]
+    refs = refs[len(offsets) :]
     if not first:
         in_ref, *refs = refs
     out_ref, kv, qs, acc = refs
-    z = place_ref[0]
-    starts = [start_ref[u] for u in range(2)]
-    ends = [start_ref[u] + len_ref[u] for u in range(2)]
-
-    size = kv_refs[0].shape[0]
+    z = info_ref[0]
+    starts = [info_ref[1 + u] for u in range(2)]
+    ends = [info_ref[1 + u] + info_ref[3 + u] for u in range(2)]
+
     for i, ref in enumerate(kv_refs):
-        kv[i * size : (i + 1) * size, :] = ref[...]
+        kv[i * KEYS : (i + 1) * KEYS, :] = ref[...]
     for s in range(NY):
         row = s * PART + ROWS
         qs[s * ROWS : s * ROWS + FOLD, :] = q_ref[row : row + FOLD, 0:DH]
@@ -155,13 +154,13 @@
             out_ref[s * FOLD + REST : (s + 1) * FOLD, DH : 2 * DH] = cands
 
 
-def attend(offsets, where, queries, users, blocks, total, last):
+def attend(offsets, info, queries, users, blocks, total, last):
     first = total is None
     shape = jax.ShapeDtypeStruct((NY * FOLD, 2 * DH), jnp.bfloat16) if last else jax.ShapeDtypeStruct((TOTAL, DH), jnp.float32)
     state = [] if first else [total]
     return pl.pallas_call(
         functools.partial(attend_kernel, offsets, first, last),
-        in_specs=[SMEM] * 3 + [VMEM] * (2 + len(blocks) + len(state)),
+        in_specs=[SMEM] + [VMEM] * (2 + len(blocks) + len(state)),
         out_specs=VMEM,
         out_shape=shape,
         scratch_shapes=[
@@ -174,7 +173,7 @@
             flops=len(offsets) * 4 * TOTAL * KEYS * DH, bytes_accessed=len(offsets) << 20, transcendentals=0
         ),
         name="attend",
-    )(*where, queries, users, *blocks, *state)
+    )(info, queries, users, *blocks, *state)
 
 
 def finish_kernel(t_ref, hg, hx, cq, ck, cv, cg, cx, w_ref, ho, co):
@@ -200,13 +199,13 @@
     tail(jnp.concatenate(cand, axis=1), cg, cx, co)
 
 
-def call(kernel, shapes, *args):
+def call(kernel, shapes, *args, limit=VMEM_LIMIT):
     return pl.pallas_call(
         kernel,
         in_specs=[VMEM] * len(args),
         out_specs=[VMEM] * len(shapes),
         out_shape=[jax.ShapeDtypeStruct(s, jnp.bfloat16) for s in shapes],
-        compiler_params=PARAMS,
+        compiler_params=pltpu.CompilerParams(vmem_limit_bytes=limit),
     )(*args)
 
 
@@ -224,24 +223,25 @@
     cand_user, hist_len, hist_start, out_weight,
 ):
     z = lax.axis_index("z")
-    where = (z.astype(jnp.int32).reshape(1), hist_start, hist_len)
+    info = jnp.concatenate([z.astype(jnp.int32).reshape(1), hist_start, hist_len])
     users = lax.dynamic_index_in_dim(cand_user.reshape(NY, NZ, CROWS), z, axis=1).reshape(NY * CROWS, 1)
-    (parts,) = call(split_kernel, [(HEADS * PART, 2 * DH)], hist_key, hist_value, hist_query, cand_query)
+    (parts,) = call(
+        split_kernel, [(HEADS * PART, 2 * DH)], hist_key, hist_value, hist_query, cand_query, limit=WIDE_LIMIT
+    )
     queries = spread(parts)
     own = queries.reshape(NY, PART, 2 * DH)[:, :ROWS].reshape(KEYS, 2 * DH)
     up, down = turn(own, 1), turn(own, -1)
-    total = attend((0,), where, queries, users, (own,), None, False)
+    total = attend((0,), info, queries, users, (own,), None, False)
     for step in (1, 2):
         up, held = lax.optimization_barrier((up, total))
         down, total = lax.optimization_barrier((down, held))
         blocks = (up, down)
         up, down = turn(up, 1), turn(down, -1)
-        total = attend((NZ - step, step), where, queries, users, blocks, total, False)
-    up, held = lax.optimization_barrier((up, total))
-    down, total = lax.optimization_barrier((down, held))
-    low, high = turn(up[: KEYS // 2], 1), turn(down[KEYS // 2 :], -1)
-    total = attend((NZ - 3, 3), where, queries, users, (up, down), total, False)
-    total = attend((4,), where, queries, users, (low, high), total, True)
+        total = attend((NZ - step, step), info, queries, users, blocks, total, False)
+    up, total = lax.optimization_barrier((up, total))
+    across = turn(up, 1)
+    total = attend((NZ - 3, 3), info, queries, users, (up, down), total, False)
+    total = attend((4,), info, queries, users, (across,), total, True)
     return tuple(
         call(
             finish_kernel, [hist_input.shape, cand_input.shape],

time: 109 us -> 110 us (level)
  waiting for transfers between devices: 20.6 us -> 27.6 us
  starting transfers between devices: 34.5 us -> 29.6 us
  local copies, waits for them, and re-layouts: 5.25 us -> 0.97 us
  Pallas kernels: 12.8 us -> 14.9 us
  blocking collectives: 34.3 us -> 35.4 us
    ppermute x8 -> x7, waiting for transfers between devices: 20.6 us -> 27.6 us  [turn(): return lax.ppermute(array, 'z', [(i, (i + step) % NZ) for i in range(NZ)])]
    ppermute x8 -> x7, starting transfers between devices: 34.5 us -> 29.6 us  [turn(): return lax.ppermute(array, 'z', [(i, (i + step) % NZ) for i in range(NZ)])]
    unnamed x30 -> x22, local copies, waits for them, and re-layouts: 4.98 us -> 0.73 us
    pallas_call x2, Pallas kernels: 1.64 us -> 3.66 us  [call(): pl.pallas_call(kernel, in_specs=[VMEM] * len(args), out_specs=[VMEM] * le...]
  transfers between devices with their start and end apart: 8 -> 7, of which waited for: 5 -> 5; matrix products, arithmetic and copies ran while one was open for 0% -> 0% of each run, Pallas kernels for 9% -> 9%
where the time goes in v8:
time: 110 us; the launch traced here: 109 us
  blocking collectives  35.4 us (32%)
  starting transfers between devices  29.6 us (27%)
  waiting for transfers between devices  27.6 us (25%)
  Pallas kernels  14.9 us (14%)
    all_to_all x2, blocking collectives, spread(): return lax.all_to_all(array, 'y', 0, 0, tiled=True)  35.4 us
    ppermute x7, starting transfers between devices, turn(): return lax.ppermute(array, 'z', [(i, (i + step) % NZ) for i in range(NZ)])  29.6 us
    ppermute x7, waiting for transfers between devices, turn(): return lax.ppermute(array, 'z', [(i, (i + step) % NZ) for i in range(NZ)])  27.6 us
    pallas_call x5, Pallas kernels, attend(): pl.pallas_call(functools.partial(attend_kernel, offsets, first, last), in...  11.2 us
    pallas_call x2, Pallas kernels, call(): pl.pallas_call(kernel, in_specs=[VMEM] * len(args), out_specs=[VMEM] * le...  3.66 us
  transfers between devices with their start and end apart: 7, of which 5 were waited for; matrix products, arithmetic and copies ran while one was open for 0% of the time, Pallas kernels for 9%

profile of v8, /device:TPU:56, one launch (start us, length us, event | category | flops | bytes accessed | tf_op | source)
XLA Modules:
  0.0 109.4 jit_solution(10366915470474230385)
XLA Ops:
  0.6 2.2 %shard_map.149 = bf16[1600,256]{1,0:T(8,128)(2,1)} custom-call(bf16[256,512]{1,0:T(8,128)(2,1)} %k_ref.1, bf16[256,512]{1,0:T(8,128)(2,1)} %v_ref.1, bf16[256,512]{1,0:T(8,128)(2,1)} %q_ref.1, bf16[32,512]{1,0:T(8,128)(2,1)} %cq.1), custom_call_target="tpu_custom_call" | custom-call | tf_op jit(solution)/shard_map/pallas_call | solution.py:203
  2.8 25.1 %all_to_all.22 = bf16[4,400,256]{2,1,0:T(8,128)(2,1)S(1)} all-to-all(bf16[4,400,256]{2,1,0:T(8,128)(2,1)} %bitcast.16), channel_id=1, replica_groups=mesh['batch'=16,'y'=4,'z'=8] {'y'}, dimensions={0} | all-to-all | bytes 1638400 | tf_op jit(solution)/shard_map/all_to_all | solution.py:217
  27.9 4.3 %collective-permute-start = (bf16[1024,256]{1,0:T(8,128)(2,1)S(1)}, bf16[1024,256]{1,0:T(8,128)(2,1)S(1)}, u32[]{:S(2)}, u32[]{:S(2)}) collective-permute-start(bf16[1024,256]{1,0:T(8,128)(2,1)S(1)} %bitcast.13), channel_id=1, source_target_pairs={{0,1},{1,2},{2,3},{3,4},{4,5},{5,6},{6,7},{7,0},{8,9},{9,10},{10,1... | collective-permute-start | bytes 1572872 | tf_op jit(solution)/shard_map/ppermute | solution.py:213
  32.2 0.7 copy-done.8
  33.0 0.1 reshape.26.user_ref
  33.2 8.6 %collective-permute-start.2 = (bf16[1024,256]{1,0:T(8,128)(2,1)S(1)}, bf16[1024,256]{1,0:T(8,128)(2,1)S(1)}, u32[]{:S(2)}, u32[]{:S(2)}) collective-permute-start(bf16[1024,256]{1,0:T(8,128)(2,1)S(1)} %bitcast.14), channel_id=1, source_target_pairs={{0,7},{1,0},{2,1},{3,2},{4,3},{5,4},{6,5},{7,6},{8,15},{9,8},{10,9... | collective-permute-start | bytes 1572872 | tf_op jit(solution)/shard_map/ppermute | solution.py:213
  41.8 0.1 pad_add_fusion.info_ref
  41.9 2.2 %attend.5.refs_2_ = f32[1152,128]{1,0:T(8,128)S(1)} custom-call(s32[5]{0:T(128)S(1)} %pad_add_fusion.info_ref, bf16[1600,256]{1,0:T(8,128)(2,1)S(1)} %bitcast.6, s32[128,1]{1,0:T(8,128)S(1)} %reshape.26.user_ref, bf16[1024,256]{1,0:T(8,128)(2,1)S(1)} %bitcast.15), custom_call_target="tpu_custom_call" | custom-call | flops 603979776 | bytes 1048576 | tf_op jit(solution)/shard_map/attend/pallas_call | solution.py:161
  44.0 6.6 %collective-permute-done.refs_0_ = bf16[1024,256]{1,0:T(8,128)(2,1)S(1)} collective-permute-done((bf16[1024,256]{1,0:T(8,128)(2,1)S(1)}, bf16[1024,256]{1,0:T(8,128)(2,1)S(1)}, u32[]{:S(2)}, u32[]{:S(2)}) %collective-permute-start) | collective-permute-done | bytes 524320 | tf_op jit(solution)/shard_map/ppermute | solution.py:213
  50.6 1.9 %collective-permute-start.1 = (bf16[1024,256]{1,0:T(8,128)(2,1)S(1)}, bf16[1024,256]{1,0:T(8,128)(2,1)S(1)}, u32[]{:S(2)}, u32[]{:S(2)}) collective-permute-start(bf16[1024,256]{1,0:T(8,128)(2,1)S(1)} %collective-permute-done.refs_0_), channel_id=1, source_target_pairs={{0,1},{1,2},{2,3},{3,4},{4,5},{5,6},{6,7},{7,0},{8,9},{9,10},{10,1... | collective-permute-start | bytes 1572872 | tf_op jit(solution)/shard_map/ppermute | solution.py:213
  52.5 0.2 collective-permute-done.2.refs_1_
  52.7 5.6 %collective-permute-start.4 = (bf16[1024,256]{1,0:T(8,128)(2,1)S(1)}, bf16[1024,256]{1,0:T(8,128)(2,1)S(1)}, u32[]{:S(2)}, u32[]{:S(2)}) collective-permute-start(bf16[1024,256]{1,0:T(8,128)(2,1)S(1)} %collective-permute-done.2.refs_1_), channel_id=1, source_target_pairs={{0,7},{1,0},{2,1},{3,2},{4,3},{5,4},{6,5},{7,6},{8,15},{9,8},{10,9... | collective-permute-start | bytes 1572872 | tf_op jit(solution)/shard_map/ppermute | solution.py:213
  58.3 2.5 %attend.6.refs_2_ = f32[1152,128]{1,0:T(8,128)S(1)} custom-call(s32[5]{0:T(128)S(1)} %pad_add_fusion.info_ref, bf16[1600,256]{1,0:T(8,128)(2,1)S(1)} %bitcast.7, s32[128,1]{1,0:T(8,128)S(1)} %reshape.26.user_ref, bf16[1024,256]{1,0:T(8,128)(2,1)S(1)} %collective-permute-done.refs_0_, bf16[1024,256]{1,0:T(8,128)(2,1)S(1)} %collective-permute-done.2.refs_1_, ...), custom_call_target="tpu_custom_call" | custom-call | flops 1207959552 | bytes 2097152 | tf_op jit(solution)/shard_map/attend/pallas_call | solution.py:161
  60.8 5.8 %collective-permute-done.1.refs_0_ = bf16[1024,256]{1,0:T(8,128)(2,1)S(1)} collective-permute-done((bf16[1024,256]{1,0:T(8,128)(2,1)S(1)}, bf16[1024,256]{1,0:T(8,128)(2,1)S(1)}, u32[]{:S(2)}, u32[]{:S(2)}) %collective-permute-start.1) | collective-permute-done | bytes 524320 | tf_op jit(solution)/shard_map/ppermute | solution.py:213
  66.6 1.9 %collective-permute-start.3 = (bf16[1024,256]{1,0:T(8,128)(2,1)S(1)}, bf16[1024,256]{1,0:T(8,128)(2,1)S(1)}, u32[]{:S(2)}, u32[]{:S(2)}) collective-permute-start(bf16[1024,256]{1,0:T(8,128)(2,1)S(1)} %collective-permute-done.1.refs_0_), channel_id=1, source_target_pairs={{0,1},{1,2},{2,3},{3,4},{4,5},{5,6},{6,7},{7,0},{8,9},{9,10},{10,1... | collective-permute-start | bytes 1572872 | tf_op jit(solution)/shard_map/ppermute | solution.py:213
  68.6 5.5 %collective-permute-start.6 = (bf16[1024,256]{1,0:T(8,128)(2,1)S(1)}, bf16[1024,256]{1,0:T(8,128)(2,1)S(1)}, u32[]{:S(2)}, u32[]{:S(2)}) collective-permute-start(bf16[1024,256]{1,0:T(8,128)(2,1)S(1)} %collective-permute-done.4.refs_1_), channel_id=1, source_target_pairs={{0,7},{1,0},{2,1},{3,2},{4,3},{5,4},{6,5},{7,6},{8,15},{9,8},{10,9... | collective-permute-start | bytes 1572872 | tf_op jit(solution)/shard_map/ppermute | solution.py:213
  74.0 2.5 %attend.7.refs_2_ = f32[1152,128]{1,0:T(8,128)S(1)} custom-call(s32[5]{0:T(128)S(1)} %pad_add_fusion.info_ref, bf16[1600,256]{1,0:T(8,128)(2,1)S(1)} %bitcast.8, s32[128,1]{1,0:T(8,128)S(1)} %reshape.26.user_ref, bf16[1024,256]{1,0:T(8,128)(2,1)S(1)} %collective-permute-done.1.refs_0_, bf16[1024,256]{1,0:T(8,128)(2,1)S(1)} %collective-permute-done.4.refs_1_, ...), custom_call_target="tpu_custom_call" | custom-call | flops 1207959552 | bytes 2097152 | tf_op jit(solution)/shard_map/attend/pallas_call | solution.py:161
  76.5 5.2 %collective-permute-done.3.refs_0_ = bf16[1024,256]{1,0:T(8,128)(2,1)S(1)} collective-permute-done((bf16[1024,256]{1,0:T(8,128)(2,1)S(1)}, bf16[1024,256]{1,0:T(8,128)(2,1)S(1)}, u32[]{:S(2)}, u32[]{:S(2)}) %collective-permute-start.3) | collective-permute-done | bytes 524320 | tf_op jit(solution)/shard_map/ppermute | solution.py:213
  81.7 1.9 %collective-permute-start.5 = (bf16[1024,256]{1,0:T(8,128)(2,1)S(1)}, bf16[1024,256]{1,0:T(8,128)(2,1)S(1)}, u32[]{:S(2)}, u32[]{:S(2)}) collective-permute-start(bf16[1024,256]{1,0:T(8,128)(2,1)S(1)} %collective-permute-done.3.refs_0_), channel_id=1, source_target_pairs={{0,1},{1,2},{2,3},{3,4},{4,5},{5,6},{6,7},{7,0},{8,9},{9,10},{10,1... | collective-permute-start | bytes 1572872 | tf_op jit(solution)/shard_map/ppermute | solution.py:213
  83.7 2.5 %attend.8.refs_1_ = f32[1152,128]{1,0:T(8,128)S(1)} custom-call(s32[5]{0:T(128)S(1)} %pad_add_fusion.info_ref, bf16[1600,256]{1,0:T(8,128)(2,1)S(1)} %bitcast.9, s32[128,1]{1,0:T(8,128)S(1)} %reshape.26.user_ref, bf16[1024,256]{1,0:T(8,128)(2,1)S(1)} %collective-permute-done.3.refs_0_, bf16[1024,256]{1,0:T(8,128)(2,1)S(1)} %collective-permute-done.6.refs_1_, ...), custom_call_target="tpu_custom_call" | custom-call | flops 1207959552 | bytes 2097152 | tf_op jit(solution)/shard_map/attend/pallas_call | solution.py:161
  86.1 9.8 %collective-permute-done.5.refs_0_ = bf16[1024,256]{1,0:T(8,128)(2,1)S(1)} collective-permute-done((bf16[1024,256]{1,0:T(8,128)(2,1)S(1)}, bf16[1024,256]{1,0:T(8,128)(2,1)S(1)}, u32[]{:S(2)}, u32[]{:S(2)}) %collective-permute-start.5) | collective-permute-done | bytes 524320 | tf_op jit(solution)/shard_map/ppermute | solution.py:213
  95.9 1.6 %attend.9 = bf16[576,256]{1,0:T(8,128)(2,1)S(1)} custom-call(s32[5]{0:T(128)S(1)} %pad_add_fusion.info_ref, bf16[1600,256]{1,0:T(8,128)(2,1)S(1)} %bitcast.10, s32[128,1]{1,0:T(8,128)S(1)} %reshape.26.user_ref, bf16[1024,256]{1,0:T(8,128)(2,1)S(1)} %collective-permute-done.5.refs_0_, f32[1152,128]{1,0:T(8,128)S(1)} %attend.8.refs_1_), custom_call_target="tpu_custom_call" | custom-call | flops 603979776 | bytes 1048576 | tf_op jit(solution)/shard_map/attend/pallas_call | solution.py:161
  97.6 10.3 %all_to_all.23 = bf16[4,144,256]{2,1,0:T(8,128)(2,1)S(1)} all-to-all(bf16[4,144,256]{2,1,0:T(8,128)(2,1)S(1)} %bitcast.11), channel_id=1, replica_groups=mesh['batch'=16,'y'=4,'z'=8] {'y'}, dimensions={0} | all-to-all | bytes 589824 | tf_op jit(solution)/shard_map/all_to_all | solution.py:217
  107.9 1.5 %shard_map.150 = (bf16[256,1024]{1,0:T(8,128)(2,1)}, bf16[32,1024]{1,0:T(8,128)(2,1)}) custom-call(bf16[576,256]{1,0:T(8,128)(2,1)S(1)} %bitcast.12, bf16[256,512]{1,0:T(8,128)(2,1)S(1)} %copy-done.2, bf16[256,1024]{1,0:T(8,128)(2,1)S(1)} %copy-done.1, bf16[32,512]{1,0:T(8,128)(2,1)S(1)} %copy-done.3, bf16[32,512]{1,0:T(8,128)(2,1)S(1)} %copy-done.5, ...), custom_call_target="tpu_custom_call" | custom-call | tf_op jit(solution)/shard_map/pallas_call | solution.py:203
  (26 shorter events, 0.2 us)
Async XLA Ops:
  27.9 22.7 %collective-permute-start = (bf16[1024,256]{1,0:T(8,128)(2,1)S(1)}, bf16[1024,256]{1,0:T(8,128)(2,1)S(1)}, u32[]{:S(2)}, u32[]{:S(2)}) collective-permute-start(bf16[1024,256]{1,0:T(8,128)(2,1)S(1)} %bitcast.13), channel_id=1, source_target_pairs={{0,1},{1,2},{2,3},{3,4},{4,5},{5,6},{6,7},{7,0},{8,9},{9,10},{10,1... | collective-permute-start | bytes 1572872 | tf_op jit(solution)/shard_map/ppermute | solution.py:213
  32.2 0.7 copy-start.8
  33.1 8.6 %copy-start.9 = (s32[2]{0:T(128)S(1)}, s32[2]{0:T(128)}, u32[]{:S(2)}) copy-start(s32[2]{0:T(128)} %param.25) | copy-start | bytes 28
  33.1 8.6 %copy-start.10 = (s32[2]{0:T(128)S(1)}, s32[2]{0:T(128)}, u32[]{:S(2)}) copy-start(s32[2]{0:T(128)} %param.26) | copy-start | bytes 28
  33.2 19.6 %collective-permute-start.2 = (bf16[1024,256]{1,0:T(8,128)(2,1)S(1)}, bf16[1024,256]{1,0:T(8,128)(2,1)S(1)}, u32[]{:S(2)}, u32[]{:S(2)}) collective-permute-start(bf16[1024,256]{1,0:T(8,128)(2,1)S(1)} %bitcast.14), channel_id=1, source_target_pairs={{0,7},{1,0},{2,1},{3,2},{4,3},{5,4},{6,5},{7,6},{8,15},{9,8},{10,9... | collective-permute-start | bytes 1572872 | tf_op jit(solution)/shard_map/ppermute | solution.py:213
  50.6 16.0 %collective-permute-start.1 = (bf16[1024,256]{1,0:T(8,128)(2,1)S(1)}, bf16[1024,256]{1,0:T(8,128)(2,1)S(1)}, u32[]{:S(2)}, u32[]{:S(2)}) collective-permute-start(bf16[1024,256]{1,0:T(8,128)(2,1)S(1)} %collective-permute-done.refs_0_), channel_id=1, source_target_pairs={{0,1},{1,2},{2,3},{3,4},{4,5},{5,6},{6,7},{7,0},{8,9},{9,10},{10,1... | collective-permute-start | bytes 1572872 | tf_op jit(solution)/shard_map/ppermute | solution.py:213
  52.7 15.8 %collective-permute-start.4 = (bf16[1024,256]{1,0:T(8,128)(2,1)S(1)}, bf16[1024,256]{1,0:T(8,128)(2,1)S(1)}, u32[]{:S(2)}, u32[]{:S(2)}) collective-permute-start(bf16[1024,256]{1,0:T(8,128)(2,1)S(1)} %collective-permute-done.2.refs_1_), channel_id=1, source_target_pairs={{0,7},{1,0},{2,1},{3,2},{4,3},{5,4},{6,5},{7,6},{8,15},{9,8},{10,9... | collective-permute-start | bytes 1572872 | tf_op jit(solution)/shard_map/ppermute | solution.py:213
  66.6 15.1 %collective-permute-start.3 = (bf16[1024,256]{1,0:T(8,128)(2,1)S(1)}, bf16[1024,256]{1,0:T(8,128)(2,1)S(1)}, u32[]{:S(2)}, u32[]{:S(2)}) collective-permute-start(bf16[1024,256]{1,0:T(8,128)(2,1)S(1)} %collective-permute-done.1.refs_0_), channel_id=1, source_target_pairs={{0,1},{1,2},{2,3},{3,4},{4,5},{5,6},{6,7},{7,0},{8,9},{9,10},{10,1... | collective-permute-start | bytes 1572872 | tf_op jit(solution)/shard_map/ppermute | solution.py:213
  68.6 15.1 %collective-permute-start.6 = (bf16[1024,256]{1,0:T(8,128)(2,1)S(1)}, bf16[1024,256]{1,0:T(8,128)(2,1)S(1)}, u32[]{:S(2)}, u32[]{:S(2)}) collective-permute-start(bf16[1024,256]{1,0:T(8,128)(2,1)S(1)} %collective-permute-done.4.refs_1_), channel_id=1, source_target_pairs={{0,7},{1,0},{2,1},{3,2},{4,3},{5,4},{6,5},{7,6},{8,15},{9,8},{10,9... | collective-permute-start | bytes 1572872 | tf_op jit(solution)/shard_map/ppermute | solution.py:213
  81.7 14.2 %collective-permute-start.5 = (bf16[1024,256]{1,0:T(8,128)(2,1)S(1)}, bf16[1024,256]{1,0:T(8,128)(2,1)S(1)}, u32[]{:S(2)}, u32[]{:S(2)}) collective-permute-start(bf16[1024,256]{1,0:T(8,128)(2,1)S(1)} %collective-permute-done.3.refs_0_), channel_id=1, source_target_pairs={{0,1},{1,2},{2,3},{3,4},{4,5},{5,6},{6,7},{7,0},{8,9},{9,10},{10,1... | collective-permute-start | bytes 1572872 | tf_op jit(solution)/shard_map/ppermute | solution.py:213
  86.1 21.7 %copy-start = (bf16[512,1024]{1,0:T(8,128)(2,1)S(1)}, bf16[512,1024]{1,0:T(8,128)(2,1)}, u32[]{:S(2)}) copy-start(bf16[512,1024]{1,0:T(8,128)(2,1)} %w_ref.1) | copy-start | bytes 3145732
  95.9 12.0 %copy-start.2 = (bf16[256,512]{1,0:T(8,128)(2,1)S(1)}, bf16[256,512]{1,0:T(8,128)(2,1)}, u32[]{:S(2)}) copy-start(bf16[256,512]{1,0:T(8,128)(2,1)} %hg.1) | copy-start | bytes 786436
  95.9 12.0 %copy-start.4 = (bf16[32,1024]{1,0:T(8,128)(2,1)S(1)}, bf16[32,1024]{1,0:T(8,128)(2,1)}, u32[]{:S(2)}) copy-start(bf16[32,1024]{1,0:T(8,128)(2,1)} %cx.1) | copy-start | bytes 196612
  95.9 12.0 %copy-start.6 = (bf16[32,512]{1,0:T(8,128)(2,1)S(1)}, bf16[32,512]{1,0:T(8,128)(2,1)}, u32[]{:S(2)}) copy-start(bf16[32,512]{1,0:T(8,128)(2,1)} %cv.1) | copy-start | bytes 98308
  95.9 12.0 %copy-start.7 = (bf16[32,512]{1,0:T(8,128)(2,1)S(1)}, bf16[32,512]{1,0:T(8,128)(2,1)}, u32[]{:S(2)}) copy-start(bf16[32,512]{1,0:T(8,128)(2,1)} %cg.1) | copy-start | bytes 98308
  97.5 10.4 %copy-start.1 = (bf16[256,1024]{1,0:T(8,128)(2,1)S(1)}, bf16[256,1024]{1,0:T(8,128)(2,1)}, u32[]{:S(2)}) copy-start(bf16[256,1024]{1,0:T(8,128)(2,1)} %hx.1) | copy-start | bytes 1572868
  97.5 10.4 %copy-start.3 = (bf16[32,512]{1,0:T(8,128)(2,1)S(1)}, bf16[32,512]{1,0:T(8,128)(2,1)}, u32[]{:S(2)}) copy-start(bf16[32,512]{1,0:T(8,128)(2,1)} %cq.1) | copy-start | bytes 98308
  97.5 10.3 %copy-start.5 = (bf16[32,512]{1,0:T(8,128)(2,1)S(1)}, bf16[32,512]{1,0:T(8,128)(2,1)}, u32[]{:S(2)}) copy-start(bf16[32,512]{1,0:T(8,128)(2,1)} %ck.1) | copy-start | bytes 98308

commit v9 on v5

--- a/solution.py
+++ b/solution.py
@@ -50,12 +50,10 @@
 
 
 def join_kernel(y_ref, *refs):
-    *pieces, low, high, whole = refs
+    *pieces, out = refs
     for i, piece in enumerate(pieces):
         strip = lax.rem(y_ref[0] + NY - i, NY)
-        whole[pl.ds(pl.multiple_of(strip * ROWS, ROWS), ROWS), :] = piece[...]
-    low[...] = whole[0 : 2 * ROWS, :]
-    high[...] = whole[2 * ROWS : KEYS, :]
+        out[pl.ds(pl.multiple_of(strip * ROWS, ROWS), ROWS), :] = piece[...]
 
 
 def unfold_kernel(y_ref, *refs):
@@ -68,25 +66,18 @@
         out[pl.ds(pl.multiple_of(KEYS + strip * CROWS, CROWS), CROWS), :] = piece[REST:FOLD, DH : 2 * DH]
 
 
-def attend_kernel(offsets, strips, first, last, z_ref, start_ref, len_ref, qs, user_ref, *refs):
-    *kv_refs, in_ref = refs[: len(refs) - (2 if last else 3)] if not first else (*refs[:-3], None)
-    out_ref, acc = (refs[-2], refs[-1]) if last else (refs[-3], refs[-1])
-    z = z_ref[0]
-    starts = [start_ref[u] for u in range(2)]
-    ends = [start_ref[u] + len_ref[u] for u in range(2)]
-    span = len(strips) * ROWS
-
-    if last:
-        (kv,) = kv_refs
-    else:
-        kv = refs[-2]
-        size = kv_refs[0].shape[0]
-        for i, ref in enumerate(kv_refs):
-            kv[i * size : (i + 1) * size, :] = ref[...]
+def attend_kernel(offsets, first, last, info_ref, qs, user_ref, *refs):
+    *ins, out_ref, kv, acc = refs
+    z = info_ref[0]
+    starts = [info_ref[1 + u] for u in range(2)]
+    ends = [info_ref[1 + u] + info_ref[3 + u] for u in range(2)]
+
+    for i in range(len(offsets)):
+        kv[i * KEYS : (i + 1) * KEYS, :] = ins[i][...]
     if first:
         acc[...] = jnp.zeros_like(acc)
     else:
-        acc[...] = in_ref[...]
+        acc[...] = ins[-1][...]
 
     lows, stops = [], []
     for half in range(2 * NY):
@@ -104,14 +95,13 @@
     column = lax.broadcasted_iota(jnp.int32, (1, ROWS), 1)
 
     def block_step(block, base, shift):
-        for i, strip in enumerate(strips):
-            slot = strip + shift
-            row = slot * ROWS
-            key = pl.multiple_of(base + i * ROWS, ROWS)
+        for strip in range(NY):
+            row = (strip + shift) * ROWS
+            key = pl.multiple_of(base + strip * ROWS, ROWS)
             events = (strip * NZ + block) * ROWS + column
             w = silu_weight(contract_lanes(qs[row:TOTAL, :], kv[pl.ds(key, ROWS), 0:DH]))
             parts = []
-            for half in range(2 * slot, 2 * NY):
+            for half in range(2 * (strip + shift), 2 * NY):
                 at = half * BLOCK - row
                 keep = jnp.where(events >= lows[half], 1.0, 0.0).astype(jnp.bfloat16)
                 parts.append(w[at : at + BLOCK] * keep)
@@ -125,15 +115,14 @@
         for n, offset in enumerate(offsets[:-1]):
             block = jnp.where(part == n, z + offset, block)
         block = lax.rem(block, NZ)
-        base = (block if last else part) * span
 
         @pl.when(block < z)
         def _():
-            block_step(block, base, 0)
+            block_step(block, part * KEYS, 0)
 
         @pl.when(block >= z)
         def _():
-            block_step(block, base, 1)
+            block_step(block, part * KEYS, 1)
 
         return carry
 
@@ -167,21 +156,21 @@
             out_ref[s * FOLD + REST : (s + 1) * FOLD, DH : 2 * DH] = cands
 
 
-def attend(offsets, strips, where, queries, users, blocks, total, last=False):
+def attend(offsets, info, queries, users, blocks, total, last=False):
     first = total is None
     shape = jax.ShapeDtypeStruct((NY * FOLD, 2 * DH), jnp.bfloat16) if last else jax.ShapeDtypeStruct((TOTAL, DH), jnp.float32)
     state = [] if first else [total]
-    keys = len(offsets) * len(strips) * ROWS
+    keys = len(offsets) * KEYS
     return pl.pallas_call(
-        functools.partial(attend_kernel, offsets, strips, first, last),
-        in_specs=[SMEM] * 3 + [VMEM] * (2 + len(blocks) + len(state)),
+        functools.partial(attend_kernel, offsets, first, last),
+        in_specs=[SMEM] + [VMEM] * (2 + len(blocks) + len(state)),
         out_specs=VMEM,
         out_shape=shape,
-        scratch_shapes=([] if last else [pltpu.VMEM((keys, 2 * DH), jnp.bfloat16)]) + [pltpu.VMEM((TOTAL, DH), jnp.float32)],
+        scratch_shapes=[pltpu.VMEM((keys, 2 * DH), jnp.bfloat16), pltpu.VMEM((TOTAL, DH), jnp.float32)],
         compiler_params=PARAMS,
         cost_estimate=pl.CostEstimate(flops=4 * TOTAL * keys * DH, bytes_accessed=1 << 20, transcendentals=0),
         name="attend",
-    )(*where, queries, users, *blocks, *state)
+    )(info, queries, users, *blocks, *state)
 
 
 def finish_kernel(t_ref, hg, hx, cq, ck, cv, cg, cx, w_ref, ho, co):
@@ -229,35 +218,32 @@
     cand_query, cand_key, cand_value, cand_gate, cand_input,
     cand_user, hist_len, hist_start, out_weight,
 ):
-    z = lax.axis_index("z")
+    z = lax.axis_index("z").astype(jnp.int32)
     y = lax.axis_index("y").astype(jnp.int32).reshape(1)
-    where = (z.astype(jnp.int32).reshape(1), hist_start, hist_len)
+    info = jnp.concatenate([z.reshape(1), hist_start, hist_len])
     users = lax.dynamic_index_in_dim(cand_user.reshape(NY, NZ, CROWS), z, axis=1).reshape(NY * CROWS, 1)
     parts = call(
         split_kernel, [(ROWS, 2 * DH)] * HEADS + [(FOLD, 2 * DH)] * HEADS,
         hist_key, hist_value, hist_query, cand_query, place=y, limit=WIDE_LIMIT,
     )
     pieces = [parts[0]] + [turn(parts[i], "y", i) for i in (1, 2, 3)]
+    (own,) = call(join_kernel, [(KEYS, 2 * DH)], *pieces, place=y)
+    up1, down1 = turn(own, "z", 1), turn(own, "z", -1)
     folds = [parts[HEADS]] + [turn(parts[HEADS + i], "y", i) for i in (1, 2, 3)]
-    near, far = call(
-        join_kernel, [(2 * ROWS, 2 * DH)] * 2, *pieces, place=y, scratch=[pltpu.VMEM((KEYS, 2 * DH), jnp.bfloat16)]
-    )
-    gathered = lax.all_gather(far, "z", axis=0, tiled=True)
-    up, down = turn(near, "z", 1), turn(near, "z", -1)
+    up1, folds[1] = lax.optimization_barrier((up1, folds[1]))
+    down1, folds[3] = lax.optimization_barrier((down1, folds[3]))
+    up2, down2 = turn(up1, "z", 1), turn(down1, "z", -1)
     (queries,) = call(unfold_kernel, [(TOTAL, DH)], *folds, place=y)
-    total = attend((0,), (0, 1, 2, 3), where, queries, users, (near, far), None)
-    for step in (1, 2):
-        up, held = lax.optimization_barrier((up, total))
-        down, total = lax.optimization_barrier((down, held))
-        blocks = (up, down)
-        up, down = turn(up, "z", 1), turn(down, "z", -1)
-        total = attend((NZ - step, step), (0, 1), where, queries, users, blocks, total)
-    up, held = lax.optimization_barrier((up, total))
-    down, total = lax.optimization_barrier((down, held))
-    low, high = turn(up[:ROWS], "z", 1), turn(down[ROWS:], "z", -1)
-    total = attend((NZ - 3, 3), (0, 1), where, queries, users, (up, down), total)
-    total = attend((4,), (0, 1), where, queries, users, (low, high), total)
-    total = attend(tuple(range(1, NZ)), (2, 3), where, queries, users, (gathered,), total, last=True)
+    total = attend((0,), info, queries, users, (own,), None)
+    total = attend((NZ - 1, 1), info, queries, users, (up1, down1), total)
+    up2, held = lax.optimization_barrier((up2, total))
+    down2, total = lax.optimization_barrier((down2, held))
+    up3, down3 = turn(up2, "z", 1), turn(down2, "z", -1)
+    total = attend((NZ - 2, 2), info, queries, users, (up2, down2), total)
+    up3, total = lax.optimization_barrier((up3, total))
+    across = turn(up3, "z", 1)
+    total = attend((NZ - 3, 3), info, queries, users, (up3, down3), total)
+    total = attend((4,), info, queries, users, (across,), total, last=True)
     total = lax.all_to_all(total, "y", 0, 0, tiled=True)
     return tuple(
         call(

time: 127 us -> 108 us (0.85)
  between operations: 14.4 us -> 0.98 us
  starting transfers between devices: 54.4 us -> 48.9 us
  waiting for transfers between devices: 24.5 us -> 29.1 us
  Pallas kernels: 18.3 us -> 14.8 us
  local copies, waits for them, and re-layouts: 4.46 us -> 1.83 us
    ppermute x14 -> x13, starting transfers between devices: 54.4 us -> 48.9 us  [turn(): lax.ppermute(array, axis, [(i, (i + step) % count) for i in range(count)])]
    ppermute x14 -> x13, waiting for transfers between devices: 24.5 us -> 29.1 us  [turn(): lax.ppermute(array, axis, [(i, (i + step) % count) for i in range(count)])]
    pallas_call x6 -> x5, Pallas kernels: 13.9 us -> 11 us  [attend(): pl.pallas_call(functools.partial(attend_kernel, offsets, first, last), in...]
    unnamed x26 -> x32, local copies, waits for them, and re-layouts: 3.55 us -> 1.62 us
  transfers between devices with their start and end apart: 15 -> 13, of which waited for: 7 -> 8; matrix products, arithmetic and copies ran while one was open for 1% -> 0% of each run, Pallas kernels for 8% -> 9%
where the time goes in v9:
time: 108 us; the launch traced here: 107 us
  starting transfers between devices  48.9 us (45%)
  waiting for transfers between devices  29.1 us (27%)
  Pallas kernels  14.8 us (14%)
  blocking collectives  11.3 us (10%)
  local copies, waits for them, and re-layouts  1.83 us (2%)
    ppermute x13, starting transfers between devices, turn(): lax.ppermute(array, axis, [(i, (i + step) % count) for i in range(count)])  48.9 us
    ppermute x13, waiting for transfers between devices, turn(): lax.ppermute(array, axis, [(i, (i + step) % count) for i in range(count)])  29.1 us
    all_to_all x1, blocking collectives, on_device(): total = lax.all_to_all(total, 'y', 0, 0, tiled=True)  11.3 us
    pallas_call x5, Pallas kernels, attend(): pl.pallas_call(functools.partial(attend_kernel, offsets, first, last), in...  11 us
    pallas_call x4, Pallas kernels, call(): pl.pallas_call(kernel, in_specs=[SMEM] * (place is not None) + [VMEM] * (...  3.76 us
  transfers between devices with their start and end apart: 13, of which 8 were waited for; matrix products, arithmetic and copies ran while one was open for 0% of the time, Pallas kernels for 9%

profile of v9, /device:TPU:56, one launch (start us, length us, event | category | flops | bytes accessed | tf_op | source)
XLA Modules:
  0.0 106.9 jit_solution(4485076054261928714)
XLA Ops:
  0.6 2.1 %shard_map.149 = (bf16[256,256]{1,0:T(8,128)(2,1)}, bf16[256,256]{1,0:T(8,128)(2,1)}, bf16[256,256]{1,0:T(8,128)(2,1)}, bf16[256,256]{1,0:T(8,128)(2,1)}, bf16[1...) custom-call(s32[1]{0:T(128)} %bitcast.1.y_ref, ...), custom_call_target="tpu_custom_call" | custom-call | tf_op jit(solution)/shard_map/pallas_call | solution.py:201
  2.8 4.8 %collective-permute-start = (bf16[256,256]{1,0:T(8,128)(2,1)}, bf16[256,256]{1,0:T(8,128)(2,1)S(1)}, u32[]{:S(2)}, u32[]{:S(2)}) collective-permute-start(bf16[256,256]{1,0:T(8,128)(2,1)} %get-tuple-element.22), channel_id=1, source_target_pairs={{0,8},{8,16},{16,24},{24,0},{1,9},{9,17},{17,25},{25,1},{2,10},{10... | collective-permute-start | bytes 393224 | tf_op jit(solution)/shard_map/ppermute | solution.py:213
  7.6 1.9 %collective-permute-start.1 = (bf16[256,256]{1,0:T(8,128)(2,1)}, bf16[256,256]{1,0:T(8,128)(2,1)S(1)}, u32[]{:S(2)}, u32[]{:S(2)}) collective-permute-start(bf16[256,256]{1,0:T(8,128)(2,1)} %get-tuple-element.23), channel_id=1, source_target_pairs={{0,16},{8,24},{16,0},{24,8},{1,17},{9,25},{17,1},{25,9},{2,18},{10... | collective-permute-start | bytes 393224 | tf_op jit(solution)/shard_map/ppermute | solution.py:213
  9.5 3.1 %collective-permute-start.2 = (bf16[256,256]{1,0:T(8,128)(2,1)}, bf16[256,256]{1,0:T(8,128)(2,1)S(1)}, u32[]{:S(2)}, u32[]{:S(2)}) collective-permute-start(bf16[256,256]{1,0:T(8,128)(2,1)} %get-tuple-element.24), channel_id=1, source_target_pairs={{0,24},{8,0},{16,8},{24,16},{1,25},{9,1},{17,9},{25,17},{2,26},{10... | collective-permute-start | bytes 393224 | tf_op jit(solution)/shard_map/ppermute | solution.py:213
  12.7 7.4 %collective-permute-done.1.refs_2_ = bf16[256,256]{1,0:T(8,128)(2,1)S(1)} collective-permute-done((bf16[256,256]{1,0:T(8,128)(2,1)}, bf16[256,256]{1,0:T(8,128)(2,1)S(1)}, u32[]{:S(2)}, u32[]{:S(2)}) %collective-permute-start.1) | collective-permute-done | bytes 131104 | tf_op jit(solution)/shard_map/ppermute | solution.py:213
  21.1 4.4 %collective-permute-start.3 = (bf16[1024,256]{1,0:T(8,128)(2,1)S(1)}, bf16[1024,256]{1,0:T(8,128)(2,1)S(1)}, u32[]{:S(2)}, u32[]{:S(2)}) collective-permute-start(bf16[1024,256]{1,0:T(8,128)(2,1)S(1)} %shard_map.150.refs_0_), channel_id=1, source_target_pairs={{0,1},{1,2},{2,3},{3,4},{4,5},{5,6},{6,7},{7,0},{8,9},{9,10},{10,1... | collective-permute-start | bytes 1572872 | tf_op jit(solution)/shard_map/ppermute | solution.py:213
  25.5 8.6 %collective-permute-start.6 = (bf16[1024,256]{1,0:T(8,128)(2,1)S(1)}, bf16[1024,256]{1,0:T(8,128)(2,1)S(1)}, u32[]{:S(2)}, u32[]{:S(2)}) collective-permute-start(bf16[1024,256]{1,0:T(8,128)(2,1)S(1)} %shard_map.150.refs_0_), channel_id=1, source_target_pairs={{0,7},{1,0},{2,1},{3,2},{4,3},{5,4},{6,5},{7,6},{8,15},{9,8},{10,9... | collective-permute-start | bytes 1572872 | tf_op jit(solution)/shard_map/ppermute | solution.py:213
  34.1 3.5 %collective-permute-start.4 = (bf16[144,256]{1,0:T(8,128)(2,1)S(1)}, bf16[144,256]{1,0:T(8,128)(2,1)S(1)}, u32[]{:S(2)}, u32[]{:S(2)}) collective-permute-start(bf16[144,256]{1,0:T(8,128)(2,1)S(1)} %copy-done.15), channel_id=1, source_target_pairs={{0,8},{8,16},{16,24},{24,0},{1,9},{9,17},{17,25},{25,1},{2,10},{10... | collective-permute-start | bytes 221192 | tf_op jit(solution)/shard_map/ppermute | solution.py:213
  37.6 2.8 %collective-permute-done.4.refs_1_ = bf16[144,256]{1,0:T(8,128)(2,1)S(1)} collective-permute-done((bf16[144,256]{1,0:T(8,128)(2,1)S(1)}, bf16[144,256]{1,0:T(8,128)(2,1)S(1)}, u32[]{:S(2)}, u32[]{:S(2)}) %collective-permute-start.4) | collective-permute-done | bytes 73760 | tf_op jit(solution)/shard_map/ppermute | solution.py:213
  40.3 3.9 %collective-permute-done.3.refs_0_ = bf16[1024,256]{1,0:T(8,128)(2,1)S(1)} collective-permute-done((bf16[1024,256]{1,0:T(8,128)(2,1)S(1)}, bf16[1024,256]{1,0:T(8,128)(2,1)S(1)}, u32[]{:S(2)}, u32[]{:S(2)}) %collective-permute-start.3) | collective-permute-done | bytes 524320 | tf_op jit(solution)/shard_map/ppermute | solution.py:213
  46.2 2.4 %collective-permute-start.7 = (bf16[144,256]{1,0:T(8,128)(2,1)S(1)}, bf16[144,256]{1,0:T(8,128)(2,1)S(1)}, u32[]{:S(2)}, u32[]{:S(2)}) collective-permute-start(bf16[144,256]{1,0:T(8,128)(2,1)S(1)} %copy-done.14), channel_id=1, source_target_pairs={{0,24},{8,0},{16,8},{24,16},{1,25},{9,1},{17,9},{25,17},{2,26},{10... | collective-permute-start | bytes 221192 | tf_op jit(solution)/shard_map/ppermute | solution.py:213
  48.6 3.7 %collective-permute-start.5 = (bf16[144,256]{1,0:T(8,128)(2,1)S(1)}, bf16[144,256]{1,0:T(8,128)(2,1)S(1)}, u32[]{:S(2)}, u32[]{:S(2)}) collective-permute-start(bf16[144,256]{1,0:T(8,128)(2,1)S(1)} %copy-done.13), channel_id=1, source_target_pairs={{0,16},{8,24},{16,0},{24,8},{1,17},{9,25},{17,1},{25,9},{2,18},{10... | collective-permute-start | bytes 221192 | tf_op jit(solution)/shard_map/ppermute | solution.py:213
  54.3 5.1 %collective-permute-start.10 = (bf16[1024,256]{1,0:T(8,128)(2,1)S(1)}, bf16[1024,256]{1,0:T(8,128)(2,1)S(1)}, u32[]{:S(2)}, u32[]{:S(2)}) collective-permute-start(bf16[1024,256]{1,0:T(8,128)(2,1)S(1)} %collective-permute-done.6.refs_1_), channel_id=1, source_target_pairs={{0,7},{1,0},{2,1},{3,2},{4,3},{5,4},{6,5},{7,6},{8,15},{9,8},{10,9... | collective-permute-start | bytes 1572872 | tf_op jit(solution)/shard_map/ppermute | solution.py:213
  59.5 2.2 %attend.5.refs_2_ = f32[1152,128]{1,0:T(8,128)S(1)} custom-call(s32[5]{0:T(128)S(1)} %pad_add_fusion.info_ref, bf16[1152,128]{1,0:T(8,128)(2,1)S(1)} %shard_map.151.qs, s32[128,1]{1,0:T(8,128)S(1)} %reshape.22.user_ref, bf16[1024,256]{1,0:T(8,128)(2,1)S(1)} %shard_map.150.refs_0_), custom_call_target="tpu_custom_call" | custom-call | flops 603979776 | bytes 1048576 | tf_op jit(solution)/shard_map/attend/pallas_call | solution.py:164
  61.7 2.4 %attend.6.refs_2_ = f32[1152,128]{1,0:T(8,128)S(1)} custom-call(s32[5]{0:T(128)S(1)} %pad_add_fusion.info_ref, bf16[1152,128]{1,0:T(8,128)(2,1)S(1)} %shard_map.151.qs, s32[128,1]{1,0:T(8,128)S(1)} %reshape.22.user_ref, bf16[1024,256]{1,0:T(8,128)(2,1)S(1)} %collective-permute-done.3.refs_0_, bf16[1024,256]{1,0:T(8,128)(2,1)S(1)} %collective-permute-done.6.refs_1_, ...), custom_call_target="tpu_custom_call" | custom-call | flops 1207959552 | bytes 1048576 | tf_op jit(solution)/shard_map/attend/pallas_call | solution.py:164
  64.2 1.9 %collective-permute-start.9 = (bf16[1024,256]{1,0:T(8,128)(2,1)S(1)}, bf16[1024,256]{1,0:T(8,128)(2,1)S(1)}, u32[]{:S(2)}, u32[]{:S(2)}) collective-permute-start(bf16[1024,256]{1,0:T(8,128)(2,1)S(1)} %collective-permute-done.8.refs_0_), channel_id=1, source_target_pairs={{0,1},{1,2},{2,3},{3,4},{4,5},{5,6},{6,7},{7,0},{8,9},{9,10},{10,1... | collective-permute-start | bytes 1572872 | tf_op jit(solution)/shard_map/ppermute | solution.py:213
  66.1 2.6 %collective-permute-done.10.refs_1_ = bf16[1024,256]{1,0:T(8,128)(2,1)S(1)} collective-permute-done((bf16[1024,256]{1,0:T(8,128)(2,1)S(1)}, bf16[1024,256]{1,0:T(8,128)(2,1)S(1)}, u32[]{:S(2)}, u32[]{:S(2)}) %collective-permute-start.10) | collective-permute-done | bytes 524320 | tf_op jit(solution)/shard_map/ppermute | solution.py:213
  68.7 5.6 %collective-permute-start.12 = (bf16[1024,256]{1,0:T(8,128)(2,1)S(1)}, bf16[1024,256]{1,0:T(8,128)(2,1)S(1)}, u32[]{:S(2)}, u32[]{:S(2)}) collective-permute-start(bf16[1024,256]{1,0:T(8,128)(2,1)S(1)} %collective-permute-done.10.refs_1_), channel_id=1, source_target_pairs={{0,7},{1,0},{2,1},{3,2},{4,3},{5,4},{6,5},{7,6},{8,15},{9,8},{10,9... | collective-permute-start | bytes 1572872 | tf_op jit(solution)/shard_map/ppermute | solution.py:213
  74.3 2.4 %attend.7.refs_2_ = f32[1152,128]{1,0:T(8,128)S(1)} custom-call(s32[5]{0:T(128)S(1)} %pad_add_fusion.info_ref, bf16[1152,128]{1,0:T(8,128)(2,1)S(1)} %shard_map.151.qs, s32[128,1]{1,0:T(8,128)S(1)} %reshape.22.user_ref, bf16[1024,256]{1,0:T(8,128)(2,1)S(1)} %collective-permute-done.8.refs_0_, bf16[1024,256]{1,0:T(8,128)(2,1)S(1)} %collective-permute-done.10.refs_1_, ...), custom_call_target="tpu_custom_call" | custom-call | flops 1207959552 | bytes 1048576 | tf_op jit(solution)/shard_map/attend/pallas_call | solution.py:164
  76.8 2.0 %collective-permute-done.9.refs_0_ = bf16[1024,256]{1,0:T(8,128)(2,1)S(1)} collective-permute-done((bf16[1024,256]{1,0:T(8,128)(2,1)S(1)}, bf16[1024,256]{1,0:T(8,128)(2,1)S(1)}, u32[]{:S(2)}, u32[]{:S(2)}) %collective-permute-start.9) | collective-permute-done | bytes 524320 | tf_op jit(solution)/shard_map/ppermute | solution.py:213
  80.7 2.0 %collective-permute-done.12.refs_1_ = bf16[1024,256]{1,0:T(8,128)(2,1)S(1)} collective-permute-done((bf16[1024,256]{1,0:T(8,128)(2,1)S(1)}, bf16[1024,256]{1,0:T(8,128)(2,1)S(1)}, u32[]{:S(2)}, u32[]{:S(2)}) %collective-permute-start.12) | collective-permute-done | bytes 524320 | tf_op jit(solution)/shard_map/ppermute | solution.py:213
  82.7 2.4 %attend.8.refs_1_ = f32[1152,128]{1,0:T(8,128)S(1)} custom-call(s32[5]{0:T(128)S(1)} %pad_add_fusion.info_ref, bf16[1152,128]{1,0:T(8,128)(2,1)S(1)} %shard_map.151.qs, s32[128,1]{1,0:T(8,128)S(1)} %reshape.22.user_ref, bf16[1024,256]{1,0:T(8,128)(2,1)S(1)} %collective-permute-done.9.refs_0_, bf16[1024,256]{1,0:T(8,128)(2,1)S(1)} %collective-permute-done.12.refs_1_, ...), custom_call_target="tpu_custom_call" | custom-call | flops 1207959552 | bytes 1048576 | tf_op jit(solution)/shard_map/attend/pallas_call | solution.py:164
  85.1 7.3 %collective-permute-done.11.refs_0_ = bf16[1024,256]{1,0:T(8,128)(2,1)S(1)} collective-permute-done((bf16[1024,256]{1,0:T(8,128)(2,1)S(1)}, bf16[1024,256]{1,0:T(8,128)(2,1)S(1)}, u32[]{:S(2)}, u32[]{:S(2)}) %collective-permute-start.11) | collective-permute-done | bytes 524320 | tf_op jit(solution)/shard_map/ppermute | solution.py:213
  94.1 11.3 %all_to_all.11 = bf16[4,144,256]{2,1,0:T(8,128)(2,1)S(1)} all-to-all(bf16[4,144,256]{2,1,0:T(8,128)(2,1)S(1)} %bitcast.5), channel_id=1, replica_groups=mesh['batch'=16,'y'=4,'z'=8] {'y'}, dimensions={0} | all-to-all | bytes 589824 | tf_op jit(solution)/shard_map/all_to_all | solution.py:247
  (48 shorter events, 10.0 us)
Async XLA Ops:
  2.8 9.9 %collective-permute-start = (bf16[256,256]{1,0:T(8,128)(2,1)}, bf16[256,256]{1,0:T(8,128)(2,1)S(1)}, u32[]{:S(2)}, u32[]{:S(2)}) collective-permute-start(bf16[256,256]{1,0:T(8,128)(2,1)} %get-tuple-element.22), channel_id=1, source_target_pairs={{0,8},{8,16},{16,24},{24,0},{1,9},{9,17},{17,25},{25,1},{2,10},{10... | collective-permute-start | bytes 393224 | tf_op jit(solution)/shard_map/ppermute | solution.py:213
  7.6 12.5 %collective-permute-start.1 = (bf16[256,256]{1,0:T(8,128)(2,1)}, bf16[256,256]{1,0:T(8,128)(2,1)S(1)}, u32[]{:S(2)}, u32[]{:S(2)}) collective-permute-start(bf16[256,256]{1,0:T(8,128)(2,1)} %get-tuple-element.23), channel_id=1, source_target_pairs={{0,16},{8,24},{16,0},{24,8},{1,17},{9,25},{17,1},{25,9},{2,18},{10... | collective-permute-start | bytes 393224 | tf_op jit(solution)/shard_map/ppermute | solution.py:213
  9.5 10.6 %collective-permute-start.2 = (bf16[256,256]{1,0:T(8,128)(2,1)}, bf16[256,256]{1,0:T(8,128)(2,1)S(1)}, u32[]{:S(2)}, u32[]{:S(2)}) collective-permute-start(bf16[256,256]{1,0:T(8,128)(2,1)} %get-tuple-element.24), channel_id=1, source_target_pairs={{0,24},{8,0},{16,8},{24,16},{1,25},{9,1},{17,9},{25,17},{2,26},{10... | collective-permute-start | bytes 393224 | tf_op jit(solution)/shard_map/ppermute | solution.py:213
  21.0 13.1 %copy-start.15 = (bf16[144,256]{1,0:T(8,128)(2,1)S(1)}, bf16[144,256]{1,0:T(8,128)(2,1)}, u32[]{:S(2)}) copy-start(bf16[144,256]{1,0:T(8,128)(2,1)} %get-tuple-element.25) | copy-start | bytes 221188
  21.0 25.2 %copy-start.14 = (bf16[144,256]{1,0:T(8,128)(2,1)S(1)}, bf16[144,256]{1,0:T(8,128)(2,1)}, u32[]{:S(2)}) copy-start(bf16[144,256]{1,0:T(8,128)(2,1)} %get-tuple-element.28) | copy-start | bytes 221188
  21.0 27.6 %copy-start.13 = (bf16[144,256]{1,0:T(8,128)(2,1)S(1)}, bf16[144,256]{1,0:T(8,128)(2,1)}, u32[]{:S(2)}) copy-start(bf16[144,256]{1,0:T(8,128)(2,1)} %get-tuple-element.27) | copy-start | bytes 221188
  21.0 31.3 %copy-start.10 = (s32[1024]{0:T(1024)S(1)}, s32[1024]{0:T(1024)}, u32[]{:S(2)}) copy-start(s32[1024]{0:T(1024)} %param.24) | copy-start | bytes 12292
  21.1 38.4 %copy-start.5 = (bf16[144,256]{1,0:T(8,128)(2,1)S(1)}, bf16[144,256]{1,0:T(8,128)(2,1)}, u32[]{:S(2)}) copy-start(bf16[144,256]{1,0:T(8,128)(2,1)} %get-tuple-element.20.refs_0_) | copy-start | bytes 221188
  21.1 23.2 %collective-permute-start.3 = (bf16[1024,256]{1,0:T(8,128)(2,1)S(1)}, bf16[1024,256]{1,0:T(8,128)(2,1)S(1)}, u32[]{:S(2)}, u32[]{:S(2)}) collective-permute-start(bf16[1024,256]{1,0:T(8,128)(2,1)S(1)} %shard_map.150.refs_0_), channel_id=1, source_target_pairs={{0,1},{1,2},{2,3},{3,4},{4,5},{5,6},{6,7},{7,0},{8,9},{9,10},{10,1... | collective-permute-start | bytes 1572872 | tf_op jit(solution)/shard_map/ppermute | solution.py:213
  25.5 28.8 %collective-permute-start.6 = (bf16[1024,256]{1,0:T(8,128)(2,1)S(1)}, bf16[1024,256]{1,0:T(8,128)(2,1)S(1)}, u32[]{:S(2)}, u32[]{:S(2)}) collective-permute-start(bf16[1024,256]{1,0:T(8,128)(2,1)S(1)} %shard_map.150.refs_0_), channel_id=1, source_target_pairs={{0,7},{1,0},{2,1},{3,2},{4,3},{5,4},{6,5},{7,6},{8,15},{9,8},{10,9... | collective-permute-start | bytes 1572872 | tf_op jit(solution)/shard_map/ppermute | solution.py:213
  34.1 6.2 %collective-permute-start.4 = (bf16[144,256]{1,0:T(8,128)(2,1)S(1)}, bf16[144,256]{1,0:T(8,128)(2,1)S(1)}, u32[]{:S(2)}, u32[]{:S(2)}) collective-permute-start(bf16[144,256]{1,0:T(8,128)(2,1)S(1)} %copy-done.15), channel_id=1, source_target_pairs={{0,8},{8,16},{16,24},{24,0},{1,9},{9,17},{17,25},{25,1},{2,10},{10... | collective-permute-start | bytes 221192 | tf_op jit(solution)/shard_map/ppermute | solution.py:213
  44.2 19.9 %collective-permute-start.8 = (bf16[1024,256]{1,0:T(8,128)(2,1)S(1)}, bf16[1024,256]{1,0:T(8,128)(2,1)S(1)}, u32[]{:S(2)}, u32[]{:S(2)}) collective-permute-start(bf16[1024,256]{1,0:T(8,128)(2,1)S(1)} %collective-permute-done.3.refs_0_), channel_id=1, source_target_pairs={{0,1},{1,2},{2,3},{3,4},{4,5},{5,6},{6,7},{7,0},{8,9},{9,10},{10,1... | collective-permute-start | bytes 1572872 | tf_op jit(solution)/shard_map/ppermute | solution.py:213
  46.2 8.1 %collective-permute-start.7 = (bf16[144,256]{1,0:T(8,128)(2,1)S(1)}, bf16[144,256]{1,0:T(8,128)(2,1)S(1)}, u32[]{:S(2)}, u32[]{:S(2)}) collective-permute-start(bf16[144,256]{1,0:T(8,128)(2,1)S(1)} %copy-done.14), channel_id=1, source_target_pairs={{0,24},{8,0},{16,8},{24,16},{1,25},{9,1},{17,9},{25,17},{2,26},{10... | collective-permute-start | bytes 221192 | tf_op jit(solution)/shard_map/ppermute | solution.py:213
  48.6 10.9 %collective-permute-start.5 = (bf16[144,256]{1,0:T(8,128)(2,1)S(1)}, bf16[144,256]{1,0:T(8,128)(2,1)S(1)}, u32[]{:S(2)}, u32[]{:S(2)}) collective-permute-start(bf16[144,256]{1,0:T(8,128)(2,1)S(1)} %copy-done.13), channel_id=1, source_target_pairs={{0,16},{8,24},{16,0},{24,8},{1,17},{9,25},{17,1},{25,9},{2,18},{10... | collective-permute-start | bytes 221192 | tf_op jit(solution)/shard_map/ppermute | solution.py:213
  54.3 14.4 %collective-permute-start.10 = (bf16[1024,256]{1,0:T(8,128)(2,1)S(1)}, bf16[1024,256]{1,0:T(8,128)(2,1)S(1)}, u32[]{:S(2)}, u32[]{:S(2)}) collective-permute-start(bf16[1024,256]{1,0:T(8,128)(2,1)S(1)} %collective-permute-done.6.refs_1_), channel_id=1, source_target_pairs={{0,7},{1,0},{2,1},{3,2},{4,3},{5,4},{6,5},{7,6},{8,15},{9,8},{10,9... | collective-permute-start | bytes 1572872 | tf_op jit(solution)/shard_map/ppermute | solution.py:213
  64.2 14.6 %collective-permute-start.9 = (bf16[1024,256]{1,0:T(8,128)(2,1)S(1)}, bf16[1024,256]{1,0:T(8,128)(2,1)S(1)}, u32[]{:S(2)}, u32[]{:S(2)}) collective-permute-start(bf16[1024,256]{1,0:T(8,128)(2,1)S(1)} %collective-permute-done.8.refs_0_), channel_id=1, source_target_pairs={{0,1},{1,2},{2,3},{3,4},{4,5},{5,6},{6,7},{7,0},{8,9},{9,10},{10,1... | collective-permute-start | bytes 1572872 | tf_op jit(solution)/shard_map/ppermute | solution.py:213
  68.7 14.0 %collective-permute-start.12 = (bf16[1024,256]{1,0:T(8,128)(2,1)S(1)}, bf16[1024,256]{1,0:T(8,128)(2,1)S(1)}, u32[]{:S(2)}, u32[]{:S(2)}) collective-permute-start(bf16[1024,256]{1,0:T(8,128)(2,1)S(1)} %collective-permute-done.10.refs_1_), channel_id=1, source_target_pairs={{0,7},{1,0},{2,1},{3,2},{4,3},{5,4},{6,5},{7,6},{8,15},{9,8},{10,9... | collective-permute-start | bytes 1572872 | tf_op jit(solution)/shard_map/ppermute | solution.py:213
  78.8 13.7 %collective-permute-start.11 = (bf16[1024,256]{1,0:T(8,128)(2,1)S(1)}, bf16[1024,256]{1,0:T(8,128)(2,1)S(1)}, u32[]{:S(2)}, u32[]{:S(2)}) collective-permute-start(bf16[1024,256]{1,0:T(8,128)(2,1)S(1)} %collective-permute-done.9.refs_0_), channel_id=1, source_target_pairs={{0,1},{1,2},{2,3},{3,4},{4,5},{5,6},{6,7},{7,0},{8,9},{9,10},{10,1... | collective-permute-start | bytes 1572872 | tf_op jit(solution)/shard_map/ppermute | solution.py:213
  85.1 20.2 %copy-start = (bf16[512,1024]{1,0:T(8,128)(2,1)S(1)}, bf16[512,1024]{1,0:T(8,128)(2,1)}, u32[]{:S(2)}) copy-start(bf16[512,1024]{1,0:T(8,128)(2,1)} %w_ref.1) | copy-start | bytes 3145732
  92.5 12.9 %copy-start.2 = (bf16[256,512]{1,0:T(8,128)(2,1)S(1)}, bf16[256,512]{1,0:T(8,128)(2,1)}, u32[]{:S(2)}) copy-start(bf16[256,512]{1,0:T(8,128)(2,1)} %hg.1) | copy-start | bytes 786436
  92.5 12.9 %copy-start.6 = (bf16[32,1024]{1,0:T(8,128)(2,1)S(1)}, bf16[32,1024]{1,0:T(8,128)(2,1)}, u32[]{:S(2)}) copy-start(bf16[32,1024]{1,0:T(8,128)(2,1)} %cx.1) | copy-start | bytes 196612
  92.5 12.9 %copy-start.8 = (bf16[32,512]{1,0:T(8,128)(2,1)S(1)}, bf16[32,512]{1,0:T(8,128)(2,1)}, u32[]{:S(2)}) copy-start(bf16[32,512]{1,0:T(8,128)(2,1)} %cv.1) | copy-start | bytes 98308
  92.5 12.9 %copy-start.9 = (bf16[32,512]{1,0:T(8,128)(2,1)S(1)}, bf16[32,512]{1,0:T(8,128)(2,1)}, u32[]{:S(2)}) copy-start(bf16[32,512]{1,0:T(8,128)(2,1)} %cg.1) | copy-start | bytes 98308
  94.0 11.3 %copy-start.1 = (bf16[256,1024]{1,0:T(8,128)(2,1)S(1)}, bf16[256,1024]{1,0:T(8,128)(2,1)}, u32[]{:S(2)}) copy-start(bf16[256,1024]{1,0:T(8,128)(2,1)} %hx.1) | copy-start | bytes 1572868
  (5 other events, 24.9 us)

commit v10 on v9

--- a/solution.py
+++ b/solution.py
@@ -236,12 +236,10 @@
     (queries,) = call(unfold_kernel, [(TOTAL, DH)], *folds, place=y)
     total = attend((0,), info, queries, users, (own,), None)
     total = attend((NZ - 1, 1), info, queries, users, (up1, down1), total)
-    up2, held = lax.optimization_barrier((up2, total))
-    down2, total = lax.optimization_barrier((down2, held))
     up3, down3 = turn(up2, "z", 1), turn(down2, "z", -1)
-    total = attend((NZ - 2, 2), info, queries, users, (up2, down2), total)
     up3, total = lax.optimization_barrier((up3, total))
     across = turn(up3, "z", 1)
+    total = attend((NZ - 2, 2), info, queries, users, (up2, down2), total)
     total = attend((NZ - 3, 3), info, queries, users, (up3, down3), total)
     total = attend((4,), info, queries, users, (across,), total, last=True)
     total = lax.all_to_all(total, "y", 0, 0, tiled=True)

time: 108 us -> 109 us (level)
  waiting for transfers between devices: 29.1 us -> 31.2 us
    ppermute x13, waiting for transfers between devices: 29.1 us -> 31.2 us  [turn(): lax.ppermute(array, axis, [(i, (i + step) % count) for i in range(count)])]
where the time goes in v10:
time: 109 us; the launch traced here: 108 us
  starting transfers between devices  48.9 us (45%)
  waiting for transfers between devices  31.2 us (29%)
  Pallas kernels  14.8 us (14%)
  blocking collectives  10.3 us (9%)
  local copies, waits for them, and re-layouts  1.82 us (2%)
    ppermute x13, starting transfers between devices, turn(): lax.ppermute(array, axis, [(i, (i + step) % count) for i in range(count)])  48.9 us
    ppermute x13, waiting for transfers between devices, turn(): lax.ppermute(array, axis, [(i, (i + step) % count) for i in range(count)])  31.2 us
    pallas_call x5, Pallas kernels, attend(): pl.pallas_call(functools.partial(attend_kernel, offsets, first, last), in...  11 us
    all_to_all x1, blocking collectives, on_device(): total = lax.all_to_all(total, 'y', 0, 0, tiled=True)  10.3 us
    pallas_call x4, Pallas kernels, call(): pl.pallas_call(kernel, in_specs=[SMEM] * (place is not None) + [VMEM] * (...  3.76 us
  transfers between devices with their start and end apart: 13, of which 8 were waited for; matrix products, arithmetic and copies ran while one was open for 0% of the time, Pallas kernels for 9%

profile of v10, /device:TPU:56, one launch (start us, length us, event | category | flops | bytes accessed | tf_op | source)
XLA Modules:
  0.0 108.0 jit_solution(7104728099309412526)
XLA Ops:
  0.6 2.1 %shard_map.149 = (bf16[256,256]{1,0:T(8,128)(2,1)}, bf16[256,256]{1,0:T(8,128)(2,1)}, bf16[256,256]{1,0:T(8,128)(2,1)}, bf16[256,256]{1,0:T(8,128)(2,1)}, bf16[1...) custom-call(s32[1]{0:T(128)} %bitcast.1.y_ref, ...), custom_call_target="tpu_custom_call" | custom-call | tf_op jit(solution)/shard_map/pallas_call | solution.py:201
  2.8 4.8 %collective-permute-start = (bf16[256,256]{1,0:T(8,128)(2,1)}, bf16[256,256]{1,0:T(8,128)(2,1)S(1)}, u32[]{:S(2)}, u32[]{:S(2)}) collective-permute-start(bf16[256,256]{1,0:T(8,128)(2,1)} %get-tuple-element.18), channel_id=1, source_target_pairs={{0,8},{8,16},{16,24},{24,0},{1,9},{9,17},{17,25},{25,1},{2,10},{10... | collective-permute-start | bytes 393224 | tf_op jit(solution)/shard_map/ppermute | solution.py:213
  7.6 1.9 %collective-permute-start.1 = (bf16[256,256]{1,0:T(8,128)(2,1)}, bf16[256,256]{1,0:T(8,128)(2,1)S(1)}, u32[]{:S(2)}, u32[]{:S(2)}) collective-permute-start(bf16[256,256]{1,0:T(8,128)(2,1)} %get-tuple-element.19), channel_id=1, source_target_pairs={{0,16},{8,24},{16,0},{24,8},{1,17},{9,25},{17,1},{25,9},{2,18},{10... | collective-permute-start | bytes 393224 | tf_op jit(solution)/shard_map/ppermute | solution.py:213
  9.5 3.1 %collective-permute-start.2 = (bf16[256,256]{1,0:T(8,128)(2,1)}, bf16[256,256]{1,0:T(8,128)(2,1)S(1)}, u32[]{:S(2)}, u32[]{:S(2)}) collective-permute-start(bf16[256,256]{1,0:T(8,128)(2,1)} %get-tuple-element.20), channel_id=1, source_target_pairs={{0,24},{8,0},{16,8},{24,16},{1,25},{9,1},{17,9},{25,17},{2,26},{10... | collective-permute-start | bytes 393224 | tf_op jit(solution)/shard_map/ppermute | solution.py:213
  12.7 7.4 %collective-permute-done.1.refs_2_ = bf16[256,256]{1,0:T(8,128)(2,1)S(1)} collective-permute-done((bf16[256,256]{1,0:T(8,128)(2,1)}, bf16[256,256]{1,0:T(8,128)(2,1)S(1)}, u32[]{:S(2)}, u32[]{:S(2)}) %collective-permute-start.1) | collective-permute-done | bytes 131104 | tf_op jit(solution)/shard_map/ppermute | solution.py:213
  21.1 4.4 %collective-permute-start.3 = (bf16[1024,256]{1,0:T(8,128)(2,1)S(1)}, bf16[1024,256]{1,0:T(8,128)(2,1)S(1)}, u32[]{:S(2)}, u32[]{:S(2)}) collective-permute-start(bf16[1024,256]{1,0:T(8,128)(2,1)S(1)} %shard_map.150.refs_0_), channel_id=1, source_target_pairs={{0,1},{1,2},{2,3},{3,4},{4,5},{5,6},{6,7},{7,0},{8,9},{9,10},{10,1... | collective-permute-start | bytes 1572872 | tf_op jit(solution)/shard_map/ppermute | solution.py:213
  25.5 8.6 %collective-permute-start.6 = (bf16[1024,256]{1,0:T(8,128)(2,1)S(1)}, bf16[1024,256]{1,0:T(8,128)(2,1)S(1)}, u32[]{:S(2)}, u32[]{:S(2)}) collective-permute-start(bf16[1024,256]{1,0:T(8,128)(2,1)S(1)} %shard_map.150.refs_0_), channel_id=1, source_target_pairs={{0,7},{1,0},{2,1},{3,2},{4,3},{5,4},{6,5},{7,6},{8,15},{9,8},{10,9... | collective-permute-start | bytes 1572872 | tf_op jit(solution)/shard_map/ppermute | solution.py:213
  34.1 3.5 %collective-permute-start.4 = (bf16[144,256]{1,0:T(8,128)(2,1)S(1)}, bf16[144,256]{1,0:T(8,128)(2,1)S(1)}, u32[]{:S(2)}, u32[]{:S(2)}) collective-permute-start(bf16[144,256]{1,0:T(8,128)(2,1)S(1)} %copy-done.14), channel_id=1, source_target_pairs={{0,8},{8,16},{16,24},{24,0},{1,9},{9,17},{17,25},{25,1},{2,10},{10... | collective-permute-start | bytes 221192 | tf_op jit(solution)/shard_map/ppermute | solution.py:213
  37.6 2.8 %collective-permute-done.4.refs_1_ = bf16[144,256]{1,0:T(8,128)(2,1)S(1)} collective-permute-done((bf16[144,256]{1,0:T(8,128)(2,1)S(1)}, bf16[144,256]{1,0:T(8,128)(2,1)S(1)}, u32[]{:S(2)}, u32[]{:S(2)}) %collective-permute-start.4) | collective-permute-done | bytes 73760 | tf_op jit(solution)/shard_map/ppermute | solution.py:213
  40.3 3.9 %collective-permute-done.3.refs_0_ = bf16[1024,256]{1,0:T(8,128)(2,1)S(1)} collective-permute-done((bf16[1024,256]{1,0:T(8,128)(2,1)S(1)}, bf16[1024,256]{1,0:T(8,128)(2,1)S(1)}, u32[]{:S(2)}, u32[]{:S(2)}) %collective-permute-start.3) | collective-permute-done | bytes 524320 | tf_op jit(solution)/shard_map/ppermute | solution.py:213
  46.2 2.4 %collective-permute-start.7 = (bf16[144,256]{1,0:T(8,128)(2,1)S(1)}, bf16[144,256]{1,0:T(8,128)(2,1)S(1)}, u32[]{:S(2)}, u32[]{:S(2)}) collective-permute-start(bf16[144,256]{1,0:T(8,128)(2,1)S(1)} %copy-done.13), channel_id=1, source_target_pairs={{0,24},{8,0},{16,8},{24,16},{1,25},{9,1},{17,9},{25,17},{2,26},{10... | collective-permute-start | bytes 221192 | tf_op jit(solution)/shard_map/ppermute | solution.py:213
  48.6 5.7 %collective-permute-done.7.refs_3_ = bf16[144,256]{1,0:T(8,128)(2,1)S(1)} collective-permute-done((bf16[144,256]{1,0:T(8,128)(2,1)S(1)}, bf16[144,256]{1,0:T(8,128)(2,1)S(1)}, u32[]{:S(2)}, u32[]{:S(2)}) %collective-permute-start.7) | collective-permute-done | bytes 73760 | tf_op jit(solution)/shard_map/ppermute | solution.py:213
  54.2 5.1 %collective-permute-start.11 = (bf16[1024,256]{1,0:T(8,128)(2,1)S(1)}, bf16[1024,256]{1,0:T(8,128)(2,1)S(1)}, u32[]{:S(2)}, u32[]{:S(2)}) collective-permute-start(bf16[1024,256]{1,0:T(8,128)(2,1)S(1)} %collective-permute-done.6.refs_1_), channel_id=1, source_target_pairs={{0,7},{1,0},{2,1},{3,2},{4,3},{5,4},{6,5},{7,6},{8,15},{9,8},{10,9... | collective-permute-start | bytes 1572872 | tf_op jit(solution)/shard_map/ppermute | solution.py:213
  62.6 4.2 %collective-permute-start.5 = (bf16[144,256]{1,0:T(8,128)(2,1)}, bf16[144,256]{1,0:T(8,128)(2,1)S(1)}, u32[]{:S(2)}, u32[]{:S(2)}) collective-permute-start(bf16[144,256]{1,0:T(8,128)(2,1)} %get-tuple-element.23), channel_id=1, source_target_pairs={{0,16},{8,24},{16,0},{24,8},{1,17},{9,25},{17,1},{25,9},{2,18},{10... | collective-permute-start | bytes 221192 | tf_op jit(solution)/shard_map/ppermute | solution.py:213
  67.7 2.9 %collective-permute-done.5.refs_2_ = bf16[144,256]{1,0:T(8,128)(2,1)S(1)} collective-permute-done((bf16[144,256]{1,0:T(8,128)(2,1)}, bf16[144,256]{1,0:T(8,128)(2,1)S(1)}, u32[]{:S(2)}, u32[]{:S(2)}) %collective-permute-start.5) | collective-permute-done | bytes 73760 | tf_op jit(solution)/shard_map/ppermute | solution.py:213
  70.7 2.2 %attend.5.refs_2_ = f32[1152,128]{1,0:T(8,128)S(1)} custom-call(s32[5]{0:T(128)S(1)} %pad_add_fusion.info_ref, bf16[1152,128]{1,0:T(8,128)(2,1)S(1)} %shard_map.151.qs, s32[128,1]{1,0:T(8,128)S(1)} %reshape.22.user_ref, bf16[1024,256]{1,0:T(8,128)(2,1)S(1)} %shard_map.150.refs_0_), custom_call_target="tpu_custom_call" | custom-call | flops 603979776 | bytes 1048576 | tf_op jit(solution)/shard_map/attend/pallas_call | solution.py:164
  72.9 5.1 %collective-permute-start.12 = (bf16[1024,256]{1,0:T(8,128)(2,1)S(1)}, bf16[1024,256]{1,0:T(8,128)(2,1)S(1)}, u32[]{:S(2)}, u32[]{:S(2)}) collective-permute-start(bf16[1024,256]{1,0:T(8,128)(2,1)S(1)} %collective-permute-done.11.refs_1_), channel_id=1, source_target_pairs={{0,7},{1,0},{2,1},{3,2},{4,3},{5,4},{6,5},{7,6},{8,15},{9,8},{10,9... | collective-permute-start | bytes 1572872 | tf_op jit(solution)/shard_map/ppermute | solution.py:213
  78.0 2.4 %attend.6.refs_2_ = f32[1152,128]{1,0:T(8,128)S(1)} custom-call(s32[5]{0:T(128)S(1)} %pad_add_fusion.info_ref, bf16[1152,128]{1,0:T(8,128)(2,1)S(1)} %shard_map.151.qs, s32[128,1]{1,0:T(8,128)S(1)} %reshape.22.user_ref, bf16[1024,256]{1,0:T(8,128)(2,1)S(1)} %collective-permute-done.3.refs_0_, bf16[1024,256]{1,0:T(8,128)(2,1)S(1)} %collective-permute-done.6.refs_1_, ...), custom_call_target="tpu_custom_call" | custom-call | flops 1207959552 | bytes 1048576 | tf_op jit(solution)/shard_map/attend/pallas_call | solution.py:164
  80.5 1.9 %collective-permute-start.10 = (bf16[1024,256]{1,0:T(8,128)(2,1)S(1)}, bf16[1024,256]{1,0:T(8,128)(2,1)S(1)}, u32[]{:S(2)}, u32[]{:S(2)}) collective-permute-start(bf16[1024,256]{1,0:T(8,128)(2,1)S(1)} %collective-permute-done.9.refs_0_), channel_id=1, source_target_pairs={{0,1},{1,2},{2,3},{3,4},{4,5},{5,6},{6,7},{7,0},{8,9},{9,10},{10,1... | collective-permute-start | bytes 1572872 | tf_op jit(solution)/shard_map/ppermute | solution.py:213
  82.4 2.4 %attend.7.refs_2_ = f32[1152,128]{1,0:T(8,128)S(1)} custom-call(s32[5]{0:T(128)S(1)} %pad_add_fusion.info_ref, bf16[1152,128]{1,0:T(8,128)(2,1)S(1)} %shard_map.151.qs, s32[128,1]{1,0:T(8,128)S(1)} %reshape.22.user_ref, bf16[1024,256]{1,0:T(8,128)(2,1)S(1)} %collective-permute-done.8.refs_0_, bf16[1024,256]{1,0:T(8,128)(2,1)S(1)} %collective-permute-done.11.refs_1_, ...), custom_call_target="tpu_custom_call" | custom-call | flops 1207959552 | bytes 1048576 | tf_op jit(solution)/shard_map/attend/pallas_call | solution.py:164
  84.8 1.9 %collective-permute-done.12.refs_1_ = bf16[1024,256]{1,0:T(8,128)(2,1)S(1)} collective-permute-done((bf16[1024,256]{1,0:T(8,128)(2,1)S(1)}, bf16[1024,256]{1,0:T(8,128)(2,1)S(1)}, u32[]{:S(2)}, u32[]{:S(2)}) %collective-permute-start.12) | collective-permute-done | bytes 524320 | tf_op jit(solution)/shard_map/ppermute | solution.py:213
  86.8 2.4 %attend.8.refs_1_ = f32[1152,128]{1,0:T(8,128)S(1)} custom-call(s32[5]{0:T(128)S(1)} %pad_add_fusion.info_ref, bf16[1152,128]{1,0:T(8,128)(2,1)S(1)} %shard_map.151.qs, s32[128,1]{1,0:T(8,128)S(1)} %reshape.22.user_ref, bf16[1024,256]{1,0:T(8,128)(2,1)S(1)} %collective-permute-done.9.refs_0_, bf16[1024,256]{1,0:T(8,128)(2,1)S(1)} %collective-permute-done.12.refs_1_, ...), custom_call_target="tpu_custom_call" | custom-call | flops 1207959552 | bytes 1048576 | tf_op jit(solution)/shard_map/attend/pallas_call | solution.py:164
  89.2 5.3 %collective-permute-done.10.refs_0_ = bf16[1024,256]{1,0:T(8,128)(2,1)S(1)} collective-permute-done((bf16[1024,256]{1,0:T(8,128)(2,1)S(1)}, bf16[1024,256]{1,0:T(8,128)(2,1)S(1)}, u32[]{:S(2)}, u32[]{:S(2)}) %collective-permute-start.10) | collective-permute-done | bytes 524320 | tf_op jit(solution)/shard_map/ppermute | solution.py:213
  96.2 10.3 %all_to_all.11 = bf16[4,144,256]{2,1,0:T(8,128)(2,1)S(1)} all-to-all(bf16[4,144,256]{2,1,0:T(8,128)(2,1)S(1)} %bitcast.5), channel_id=1, replica_groups=mesh['batch'=16,'y'=4,'z'=8] {'y'}, dimensions={0} | all-to-all | bytes 589824 | tf_op jit(solution)/shard_map/all_to_all | solution.py:245
  (46 shorter events, 10.2 us)
Async XLA Ops:
  2.8 9.9 %collective-permute-start = (bf16[256,256]{1,0:T(8,128)(2,1)}, bf16[256,256]{1,0:T(8,128)(2,1)S(1)}, u32[]{:S(2)}, u32[]{:S(2)}) collective-permute-start(bf16[256,256]{1,0:T(8,128)(2,1)} %get-tuple-element.18), channel_id=1, source_target_pairs={{0,8},{8,16},{16,24},{24,0},{1,9},{9,17},{17,25},{25,1},{2,10},{10... | collective-permute-start | bytes 393224 | tf_op jit(solution)/shard_map/ppermute | solution.py:213
  7.6 12.5 %collective-permute-start.1 = (bf16[256,256]{1,0:T(8,128)(2,1)}, bf16[256,256]{1,0:T(8,128)(2,1)S(1)}, u32[]{:S(2)}, u32[]{:S(2)}) collective-permute-start(bf16[256,256]{1,0:T(8,128)(2,1)} %get-tuple-element.19), channel_id=1, source_target_pairs={{0,16},{8,24},{16,0},{24,8},{1,17},{9,25},{17,1},{25,9},{2,18},{10... | collective-permute-start | bytes 393224 | tf_op jit(solution)/shard_map/ppermute | solution.py:213
  9.5 10.6 %collective-permute-start.2 = (bf16[256,256]{1,0:T(8,128)(2,1)}, bf16[256,256]{1,0:T(8,128)(2,1)S(1)}, u32[]{:S(2)}, u32[]{:S(2)}) collective-permute-start(bf16[256,256]{1,0:T(8,128)(2,1)} %get-tuple-element.20), channel_id=1, source_target_pairs={{0,24},{8,0},{16,8},{24,16},{1,25},{9,1},{17,9},{25,17},{2,26},{10... | collective-permute-start | bytes 393224 | tf_op jit(solution)/shard_map/ppermute | solution.py:213
  21.0 13.1 %copy-start.14 = (bf16[144,256]{1,0:T(8,128)(2,1)S(1)}, bf16[144,256]{1,0:T(8,128)(2,1)}, u32[]{:S(2)}) copy-start(bf16[144,256]{1,0:T(8,128)(2,1)} %get-tuple-element.21) | copy-start | bytes 221188
  21.0 25.2 %copy-start.13 = (bf16[144,256]{1,0:T(8,128)(2,1)S(1)}, bf16[144,256]{1,0:T(8,128)(2,1)}, u32[]{:S(2)}) copy-start(bf16[144,256]{1,0:T(8,128)(2,1)} %get-tuple-element.24) | copy-start | bytes 221188
  21.0 45.8 %copy-start.10 = (s32[1024]{0:T(1024)S(1)}, s32[1024]{0:T(1024)}, u32[]{:S(2)}) copy-start(s32[1024]{0:T(1024)} %param.24) | copy-start | bytes 12292
  21.1 49.6 %copy-start.5 = (bf16[144,256]{1,0:T(8,128)(2,1)S(1)}, bf16[144,256]{1,0:T(8,128)(2,1)}, u32[]{:S(2)}) copy-start(bf16[144,256]{1,0:T(8,128)(2,1)} %get-tuple-element.16.refs_0_) | copy-start | bytes 221188
  21.1 23.2 %collective-permute-start.3 = (bf16[1024,256]{1,0:T(8,128)(2,1)S(1)}, bf16[1024,256]{1,0:T(8,128)(2,1)S(1)}, u32[]{:S(2)}, u32[]{:S(2)}) collective-permute-start(bf16[1024,256]{1,0:T(8,128)(2,1)S(1)} %shard_map.150.refs_0_), channel_id=1, source_target_pairs={{0,1},{1,2},{2,3},{3,4},{4,5},{5,6},{6,7},{7,0},{8,9},{9,10},{10,1... | collective-permute-start | bytes 1572872 | tf_op jit(solution)/shard_map/ppermute | solution.py:213
  25.5 28.7 %collective-permute-start.6 = (bf16[1024,256]{1,0:T(8,128)(2,1)S(1)}, bf16[1024,256]{1,0:T(8,128)(2,1)S(1)}, u32[]{:S(2)}, u32[]{:S(2)}) collective-permute-start(bf16[1024,256]{1,0:T(8,128)(2,1)S(1)} %shard_map.150.refs_0_), channel_id=1, source_target_pairs={{0,7},{1,0},{2,1},{3,2},{4,3},{5,4},{6,5},{7,6},{8,15},{9,8},{10,9... | collective-permute-start | bytes 1572872 | tf_op jit(solution)/shard_map/ppermute | solution.py:213
  34.1 6.2 %collective-permute-start.4 = (bf16[144,256]{1,0:T(8,128)(2,1)S(1)}, bf16[144,256]{1,0:T(8,128)(2,1)S(1)}, u32[]{:S(2)}, u32[]{:S(2)}) collective-permute-start(bf16[144,256]{1,0:T(8,128)(2,1)S(1)} %copy-done.14), channel_id=1, source_target_pairs={{0,8},{8,16},{16,24},{24,0},{1,9},{9,17},{17,25},{25,1},{2,10},{10... | collective-permute-start | bytes 221192 | tf_op jit(solution)/shard_map/ppermute | solution.py:213
  44.2 16.4 %collective-permute-start.8 = (bf16[1024,256]{1,0:T(8,128)(2,1)S(1)}, bf16[1024,256]{1,0:T(8,128)(2,1)S(1)}, u32[]{:S(2)}, u32[]{:S(2)}) collective-permute-start(bf16[1024,256]{1,0:T(8,128)(2,1)S(1)} %collective-permute-done.3.refs_0_), channel_id=1, source_target_pairs={{0,1},{1,2},{2,3},{3,4},{4,5},{5,6},{6,7},{7,0},{8,9},{9,10},{10,1... | collective-permute-start | bytes 1572872 | tf_op jit(solution)/shard_map/ppermute | solution.py:213
  46.2 8.0 %collective-permute-start.7 = (bf16[144,256]{1,0:T(8,128)(2,1)S(1)}, bf16[144,256]{1,0:T(8,128)(2,1)S(1)}, u32[]{:S(2)}, u32[]{:S(2)}) collective-permute-start(bf16[144,256]{1,0:T(8,128)(2,1)S(1)} %copy-done.13), channel_id=1, source_target_pairs={{0,24},{8,0},{16,8},{24,16},{1,25},{9,1},{17,9},{25,17},{2,26},{10... | collective-permute-start | bytes 221192 | tf_op jit(solution)/shard_map/ppermute | solution.py:213
  54.2 18.6 %collective-permute-start.11 = (bf16[1024,256]{1,0:T(8,128)(2,1)S(1)}, bf16[1024,256]{1,0:T(8,128)(2,1)S(1)}, u32[]{:S(2)}, u32[]{:S(2)}) collective-permute-start(bf16[1024,256]{1,0:T(8,128)(2,1)S(1)} %collective-permute-done.6.refs_1_), channel_id=1, source_target_pairs={{0,7},{1,0},{2,1},{3,2},{4,3},{5,4},{6,5},{7,6},{8,15},{9,8},{10,9... | collective-permute-start | bytes 1572872 | tf_op jit(solution)/shard_map/ppermute | solution.py:213
  60.7 19.8 %collective-permute-start.9 = (bf16[1024,256]{1,0:T(8,128)(2,1)S(1)}, bf16[1024,256]{1,0:T(8,128)(2,1)S(1)}, u32[]{:S(2)}, u32[]{:S(2)}) collective-permute-start(bf16[1024,256]{1,0:T(8,128)(2,1)S(1)} %collective-permute-done.8.refs_0_), channel_id=1, source_target_pairs={{0,1},{1,2},{2,3},{3,4},{4,5},{5,6},{6,7},{7,0},{8,9},{9,10},{10,1... | collective-permute-start | bytes 1572872 | tf_op jit(solution)/shard_map/ppermute | solution.py:213
  62.6 8.1 %collective-permute-start.5 = (bf16[144,256]{1,0:T(8,128)(2,1)}, bf16[144,256]{1,0:T(8,128)(2,1)S(1)}, u32[]{:S(2)}, u32[]{:S(2)}) collective-permute-start(bf16[144,256]{1,0:T(8,128)(2,1)} %get-tuple-element.23), channel_id=1, source_target_pairs={{0,16},{8,24},{16,0},{24,8},{1,17},{9,25},{17,1},{25,9},{2,18},{10... | collective-permute-start | bytes 221192 | tf_op jit(solution)/shard_map/ppermute | solution.py:213
  72.9 13.9 %collective-permute-start.12 = (bf16[1024,256]{1,0:T(8,128)(2,1)S(1)}, bf16[1024,256]{1,0:T(8,128)(2,1)S(1)}, u32[]{:S(2)}, u32[]{:S(2)}) collective-permute-start(bf16[1024,256]{1,0:T(8,128)(2,1)S(1)} %collective-permute-done.11.refs_1_), channel_id=1, source_target_pairs={{0,7},{1,0},{2,1},{3,2},{4,3},{5,4},{6,5},{7,6},{8,15},{9,8},{10,9... | collective-permute-start | bytes 1572872 | tf_op jit(solution)/shard_map/ppermute | solution.py:213
  80.5 14.1 %collective-permute-start.10 = (bf16[1024,256]{1,0:T(8,128)(2,1)S(1)}, bf16[1024,256]{1,0:T(8,128)(2,1)S(1)}, u32[]{:S(2)}, u32[]{:S(2)}) collective-permute-start(bf16[1024,256]{1,0:T(8,128)(2,1)S(1)} %collective-permute-done.9.refs_0_), channel_id=1, source_target_pairs={{0,1},{1,2},{2,3},{3,4},{4,5},{5,6},{6,7},{7,0},{8,9},{9,10},{10,1... | collective-permute-start | bytes 1572872 | tf_op jit(solution)/shard_map/ppermute | solution.py:213
  89.2 17.2 %copy-start = (bf16[512,1024]{1,0:T(8,128)(2,1)S(1)}, bf16[512,1024]{1,0:T(8,128)(2,1)}, u32[]{:S(2)}) copy-start(bf16[512,1024]{1,0:T(8,128)(2,1)} %w_ref.1) | copy-start | bytes 3145732
  94.6 11.9 %copy-start.2 = (bf16[256,512]{1,0:T(8,128)(2,1)S(1)}, bf16[256,512]{1,0:T(8,128)(2,1)}, u32[]{:S(2)}) copy-start(bf16[256,512]{1,0:T(8,128)(2,1)} %hg.1) | copy-start | bytes 786436
  94.6 11.9 %copy-start.6 = (bf16[32,1024]{1,0:T(8,128)(2,1)S(1)}, bf16[32,1024]{1,0:T(8,128)(2,1)}, u32[]{:S(2)}) copy-start(bf16[32,1024]{1,0:T(8,128)(2,1)} %cx.1) | copy-start | bytes 196612
  94.6 11.9 %copy-start.8 = (bf16[32,512]{1,0:T(8,128)(2,1)S(1)}, bf16[32,512]{1,0:T(8,128)(2,1)}, u32[]{:S(2)}) copy-start(bf16[32,512]{1,0:T(8,128)(2,1)} %cv.1) | copy-start | bytes 98308
  94.6 11.9 %copy-start.9 = (bf16[32,512]{1,0:T(8,128)(2,1)S(1)}, bf16[32,512]{1,0:T(8,128)(2,1)}, u32[]{:S(2)}) copy-start(bf16[32,512]{1,0:T(8,128)(2,1)} %cg.1) | copy-start | bytes 98308
  96.1 10.4 %copy-start.1 = (bf16[256,1024]{1,0:T(8,128)(2,1)S(1)}, bf16[256,1024]{1,0:T(8,128)(2,1)}, u32[]{:S(2)}) copy-start(bf16[256,1024]{1,0:T(8,128)(2,1)} %hx.1) | copy-start | bytes 1572868
  96.1 10.4 %copy-start.3 = (bf16[32,512]{1,0:T(8,128)(2,1)S(1)}, bf16[32,512]{1,0:T(8,128)(2,1)}, u32[]{:S(2)}) copy-start(bf16[32,512]{1,0:T(8,128)(2,1)} %cq.1) | copy-start | bytes 98308
  (4 other events, 12.6 us)

commit v11 on v10

--- a/solution.py
+++ b/solution.py
@@ -231,13 +231,13 @@
     up1, down1 = turn(own, "z", 1), turn(own, "z", -1)
     folds = [parts[HEADS]] + [turn(parts[HEADS + i], "y", i) for i in (1, 2, 3)]
     up1, folds[1] = lax.optimization_barrier((up1, folds[1]))
-    down1, folds[3] = lax.optimization_barrier((down1, folds[3]))
+    down1, folds[2], folds[3] = lax.optimization_barrier((down1, folds[2], folds[3]))
     up2, down2 = turn(up1, "z", 1), turn(down1, "z", -1)
     (queries,) = call(unfold_kernel, [(TOTAL, DH)], *folds, place=y)
     total = attend((0,), info, queries, users, (own,), None)
     total = attend((NZ - 1, 1), info, queries, users, (up1, down1), total)
+    down2, total = lax.optimization_barrier((down2, total))
     up3, down3 = turn(up2, "z", 1), turn(down2, "z", -1)
-    up3, total = lax.optimization_barrier((up3, total))
     across = turn(up3, "z", 1)
     total = attend((NZ - 2, 2), info, queries, users, (up2, down2), total)
     total = attend((NZ - 3, 3), info, queries, users, (up3, down3), total)

time: 109 us -> 106 us (0.972)
  waiting for transfers between devices: 31.2 us -> 28.4 us
    ppermute x13, waiting for transfers between devices: 31.2 us -> 28.4 us  [turn(): lax.ppermute(array, axis, [(i, (i + step) % count) for i in range(count)])]
where the time goes in v11:
time: 106 us; the launch traced here: 105 us
  starting transfers between devices  48.9 us (46%)
  waiting for transfers between devices  28.4 us (27%)
  Pallas kernels  14.8 us (14%)
  blocking collectives  10.3 us (10%)
  local copies, waits for them, and re-layouts  1.83 us (2%)
    ppermute x13, starting transfers between devices, turn(): lax.ppermute(array, axis, [(i, (i + step) % count) for i in range(count)])  48.9 us
    ppermute x13, waiting for transfers between devices, turn(): lax.ppermute(array, axis, [(i, (i + step) % count) for i in range(count)])  28.4 us
    pallas_call x5, Pallas kernels, attend(): pl.pallas_call(functools.partial(attend_kernel, offsets, first, last), in...  11 us
    all_to_all x1, blocking collectives, on_device(): total = lax.all_to_all(total, 'y', 0, 0, tiled=True)  10.3 us
    pallas_call x4, Pallas kernels, call(): pl.pallas_call(kernel, in_specs=[SMEM] * (place is not None) + [VMEM] * (...  3.75 us
  transfers between devices with their start and end apart: 13, of which 8 were waited for; matrix products, arithmetic and copies ran while one was open for 0% of the time, Pallas kernels for 9%

profile of v11, /device:TPU:56, one launch (start us, length us, event | category | flops | bytes accessed | tf_op | source)
XLA Modules:
  0.0 105.3 jit_solution(7766557661483517577)
XLA Ops:
  0.6 2.1 %shard_map.149 = (bf16[256,256]{1,0:T(8,128)(2,1)}, bf16[256,256]{1,0:T(8,128)(2,1)}, bf16[256,256]{1,0:T(8,128)(2,1)}, bf16[256,256]{1,0:T(8,128)(2,1)}, bf16[1...) custom-call(s32[1]{0:T(128)} %bitcast.1.y_ref, ...), custom_call_target="tpu_custom_call" | custom-call | tf_op jit(solution)/shard_map/pallas_call | solution.py:201
  2.8 4.8 %collective-permute-start = (bf16[256,256]{1,0:T(8,128)(2,1)}, bf16[256,256]{1,0:T(8,128)(2,1)S(1)}, u32[]{:S(2)}, u32[]{:S(2)}) collective-permute-start(bf16[256,256]{1,0:T(8,128)(2,1)} %get-tuple-element.19), channel_id=1, source_target_pairs={{0,8},{8,16},{16,24},{24,0},{1,9},{9,17},{17,25},{25,1},{2,10},{10... | collective-permute-start | bytes 393224 | tf_op jit(solution)/shard_map/ppermute | solution.py:213
  7.6 1.9 %collective-permute-start.1 = (bf16[256,256]{1,0:T(8,128)(2,1)}, bf16[256,256]{1,0:T(8,128)(2,1)S(1)}, u32[]{:S(2)}, u32[]{:S(2)}) collective-permute-start(bf16[256,256]{1,0:T(8,128)(2,1)} %get-tuple-element.20), channel_id=1, source_target_pairs={{0,16},{8,24},{16,0},{24,8},{1,17},{9,25},{17,1},{25,9},{2,18},{10... | collective-permute-start | bytes 393224 | tf_op jit(solution)/shard_map/ppermute | solution.py:213
  9.5 3.1 %collective-permute-start.2 = (bf16[256,256]{1,0:T(8,128)(2,1)}, bf16[256,256]{1,0:T(8,128)(2,1)S(1)}, u32[]{:S(2)}, u32[]{:S(2)}) collective-permute-start(bf16[256,256]{1,0:T(8,128)(2,1)} %get-tuple-element.21), channel_id=1, source_target_pairs={{0,24},{8,0},{16,8},{24,16},{1,25},{9,1},{17,9},{25,17},{2,26},{10... | collective-permute-start | bytes 393224 | tf_op jit(solution)/shard_map/ppermute | solution.py:213
  12.7 7.4 %collective-permute-done.1.refs_2_ = bf16[256,256]{1,0:T(8,128)(2,1)S(1)} collective-permute-done((bf16[256,256]{1,0:T(8,128)(2,1)}, bf16[256,256]{1,0:T(8,128)(2,1)S(1)}, u32[]{:S(2)}, u32[]{:S(2)}) %collective-permute-start.1) | collective-permute-done | bytes 131104 | tf_op jit(solution)/shard_map/ppermute | solution.py:213
  21.1 4.4 %collective-permute-start.3 = (bf16[1024,256]{1,0:T(8,128)(2,1)S(1)}, bf16[1024,256]{1,0:T(8,128)(2,1)S(1)}, u32[]{:S(2)}, u32[]{:S(2)}) collective-permute-start(bf16[1024,256]{1,0:T(8,128)(2,1)S(1)} %shard_map.150.refs_0_), channel_id=1, source_target_pairs={{0,1},{1,2},{2,3},{3,4},{4,5},{5,6},{6,7},{7,0},{8,9},{9,10},{10,1... | collective-permute-start | bytes 1572872 | tf_op jit(solution)/shard_map/ppermute | solution.py:213
  25.5 8.6 %collective-permute-start.5 = (bf16[1024,256]{1,0:T(8,128)(2,1)S(1)}, bf16[1024,256]{1,0:T(8,128)(2,1)S(1)}, u32[]{:S(2)}, u32[]{:S(2)}) collective-permute-start(bf16[1024,256]{1,0:T(8,128)(2,1)S(1)} %shard_map.150.refs_0_), channel_id=1, source_target_pairs={{0,7},{1,0},{2,1},{3,2},{4,3},{5,4},{6,5},{7,6},{8,15},{9,8},{10,9... | collective-permute-start | bytes 1572872 | tf_op jit(solution)/shard_map/ppermute | solution.py:213
  34.1 3.5 %collective-permute-start.4 = (bf16[144,256]{1,0:T(8,128)(2,1)S(1)}, bf16[144,256]{1,0:T(8,128)(2,1)S(1)}, u32[]{:S(2)}, u32[]{:S(2)}) collective-permute-start(bf16[144,256]{1,0:T(8,128)(2,1)S(1)} %copy-done.15), channel_id=1, source_target_pairs={{0,8},{8,16},{16,24},{24,0},{1,9},{9,17},{17,25},{25,1},{2,10},{10... | collective-permute-start | bytes 221192 | tf_op jit(solution)/shard_map/ppermute | solution.py:213
  37.6 2.8 %collective-permute-done.4.refs_1_ = bf16[144,256]{1,0:T(8,128)(2,1)S(1)} collective-permute-done((bf16[144,256]{1,0:T(8,128)(2,1)S(1)}, bf16[144,256]{1,0:T(8,128)(2,1)S(1)}, u32[]{:S(2)}, u32[]{:S(2)}) %collective-permute-start.4) | collective-permute-done | bytes 73760 | tf_op jit(solution)/shard_map/ppermute | solution.py:213
  40.3 3.9 %collective-permute-done.3.refs_0_ = bf16[1024,256]{1,0:T(8,128)(2,1)S(1)} collective-permute-done((bf16[1024,256]{1,0:T(8,128)(2,1)S(1)}, bf16[1024,256]{1,0:T(8,128)(2,1)S(1)}, u32[]{:S(2)}, u32[]{:S(2)}) %collective-permute-start.3) | collective-permute-done | bytes 524320 | tf_op jit(solution)/shard_map/ppermute | solution.py:213
  46.2 4.2 %collective-permute-start.6 = (bf16[144,256]{1,0:T(8,128)(2,1)S(1)}, bf16[144,256]{1,0:T(8,128)(2,1)S(1)}, u32[]{:S(2)}, u32[]{:S(2)}) collective-permute-start(bf16[144,256]{1,0:T(8,128)(2,1)S(1)} %copy-done.14), channel_id=1, source_target_pairs={{0,16},{8,24},{16,0},{24,8},{1,17},{9,25},{17,1},{25,9},{2,18},{10... | collective-permute-start | bytes 221192 | tf_op jit(solution)/shard_map/ppermute | solution.py:213
  50.4 1.9 %collective-permute-start.7 = (bf16[144,256]{1,0:T(8,128)(2,1)S(1)}, bf16[144,256]{1,0:T(8,128)(2,1)S(1)}, u32[]{:S(2)}, u32[]{:S(2)}) collective-permute-start(bf16[144,256]{1,0:T(8,128)(2,1)S(1)} %copy-done.13), channel_id=1, source_target_pairs={{0,24},{8,0},{16,8},{24,16},{1,25},{9,1},{17,9},{25,17},{2,26},{10... | collective-permute-start | bytes 221192 | tf_op jit(solution)/shard_map/ppermute | solution.py:213
  54.1 4.3 %collective-permute-done.7.refs_3_ = bf16[144,256]{1,0:T(8,128)(2,1)S(1)} collective-permute-done((bf16[144,256]{1,0:T(8,128)(2,1)S(1)}, bf16[144,256]{1,0:T(8,128)(2,1)S(1)}, u32[]{:S(2)}, u32[]{:S(2)}) %collective-permute-start.7) | collective-permute-done | bytes 73760 | tf_op jit(solution)/shard_map/ppermute | solution.py:213
  58.4 5.1 %collective-permute-start.11 = (bf16[1024,256]{1,0:T(8,128)(2,1)S(1)}, bf16[1024,256]{1,0:T(8,128)(2,1)S(1)}, u32[]{:S(2)}, u32[]{:S(2)}) collective-permute-start(bf16[1024,256]{1,0:T(8,128)(2,1)S(1)} %collective-permute-done.5.refs_1_), channel_id=1, source_target_pairs={{0,7},{1,0},{2,1},{3,2},{4,3},{5,4},{6,5},{7,6},{8,15},{9,8},{10,9... | collective-permute-start | bytes 1572872 | tf_op jit(solution)/shard_map/ppermute | solution.py:213
  63.6 1.9 %collective-permute-start.9 = (bf16[1024,256]{1,0:T(8,128)(2,1)S(1)}, bf16[1024,256]{1,0:T(8,128)(2,1)S(1)}, u32[]{:S(2)}, u32[]{:S(2)}) collective-permute-start(bf16[1024,256]{1,0:T(8,128)(2,1)S(1)} %collective-permute-done.8.refs_0_), channel_id=1, source_target_pairs={{0,1},{1,2},{2,3},{3,4},{4,5},{5,6},{6,7},{7,0},{8,9},{9,10},{10,1... | collective-permute-start | bytes 1572872 | tf_op jit(solution)/shard_map/ppermute | solution.py:213
  66.5 2.2 %attend.5.refs_2_ = f32[1152,128]{1,0:T(8,128)S(1)} custom-call(s32[5]{0:T(128)S(1)} %pad_add_fusion.info_ref, bf16[1152,128]{1,0:T(8,128)(2,1)S(1)} %shard_map.151.qs, s32[128,1]{1,0:T(8,128)S(1)} %reshape.22.user_ref, bf16[1024,256]{1,0:T(8,128)(2,1)S(1)} %shard_map.150.refs_0_), custom_call_target="tpu_custom_call" | custom-call | flops 603979776 | bytes 1048576 | tf_op jit(solution)/shard_map/attend/pallas_call | solution.py:164
  68.7 2.4 %attend.6.refs_2_ = f32[1152,128]{1,0:T(8,128)S(1)} custom-call(s32[5]{0:T(128)S(1)} %pad_add_fusion.info_ref, bf16[1152,128]{1,0:T(8,128)(2,1)S(1)} %shard_map.151.qs, s32[128,1]{1,0:T(8,128)S(1)} %reshape.22.user_ref, bf16[1024,256]{1,0:T(8,128)(2,1)S(1)} %collective-permute-done.3.refs_0_, bf16[1024,256]{1,0:T(8,128)(2,1)S(1)} %collective-permute-done.5.refs_1_, ...), custom_call_target="tpu_custom_call" | custom-call | flops 1207959552 | bytes 1048576 | tf_op jit(solution)/shard_map/attend/pallas_call | solution.py:164
  72.7 5.6 %collective-permute-start.12 = (bf16[1024,256]{1,0:T(8,128)(2,1)S(1)}, bf16[1024,256]{1,0:T(8,128)(2,1)S(1)}, u32[]{:S(2)}, u32[]{:S(2)}) collective-permute-start(bf16[1024,256]{1,0:T(8,128)(2,1)S(1)} %collective-permute-done.11.refs_1_), channel_id=1, source_target_pairs={{0,7},{1,0},{2,1},{3,2},{4,3},{5,4},{6,5},{7,6},{8,15},{9,8},{10,9... | collective-permute-start | bytes 1572872 | tf_op jit(solution)/shard_map/ppermute | solution.py:213
  78.3 1.9 %collective-permute-start.10 = (bf16[1024,256]{1,0:T(8,128)(2,1)S(1)}, bf16[1024,256]{1,0:T(8,128)(2,1)S(1)}, u32[]{:S(2)}, u32[]{:S(2)}) collective-permute-start(bf16[1024,256]{1,0:T(8,128)(2,1)S(1)} %collective-permute-done.9.refs_0_), channel_id=1, source_target_pairs={{0,1},{1,2},{2,3},{3,4},{4,5},{5,6},{6,7},{7,0},{8,9},{9,10},{10,1... | collective-permute-start | bytes 1572872 | tf_op jit(solution)/shard_map/ppermute | solution.py:213
  80.2 2.4 %attend.7.refs_2_ = f32[1152,128]{1,0:T(8,128)S(1)} custom-call(s32[5]{0:T(128)S(1)} %pad_add_fusion.info_ref, bf16[1152,128]{1,0:T(8,128)(2,1)S(1)} %shard_map.151.qs, s32[128,1]{1,0:T(8,128)S(1)} %reshape.22.user_ref, bf16[1024,256]{1,0:T(8,128)(2,1)S(1)} %collective-permute-done.8.refs_0_, bf16[1024,256]{1,0:T(8,128)(2,1)S(1)} %collective-permute-done.11.refs_1_, ...), custom_call_target="tpu_custom_call" | custom-call | flops 1207959552 | bytes 1048576 | tf_op jit(solution)/shard_map/attend/pallas_call | solution.py:164
  82.6 3.8 %collective-permute-done.12.refs_1_ = bf16[1024,256]{1,0:T(8,128)(2,1)S(1)} collective-permute-done((bf16[1024,256]{1,0:T(8,128)(2,1)S(1)}, bf16[1024,256]{1,0:T(8,128)(2,1)S(1)}, u32[]{:S(2)}, u32[]{:S(2)}) %collective-permute-start.12) | collective-permute-done | bytes 524320 | tf_op jit(solution)/shard_map/ppermute | solution.py:213
  86.4 2.4 %attend.8.refs_1_ = f32[1152,128]{1,0:T(8,128)S(1)} custom-call(s32[5]{0:T(128)S(1)} %pad_add_fusion.info_ref, bf16[1152,128]{1,0:T(8,128)(2,1)S(1)} %shard_map.151.qs, s32[128,1]{1,0:T(8,128)S(1)} %reshape.22.user_ref, bf16[1024,256]{1,0:T(8,128)(2,1)S(1)} %collective-permute-done.9.refs_0_, bf16[1024,256]{1,0:T(8,128)(2,1)S(1)} %collective-permute-done.12.refs_1_, ...), custom_call_target="tpu_custom_call" | custom-call | flops 1207959552 | bytes 1048576 | tf_op jit(solution)/shard_map/attend/pallas_call | solution.py:164
  88.9 2.9 %collective-permute-done.10.refs_0_ = bf16[1024,256]{1,0:T(8,128)(2,1)S(1)} collective-permute-done((bf16[1024,256]{1,0:T(8,128)(2,1)S(1)}, bf16[1024,256]{1,0:T(8,128)(2,1)S(1)}, u32[]{:S(2)}, u32[]{:S(2)}) %collective-permute-start.10) | collective-permute-done | bytes 524320 | tf_op jit(solution)/shard_map/ppermute | solution.py:213
  93.4 10.3 %all_to_all.11 = bf16[4,144,256]{2,1,0:T(8,128)(2,1)S(1)} all-to-all(bf16[4,144,256]{2,1,0:T(8,128)(2,1)S(1)} %bitcast.5), channel_id=1, replica_groups=mesh['batch'=16,'y'=4,'z'=8] {'y'}, dimensions={0} | all-to-all | bytes 589824 | tf_op jit(solution)/shard_map/all_to_all | solution.py:245
  (48 shorter events, 10.3 us)
Async XLA Ops:
  2.8 9.9 %collective-permute-start = (bf16[256,256]{1,0:T(8,128)(2,1)}, bf16[256,256]{1,0:T(8,128)(2,1)S(1)}, u32[]{:S(2)}, u32[]{:S(2)}) collective-permute-start(bf16[256,256]{1,0:T(8,128)(2,1)} %get-tuple-element.19), channel_id=1, source_target_pairs={{0,8},{8,16},{16,24},{24,0},{1,9},{9,17},{17,25},{25,1},{2,10},{10... | collective-permute-start | bytes 393224 | tf_op jit(solution)/shard_map/ppermute | solution.py:213
  7.6 12.5 %collective-permute-start.1 = (bf16[256,256]{1,0:T(8,128)(2,1)}, bf16[256,256]{1,0:T(8,128)(2,1)S(1)}, u32[]{:S(2)}, u32[]{:S(2)}) collective-permute-start(bf16[256,256]{1,0:T(8,128)(2,1)} %get-tuple-element.20), channel_id=1, source_target_pairs={{0,16},{8,24},{16,0},{24,8},{1,17},{9,25},{17,1},{25,9},{2,18},{10... | collective-permute-start | bytes 393224 | tf_op jit(solution)/shard_map/ppermute | solution.py:213
  9.5 10.6 %collective-permute-start.2 = (bf16[256,256]{1,0:T(8,128)(2,1)}, bf16[256,256]{1,0:T(8,128)(2,1)S(1)}, u32[]{:S(2)}, u32[]{:S(2)}) collective-permute-start(bf16[256,256]{1,0:T(8,128)(2,1)} %get-tuple-element.21), channel_id=1, source_target_pairs={{0,24},{8,0},{16,8},{24,16},{1,25},{9,1},{17,9},{25,17},{2,26},{10... | collective-permute-start | bytes 393224 | tf_op jit(solution)/shard_map/ppermute | solution.py:213
  21.0 13.1 %copy-start.15 = (bf16[144,256]{1,0:T(8,128)(2,1)S(1)}, bf16[144,256]{1,0:T(8,128)(2,1)}, u32[]{:S(2)}) copy-start(bf16[144,256]{1,0:T(8,128)(2,1)} %get-tuple-element.22) | copy-start | bytes 221188
  21.0 25.2 %copy-start.14 = (bf16[144,256]{1,0:T(8,128)(2,1)S(1)}, bf16[144,256]{1,0:T(8,128)(2,1)}, u32[]{:S(2)}) copy-start(bf16[144,256]{1,0:T(8,128)(2,1)} %get-tuple-element.24) | copy-start | bytes 221188
  21.0 29.4 %copy-start.13 = (bf16[144,256]{1,0:T(8,128)(2,1)S(1)}, bf16[144,256]{1,0:T(8,128)(2,1)}, u32[]{:S(2)}) copy-start(bf16[144,256]{1,0:T(8,128)(2,1)} %get-tuple-element.25) | copy-start | bytes 221188
  21.0 44.5 %copy-start.10 = (s32[1024]{0:T(1024)S(1)}, s32[1024]{0:T(1024)}, u32[]{:S(2)}) copy-start(s32[1024]{0:T(1024)} %param.24) | copy-start | bytes 12292
  21.1 45.4 %copy-start.5 = (bf16[144,256]{1,0:T(8,128)(2,1)S(1)}, bf16[144,256]{1,0:T(8,128)(2,1)}, u32[]{:S(2)}) copy-start(bf16[144,256]{1,0:T(8,128)(2,1)} %get-tuple-element.17.refs_0_) | copy-start | bytes 221188
  21.1 23.2 %collective-permute-start.3 = (bf16[1024,256]{1,0:T(8,128)(2,1)S(1)}, bf16[1024,256]{1,0:T(8,128)(2,1)S(1)}, u32[]{:S(2)}, u32[]{:S(2)}) collective-permute-start(bf16[1024,256]{1,0:T(8,128)(2,1)S(1)} %shard_map.150.refs_0_), channel_id=1, source_target_pairs={{0,1},{1,2},{2,3},{3,4},{4,5},{5,6},{6,7},{7,0},{8,9},{9,10},{10,1... | collective-permute-start | bytes 1572872 | tf_op jit(solution)/shard_map/ppermute | solution.py:213
  25.5 32.9 %collective-permute-start.5 = (bf16[1024,256]{1,0:T(8,128)(2,1)S(1)}, bf16[1024,256]{1,0:T(8,128)(2,1)S(1)}, u32[]{:S(2)}, u32[]{:S(2)}) collective-permute-start(bf16[1024,256]{1,0:T(8,128)(2,1)S(1)} %shard_map.150.refs_0_), channel_id=1, source_target_pairs={{0,7},{1,0},{2,1},{3,2},{4,3},{5,4},{6,5},{7,6},{8,15},{9,8},{10,9... | collective-permute-start | bytes 1572872 | tf_op jit(solution)/shard_map/ppermute | solution.py:213
  34.1 6.2 %collective-permute-start.4 = (bf16[144,256]{1,0:T(8,128)(2,1)S(1)}, bf16[144,256]{1,0:T(8,128)(2,1)S(1)}, u32[]{:S(2)}, u32[]{:S(2)}) collective-permute-start(bf16[144,256]{1,0:T(8,128)(2,1)S(1)} %copy-done.15), channel_id=1, source_target_pairs={{0,8},{8,16},{16,24},{24,0},{1,9},{9,17},{17,25},{25,1},{2,10},{10... | collective-permute-start | bytes 221192 | tf_op jit(solution)/shard_map/ppermute | solution.py:213
  44.2 19.3 %collective-permute-start.8 = (bf16[1024,256]{1,0:T(8,128)(2,1)S(1)}, bf16[1024,256]{1,0:T(8,128)(2,1)S(1)}, u32[]{:S(2)}, u32[]{:S(2)}) collective-permute-start(bf16[1024,256]{1,0:T(8,128)(2,1)S(1)} %collective-permute-done.3.refs_0_), channel_id=1, source_target_pairs={{0,1},{1,2},{2,3},{3,4},{4,5},{5,6},{6,7},{7,0},{8,9},{9,10},{10,1... | collective-permute-start | bytes 1572872 | tf_op jit(solution)/shard_map/ppermute | solution.py:213
  46.2 7.9 %collective-permute-start.6 = (bf16[144,256]{1,0:T(8,128)(2,1)S(1)}, bf16[144,256]{1,0:T(8,128)(2,1)S(1)}, u32[]{:S(2)}, u32[]{:S(2)}) collective-permute-start(bf16[144,256]{1,0:T(8,128)(2,1)S(1)} %copy-done.14), channel_id=1, source_target_pairs={{0,16},{8,24},{16,0},{24,8},{1,17},{9,25},{17,1},{25,9},{2,18},{10... | collective-permute-start | bytes 221192 | tf_op jit(solution)/shard_map/ppermute | solution.py:213
  50.4 8.0 %collective-permute-start.7 = (bf16[144,256]{1,0:T(8,128)(2,1)S(1)}, bf16[144,256]{1,0:T(8,128)(2,1)S(1)}, u32[]{:S(2)}, u32[]{:S(2)}) collective-permute-start(bf16[144,256]{1,0:T(8,128)(2,1)S(1)} %copy-done.13), channel_id=1, source_target_pairs={{0,24},{8,0},{16,8},{24,16},{1,25},{9,1},{17,9},{25,17},{2,26},{10... | collective-permute-start | bytes 221192 | tf_op jit(solution)/shard_map/ppermute | solution.py:213
  58.4 14.2 %collective-permute-start.11 = (bf16[1024,256]{1,0:T(8,128)(2,1)S(1)}, bf16[1024,256]{1,0:T(8,128)(2,1)S(1)}, u32[]{:S(2)}, u32[]{:S(2)}) collective-permute-start(bf16[1024,256]{1,0:T(8,128)(2,1)S(1)} %collective-permute-done.5.refs_1_), channel_id=1, source_target_pairs={{0,7},{1,0},{2,1},{3,2},{4,3},{5,4},{6,5},{7,6},{8,15},{9,8},{10,9... | collective-permute-start | bytes 1572872 | tf_op jit(solution)/shard_map/ppermute | solution.py:213
  63.6 14.7 %collective-permute-start.9 = (bf16[1024,256]{1,0:T(8,128)(2,1)S(1)}, bf16[1024,256]{1,0:T(8,128)(2,1)S(1)}, u32[]{:S(2)}, u32[]{:S(2)}) collective-permute-start(bf16[1024,256]{1,0:T(8,128)(2,1)S(1)} %collective-permute-done.8.refs_0_), channel_id=1, source_target_pairs={{0,1},{1,2},{2,3},{3,4},{4,5},{5,6},{6,7},{7,0},{8,9},{9,10},{10,1... | collective-permute-start | bytes 1572872 | tf_op jit(solution)/shard_map/ppermute | solution.py:213
  72.7 13.8 %collective-permute-start.12 = (bf16[1024,256]{1,0:T(8,128)(2,1)S(1)}, bf16[1024,256]{1,0:T(8,128)(2,1)S(1)}, u32[]{:S(2)}, u32[]{:S(2)}) collective-permute-start(bf16[1024,256]{1,0:T(8,128)(2,1)S(1)} %collective-permute-done.11.refs_1_), channel_id=1, source_target_pairs={{0,7},{1,0},{2,1},{3,2},{4,3},{5,4},{6,5},{7,6},{8,15},{9,8},{10,9... | collective-permute-start | bytes 1572872 | tf_op jit(solution)/shard_map/ppermute | solution.py:213
  78.3 13.5 %collective-permute-start.10 = (bf16[1024,256]{1,0:T(8,128)(2,1)S(1)}, bf16[1024,256]{1,0:T(8,128)(2,1)S(1)}, u32[]{:S(2)}, u32[]{:S(2)}) collective-permute-start(bf16[1024,256]{1,0:T(8,128)(2,1)S(1)} %collective-permute-done.9.refs_0_), channel_id=1, source_target_pairs={{0,1},{1,2},{2,3},{3,4},{4,5},{5,6},{6,7},{7,0},{8,9},{9,10},{10,1... | collective-permute-start | bytes 1572872 | tf_op jit(solution)/shard_map/ppermute | solution.py:213
  88.9 14.8 %copy-start = (bf16[512,1024]{1,0:T(8,128)(2,1)S(1)}, bf16[512,1024]{1,0:T(8,128)(2,1)}, u32[]{:S(2)}) copy-start(bf16[512,1024]{1,0:T(8,128)(2,1)} %w_ref.1) | copy-start | bytes 3145732
  91.8 11.9 %copy-start.2 = (bf16[256,512]{1,0:T(8,128)(2,1)S(1)}, bf16[256,512]{1,0:T(8,128)(2,1)}, u32[]{:S(2)}) copy-start(bf16[256,512]{1,0:T(8,128)(2,1)} %hg.1) | copy-start | bytes 786436
  91.8 11.9 %copy-start.6 = (bf16[32,1024]{1,0:T(8,128)(2,1)S(1)}, bf16[32,1024]{1,0:T(8,128)(2,1)}, u32[]{:S(2)}) copy-start(bf16[32,1024]{1,0:T(8,128)(2,1)} %cx.1) | copy-start | bytes 196612
  91.8 11.9 %copy-start.8 = (bf16[32,512]{1,0:T(8,128)(2,1)S(1)}, bf16[32,512]{1,0:T(8,128)(2,1)}, u32[]{:S(2)}) copy-start(bf16[32,512]{1,0:T(8,128)(2,1)} %cv.1) | copy-start | bytes 98308
  91.8 11.9 %copy-start.9 = (bf16[32,512]{1,0:T(8,128)(2,1)S(1)}, bf16[32,512]{1,0:T(8,128)(2,1)}, u32[]{:S(2)}) copy-start(bf16[32,512]{1,0:T(8,128)(2,1)} %cg.1) | copy-start | bytes 98308
  93.4 10.4 %copy-start.1 = (bf16[256,1024]{1,0:T(8,128)(2,1)S(1)}, bf16[256,1024]{1,0:T(8,128)(2,1)}, u32[]{:S(2)}) copy-start(bf16[256,1024]{1,0:T(8,128)(2,1)} %hx.1) | copy-start | bytes 1572868
  (5 other events, 22.9 us)

commit v12 on v11

--- a/solution.py
+++ b/solution.py
@@ -230,8 +230,8 @@
     (own,) = call(join_kernel, [(KEYS, 2 * DH)], *pieces, place=y)
     up1, down1 = turn(own, "z", 1), turn(own, "z", -1)
     folds = [parts[HEADS]] + [turn(parts[HEADS + i], "y", i) for i in (1, 2, 3)]
-    up1, folds[1] = lax.optimization_barrier((up1, folds[1]))
-    down1, folds[2], folds[3] = lax.optimization_barrier((down1, folds[2], folds[3]))
+    up1, folds[3] = lax.optimization_barrier((up1, folds[3]))
+    down1, folds[1], folds[2] = lax.optimization_barrier((down1, folds[1], folds[2]))
     up2, down2 = turn(up1, "z", 1), turn(down1, "z", -1)
     (queries,) = call(unfold_kernel, [(TOTAL, DH)], *folds, place=y)
     total = attend((0,), info, queries, users, (own,), None)

time: 106 us -> 106 us (level); the launches traced: 105 us -> 104 us
  starting transfers between devices: 48.9 us -> 47.8 us
    ppermute x13, starting transfers between devices: 48.9 us -> 47.8 us  [turn(): lax.ppermute(array, axis, [(i, (i + step) % count) for i in range(count)])]
  transfers between devices with their start and end apart: 13 -> 13, of which waited for: 8 -> 9; matrix products, arithmetic and copies ran while one was open for 0% -> 0% of each run, Pallas kernels for 9% -> 9%
where the time goes in v12:
time: 106 us; the launch traced here: 104 us
  starting transfers between devices  47.8 us (45%)
  waiting for transfers between devices  28.3 us (27%)
  Pallas kernels  14.8 us (14%)
  blocking collectives  10.4 us (10%)
  local copies, waits for them, and re-layouts  1.83 us (2%)
    ppermute x13, starting transfers between devices, turn(): lax.ppermute(array, axis, [(i, (i + step) % count) for i in range(count)])  47.8 us
    ppermute x13, waiting for transfers between devices, turn(): lax.ppermute(array, axis, [(i, (i + step) % count) for i in range(count)])  28.3 us
    pallas_call x5, Pallas kernels, attend(): pl.pallas_call(functools.partial(attend_kernel, offsets, first, last), in...  11 us
    all_to_all x1, blocking collectives, on_device(): total = lax.all_to_all(total, 'y', 0, 0, tiled=True)  10.4 us
    pallas_call x4, Pallas kernels, call(): pl.pallas_call(kernel, in_specs=[SMEM] * (place is not None) + [VMEM] * (...  3.75 us
  transfers between devices with their start and end apart: 13, of which 9 were waited for; matrix products, arithmetic and copies ran while one was open for 0% of the time, Pallas kernels for 9%

profile of v12, /device:TPU:56, one launch (start us, length us, event | category | flops | bytes accessed | tf_op | source)
XLA Modules:
  0.0 104.1 jit_solution(9553603358500726338)
XLA Ops:
  0.6 2.1 %shard_map.149 = (bf16[256,256]{1,0:T(8,128)(2,1)}, bf16[256,256]{1,0:T(8,128)(2,1)}, bf16[256,256]{1,0:T(8,128)(2,1)}, bf16[256,256]{1,0:T(8,128)(2,1)}, bf16[1...) custom-call(s32[1]{0:T(128)} %bitcast.1.y_ref, ...), custom_call_target="tpu_custom_call" | custom-call | tf_op jit(solution)/shard_map/pallas_call | solution.py:201
  2.8 4.8 %collective-permute-start = (bf16[256,256]{1,0:T(8,128)(2,1)}, bf16[256,256]{1,0:T(8,128)(2,1)S(1)}, u32[]{:S(2)}, u32[]{:S(2)}) collective-permute-start(bf16[256,256]{1,0:T(8,128)(2,1)} %get-tuple-element.19), channel_id=1, source_target_pairs={{0,8},{8,16},{16,24},{24,0},{1,9},{9,17},{17,25},{25,1},{2,10},{10... | collective-permute-start | bytes 393224 | tf_op jit(solution)/shard_map/ppermute | solution.py:213
  7.6 1.9 %collective-permute-start.1 = (bf16[256,256]{1,0:T(8,128)(2,1)}, bf16[256,256]{1,0:T(8,128)(2,1)S(1)}, u32[]{:S(2)}, u32[]{:S(2)}) collective-permute-start(bf16[256,256]{1,0:T(8,128)(2,1)} %get-tuple-element.20), channel_id=1, source_target_pairs={{0,16},{8,24},{16,0},{24,8},{1,17},{9,25},{17,1},{25,9},{2,18},{10... | collective-permute-start | bytes 393224 | tf_op jit(solution)/shard_map/ppermute | solution.py:213
  9.5 3.1 %collective-permute-start.2 = (bf16[256,256]{1,0:T(8,128)(2,1)}, bf16[256,256]{1,0:T(8,128)(2,1)S(1)}, u32[]{:S(2)}, u32[]{:S(2)}) collective-permute-start(bf16[256,256]{1,0:T(8,128)(2,1)} %get-tuple-element.21), channel_id=1, source_target_pairs={{0,24},{8,0},{16,8},{24,16},{1,25},{9,1},{17,9},{25,17},{2,26},{10... | collective-permute-start | bytes 393224 | tf_op jit(solution)/shard_map/ppermute | solution.py:213
  12.7 7.4 %collective-permute-done.1.refs_2_ = bf16[256,256]{1,0:T(8,128)(2,1)S(1)} collective-permute-done((bf16[256,256]{1,0:T(8,128)(2,1)}, bf16[256,256]{1,0:T(8,128)(2,1)S(1)}, u32[]{:S(2)}, u32[]{:S(2)}) %collective-permute-start.1) | collective-permute-done | bytes 131104 | tf_op jit(solution)/shard_map/ppermute | solution.py:213
  21.1 4.4 %collective-permute-start.6 = (bf16[1024,256]{1,0:T(8,128)(2,1)S(1)}, bf16[1024,256]{1,0:T(8,128)(2,1)S(1)}, u32[]{:S(2)}, u32[]{:S(2)}) collective-permute-start(bf16[1024,256]{1,0:T(8,128)(2,1)S(1)} %shard_map.150.refs_0_), channel_id=1, source_target_pairs={{0,1},{1,2},{2,3},{3,4},{4,5},{5,6},{6,7},{7,0},{8,9},{9,10},{10,1... | collective-permute-start | bytes 1572872 | tf_op jit(solution)/shard_map/ppermute | solution.py:213
  25.5 8.6 %collective-permute-start.3 = (bf16[1024,256]{1,0:T(8,128)(2,1)S(1)}, bf16[1024,256]{1,0:T(8,128)(2,1)S(1)}, u32[]{:S(2)}, u32[]{:S(2)}) collective-permute-start(bf16[1024,256]{1,0:T(8,128)(2,1)S(1)} %shard_map.150.refs_0_), channel_id=1, source_target_pairs={{0,7},{1,0},{2,1},{3,2},{4,3},{5,4},{6,5},{7,6},{8,15},{9,8},{10,9... | collective-permute-start | bytes 1572872 | tf_op jit(solution)/shard_map/ppermute | solution.py:213
  34.1 2.4 %collective-permute-start.7 = (bf16[144,256]{1,0:T(8,128)(2,1)S(1)}, bf16[144,256]{1,0:T(8,128)(2,1)S(1)}, u32[]{:S(2)}, u32[]{:S(2)}) collective-permute-start(bf16[144,256]{1,0:T(8,128)(2,1)S(1)} %copy-done.15), channel_id=1, source_target_pairs={{0,24},{8,0},{16,8},{24,16},{1,25},{9,1},{17,9},{25,17},{2,26},{10... | collective-permute-start | bytes 221192 | tf_op jit(solution)/shard_map/ppermute | solution.py:213
  36.5 5.7 %collective-permute-done.7.refs_3_ = bf16[144,256]{1,0:T(8,128)(2,1)S(1)} collective-permute-done((bf16[144,256]{1,0:T(8,128)(2,1)S(1)}, bf16[144,256]{1,0:T(8,128)(2,1)S(1)}, u32[]{:S(2)}, u32[]{:S(2)}) %collective-permute-start.7) | collective-permute-done | bytes 73760 | tf_op jit(solution)/shard_map/ppermute | solution.py:213
  42.1 2.1 %collective-permute-done.6.refs_0_ = bf16[1024,256]{1,0:T(8,128)(2,1)S(1)} collective-permute-done((bf16[1024,256]{1,0:T(8,128)(2,1)S(1)}, bf16[1024,256]{1,0:T(8,128)(2,1)S(1)}, u32[]{:S(2)}, u32[]{:S(2)}) %collective-permute-start.6) | collective-permute-done | bytes 524320 | tf_op jit(solution)/shard_map/ppermute | solution.py:213
  44.2 1.9 %collective-permute-start.8 = (bf16[1024,256]{1,0:T(8,128)(2,1)S(1)}, bf16[1024,256]{1,0:T(8,128)(2,1)S(1)}, u32[]{:S(2)}, u32[]{:S(2)}) collective-permute-start(bf16[1024,256]{1,0:T(8,128)(2,1)S(1)} %collective-permute-done.6.refs_0_), channel_id=1, source_target_pairs={{0,1},{1,2},{2,3},{3,4},{4,5},{5,6},{6,7},{7,0},{8,9},{9,10},{10,1... | collective-permute-start | bytes 1572872 | tf_op jit(solution)/shard_map/ppermute | solution.py:213
  46.2 2.3 %collective-permute-start.4 = (bf16[144,256]{1,0:T(8,128)(2,1)S(1)}, bf16[144,256]{1,0:T(8,128)(2,1)S(1)}, u32[]{:S(2)}, u32[]{:S(2)}) collective-permute-start(bf16[144,256]{1,0:T(8,128)(2,1)S(1)} %copy-done.14), channel_id=1, source_target_pairs={{0,8},{8,16},{16,24},{24,0},{1,9},{9,17},{17,25},{25,1},{2,10},{10... | collective-permute-start | bytes 221192 | tf_op jit(solution)/shard_map/ppermute | solution.py:213
  48.5 3.8 %collective-permute-start.5 = (bf16[144,256]{1,0:T(8,128)(2,1)S(1)}, bf16[144,256]{1,0:T(8,128)(2,1)S(1)}, u32[]{:S(2)}, u32[]{:S(2)}) collective-permute-start(bf16[144,256]{1,0:T(8,128)(2,1)S(1)} %copy-done.13), channel_id=1, source_target_pairs={{0,16},{8,24},{16,0},{24,8},{1,17},{9,25},{17,1},{25,9},{2,18},{10... | collective-permute-start | bytes 221192 | tf_op jit(solution)/shard_map/ppermute | solution.py:213
  52.4 3.3 %collective-permute-done.5.refs_2_ = bf16[144,256]{1,0:T(8,128)(2,1)S(1)} collective-permute-done((bf16[144,256]{1,0:T(8,128)(2,1)S(1)}, bf16[144,256]{1,0:T(8,128)(2,1)S(1)}, u32[]{:S(2)}, u32[]{:S(2)}) %collective-permute-start.5) | collective-permute-done | bytes 73760 | tf_op jit(solution)/shard_map/ppermute | solution.py:213
  55.7 5.1 %collective-permute-start.11 = (bf16[1024,256]{1,0:T(8,128)(2,1)S(1)}, bf16[1024,256]{1,0:T(8,128)(2,1)S(1)}, u32[]{:S(2)}, u32[]{:S(2)}) collective-permute-start(bf16[1024,256]{1,0:T(8,128)(2,1)S(1)} %collective-permute-done.3.refs_1_), channel_id=1, source_target_pairs={{0,7},{1,0},{2,1},{3,2},{4,3},{5,4},{6,5},{7,6},{8,15},{9,8},{10,9... | collective-permute-start | bytes 1572872 | tf_op jit(solution)/shard_map/ppermute | solution.py:213
  60.9 1.9 %collective-permute-start.9 = (bf16[1024,256]{1,0:T(8,128)(2,1)S(1)}, bf16[1024,256]{1,0:T(8,128)(2,1)S(1)}, u32[]{:S(2)}, u32[]{:S(2)}) collective-permute-start(bf16[1024,256]{1,0:T(8,128)(2,1)S(1)} %collective-permute-done.8.refs_0_), channel_id=1, source_target_pairs={{0,1},{1,2},{2,3},{3,4},{4,5},{5,6},{6,7},{7,0},{8,9},{9,10},{10,1... | collective-permute-start | bytes 1572872 | tf_op jit(solution)/shard_map/ppermute | solution.py:213
  63.8 2.2 %attend.5.refs_2_ = f32[1152,128]{1,0:T(8,128)S(1)} custom-call(s32[5]{0:T(128)S(1)} %pad_add_fusion.info_ref, bf16[1152,128]{1,0:T(8,128)(2,1)S(1)} %shard_map.151.qs, s32[128,1]{1,0:T(8,128)S(1)} %reshape.22.user_ref, bf16[1024,256]{1,0:T(8,128)(2,1)S(1)} %shard_map.150.refs_0_), custom_call_target="tpu_custom_call" | custom-call | flops 603979776 | bytes 1048576 | tf_op jit(solution)/shard_map/attend/pallas_call | solution.py:164
  66.0 2.4 %attend.6.refs_2_ = f32[1152,128]{1,0:T(8,128)S(1)} custom-call(s32[5]{0:T(128)S(1)} %pad_add_fusion.info_ref, bf16[1152,128]{1,0:T(8,128)(2,1)S(1)} %shard_map.151.qs, s32[128,1]{1,0:T(8,128)S(1)} %reshape.22.user_ref, bf16[1024,256]{1,0:T(8,128)(2,1)S(1)} %collective-permute-done.6.refs_0_, bf16[1024,256]{1,0:T(8,128)(2,1)S(1)} %collective-permute-done.3.refs_1_, ...), custom_call_target="tpu_custom_call" | custom-call | flops 1207959552 | bytes 1048576 | tf_op jit(solution)/shard_map/attend/pallas_call | solution.py:164
  69.8 5.6 %collective-permute-start.12 = (bf16[1024,256]{1,0:T(8,128)(2,1)S(1)}, bf16[1024,256]{1,0:T(8,128)(2,1)S(1)}, u32[]{:S(2)}, u32[]{:S(2)}) collective-permute-start(bf16[1024,256]{1,0:T(8,128)(2,1)S(1)} %collective-permute-done.11.refs_1_), channel_id=1, source_target_pairs={{0,7},{1,0},{2,1},{3,2},{4,3},{5,4},{6,5},{7,6},{8,15},{9,8},{10,9... | collective-permute-start | bytes 1572872 | tf_op jit(solution)/shard_map/ppermute | solution.py:213
  78.1 2.4 %attend.7.refs_2_ = f32[1152,128]{1,0:T(8,128)S(1)} custom-call(s32[5]{0:T(128)S(1)} %pad_add_fusion.info_ref, bf16[1152,128]{1,0:T(8,128)(2,1)S(1)} %shard_map.151.qs, s32[128,1]{1,0:T(8,128)S(1)} %reshape.22.user_ref, bf16[1024,256]{1,0:T(8,128)(2,1)S(1)} %collective-permute-done.8.refs_0_, bf16[1024,256]{1,0:T(8,128)(2,1)S(1)} %collective-permute-done.11.refs_1_, ...), custom_call_target="tpu_custom_call" | custom-call | flops 1207959552 | bytes 1048576 | tf_op jit(solution)/shard_map/attend/pallas_call | solution.py:164
  80.5 3.0 %collective-permute-done.12.refs_1_ = bf16[1024,256]{1,0:T(8,128)(2,1)S(1)} collective-permute-done((bf16[1024,256]{1,0:T(8,128)(2,1)S(1)}, bf16[1024,256]{1,0:T(8,128)(2,1)S(1)}, u32[]{:S(2)}, u32[]{:S(2)}) %collective-permute-start.12) | collective-permute-done | bytes 524320 | tf_op jit(solution)/shard_map/ppermute | solution.py:213
  83.5 2.4 %attend.8.refs_1_ = f32[1152,128]{1,0:T(8,128)S(1)} custom-call(s32[5]{0:T(128)S(1)} %pad_add_fusion.info_ref, bf16[1152,128]{1,0:T(8,128)(2,1)S(1)} %shard_map.151.qs, s32[128,1]{1,0:T(8,128)S(1)} %reshape.22.user_ref, bf16[1024,256]{1,0:T(8,128)(2,1)S(1)} %collective-permute-done.9.refs_0_, bf16[1024,256]{1,0:T(8,128)(2,1)S(1)} %collective-permute-done.12.refs_1_, ...), custom_call_target="tpu_custom_call" | custom-call | flops 1207959552 | bytes 1048576 | tf_op jit(solution)/shard_map/attend/pallas_call | solution.py:164
  86.0 4.5 %collective-permute-done.10.refs_0_ = bf16[1024,256]{1,0:T(8,128)(2,1)S(1)} collective-permute-done((bf16[1024,256]{1,0:T(8,128)(2,1)S(1)}, bf16[1024,256]{1,0:T(8,128)(2,1)S(1)}, u32[]{:S(2)}, u32[]{:S(2)}) %collective-permute-start.10) | collective-permute-done | bytes 524320 | tf_op jit(solution)/shard_map/ppermute | solution.py:213
  92.1 10.4 %all_to_all.11 = bf16[4,144,256]{2,1,0:T(8,128)(2,1)S(1)} all-to-all(bf16[4,144,256]{2,1,0:T(8,128)(2,1)S(1)} %bitcast.5), channel_id=1, replica_groups=mesh['batch'=16,'y'=4,'z'=8] {'y'}, dimensions={0} | all-to-all | bytes 589824 | tf_op jit(solution)/shard_map/all_to_all | solution.py:245
  (48 shorter events, 9.2 us)
Async XLA Ops:
  2.8 9.9 %collective-permute-start = (bf16[256,256]{1,0:T(8,128)(2,1)}, bf16[256,256]{1,0:T(8,128)(2,1)S(1)}, u32[]{:S(2)}, u32[]{:S(2)}) collective-permute-start(bf16[256,256]{1,0:T(8,128)(2,1)} %get-tuple-element.19), channel_id=1, source_target_pairs={{0,8},{8,16},{16,24},{24,0},{1,9},{9,17},{17,25},{25,1},{2,10},{10... | collective-permute-start | bytes 393224 | tf_op jit(solution)/shard_map/ppermute | solution.py:213
  7.6 12.5 %collective-permute-start.1 = (bf16[256,256]{1,0:T(8,128)(2,1)}, bf16[256,256]{1,0:T(8,128)(2,1)S(1)}, u32[]{:S(2)}, u32[]{:S(2)}) collective-permute-start(bf16[256,256]{1,0:T(8,128)(2,1)} %get-tuple-element.20), channel_id=1, source_target_pairs={{0,16},{8,24},{16,0},{24,8},{1,17},{9,25},{17,1},{25,9},{2,18},{10... | collective-permute-start | bytes 393224 | tf_op jit(solution)/shard_map/ppermute | solution.py:213
  9.5 10.6 %collective-permute-start.2 = (bf16[256,256]{1,0:T(8,128)(2,1)}, bf16[256,256]{1,0:T(8,128)(2,1)S(1)}, u32[]{:S(2)}, u32[]{:S(2)}) collective-permute-start(bf16[256,256]{1,0:T(8,128)(2,1)} %get-tuple-element.21), channel_id=1, source_target_pairs={{0,24},{8,0},{16,8},{24,16},{1,25},{9,1},{17,9},{25,17},{2,26},{10... | collective-permute-start | bytes 393224 | tf_op jit(solution)/shard_map/ppermute | solution.py:213
  21.0 13.1 %copy-start.15 = (bf16[144,256]{1,0:T(8,128)(2,1)S(1)}, bf16[144,256]{1,0:T(8,128)(2,1)}, u32[]{:S(2)}) copy-start(bf16[144,256]{1,0:T(8,128)(2,1)} %get-tuple-element.26) | copy-start | bytes 221188
  21.0 25.2 %copy-start.14 = (bf16[144,256]{1,0:T(8,128)(2,1)S(1)}, bf16[144,256]{1,0:T(8,128)(2,1)}, u32[]{:S(2)}) copy-start(bf16[144,256]{1,0:T(8,128)(2,1)} %get-tuple-element.22) | copy-start | bytes 221188
  21.0 27.5 %copy-start.13 = (bf16[144,256]{1,0:T(8,128)(2,1)S(1)}, bf16[144,256]{1,0:T(8,128)(2,1)}, u32[]{:S(2)}) copy-start(bf16[144,256]{1,0:T(8,128)(2,1)} %get-tuple-element.23) | copy-start | bytes 221188
  21.0 41.8 %copy-start.10 = (s32[1024]{0:T(1024)S(1)}, s32[1024]{0:T(1024)}, u32[]{:S(2)}) copy-start(s32[1024]{0:T(1024)} %param.24) | copy-start | bytes 12292
  21.1 42.7 %copy-start.5 = (bf16[144,256]{1,0:T(8,128)(2,1)S(1)}, bf16[144,256]{1,0:T(8,128)(2,1)}, u32[]{:S(2)}) copy-start(bf16[144,256]{1,0:T(8,128)(2,1)} %get-tuple-element.17.refs_0_) | copy-start | bytes 221188
  21.1 23.2 %collective-permute-start.6 = (bf16[1024,256]{1,0:T(8,128)(2,1)S(1)}, bf16[1024,256]{1,0:T(8,128)(2,1)S(1)}, u32[]{:S(2)}, u32[]{:S(2)}) collective-permute-start(bf16[1024,256]{1,0:T(8,128)(2,1)S(1)} %shard_map.150.refs_0_), channel_id=1, source_target_pairs={{0,1},{1,2},{2,3},{3,4},{4,5},{5,6},{6,7},{7,0},{8,9},{9,10},{10,1... | collective-permute-start | bytes 1572872 | tf_op jit(solution)/shard_map/ppermute | solution.py:213
  25.5 30.3 %collective-permute-start.3 = (bf16[1024,256]{1,0:T(8,128)(2,1)S(1)}, bf16[1024,256]{1,0:T(8,128)(2,1)S(1)}, u32[]{:S(2)}, u32[]{:S(2)}) collective-permute-start(bf16[1024,256]{1,0:T(8,128)(2,1)S(1)} %shard_map.150.refs_0_), channel_id=1, source_target_pairs={{0,7},{1,0},{2,1},{3,2},{4,3},{5,4},{6,5},{7,6},{8,15},{9,8},{10,9... | collective-permute-start | bytes 1572872 | tf_op jit(solution)/shard_map/ppermute | solution.py:213
  34.1 8.0 %collective-permute-start.7 = (bf16[144,256]{1,0:T(8,128)(2,1)S(1)}, bf16[144,256]{1,0:T(8,128)(2,1)S(1)}, u32[]{:S(2)}, u32[]{:S(2)}) collective-permute-start(bf16[144,256]{1,0:T(8,128)(2,1)S(1)} %copy-done.15), channel_id=1, source_target_pairs={{0,24},{8,0},{16,8},{24,16},{1,25},{9,1},{17,9},{25,17},{2,26},{10... | collective-permute-start | bytes 221192 | tf_op jit(solution)/shard_map/ppermute | solution.py:213
  44.2 16.6 %collective-permute-start.8 = (bf16[1024,256]{1,0:T(8,128)(2,1)S(1)}, bf16[1024,256]{1,0:T(8,128)(2,1)S(1)}, u32[]{:S(2)}, u32[]{:S(2)}) collective-permute-start(bf16[1024,256]{1,0:T(8,128)(2,1)S(1)} %collective-permute-done.6.refs_0_), channel_id=1, source_target_pairs={{0,1},{1,2},{2,3},{3,4},{4,5},{5,6},{6,7},{7,0},{8,9},{9,10},{10,1... | collective-permute-start | bytes 1572872 | tf_op jit(solution)/shard_map/ppermute | solution.py:213
  46.2 6.2 %collective-permute-start.4 = (bf16[144,256]{1,0:T(8,128)(2,1)S(1)}, bf16[144,256]{1,0:T(8,128)(2,1)S(1)}, u32[]{:S(2)}, u32[]{:S(2)}) collective-permute-start(bf16[144,256]{1,0:T(8,128)(2,1)S(1)} %copy-done.14), channel_id=1, source_target_pairs={{0,8},{8,16},{16,24},{24,0},{1,9},{9,17},{17,25},{25,1},{2,10},{10... | collective-permute-start | bytes 221192 | tf_op jit(solution)/shard_map/ppermute | solution.py:213
  48.5 7.3 %collective-permute-start.5 = (bf16[144,256]{1,0:T(8,128)(2,1)S(1)}, bf16[144,256]{1,0:T(8,128)(2,1)S(1)}, u32[]{:S(2)}, u32[]{:S(2)}) collective-permute-start(bf16[144,256]{1,0:T(8,128)(2,1)S(1)} %copy-done.13), channel_id=1, source_target_pairs={{0,16},{8,24},{16,0},{24,8},{1,17},{9,25},{17,1},{25,9},{2,18},{10... | collective-permute-start | bytes 221192 | tf_op jit(solution)/shard_map/ppermute | solution.py:213
  55.7 14.0 %collective-permute-start.11 = (bf16[1024,256]{1,0:T(8,128)(2,1)S(1)}, bf16[1024,256]{1,0:T(8,128)(2,1)S(1)}, u32[]{:S(2)}, u32[]{:S(2)}) collective-permute-start(bf16[1024,256]{1,0:T(8,128)(2,1)S(1)} %collective-permute-done.3.refs_1_), channel_id=1, source_target_pairs={{0,7},{1,0},{2,1},{3,2},{4,3},{5,4},{6,5},{7,6},{8,15},{9,8},{10,9... | collective-permute-start | bytes 1572872 | tf_op jit(solution)/shard_map/ppermute | solution.py:213
  60.9 15.3 %collective-permute-start.9 = (bf16[1024,256]{1,0:T(8,128)(2,1)S(1)}, bf16[1024,256]{1,0:T(8,128)(2,1)S(1)}, u32[]{:S(2)}, u32[]{:S(2)}) collective-permute-start(bf16[1024,256]{1,0:T(8,128)(2,1)S(1)} %collective-permute-done.8.refs_0_), channel_id=1, source_target_pairs={{0,1},{1,2},{2,3},{3,4},{4,5},{5,6},{6,7},{7,0},{8,9},{9,10},{10,1... | collective-permute-start | bytes 1572872 | tf_op jit(solution)/shard_map/ppermute | solution.py:213
  69.8 13.8 %collective-permute-start.12 = (bf16[1024,256]{1,0:T(8,128)(2,1)S(1)}, bf16[1024,256]{1,0:T(8,128)(2,1)S(1)}, u32[]{:S(2)}, u32[]{:S(2)}) collective-permute-start(bf16[1024,256]{1,0:T(8,128)(2,1)S(1)} %collective-permute-done.11.refs_1_), channel_id=1, source_target_pairs={{0,7},{1,0},{2,1},{3,2},{4,3},{5,4},{6,5},{7,6},{8,15},{9,8},{10,9... | collective-permute-start | bytes 1572872 | tf_op jit(solution)/shard_map/ppermute | solution.py:213
  76.1 14.3 %collective-permute-start.10 = (bf16[1024,256]{1,0:T(8,128)(2,1)S(1)}, bf16[1024,256]{1,0:T(8,128)(2,1)S(1)}, u32[]{:S(2)}, u32[]{:S(2)}) collective-permute-start(bf16[1024,256]{1,0:T(8,128)(2,1)S(1)} %collective-permute-done.9.refs_0_), channel_id=1, source_target_pairs={{0,1},{1,2},{2,3},{3,4},{4,5},{5,6},{6,7},{7,0},{8,9},{9,10},{10,1... | collective-permute-start | bytes 1572872 | tf_op jit(solution)/shard_map/ppermute | solution.py:213
  86.0 16.6 %copy-start = (bf16[512,1024]{1,0:T(8,128)(2,1)S(1)}, bf16[512,1024]{1,0:T(8,128)(2,1)}, u32[]{:S(2)}) copy-start(bf16[512,1024]{1,0:T(8,128)(2,1)} %w_ref.1) | copy-start | bytes 3145732
  90.5 12.1 %copy-start.2 = (bf16[256,512]{1,0:T(8,128)(2,1)S(1)}, bf16[256,512]{1,0:T(8,128)(2,1)}, u32[]{:S(2)}) copy-start(bf16[256,512]{1,0:T(8,128)(2,1)} %hg.1) | copy-start | bytes 786436
  90.5 12.1 %copy-start.6 = (bf16[32,1024]{1,0:T(8,128)(2,1)S(1)}, bf16[32,1024]{1,0:T(8,128)(2,1)}, u32[]{:S(2)}) copy-start(bf16[32,1024]{1,0:T(8,128)(2,1)} %cx.1) | copy-start | bytes 196612
  90.5 12.1 %copy-start.8 = (bf16[32,512]{1,0:T(8,128)(2,1)S(1)}, bf16[32,512]{1,0:T(8,128)(2,1)}, u32[]{:S(2)}) copy-start(bf16[32,512]{1,0:T(8,128)(2,1)} %cv.1) | copy-start | bytes 98308
  90.5 12.1 %copy-start.9 = (bf16[32,512]{1,0:T(8,128)(2,1)S(1)}, bf16[32,512]{1,0:T(8,128)(2,1)}, u32[]{:S(2)}) copy-start(bf16[32,512]{1,0:T(8,128)(2,1)} %cg.1) | copy-start | bytes 98308
  92.1 10.5 %copy-start.1 = (bf16[256,1024]{1,0:T(8,128)(2,1)S(1)}, bf16[256,1024]{1,0:T(8,128)(2,1)}, u32[]{:S(2)}) copy-start(bf16[256,1024]{1,0:T(8,128)(2,1)} %hx.1) | copy-start | bytes 1572868
  (5 other events, 23.2 us)

commit v13 on v12

--- a/solution.py
+++ b/solution.py
@@ -231,14 +231,14 @@
     up1, down1 = turn(own, "z", 1), turn(own, "z", -1)
     folds = [parts[HEADS]] + [turn(parts[HEADS + i], "y", i) for i in (1, 2, 3)]
     up1, folds[3] = lax.optimization_barrier((up1, folds[3]))
-    down1, folds[1], folds[2] = lax.optimization_barrier((down1, folds[1], folds[2]))
+    down1, folds[1] = lax.optimization_barrier((down1, folds[1]))
     up2, down2 = turn(up1, "z", 1), turn(down1, "z", -1)
     (queries,) = call(unfold_kernel, [(TOTAL, DH)], *folds, place=y)
     total = attend((0,), info, queries, users, (own,), None)
-    total = attend((NZ - 1, 1), info, queries, users, (up1, down1), total)
     down2, total = lax.optimization_barrier((down2, total))
     up3, down3 = turn(up2, "z", 1), turn(down2, "z", -1)
     across = turn(up3, "z", 1)
+    total = attend((NZ - 1, 1), info, queries, users, (up1, down1), total)
     total = attend((NZ - 2, 2), info, queries, users, (up2, down2), total)
     total = attend((NZ - 3, 3), info, queries, users, (up3, down3), total)
     total = attend((4,), info, queries, users, (across,), total, last=True)

time: 106 us -> 106 us (level); the launches traced: 104 us -> 105 us
  waiting for transfers between devices: 28.3 us -> 29.7 us
    ppermute x13, waiting for transfers between devices: 28.3 us -> 29.7 us  [turn(): lax.ppermute(array, axis, [(i, (i + step) % count) for i in range(count)])]
  transfers between devices with their start and end apart: 13 -> 13, of which waited for: 9 -> 8; matrix products, arithmetic and copies ran while one was open for 0% -> 0% of each run, Pallas kernels for 9% -> 9%
where the time goes in v13:
time: 106 us; the launch traced here: 105 us
  starting transfers between devices  47.7 us (45%)
  waiting for transfers between devices  29.7 us (28%)
  Pallas kernels  14.8 us (14%)
  blocking collectives  10.3 us (10%)
  local copies, waits for them, and re-layouts  1.82 us (2%)
    ppermute x13, starting transfers between devices, turn(): lax.ppermute(array, axis, [(i, (i + step) % count) for i in range(count)])  47.7 us
    ppermute x13, waiting for transfers between devices, turn(): lax.ppermute(array, axis, [(i, (i + step) % count) for i in range(count)])  29.7 us
    pallas_call x5, Pallas kernels, attend(): pl.pallas_call(functools.partial(attend_kernel, offsets, first, last), in...  11 us
    all_to_all x1, blocking collectives, on_device(): total = lax.all_to_all(total, 'y', 0, 0, tiled=True)  10.3 us
    pallas_call x4, Pallas kernels, call(): pl.pallas_call(kernel, in_specs=[SMEM] * (place is not None) + [VMEM] * (...  3.76 us
  transfers between devices with their start and end apart: 13, of which 8 were waited for; matrix products, arithmetic and copies ran while one was open for 0% of the time, Pallas kernels for 9%

profile of v13, /device:TPU:56, one launch (start us, length us, event | category | flops | bytes accessed | tf_op | source)
XLA Modules:
  0.0 105.4 jit_solution(13123098019316442446)
XLA Ops:
  0.6 2.1 %shard_map.149 = (bf16[256,256]{1,0:T(8,128)(2,1)}, bf16[256,256]{1,0:T(8,128)(2,1)}, bf16[256,256]{1,0:T(8,128)(2,1)}, bf16[256,256]{1,0:T(8,128)(2,1)}, bf16[1...) custom-call(s32[1]{0:T(128)} %bitcast.1.y_ref, ...), custom_call_target="tpu_custom_call" | custom-call | tf_op jit(solution)/shard_map/pallas_call | solution.py:201
  2.8 4.8 %collective-permute-start = (bf16[256,256]{1,0:T(8,128)(2,1)}, bf16[256,256]{1,0:T(8,128)(2,1)S(1)}, u32[]{:S(2)}, u32[]{:S(2)}) collective-permute-start(bf16[256,256]{1,0:T(8,128)(2,1)} %get-tuple-element.18), channel_id=1, source_target_pairs={{0,8},{8,16},{16,24},{24,0},{1,9},{9,17},{17,25},{25,1},{2,10},{10... | collective-permute-start | bytes 393224 | tf_op jit(solution)/shard_map/ppermute | solution.py:213
  7.6 1.9 %collective-permute-start.1 = (bf16[256,256]{1,0:T(8,128)(2,1)}, bf16[256,256]{1,0:T(8,128)(2,1)S(1)}, u32[]{:S(2)}, u32[]{:S(2)}) collective-permute-start(bf16[256,256]{1,0:T(8,128)(2,1)} %get-tuple-element.19), channel_id=1, source_target_pairs={{0,16},{8,24},{16,0},{24,8},{1,17},{9,25},{17,1},{25,9},{2,18},{10... | collective-permute-start | bytes 393224 | tf_op jit(solution)/shard_map/ppermute | solution.py:213
  9.5 3.1 %collective-permute-start.2 = (bf16[256,256]{1,0:T(8,128)(2,1)}, bf16[256,256]{1,0:T(8,128)(2,1)S(1)}, u32[]{:S(2)}, u32[]{:S(2)}) collective-permute-start(bf16[256,256]{1,0:T(8,128)(2,1)} %get-tuple-element.20), channel_id=1, source_target_pairs={{0,24},{8,0},{16,8},{24,16},{1,25},{9,1},{17,9},{25,17},{2,26},{10... | collective-permute-start | bytes 393224 | tf_op jit(solution)/shard_map/ppermute | solution.py:213
  12.7 7.4 %collective-permute-done.1.refs_2_ = bf16[256,256]{1,0:T(8,128)(2,1)S(1)} collective-permute-done((bf16[256,256]{1,0:T(8,128)(2,1)}, bf16[256,256]{1,0:T(8,128)(2,1)S(1)}, u32[]{:S(2)}, u32[]{:S(2)}) %collective-permute-start.1) | collective-permute-done | bytes 131104 | tf_op jit(solution)/shard_map/ppermute | solution.py:213
  21.1 4.4 %collective-permute-start.6 = (bf16[1024,256]{1,0:T(8,128)(2,1)S(1)}, bf16[1024,256]{1,0:T(8,128)(2,1)S(1)}, u32[]{:S(2)}, u32[]{:S(2)}) collective-permute-start(bf16[1024,256]{1,0:T(8,128)(2,1)S(1)} %shard_map.150.refs_0_), channel_id=1, source_target_pairs={{0,1},{1,2},{2,3},{3,4},{4,5},{5,6},{6,7},{7,0},{8,9},{9,10},{10,1... | collective-permute-start | bytes 1572872 | tf_op jit(solution)/shard_map/ppermute | solution.py:213
  25.5 8.6 %collective-permute-start.3 = (bf16[1024,256]{1,0:T(8,128)(2,1)S(1)}, bf16[1024,256]{1,0:T(8,128)(2,1)S(1)}, u32[]{:S(2)}, u32[]{:S(2)}) collective-permute-start(bf16[1024,256]{1,0:T(8,128)(2,1)S(1)} %shard_map.150.refs_0_), channel_id=1, source_target_pairs={{0,7},{1,0},{2,1},{3,2},{4,3},{5,4},{6,5},{7,6},{8,15},{9,8},{10,9... | collective-permute-start | bytes 1572872 | tf_op jit(solution)/shard_map/ppermute | solution.py:213
  34.1 2.4 %collective-permute-start.7 = (bf16[144,256]{1,0:T(8,128)(2,1)S(1)}, bf16[144,256]{1,0:T(8,128)(2,1)S(1)}, u32[]{:S(2)}, u32[]{:S(2)}) collective-permute-start(bf16[144,256]{1,0:T(8,128)(2,1)S(1)} %copy-done.14), channel_id=1, source_target_pairs={{0,24},{8,0},{16,8},{24,16},{1,25},{9,1},{17,9},{25,17},{2,26},{10... | collective-permute-start | bytes 221192 | tf_op jit(solution)/shard_map/ppermute | solution.py:213
  36.5 5.7 %collective-permute-done.7.refs_3_ = bf16[144,256]{1,0:T(8,128)(2,1)S(1)} collective-permute-done((bf16[144,256]{1,0:T(8,128)(2,1)S(1)}, bf16[144,256]{1,0:T(8,128)(2,1)S(1)}, u32[]{:S(2)}, u32[]{:S(2)}) %collective-permute-start.7) | collective-permute-done | bytes 73760 | tf_op jit(solution)/shard_map/ppermute | solution.py:213
  42.1 2.1 %collective-permute-done.6.refs_0_ = bf16[1024,256]{1,0:T(8,128)(2,1)S(1)} collective-permute-done((bf16[1024,256]{1,0:T(8,128)(2,1)S(1)}, bf16[1024,256]{1,0:T(8,128)(2,1)S(1)}, u32[]{:S(2)}, u32[]{:S(2)}) %collective-permute-start.6) | collective-permute-done | bytes 524320 | tf_op jit(solution)/shard_map/ppermute | solution.py:213
  46.2 2.3 %collective-permute-start.4 = (bf16[144,256]{1,0:T(8,128)(2,1)S(1)}, bf16[144,256]{1,0:T(8,128)(2,1)S(1)}, u32[]{:S(2)}, u32[]{:S(2)}) collective-permute-start(bf16[144,256]{1,0:T(8,128)(2,1)S(1)} %copy-done.13), channel_id=1, source_target_pairs={{0,8},{8,16},{16,24},{24,0},{1,9},{9,17},{17,25},{25,1},{2,10},{10... | collective-permute-start | bytes 221192 | tf_op jit(solution)/shard_map/ppermute | solution.py:213
  48.5 3.9 %collective-permute-done.4.refs_1_ = bf16[144,256]{1,0:T(8,128)(2,1)S(1)} collective-permute-done((bf16[144,256]{1,0:T(8,128)(2,1)S(1)}, bf16[144,256]{1,0:T(8,128)(2,1)S(1)}, u32[]{:S(2)}, u32[]{:S(2)}) %collective-permute-start.4) | collective-permute-done | bytes 73760 | tf_op jit(solution)/shard_map/ppermute | solution.py:213
  52.4 5.1 %collective-permute-start.11 = (bf16[1024,256]{1,0:T(8,128)(2,1)S(1)}, bf16[1024,256]{1,0:T(8,128)(2,1)S(1)}, u32[]{:S(2)}, u32[]{:S(2)}) collective-permute-start(bf16[1024,256]{1,0:T(8,128)(2,1)S(1)} %collective-permute-done.3.refs_1_), channel_id=1, source_target_pairs={{0,7},{1,0},{2,1},{3,2},{4,3},{5,4},{6,5},{7,6},{8,15},{9,8},{10,9... | collective-permute-start | bytes 1572872 | tf_op jit(solution)/shard_map/ppermute | solution.py:213
  57.5 3.1 %collective-permute-done.8.refs_0_ = bf16[1024,256]{1,0:T(8,128)(2,1)S(1)} collective-permute-done((bf16[1024,256]{1,0:T(8,128)(2,1)S(1)}, bf16[1024,256]{1,0:T(8,128)(2,1)S(1)}, u32[]{:S(2)}, u32[]{:S(2)}) %collective-permute-start.8) | collective-permute-done | bytes 524320 | tf_op jit(solution)/shard_map/ppermute | solution.py:213
  62.6 4.2 %collective-permute-start.5 = (bf16[144,256]{1,0:T(8,128)(2,1)}, bf16[144,256]{1,0:T(8,128)(2,1)S(1)}, u32[]{:S(2)}, u32[]{:S(2)}) collective-permute-start(bf16[144,256]{1,0:T(8,128)(2,1)} %get-tuple-element.23), channel_id=1, source_target_pairs={{0,16},{8,24},{16,0},{24,8},{1,17},{9,25},{17,1},{25,9},{2,18},{10... | collective-permute-start | bytes 221192 | tf_op jit(solution)/shard_map/ppermute | solution.py:213
  67.7 2.9 %collective-permute-done.5.refs_2_ = bf16[144,256]{1,0:T(8,128)(2,1)S(1)} collective-permute-done((bf16[144,256]{1,0:T(8,128)(2,1)}, bf16[144,256]{1,0:T(8,128)(2,1)S(1)}, u32[]{:S(2)}, u32[]{:S(2)}) %collective-permute-start.5) | collective-permute-done | bytes 73760 | tf_op jit(solution)/shard_map/ppermute | solution.py:213
  70.7 2.2 %attend.5.refs_2_ = f32[1152,128]{1,0:T(8,128)S(1)} custom-call(s32[5]{0:T(128)S(1)} %pad_add_fusion.info_ref, bf16[1152,128]{1,0:T(8,128)(2,1)S(1)} %shard_map.151.qs, s32[128,1]{1,0:T(8,128)S(1)} %reshape.22.user_ref, bf16[1024,256]{1,0:T(8,128)(2,1)S(1)} %shard_map.150.refs_0_), custom_call_target="tpu_custom_call" | custom-call | flops 603979776 | bytes 1048576 | tf_op jit(solution)/shard_map/attend/pallas_call | solution.py:164
  72.9 5.1 %collective-permute-start.12 = (bf16[1024,256]{1,0:T(8,128)(2,1)S(1)}, bf16[1024,256]{1,0:T(8,128)(2,1)S(1)}, u32[]{:S(2)}, u32[]{:S(2)}) collective-permute-start(bf16[1024,256]{1,0:T(8,128)(2,1)S(1)} %collective-permute-done.11.refs_1_), channel_id=1, source_target_pairs={{0,7},{1,0},{2,1},{3,2},{4,3},{5,4},{6,5},{7,6},{8,15},{9,8},{10,9... | collective-permute-start | bytes 1572872 | tf_op jit(solution)/shard_map/ppermute | solution.py:213
  78.0 1.9 %collective-permute-start.10 = (bf16[1024,256]{1,0:T(8,128)(2,1)S(1)}, bf16[1024,256]{1,0:T(8,128)(2,1)S(1)}, u32[]{:S(2)}, u32[]{:S(2)}) collective-permute-start(bf16[1024,256]{1,0:T(8,128)(2,1)S(1)} %collective-permute-done.9.refs_0_), channel_id=1, source_target_pairs={{0,1},{1,2},{2,3},{3,4},{4,5},{5,6},{6,7},{7,0},{8,9},{9,10},{10,1... | collective-permute-start | bytes 1572872 | tf_op jit(solution)/shard_map/ppermute | solution.py:213
  80.0 2.4 %attend.6.refs_2_ = f32[1152,128]{1,0:T(8,128)S(1)} custom-call(s32[5]{0:T(128)S(1)} %pad_add_fusion.info_ref, bf16[1152,128]{1,0:T(8,128)(2,1)S(1)} %shard_map.151.qs, s32[128,1]{1,0:T(8,128)S(1)} %reshape.22.user_ref, bf16[1024,256]{1,0:T(8,128)(2,1)S(1)} %collective-permute-done.6.refs_0_, bf16[1024,256]{1,0:T(8,128)(2,1)S(1)} %collective-permute-done.3.refs_1_, ...), custom_call_target="tpu_custom_call" | custom-call | flops 1207959552 | bytes 1048576 | tf_op jit(solution)/shard_map/attend/pallas_call | solution.py:164
  82.4 2.4 %attend.7.refs_2_ = f32[1152,128]{1,0:T(8,128)S(1)} custom-call(s32[5]{0:T(128)S(1)} %pad_add_fusion.info_ref, bf16[1152,128]{1,0:T(8,128)(2,1)S(1)} %shard_map.151.qs, s32[128,1]{1,0:T(8,128)S(1)} %reshape.22.user_ref, bf16[1024,256]{1,0:T(8,128)(2,1)S(1)} %collective-permute-done.8.refs_0_, bf16[1024,256]{1,0:T(8,128)(2,1)S(1)} %collective-permute-done.11.refs_1_, ...), custom_call_target="tpu_custom_call" | custom-call | flops 1207959552 | bytes 1048576 | tf_op jit(solution)/shard_map/attend/pallas_call | solution.py:164
  86.5 2.4 %attend.8.refs_1_ = f32[1152,128]{1,0:T(8,128)S(1)} custom-call(s32[5]{0:T(128)S(1)} %pad_add_fusion.info_ref, bf16[1152,128]{1,0:T(8,128)(2,1)S(1)} %shard_map.151.qs, s32[128,1]{1,0:T(8,128)S(1)} %reshape.22.user_ref, bf16[1024,256]{1,0:T(8,128)(2,1)S(1)} %collective-permute-done.9.refs_0_, bf16[1024,256]{1,0:T(8,128)(2,1)S(1)} %collective-permute-done.12.refs_1_, ...), custom_call_target="tpu_custom_call" | custom-call | flops 1207959552 | bytes 1048576 | tf_op jit(solution)/shard_map/attend/pallas_call | solution.py:164
  89.0 2.9 %collective-permute-done.10.refs_0_ = bf16[1024,256]{1,0:T(8,128)(2,1)S(1)} collective-permute-done((bf16[1024,256]{1,0:T(8,128)(2,1)S(1)}, bf16[1024,256]{1,0:T(8,128)(2,1)S(1)}, u32[]{:S(2)}, u32[]{:S(2)}) %collective-permute-start.10) | collective-permute-done | bytes 524320 | tf_op jit(solution)/shard_map/ppermute | solution.py:213
  93.5 10.3 %all_to_all.11 = bf16[4,144,256]{2,1,0:T(8,128)(2,1)S(1)} all-to-all(bf16[4,144,256]{2,1,0:T(8,128)(2,1)S(1)} %bitcast.5), channel_id=1, replica_groups=mesh['batch'=16,'y'=4,'z'=8] {'y'}, dimensions={0} | all-to-all | bytes 589824 | tf_op jit(solution)/shard_map/all_to_all | solution.py:245
  (46 shorter events, 10.6 us)
Async XLA Ops:
  2.8 9.9 %collective-permute-start = (bf16[256,256]{1,0:T(8,128)(2,1)}, bf16[256,256]{1,0:T(8,128)(2,1)S(1)}, u32[]{:S(2)}, u32[]{:S(2)}) collective-permute-start(bf16[256,256]{1,0:T(8,128)(2,1)} %get-tuple-element.18), channel_id=1, source_target_pairs={{0,8},{8,16},{16,24},{24,0},{1,9},{9,17},{17,25},{25,1},{2,10},{10... | collective-permute-start | bytes 393224 | tf_op jit(solution)/shard_map/ppermute | solution.py:213
  7.6 12.5 %collective-permute-start.1 = (bf16[256,256]{1,0:T(8,128)(2,1)}, bf16[256,256]{1,0:T(8,128)(2,1)S(1)}, u32[]{:S(2)}, u32[]{:S(2)}) collective-permute-start(bf16[256,256]{1,0:T(8,128)(2,1)} %get-tuple-element.19), channel_id=1, source_target_pairs={{0,16},{8,24},{16,0},{24,8},{1,17},{9,25},{17,1},{25,9},{2,18},{10... | collective-permute-start | bytes 393224 | tf_op jit(solution)/shard_map/ppermute | solution.py:213
  9.5 10.6 %collective-permute-start.2 = (bf16[256,256]{1,0:T(8,128)(2,1)}, bf16[256,256]{1,0:T(8,128)(2,1)S(1)}, u32[]{:S(2)}, u32[]{:S(2)}) collective-permute-start(bf16[256,256]{1,0:T(8,128)(2,1)} %get-tuple-element.20), channel_id=1, source_target_pairs={{0,24},{8,0},{16,8},{24,16},{1,25},{9,1},{17,9},{25,17},{2,26},{10... | collective-permute-start | bytes 393224 | tf_op jit(solution)/shard_map/ppermute | solution.py:213
  21.0 13.1 %copy-start.14 = (bf16[144,256]{1,0:T(8,128)(2,1)S(1)}, bf16[144,256]{1,0:T(8,128)(2,1)}, u32[]{:S(2)}) copy-start(bf16[144,256]{1,0:T(8,128)(2,1)} %get-tuple-element.24) | copy-start | bytes 221188
  21.0 25.2 %copy-start.13 = (bf16[144,256]{1,0:T(8,128)(2,1)S(1)}, bf16[144,256]{1,0:T(8,128)(2,1)}, u32[]{:S(2)}) copy-start(bf16[144,256]{1,0:T(8,128)(2,1)} %get-tuple-element.21) | copy-start | bytes 221188
  21.0 45.8 %copy-start.10 = (s32[1024]{0:T(1024)S(1)}, s32[1024]{0:T(1024)}, u32[]{:S(2)}) copy-start(s32[1024]{0:T(1024)} %param.24) | copy-start | bytes 12292
  21.1 49.6 %copy-start.5 = (bf16[144,256]{1,0:T(8,128)(2,1)S(1)}, bf16[144,256]{1,0:T(8,128)(2,1)}, u32[]{:S(2)}) copy-start(bf16[144,256]{1,0:T(8,128)(2,1)} %get-tuple-element.16.refs_0_) | copy-start | bytes 221188
  21.1 23.2 %collective-permute-start.6 = (bf16[1024,256]{1,0:T(8,128)(2,1)S(1)}, bf16[1024,256]{1,0:T(8,128)(2,1)S(1)}, u32[]{:S(2)}, u32[]{:S(2)}) collective-permute-start(bf16[1024,256]{1,0:T(8,128)(2,1)S(1)} %shard_map.150.refs_0_), channel_id=1, source_target_pairs={{0,1},{1,2},{2,3},{3,4},{4,5},{5,6},{6,7},{7,0},{8,9},{9,10},{10,1... | collective-permute-start | bytes 1572872 | tf_op jit(solution)/shard_map/ppermute | solution.py:213
  25.5 26.9 %collective-permute-start.3 = (bf16[1024,256]{1,0:T(8,128)(2,1)S(1)}, bf16[1024,256]{1,0:T(8,128)(2,1)S(1)}, u32[]{:S(2)}, u32[]{:S(2)}) collective-permute-start(bf16[1024,256]{1,0:T(8,128)(2,1)S(1)} %shard_map.150.refs_0_), channel_id=1, source_target_pairs={{0,7},{1,0},{2,1},{3,2},{4,3},{5,4},{6,5},{7,6},{8,15},{9,8},{10,9... | collective-permute-start | bytes 1572872 | tf_op jit(solution)/shard_map/ppermute | solution.py:213
  34.1 8.0 %collective-permute-start.7 = (bf16[144,256]{1,0:T(8,128)(2,1)S(1)}, bf16[144,256]{1,0:T(8,128)(2,1)S(1)}, u32[]{:S(2)}, u32[]{:S(2)}) collective-permute-start(bf16[144,256]{1,0:T(8,128)(2,1)S(1)} %copy-done.14), channel_id=1, source_target_pairs={{0,24},{8,0},{16,8},{24,16},{1,25},{9,1},{17,9},{25,17},{2,26},{10... | collective-permute-start | bytes 221192 | tf_op jit(solution)/shard_map/ppermute | solution.py:213
  44.2 16.4 %collective-permute-start.8 = (bf16[1024,256]{1,0:T(8,128)(2,1)S(1)}, bf16[1024,256]{1,0:T(8,128)(2,1)S(1)}, u32[]{:S(2)}, u32[]{:S(2)}) collective-permute-start(bf16[1024,256]{1,0:T(8,128)(2,1)S(1)} %collective-permute-done.6.refs_0_), channel_id=1, source_target_pairs={{0,1},{1,2},{2,3},{3,4},{4,5},{5,6},{6,7},{7,0},{8,9},{9,10},{10,1... | collective-permute-start | bytes 1572872 | tf_op jit(solution)/shard_map/ppermute | solution.py:213
  46.2 6.2 %collective-permute-start.4 = (bf16[144,256]{1,0:T(8,128)(2,1)S(1)}, bf16[144,256]{1,0:T(8,128)(2,1)S(1)}, u32[]{:S(2)}, u32[]{:S(2)}) collective-permute-start(bf16[144,256]{1,0:T(8,128)(2,1)S(1)} %copy-done.13), channel_id=1, source_target_pairs={{0,8},{8,16},{16,24},{24,0},{1,9},{9,17},{17,25},{25,1},{2,10},{10... | collective-permute-start | bytes 221192 | tf_op jit(solution)/shard_map/ppermute | solution.py:213
  52.4 20.4 %collective-permute-start.11 = (bf16[1024,256]{1,0:T(8,128)(2,1)S(1)}, bf16[1024,256]{1,0:T(8,128)(2,1)S(1)}, u32[]{:S(2)}, u32[]{:S(2)}) collective-permute-start(bf16[1024,256]{1,0:T(8,128)(2,1)S(1)} %collective-permute-done.3.refs_1_), channel_id=1, source_target_pairs={{0,7},{1,0},{2,1},{3,2},{4,3},{5,4},{6,5},{7,6},{8,15},{9,8},{10,9... | collective-permute-start | bytes 1572872 | tf_op jit(solution)/shard_map/ppermute | solution.py:213
  60.7 17.4 %collective-permute-start.9 = (bf16[1024,256]{1,0:T(8,128)(2,1)S(1)}, bf16[1024,256]{1,0:T(8,128)(2,1)S(1)}, u32[]{:S(2)}, u32[]{:S(2)}) collective-permute-start(bf16[1024,256]{1,0:T(8,128)(2,1)S(1)} %collective-permute-done.8.refs_0_), channel_id=1, source_target_pairs={{0,1},{1,2},{2,3},{3,4},{4,5},{5,6},{6,7},{7,0},{8,9},{9,10},{10,1... | collective-permute-start | bytes 1572872 | tf_op jit(solution)/shard_map/ppermute | solution.py:213
  62.6 8.1 %collective-permute-start.5 = (bf16[144,256]{1,0:T(8,128)(2,1)}, bf16[144,256]{1,0:T(8,128)(2,1)S(1)}, u32[]{:S(2)}, u32[]{:S(2)}) collective-permute-start(bf16[144,256]{1,0:T(8,128)(2,1)} %get-tuple-element.23), channel_id=1, source_target_pairs={{0,16},{8,24},{16,0},{24,8},{1,17},{9,25},{17,1},{25,9},{2,18},{10... | collective-permute-start | bytes 221192 | tf_op jit(solution)/shard_map/ppermute | solution.py:213
  72.9 13.6 %collective-permute-start.12 = (bf16[1024,256]{1,0:T(8,128)(2,1)S(1)}, bf16[1024,256]{1,0:T(8,128)(2,1)S(1)}, u32[]{:S(2)}, u32[]{:S(2)}) collective-permute-start(bf16[1024,256]{1,0:T(8,128)(2,1)S(1)} %collective-permute-done.11.refs_1_), channel_id=1, source_target_pairs={{0,7},{1,0},{2,1},{3,2},{4,3},{5,4},{6,5},{7,6},{8,15},{9,8},{10,9... | collective-permute-start | bytes 1572872 | tf_op jit(solution)/shard_map/ppermute | solution.py:213
  78.0 13.8 %collective-permute-start.10 = (bf16[1024,256]{1,0:T(8,128)(2,1)S(1)}, bf16[1024,256]{1,0:T(8,128)(2,1)S(1)}, u32[]{:S(2)}, u32[]{:S(2)}) collective-permute-start(bf16[1024,256]{1,0:T(8,128)(2,1)S(1)} %collective-permute-done.9.refs_0_), channel_id=1, source_target_pairs={{0,1},{1,2},{2,3},{3,4},{4,5},{5,6},{6,7},{7,0},{8,9},{9,10},{10,1... | collective-permute-start | bytes 1572872 | tf_op jit(solution)/shard_map/ppermute | solution.py:213
  89.0 14.8 %copy-start = (bf16[512,1024]{1,0:T(8,128)(2,1)S(1)}, bf16[512,1024]{1,0:T(8,128)(2,1)}, u32[]{:S(2)}) copy-start(bf16[512,1024]{1,0:T(8,128)(2,1)} %w_ref.1) | copy-start | bytes 3145732
  91.9 11.9 %copy-start.2 = (bf16[256,512]{1,0:T(8,128)(2,1)S(1)}, bf16[256,512]{1,0:T(8,128)(2,1)}, u32[]{:S(2)}) copy-start(bf16[256,512]{1,0:T(8,128)(2,1)} %hg.1) | copy-start | bytes 786436
  91.9 11.9 %copy-start.6 = (bf16[32,1024]{1,0:T(8,128)(2,1)S(1)}, bf16[32,1024]{1,0:T(8,128)(2,1)}, u32[]{:S(2)}) copy-start(bf16[32,1024]{1,0:T(8,128)(2,1)} %cx.1) | copy-start | bytes 196612
  91.9 11.9 %copy-start.8 = (bf16[32,512]{1,0:T(8,128)(2,1)S(1)}, bf16[32,512]{1,0:T(8,128)(2,1)}, u32[]{:S(2)}) copy-start(bf16[32,512]{1,0:T(8,128)(2,1)} %cv.1) | copy-start | bytes 98308
  91.9 11.9 %copy-start.9 = (bf16[32,512]{1,0:T(8,128)(2,1)S(1)}, bf16[32,512]{1,0:T(8,128)(2,1)}, u32[]{:S(2)}) copy-start(bf16[32,512]{1,0:T(8,128)(2,1)} %cg.1) | copy-start | bytes 98308
  93.4 10.4 %copy-start.1 = (bf16[256,1024]{1,0:T(8,128)(2,1)S(1)}, bf16[256,1024]{1,0:T(8,128)(2,1)}, u32[]{:S(2)}) copy-start(bf16[256,1024]{1,0:T(8,128)(2,1)} %hx.1) | copy-start | bytes 1572868
  93.5 10.4 %copy-start.3 = (bf16[32,512]{1,0:T(8,128)(2,1)S(1)}, bf16[32,512]{1,0:T(8,128)(2,1)}, u32[]{:S(2)}) copy-start(bf16[32,512]{1,0:T(8,128)(2,1)} %cq.1) | copy-start | bytes 98308
  (4 other events, 12.6 us)

commit v14 on v13

--- a/solution.py
+++ b/solution.py
@@ -233,12 +233,11 @@
     up1, folds[3] = lax.optimization_barrier((up1, folds[3]))
     down1, folds[1] = lax.optimization_barrier((down1, folds[1]))
     up2, down2 = turn(up1, "z", 1), turn(down1, "z", -1)
+    down2, folds[2] = lax.optimization_barrier((down2, folds[2]))
     (queries,) = call(unfold_kernel, [(TOTAL, DH)], *folds, place=y)
-    total = attend((0,), info, queries, users, (own,), None)
-    down2, total = lax.optimization_barrier((down2, total))
     up3, down3 = turn(up2, "z", 1), turn(down2, "z", -1)
     across = turn(up3, "z", 1)
-    total = attend((NZ - 1, 1), info, queries, users, (up1, down1), total)
+    total = attend((0, NZ - 1, 1), info, queries, users, (own, up1, down1), None)
     total = attend((NZ - 2, 2), info, queries, users, (up2, down2), total)
     total = attend((NZ - 3, 3), info, queries, users, (up3, down3), total)
     total = attend((4,), info, queries, users, (across,), total, last=True)

time: 106 us -> 106 us (level)
    pallas_call x5 -> x4, Pallas kernels: 11 us -> 11.5 us  [attend(): pl.pallas_call(functools.partial(attend_kernel, offsets, first, last), in...]
where the time goes in v14:
time: 106 us; the launch traced here: 105 us
  starting transfers between devices  47.7 us (45%)
  waiting for transfers between devices  28.8 us (27%)
  Pallas kernels  15.2 us (14%)
  blocking collectives  10.3 us (10%)
  local copies, waits for them, and re-layouts  1.83 us (2%)
    ppermute x13, starting transfers between devices, turn(): lax.ppermute(array, axis, [(i, (i + step) % count) for i in range(count)])  47.7 us
    ppermute x13, waiting for transfers between devices, turn(): lax.ppermute(array, axis, [(i, (i + step) % count) for i in range(count)])  28.8 us
    pallas_call x4, Pallas kernels, attend(): pl.pallas_call(functools.partial(attend_kernel, offsets, first, last), in...  11.5 us
    all_to_all x1, blocking collectives, on_device(): total = lax.all_to_all(total, 'y', 0, 0, tiled=True)  10.3 us
    pallas_call x4, Pallas kernels, call(): pl.pallas_call(kernel, in_specs=[SMEM] * (place is not None) + [VMEM] * (...  3.76 us
  transfers between devices with their start and end apart: 13, of which 8 were waited for; matrix products, arithmetic and copies ran while one was open for 0% of the time, Pallas kernels for 9%

profile of v14, /device:TPU:56, one launch (start us, length us, event | category | flops | bytes accessed | tf_op | source)
XLA Modules:
  0.0 104.9 jit_solution(1654561934691531770)
XLA Ops:
  0.6 2.1 %shard_map.149 = (bf16[256,256]{1,0:T(8,128)(2,1)}, bf16[256,256]{1,0:T(8,128)(2,1)}, bf16[256,256]{1,0:T(8,128)(2,1)}, bf16[256,256]{1,0:T(8,128)(2,1)}, bf16[1...) custom-call(s32[1]{0:T(128)} %bitcast.1.y_ref, ...), custom_call_target="tpu_custom_call" | custom-call | tf_op jit(solution)/shard_map/pallas_call | solution.py:201
  2.8 4.8 %collective-permute-start = (bf16[256,256]{1,0:T(8,128)(2,1)}, bf16[256,256]{1,0:T(8,128)(2,1)S(1)}, u32[]{:S(2)}, u32[]{:S(2)}) collective-permute-start(bf16[256,256]{1,0:T(8,128)(2,1)} %get-tuple-element.18), channel_id=1, source_target_pairs={{0,8},{8,16},{16,24},{24,0},{1,9},{9,17},{17,25},{25,1},{2,10},{10... | collective-permute-start | bytes 393224 | tf_op jit(solution)/shard_map/ppermute | solution.py:213
  7.6 1.9 %collective-permute-start.1 = (bf16[256,256]{1,0:T(8,128)(2,1)}, bf16[256,256]{1,0:T(8,128)(2,1)S(1)}, u32[]{:S(2)}, u32[]{:S(2)}) collective-permute-start(bf16[256,256]{1,0:T(8,128)(2,1)} %get-tuple-element.19), channel_id=1, source_target_pairs={{0,16},{8,24},{16,0},{24,8},{1,17},{9,25},{17,1},{25,9},{2,18},{10... | collective-permute-start | bytes 393224 | tf_op jit(solution)/shard_map/ppermute | solution.py:213
  9.5 3.1 %collective-permute-start.2 = (bf16[256,256]{1,0:T(8,128)(2,1)}, bf16[256,256]{1,0:T(8,128)(2,1)S(1)}, u32[]{:S(2)}, u32[]{:S(2)}) collective-permute-start(bf16[256,256]{1,0:T(8,128)(2,1)} %get-tuple-element.20), channel_id=1, source_target_pairs={{0,24},{8,0},{16,8},{24,16},{1,25},{9,1},{17,9},{25,17},{2,26},{10... | collective-permute-start | bytes 393224 | tf_op jit(solution)/shard_map/ppermute | solution.py:213
  12.7 7.4 %collective-permute-done.1.refs_2_ = bf16[256,256]{1,0:T(8,128)(2,1)S(1)} collective-permute-done((bf16[256,256]{1,0:T(8,128)(2,1)}, bf16[256,256]{1,0:T(8,128)(2,1)S(1)}, u32[]{:S(2)}, u32[]{:S(2)}) %collective-permute-start.1) | collective-permute-done | bytes 131104 | tf_op jit(solution)/shard_map/ppermute | solution.py:213
  21.1 4.4 %collective-permute-start.7 = (bf16[1024,256]{1,0:T(8,128)(2,1)S(1)}, bf16[1024,256]{1,0:T(8,128)(2,1)S(1)}, u32[]{:S(2)}, u32[]{:S(2)}) collective-permute-start(bf16[1024,256]{1,0:T(8,128)(2,1)S(1)} %shard_map.150.refs_0_), channel_id=1, source_target_pairs={{0,1},{1,2},{2,3},{3,4},{4,5},{5,6},{6,7},{7,0},{8,9},{9,10},{10,1... | collective-permute-start | bytes 1572872 | tf_op jit(solution)/shard_map/ppermute | solution.py:213
  25.5 8.6 %collective-permute-start.3 = (bf16[1024,256]{1,0:T(8,128)(2,1)S(1)}, bf16[1024,256]{1,0:T(8,128)(2,1)S(1)}, u32[]{:S(2)}, u32[]{:S(2)}) collective-permute-start(bf16[1024,256]{1,0:T(8,128)(2,1)S(1)} %shard_map.150.refs_0_), channel_id=1, source_target_pairs={{0,7},{1,0},{2,1},{3,2},{4,3},{5,4},{6,5},{7,6},{8,15},{9,8},{10,9... | collective-permute-start | bytes 1572872 | tf_op jit(solution)/shard_map/ppermute | solution.py:213
  34.1 2.4 %collective-permute-start.8 = (bf16[144,256]{1,0:T(8,128)(2,1)S(1)}, bf16[144,256]{1,0:T(8,128)(2,1)S(1)}, u32[]{:S(2)}, u32[]{:S(2)}) collective-permute-start(bf16[144,256]{1,0:T(8,128)(2,1)S(1)} %copy-done.15), channel_id=1, source_target_pairs={{0,24},{8,0},{16,8},{24,16},{1,25},{9,1},{17,9},{25,17},{2,26},{10... | collective-permute-start | bytes 221192 | tf_op jit(solution)/shard_map/ppermute | solution.py:213
  36.5 5.7 %collective-permute-done.8.refs_3_ = bf16[144,256]{1,0:T(8,128)(2,1)S(1)} collective-permute-done((bf16[144,256]{1,0:T(8,128)(2,1)S(1)}, bf16[144,256]{1,0:T(8,128)(2,1)S(1)}, u32[]{:S(2)}, u32[]{:S(2)}) %collective-permute-start.8) | collective-permute-done | bytes 73760 | tf_op jit(solution)/shard_map/ppermute | solution.py:213
  42.1 2.1 %collective-permute-done.7.refs_1_ = bf16[1024,256]{1,0:T(8,128)(2,1)S(1)} collective-permute-done((bf16[1024,256]{1,0:T(8,128)(2,1)S(1)}, bf16[1024,256]{1,0:T(8,128)(2,1)S(1)}, u32[]{:S(2)}, u32[]{:S(2)}) %collective-permute-start.7) | collective-permute-done | bytes 524320 | tf_op jit(solution)/shard_map/ppermute | solution.py:213
  46.2 2.3 %collective-permute-start.4 = (bf16[144,256]{1,0:T(8,128)(2,1)S(1)}, bf16[144,256]{1,0:T(8,128)(2,1)S(1)}, u32[]{:S(2)}, u32[]{:S(2)}) collective-permute-start(bf16[144,256]{1,0:T(8,128)(2,1)S(1)} %copy-done.14), channel_id=1, source_target_pairs={{0,8},{8,16},{16,24},{24,0},{1,9},{9,17},{17,25},{25,1},{2,10},{10... | collective-permute-start | bytes 221192 | tf_op jit(solution)/shard_map/ppermute | solution.py:213
  48.5 3.9 %collective-permute-done.4.refs_1_ = bf16[144,256]{1,0:T(8,128)(2,1)S(1)} collective-permute-done((bf16[144,256]{1,0:T(8,128)(2,1)S(1)}, bf16[144,256]{1,0:T(8,128)(2,1)S(1)}, u32[]{:S(2)}, u32[]{:S(2)}) %collective-permute-start.4) | collective-permute-done | bytes 73760 | tf_op jit(solution)/shard_map/ppermute | solution.py:213
  52.4 5.1 %collective-permute-start.5 = (bf16[1024,256]{1,0:T(8,128)(2,1)S(1)}, bf16[1024,256]{1,0:T(8,128)(2,1)S(1)}, u32[]{:S(2)}, u32[]{:S(2)}) collective-permute-start(bf16[1024,256]{1,0:T(8,128)(2,1)S(1)} %collective-permute-done.3.refs_2_), channel_id=1, source_target_pairs={{0,7},{1,0},{2,1},{3,2},{4,3},{5,4},{6,5},{7,6},{8,15},{9,8},{10,9... | collective-permute-start | bytes 1572872 | tf_op jit(solution)/shard_map/ppermute | solution.py:213
  57.6 3.1 %collective-permute-done.9.refs_0_ = bf16[1024,256]{1,0:T(8,128)(2,1)S(1)} collective-permute-done((bf16[1024,256]{1,0:T(8,128)(2,1)S(1)}, bf16[1024,256]{1,0:T(8,128)(2,1)S(1)}, u32[]{:S(2)}, u32[]{:S(2)}) %collective-permute-start.9) | collective-permute-done | bytes 524320 | tf_op jit(solution)/shard_map/ppermute | solution.py:213
  62.6 4.2 %collective-permute-start.6 = (bf16[144,256]{1,0:T(8,128)(2,1)S(1)}, bf16[144,256]{1,0:T(8,128)(2,1)S(1)}, u32[]{:S(2)}, u32[]{:S(2)}) collective-permute-start(bf16[144,256]{1,0:T(8,128)(2,1)S(1)} %copy-done.13), channel_id=1, source_target_pairs={{0,16},{8,24},{16,0},{24,8},{1,17},{9,25},{17,1},{25,9},{2,18},{10... | collective-permute-start | bytes 221192 | tf_op jit(solution)/shard_map/ppermute | solution.py:213
  66.8 3.6 %collective-permute-done.6.refs_2_ = bf16[144,256]{1,0:T(8,128)(2,1)S(1)} collective-permute-done((bf16[144,256]{1,0:T(8,128)(2,1)S(1)}, bf16[144,256]{1,0:T(8,128)(2,1)S(1)}, u32[]{:S(2)}, u32[]{:S(2)}) %collective-permute-start.6) | collective-permute-done | bytes 73760 | tf_op jit(solution)/shard_map/ppermute | solution.py:213
  70.4 5.1 %collective-permute-start.12 = (bf16[1024,256]{1,0:T(8,128)(2,1)S(1)}, bf16[1024,256]{1,0:T(8,128)(2,1)}, u32[]{:S(2)}, u32[]{:S(2)}) collective-permute-start(bf16[1024,256]{1,0:T(8,128)(2,1)S(1)} %collective-permute-done.5.refs_1_), channel_id=1, source_target_pairs={{0,7},{1,0},{2,1},{3,2},{4,3},{5,4},{6,5},{7,6},{8,15},{9,8},{10,9... | collective-permute-start | bytes 1572872 | tf_op jit(solution)/shard_map/ppermute | solution.py:213
  76.1 1.9 %collective-permute-start.11 = (bf16[1024,256]{1,0:T(8,128)(2,1)S(1)}, bf16[1024,256]{1,0:T(8,128)(2,1)}, u32[]{:S(2)}, u32[]{:S(2)}) collective-permute-start(bf16[1024,256]{1,0:T(8,128)(2,1)S(1)} %collective-permute-done.10.refs_0_), channel_id=1, source_target_pairs={{0,1},{1,2},{2,3},{3,4},{4,5},{5,6},{6,7},{7,0},{8,9},{9,10},{10,1... | collective-permute-start | bytes 1572872 | tf_op jit(solution)/shard_map/ppermute | solution.py:213
  79.1 4.0 %attend.4.refs_2_ = f32[1152,128]{1,0:T(8,128)S(1)} custom-call(s32[5]{0:T(128)S(1)} %pad_add_fusion.info_ref, bf16[1152,128]{1,0:T(8,128)(2,1)S(1)} %shard_map.151.qs, s32[128,1]{1,0:T(8,128)S(1)} %reshape.22.user_ref, bf16[1024,256]{1,0:T(8,128)(2,1)S(1)} %shard_map.150.refs_0_, bf16[1024,256]{1,0:T(8,128)(2,1)S(1)} %collective-permute-done.7.refs_1_, ...), custom_call_target="tpu_custom_call" | custom-call | flops 1811939328 | bytes 1048576 | tf_op jit(solution)/shard_map/attend/pallas_call | solution.py:164
  83.1 2.4 %attend.5.refs_2_ = f32[1152,128]{1,0:T(8,128)S(1)} custom-call(s32[5]{0:T(128)S(1)} %pad_add_fusion.info_ref, bf16[1152,128]{1,0:T(8,128)(2,1)S(1)} %shard_map.151.qs, s32[128,1]{1,0:T(8,128)S(1)} %reshape.22.user_ref, bf16[1024,256]{1,0:T(8,128)(2,1)S(1)} %collective-permute-done.9.refs_0_, bf16[1024,256]{1,0:T(8,128)(2,1)S(1)} %collective-permute-done.5.refs_1_, ...), custom_call_target="tpu_custom_call" | custom-call | flops 1207959552 | bytes 1048576 | tf_op jit(solution)/shard_map/attend/pallas_call | solution.py:164
  85.5 2.9 %attend.6.refs_1_ = f32[1152,128]{1,0:T(8,128)S(1)} custom-call(s32[5]{0:T(128)S(1)} %pad_add_fusion.info_ref, bf16[1152,128]{1,0:T(8,128)(2,1)S(1)} %shard_map.151.qs, s32[128,1]{1,0:T(8,128)S(1)} %reshape.22.user_ref, bf16[1024,256]{1,0:T(8,128)(2,1)S(1)} %collective-permute-done.10.refs_0_, bf16[1024,256]{1,0:T(8,128)(2,1)} %collective-permute-done.12.refs_1_, ...), custom_call_target="tpu_custom_call" | custom-call | flops 1207959552 | bytes 1048576 | tf_op jit(solution)/shard_map/attend/pallas_call | solution.py:164
  88.5 2.3 %collective-permute-done.11.refs_0_ = bf16[1024,256]{1,0:T(8,128)(2,1)} collective-permute-done((bf16[1024,256]{1,0:T(8,128)(2,1)S(1)}, bf16[1024,256]{1,0:T(8,128)(2,1)}, u32[]{:S(2)}, u32[]{:S(2)}) %collective-permute-start.11) | collective-permute-done | bytes 524320 | tf_op jit(solution)/shard_map/ppermute | solution.py:213
  90.8 2.1 %attend.7 = bf16[576,256]{1,0:T(8,128)(2,1)S(1)} custom-call(s32[5]{0:T(128)S(1)} %pad_add_fusion.info_ref, bf16[1152,128]{1,0:T(8,128)(2,1)S(1)} %shard_map.151.qs, s32[128,1]{1,0:T(8,128)S(1)} %reshape.22.user_ref, bf16[1024,256]{1,0:T(8,128)(2,1)} %collective-permute-done.11.refs_0_, f32[1152,128]{1,0:T(8,128)S(1)} %attend.6.refs_1_), custom_call_target="tpu_custom_call" | custom-call | flops 603979776 | bytes 1048576 | tf_op jit(solution)/shard_map/attend/pallas_call | solution.py:164
  93.0 10.3 %all_to_all.11 = bf16[4,144,256]{2,1,0:T(8,128)(2,1)S(1)} all-to-all(bf16[4,144,256]{2,1,0:T(8,128)(2,1)S(1)} %bitcast.5), channel_id=1, replica_groups=mesh['batch'=16,'y'=4,'z'=8] {'y'}, dimensions={0} | all-to-all | bytes 589824 | tf_op jit(solution)/shard_map/all_to_all | solution.py:244
  (47 shorter events, 7.9 us)
Async XLA Ops:
  2.8 9.9 %collective-permute-start = (bf16[256,256]{1,0:T(8,128)(2,1)}, bf16[256,256]{1,0:T(8,128)(2,1)S(1)}, u32[]{:S(2)}, u32[]{:S(2)}) collective-permute-start(bf16[256,256]{1,0:T(8,128)(2,1)} %get-tuple-element.18), channel_id=1, source_target_pairs={{0,8},{8,16},{16,24},{24,0},{1,9},{9,17},{17,25},{25,1},{2,10},{10... | collective-permute-start | bytes 393224 | tf_op jit(solution)/shard_map/ppermute | solution.py:213
  7.6 12.5 %collective-permute-start.1 = (bf16[256,256]{1,0:T(8,128)(2,1)}, bf16[256,256]{1,0:T(8,128)(2,1)S(1)}, u32[]{:S(2)}, u32[]{:S(2)}) collective-permute-start(bf16[256,256]{1,0:T(8,128)(2,1)} %get-tuple-element.19), channel_id=1, source_target_pairs={{0,16},{8,24},{16,0},{24,8},{1,17},{9,25},{17,1},{25,9},{2,18},{10... | collective-permute-start | bytes 393224 | tf_op jit(solution)/shard_map/ppermute | solution.py:213
  9.5 10.6 %collective-permute-start.2 = (bf16[256,256]{1,0:T(8,128)(2,1)}, bf16[256,256]{1,0:T(8,128)(2,1)S(1)}, u32[]{:S(2)}, u32[]{:S(2)}) collective-permute-start(bf16[256,256]{1,0:T(8,128)(2,1)} %get-tuple-element.20), channel_id=1, source_target_pairs={{0,24},{8,0},{16,8},{24,16},{1,25},{9,1},{17,9},{25,17},{2,26},{10... | collective-permute-start | bytes 393224 | tf_op jit(solution)/shard_map/ppermute | solution.py:213
  21.0 13.1 %copy-start.15 = (bf16[144,256]{1,0:T(8,128)(2,1)S(1)}, bf16[144,256]{1,0:T(8,128)(2,1)}, u32[]{:S(2)}) copy-start(bf16[144,256]{1,0:T(8,128)(2,1)} %get-tuple-element.26) | copy-start | bytes 221188
  21.0 25.2 %copy-start.14 = (bf16[144,256]{1,0:T(8,128)(2,1)S(1)}, bf16[144,256]{1,0:T(8,128)(2,1)}, u32[]{:S(2)}) copy-start(bf16[144,256]{1,0:T(8,128)(2,1)} %get-tuple-element.21) | copy-start | bytes 221188
  21.0 41.6 %copy-start.13 = (bf16[144,256]{1,0:T(8,128)(2,1)S(1)}, bf16[144,256]{1,0:T(8,128)(2,1)}, u32[]{:S(2)}) copy-start(bf16[144,256]{1,0:T(8,128)(2,1)} %get-tuple-element.24) | copy-start | bytes 221188
  21.0 57.1 %copy-start.10 = (s32[1024]{0:T(1024)S(1)}, s32[1024]{0:T(1024)}, u32[]{:S(2)}) copy-start(s32[1024]{0:T(1024)} %param.24) | copy-start | bytes 12292
  21.1 58.0 %copy-start.5 = (bf16[144,256]{1,0:T(8,128)(2,1)S(1)}, bf16[144,256]{1,0:T(8,128)(2,1)}, u32[]{:S(2)}) copy-start(bf16[144,256]{1,0:T(8,128)(2,1)} %get-tuple-element.16.refs_0_) | copy-start | bytes 221188
  21.1 23.2 %collective-permute-start.7 = (bf16[1024,256]{1,0:T(8,128)(2,1)S(1)}, bf16[1024,256]{1,0:T(8,128)(2,1)S(1)}, u32[]{:S(2)}, u32[]{:S(2)}) collective-permute-start(bf16[1024,256]{1,0:T(8,128)(2,1)S(1)} %shard_map.150.refs_0_), channel_id=1, source_target_pairs={{0,1},{1,2},{2,3},{3,4},{4,5},{5,6},{6,7},{7,0},{8,9},{9,10},{10,1... | collective-permute-start | bytes 1572872 | tf_op jit(solution)/shard_map/ppermute | solution.py:213
  25.5 26.9 %collective-permute-start.3 = (bf16[1024,256]{1,0:T(8,128)(2,1)S(1)}, bf16[1024,256]{1,0:T(8,128)(2,1)S(1)}, u32[]{:S(2)}, u32[]{:S(2)}) collective-permute-start(bf16[1024,256]{1,0:T(8,128)(2,1)S(1)} %shard_map.150.refs_0_), channel_id=1, source_target_pairs={{0,7},{1,0},{2,1},{3,2},{4,3},{5,4},{6,5},{7,6},{8,15},{9,8},{10,9... | collective-permute-start | bytes 1572872 | tf_op jit(solution)/shard_map/ppermute | solution.py:213
  34.1 8.0 %collective-permute-start.8 = (bf16[144,256]{1,0:T(8,128)(2,1)S(1)}, bf16[144,256]{1,0:T(8,128)(2,1)S(1)}, u32[]{:S(2)}, u32[]{:S(2)}) collective-permute-start(bf16[144,256]{1,0:T(8,128)(2,1)S(1)} %copy-done.15), channel_id=1, source_target_pairs={{0,24},{8,0},{16,8},{24,16},{1,25},{9,1},{17,9},{25,17},{2,26},{10... | collective-permute-start | bytes 221192 | tf_op jit(solution)/shard_map/ppermute | solution.py:213
  44.2 16.4 %collective-permute-start.9 = (bf16[1024,256]{1,0:T(8,128)(2,1)S(1)}, bf16[1024,256]{1,0:T(8,128)(2,1)S(1)}, u32[]{:S(2)}, u32[]{:S(2)}) collective-permute-start(bf16[1024,256]{1,0:T(8,128)(2,1)S(1)} %collective-permute-done.7.refs_1_), channel_id=1, source_target_pairs={{0,1},{1,2},{2,3},{3,4},{4,5},{5,6},{6,7},{7,0},{8,9},{9,10},{10,1... | collective-permute-start | bytes 1572872 | tf_op jit(solution)/shard_map/ppermute | solution.py:213
  46.2 6.2 %collective-permute-start.4 = (bf16[144,256]{1,0:T(8,128)(2,1)S(1)}, bf16[144,256]{1,0:T(8,128)(2,1)S(1)}, u32[]{:S(2)}, u32[]{:S(2)}) collective-permute-start(bf16[144,256]{1,0:T(8,128)(2,1)S(1)} %copy-done.14), channel_id=1, source_target_pairs={{0,8},{8,16},{16,24},{24,0},{1,9},{9,17},{17,25},{25,1},{2,10},{10... | collective-permute-start | bytes 221192 | tf_op jit(solution)/shard_map/ppermute | solution.py:213
  52.4 18.0 %collective-permute-start.5 = (bf16[1024,256]{1,0:T(8,128)(2,1)S(1)}, bf16[1024,256]{1,0:T(8,128)(2,1)S(1)}, u32[]{:S(2)}, u32[]{:S(2)}) collective-permute-start(bf16[1024,256]{1,0:T(8,128)(2,1)S(1)} %collective-permute-done.3.refs_2_), channel_id=1, source_target_pairs={{0,7},{1,0},{2,1},{3,2},{4,3},{5,4},{6,5},{7,6},{8,15},{9,8},{10,9... | collective-permute-start | bytes 1572872 | tf_op jit(solution)/shard_map/ppermute | solution.py:213
  60.7 15.5 %collective-permute-start.10 = (bf16[1024,256]{1,0:T(8,128)(2,1)S(1)}, bf16[1024,256]{1,0:T(8,128)(2,1)S(1)}, u32[]{:S(2)}, u32[]{:S(2)}) collective-permute-start(bf16[1024,256]{1,0:T(8,128)(2,1)S(1)} %collective-permute-done.9.refs_0_), channel_id=1, source_target_pairs={{0,1},{1,2},{2,3},{3,4},{4,5},{5,6},{6,7},{7,0},{8,9},{9,10},{10,1... | collective-permute-start | bytes 1572872 | tf_op jit(solution)/shard_map/ppermute | solution.py:213
  62.6 7.8 %collective-permute-start.6 = (bf16[144,256]{1,0:T(8,128)(2,1)S(1)}, bf16[144,256]{1,0:T(8,128)(2,1)S(1)}, u32[]{:S(2)}, u32[]{:S(2)}) collective-permute-start(bf16[144,256]{1,0:T(8,128)(2,1)S(1)} %copy-done.13), channel_id=1, source_target_pairs={{0,16},{8,24},{16,0},{24,8},{1,17},{9,25},{17,1},{25,9},{2,18},{10... | collective-permute-start | bytes 221192 | tf_op jit(solution)/shard_map/ppermute | solution.py:213
  70.4 15.1 %collective-permute-start.12 = (bf16[1024,256]{1,0:T(8,128)(2,1)S(1)}, bf16[1024,256]{1,0:T(8,128)(2,1)}, u32[]{:S(2)}, u32[]{:S(2)}) collective-permute-start(bf16[1024,256]{1,0:T(8,128)(2,1)S(1)} %collective-permute-done.5.refs_1_), channel_id=1, source_target_pairs={{0,7},{1,0},{2,1},{3,2},{4,3},{5,4},{6,5},{7,6},{8,15},{9,8},{10,9... | collective-permute-start | bytes 1572872 | tf_op jit(solution)/shard_map/ppermute | solution.py:213
  76.1 14.7 %collective-permute-start.11 = (bf16[1024,256]{1,0:T(8,128)(2,1)S(1)}, bf16[1024,256]{1,0:T(8,128)(2,1)}, u32[]{:S(2)}, u32[]{:S(2)}) collective-permute-start(bf16[1024,256]{1,0:T(8,128)(2,1)S(1)} %collective-permute-done.10.refs_0_), channel_id=1, source_target_pairs={{0,1},{1,2},{2,3},{3,4},{4,5},{5,6},{6,7},{7,0},{8,9},{9,10},{10,1... | collective-permute-start | bytes 1572872 | tf_op jit(solution)/shard_map/ppermute | solution.py:213
  88.5 14.8 %copy-start = (bf16[512,1024]{1,0:T(8,128)(2,1)S(1)}, bf16[512,1024]{1,0:T(8,128)(2,1)}, u32[]{:S(2)}) copy-start(bf16[512,1024]{1,0:T(8,128)(2,1)} %w_ref.1) | copy-start | bytes 3145732
  90.8 12.5 %copy-start.2 = (bf16[256,512]{1,0:T(8,128)(2,1)S(1)}, bf16[256,512]{1,0:T(8,128)(2,1)}, u32[]{:S(2)}) copy-start(bf16[256,512]{1,0:T(8,128)(2,1)} %hg.1) | copy-start | bytes 786436
  90.8 12.5 %copy-start.6 = (bf16[32,1024]{1,0:T(8,128)(2,1)S(1)}, bf16[32,1024]{1,0:T(8,128)(2,1)}, u32[]{:S(2)}) copy-start(bf16[32,1024]{1,0:T(8,128)(2,1)} %cx.1) | copy-start | bytes 196612
  90.8 12.5 %copy-start.8 = (bf16[32,512]{1,0:T(8,128)(2,1)S(1)}, bf16[32,512]{1,0:T(8,128)(2,1)}, u32[]{:S(2)}) copy-start(bf16[32,512]{1,0:T(8,128)(2,1)} %cv.1) | copy-start | bytes 98308
  90.8 12.5 %copy-start.9 = (bf16[32,512]{1,0:T(8,128)(2,1)S(1)}, bf16[32,512]{1,0:T(8,128)(2,1)}, u32[]{:S(2)}) copy-start(bf16[32,512]{1,0:T(8,128)(2,1)} %cg.1) | copy-start | bytes 98308
  93.0 10.4 %copy-start.1 = (bf16[256,1024]{1,0:T(8,128)(2,1)S(1)}, bf16[256,1024]{1,0:T(8,128)(2,1)}, u32[]{:S(2)}) copy-start(bf16[256,1024]{1,0:T(8,128)(2,1)} %hx.1) | copy-start | bytes 1572868
  (5 other events, 22.9 us)

commit v15 on v14

--- a/solution.py
+++ b/solution.py
@@ -237,8 +237,7 @@
     (queries,) = call(unfold_kernel, [(TOTAL, DH)], *folds, place=y)
     up3, down3 = turn(up2, "z", 1), turn(down2, "z", -1)
     across = turn(up3, "z", 1)
-    total = attend((0, NZ - 1, 1), info, queries, users, (own, up1, down1), None)
-    total = attend((NZ - 2, 2), info, queries, users, (up2, down2), total)
+    total = attend((0, NZ - 1, 1, NZ - 2, 2), info, queries, users, (own, up1, down1, up2, down2), None)
     total = attend((NZ - 3, 3), info, queries, users, (up3, down3), total)
     total = attend((4,), info, queries, users, (across,), total, last=True)
     total = lax.all_to_all(total, "y", 0, 0, tiled=True)

time: 106 us -> 106 us (level)
    pallas_call x4 -> x3, Pallas kernels: 11.5 us -> 10.9 us  [attend(): pl.pallas_call(functools.partial(attend_kernel, offsets, first, last), in...]
  transfers between devices with their start and end apart: 13 -> 13, of which waited for: 8 -> 8; matrix products, arithmetic and copies ran while one was open for 0% -> 0% of each run, Pallas kernels for 9% -> 8%
where the time goes in v15:
time: 106 us; the launch traced here: 105 us
  starting transfers between devices  47.7 us (45%)
  waiting for transfers between devices  29.4 us (28%)
  Pallas kernels  14.6 us (14%)
  blocking collectives  10.3 us (10%)
  local copies, waits for them, and re-layouts  1.83 us (2%)
    ppermute x13, starting transfers between devices, turn(): lax.ppermute(array, axis, [(i, (i + step) % count) for i in range(count)])  47.7 us
    ppermute x13, waiting for transfers between devices, turn(): lax.ppermute(array, axis, [(i, (i + step) % count) for i in range(count)])  29.4 us
    pallas_call x3, Pallas kernels, attend(): pl.pallas_call(functools.partial(attend_kernel, offsets, first, last), in...  10.9 us
    all_to_all x1, blocking collectives, on_device(): total = lax.all_to_all(total, 'y', 0, 0, tiled=True)  10.3 us
    pallas_call x4, Pallas kernels, call(): pl.pallas_call(kernel, in_specs=[SMEM] * (place is not None) + [VMEM] * (...  3.76 us
  transfers between devices with their start and end apart: 13, of which 8 were waited for; matrix products, arithmetic and copies ran while one was open for 0% of the time, Pallas kernels for 8%

profile of v15, /device:TPU:56, one launch (start us, length us, event | category | flops | bytes accessed | tf_op | source)
XLA Modules:
  0.0 104.9 jit_solution(6714427910548734506)
XLA Ops:
  0.6 2.1 %shard_map.149 = (bf16[256,256]{1,0:T(8,128)(2,1)}, bf16[256,256]{1,0:T(8,128)(2,1)}, bf16[256,256]{1,0:T(8,128)(2,1)}, bf16[256,256]{1,0:T(8,128)(2,1)}, bf16[1...) custom-call(s32[1]{0:T(128)} %bitcast.1.y_ref, ...), custom_call_target="tpu_custom_call" | custom-call | tf_op jit(solution)/shard_map/pallas_call | solution.py:201
  2.8 4.8 %collective-permute-start = (bf16[256,256]{1,0:T(8,128)(2,1)}, bf16[256,256]{1,0:T(8,128)(2,1)S(1)}, u32[]{:S(2)}, u32[]{:S(2)}) collective-permute-start(bf16[256,256]{1,0:T(8,128)(2,1)} %get-tuple-element.18), channel_id=1, source_target_pairs={{0,8},{8,16},{16,24},{24,0},{1,9},{9,17},{17,25},{25,1},{2,10},{10... | collective-permute-start | bytes 393224 | tf_op jit(solution)/shard_map/ppermute | solution.py:213
  7.6 1.9 %collective-permute-start.1 = (bf16[256,256]{1,0:T(8,128)(2,1)}, bf16[256,256]{1,0:T(8,128)(2,1)S(1)}, u32[]{:S(2)}, u32[]{:S(2)}) collective-permute-start(bf16[256,256]{1,0:T(8,128)(2,1)} %get-tuple-element.19), channel_id=1, source_target_pairs={{0,16},{8,24},{16,0},{24,8},{1,17},{9,25},{17,1},{25,9},{2,18},{10... | collective-permute-start | bytes 393224 | tf_op jit(solution)/shard_map/ppermute | solution.py:213
  9.5 3.1 %collective-permute-start.2 = (bf16[256,256]{1,0:T(8,128)(2,1)}, bf16[256,256]{1,0:T(8,128)(2,1)S(1)}, u32[]{:S(2)}, u32[]{:S(2)}) collective-permute-start(bf16[256,256]{1,0:T(8,128)(2,1)} %get-tuple-element.20), channel_id=1, source_target_pairs={{0,24},{8,0},{16,8},{24,16},{1,25},{9,1},{17,9},{25,17},{2,26},{10... | collective-permute-start | bytes 393224 | tf_op jit(solution)/shard_map/ppermute | solution.py:213
  12.7 7.4 %collective-permute-done.1.refs_2_ = bf16[256,256]{1,0:T(8,128)(2,1)S(1)} collective-permute-done((bf16[256,256]{1,0:T(8,128)(2,1)}, bf16[256,256]{1,0:T(8,128)(2,1)S(1)}, u32[]{:S(2)}, u32[]{:S(2)}) %collective-permute-start.1) | collective-permute-done | bytes 131104 | tf_op jit(solution)/shard_map/ppermute | solution.py:213
  21.1 4.4 %collective-permute-start.7 = (bf16[1024,256]{1,0:T(8,128)(2,1)S(1)}, bf16[1024,256]{1,0:T(8,128)(2,1)S(1)}, u32[]{:S(2)}, u32[]{:S(2)}) collective-permute-start(bf16[1024,256]{1,0:T(8,128)(2,1)S(1)} %shard_map.150.refs_0_), channel_id=1, source_target_pairs={{0,1},{1,2},{2,3},{3,4},{4,5},{5,6},{6,7},{7,0},{8,9},{9,10},{10,1... | collective-permute-start | bytes 1572872 | tf_op jit(solution)/shard_map/ppermute | solution.py:213
  25.5 8.6 %collective-permute-start.3 = (bf16[1024,256]{1,0:T(8,128)(2,1)S(1)}, bf16[1024,256]{1,0:T(8,128)(2,1)S(1)}, u32[]{:S(2)}, u32[]{:S(2)}) collective-permute-start(bf16[1024,256]{1,0:T(8,128)(2,1)S(1)} %shard_map.150.refs_0_), channel_id=1, source_target_pairs={{0,7},{1,0},{2,1},{3,2},{4,3},{5,4},{6,5},{7,6},{8,15},{9,8},{10,9... | collective-permute-start | bytes 1572872 | tf_op jit(solution)/shard_map/ppermute | solution.py:213
  34.1 2.4 %collective-permute-start.8 = (bf16[144,256]{1,0:T(8,128)(2,1)S(1)}, bf16[144,256]{1,0:T(8,128)(2,1)S(1)}, u32[]{:S(2)}, u32[]{:S(2)}) collective-permute-start(bf16[144,256]{1,0:T(8,128)(2,1)S(1)} %copy-done.15), channel_id=1, source_target_pairs={{0,24},{8,0},{16,8},{24,16},{1,25},{9,1},{17,9},{25,17},{2,26},{10... | collective-permute-start | bytes 221192 | tf_op jit(solution)/shard_map/ppermute | solution.py:213
  36.5 5.7 %collective-permute-done.8.refs_3_ = bf16[144,256]{1,0:T(8,128)(2,1)S(1)} collective-permute-done((bf16[144,256]{1,0:T(8,128)(2,1)S(1)}, bf16[144,256]{1,0:T(8,128)(2,1)S(1)}, u32[]{:S(2)}, u32[]{:S(2)}) %collective-permute-start.8) | collective-permute-done | bytes 73760 | tf_op jit(solution)/shard_map/ppermute | solution.py:213
  42.1 2.1 %collective-permute-done.7.refs_1_ = bf16[1024,256]{1,0:T(8,128)(2,1)S(1)} collective-permute-done((bf16[1024,256]{1,0:T(8,128)(2,1)S(1)}, bf16[1024,256]{1,0:T(8,128)(2,1)S(1)}, u32[]{:S(2)}, u32[]{:S(2)}) %collective-permute-start.7) | collective-permute-done | bytes 524320 | tf_op jit(solution)/shard_map/ppermute | solution.py:213
  44.2 1.9 %collective-permute-start.9 = (bf16[1024,256]{1,0:T(8,128)(2,1)S(1)}, bf16[1024,256]{1,0:T(8,128)(2,1)S(1)}, u32[]{:S(2)}, u32[]{:S(2)}) collective-permute-start(bf16[1024,256]{1,0:T(8,128)(2,1)S(1)} %collective-permute-done.7.refs_1_), channel_id=1, source_target_pairs={{0,1},{1,2},{2,3},{3,4},{4,5},{5,6},{6,7},{7,0},{8,9},{9,10},{10,1... | collective-permute-start | bytes 1572872 | tf_op jit(solution)/shard_map/ppermute | solution.py:213
  46.2 2.3 %collective-permute-start.4 = (bf16[144,256]{1,0:T(8,128)(2,1)S(1)}, bf16[144,256]{1,0:T(8,128)(2,1)S(1)}, u32[]{:S(2)}, u32[]{:S(2)}) collective-permute-start(bf16[144,256]{1,0:T(8,128)(2,1)S(1)} %copy-done.14), channel_id=1, source_target_pairs={{0,8},{8,16},{16,24},{24,0},{1,9},{9,17},{17,25},{25,1},{2,10},{10... | collective-permute-start | bytes 221192 | tf_op jit(solution)/shard_map/ppermute | solution.py:213
  48.5 3.9 %collective-permute-done.4.refs_1_ = bf16[144,256]{1,0:T(8,128)(2,1)S(1)} collective-permute-done((bf16[144,256]{1,0:T(8,128)(2,1)S(1)}, bf16[144,256]{1,0:T(8,128)(2,1)S(1)}, u32[]{:S(2)}, u32[]{:S(2)}) %collective-permute-start.4) | collective-permute-done | bytes 73760 | tf_op jit(solution)/shard_map/ppermute | solution.py:213
  52.4 5.1 %collective-permute-start.5 = (bf16[1024,256]{1,0:T(8,128)(2,1)S(1)}, bf16[1024,256]{1,0:T(8,128)(2,1)S(1)}, u32[]{:S(2)}, u32[]{:S(2)}) collective-permute-start(bf16[1024,256]{1,0:T(8,128)(2,1)S(1)} %collective-permute-done.3.refs_2_), channel_id=1, source_target_pairs={{0,7},{1,0},{2,1},{3,2},{4,3},{5,4},{6,5},{7,6},{8,15},{9,8},{10,9... | collective-permute-start | bytes 1572872 | tf_op jit(solution)/shard_map/ppermute | solution.py:213
  57.6 3.1 %collective-permute-done.9.refs_3_ = bf16[1024,256]{1,0:T(8,128)(2,1)S(1)} collective-permute-done((bf16[1024,256]{1,0:T(8,128)(2,1)S(1)}, bf16[1024,256]{1,0:T(8,128)(2,1)S(1)}, u32[]{:S(2)}, u32[]{:S(2)}) %collective-permute-start.9) | collective-permute-done | bytes 524320 | tf_op jit(solution)/shard_map/ppermute | solution.py:213
  62.6 4.2 %collective-permute-start.6 = (bf16[144,256]{1,0:T(8,128)(2,1)S(1)}, bf16[144,256]{1,0:T(8,128)(2,1)S(1)}, u32[]{:S(2)}, u32[]{:S(2)}) collective-permute-start(bf16[144,256]{1,0:T(8,128)(2,1)S(1)} %copy-done.13), channel_id=1, source_target_pairs={{0,16},{8,24},{16,0},{24,8},{1,17},{9,25},{17,1},{25,9},{2,18},{10... | collective-permute-start | bytes 221192 | tf_op jit(solution)/shard_map/ppermute | solution.py:213
  66.8 3.6 %collective-permute-done.6.refs_2_ = bf16[144,256]{1,0:T(8,128)(2,1)S(1)} collective-permute-done((bf16[144,256]{1,0:T(8,128)(2,1)S(1)}, bf16[144,256]{1,0:T(8,128)(2,1)S(1)}, u32[]{:S(2)}, u32[]{:S(2)}) %collective-permute-start.6) | collective-permute-done | bytes 73760 | tf_op jit(solution)/shard_map/ppermute | solution.py:213
  70.4 5.1 %collective-permute-start.12 = (bf16[1024,256]{1,0:T(8,128)(2,1)S(1)}, bf16[1024,256]{1,0:T(8,128)(2,1)}, u32[]{:S(2)}, u32[]{:S(2)}) collective-permute-start(bf16[1024,256]{1,0:T(8,128)(2,1)S(1)} %collective-permute-done.5.refs_4_), channel_id=1, source_target_pairs={{0,7},{1,0},{2,1},{3,2},{4,3},{5,4},{6,5},{7,6},{8,15},{9,8},{10,9... | collective-permute-start | bytes 1572872 | tf_op jit(solution)/shard_map/ppermute | solution.py:213
  76.1 1.9 %collective-permute-start.11 = (bf16[1024,256]{1,0:T(8,128)(2,1)S(1)}, bf16[1024,256]{1,0:T(8,128)(2,1)}, u32[]{:S(2)}, u32[]{:S(2)}) collective-permute-start(bf16[1024,256]{1,0:T(8,128)(2,1)S(1)} %collective-permute-done.10.refs_0_), channel_id=1, source_target_pairs={{0,1},{1,2},{2,3},{3,4},{4,5},{5,6},{6,7},{7,0},{8,9},{9,10},{10,1... | collective-permute-start | bytes 1572872 | tf_op jit(solution)/shard_map/ppermute | solution.py:213
  79.1 5.8 %attend.3.refs_2_ = f32[1152,128]{1,0:T(8,128)S(1)} custom-call(s32[5]{0:T(128)S(1)} %pad_add_fusion.info_ref, bf16[1152,128]{1,0:T(8,128)(2,1)S(1)} %shard_map.151.qs, s32[128,1]{1,0:T(8,128)S(1)} %reshape.22.user_ref, bf16[1024,256]{1,0:T(8,128)(2,1)S(1)} %shard_map.150.refs_0_, bf16[1024,256]{1,0:T(8,128)(2,1)S(1)} %collective-permute-done.7.refs_1_, ...), custom_call_target="tpu_custom_call" | custom-call | flops 3019898880 | bytes 1048576 | tf_op jit(solution)/shard_map/attend/pallas_call | solution.py:164
  84.9 2.9 %attend.4.refs_1_ = f32[1152,128]{1,0:T(8,128)S(1)} custom-call(s32[5]{0:T(128)S(1)} %pad_add_fusion.info_ref, bf16[1152,128]{1,0:T(8,128)(2,1)S(1)} %shard_map.151.qs, s32[128,1]{1,0:T(8,128)S(1)} %reshape.22.user_ref, bf16[1024,256]{1,0:T(8,128)(2,1)S(1)} %collective-permute-done.10.refs_0_, bf16[1024,256]{1,0:T(8,128)(2,1)} %collective-permute-done.12.refs_1_, ...), custom_call_target="tpu_custom_call" | custom-call | flops 1207959552 | bytes 1048576 | tf_op jit(solution)/shard_map/attend/pallas_call | solution.py:164
  87.9 2.9 %collective-permute-done.11.refs_0_ = bf16[1024,256]{1,0:T(8,128)(2,1)} collective-permute-done((bf16[1024,256]{1,0:T(8,128)(2,1)S(1)}, bf16[1024,256]{1,0:T(8,128)(2,1)}, u32[]{:S(2)}, u32[]{:S(2)}) %collective-permute-start.11) | collective-permute-done | bytes 524320 | tf_op jit(solution)/shard_map/ppermute | solution.py:213
  90.8 2.1 %attend.5 = bf16[576,256]{1,0:T(8,128)(2,1)S(1)} custom-call(s32[5]{0:T(128)S(1)} %pad_add_fusion.info_ref, bf16[1152,128]{1,0:T(8,128)(2,1)S(1)} %shard_map.151.qs, s32[128,1]{1,0:T(8,128)S(1)} %reshape.22.user_ref, bf16[1024,256]{1,0:T(8,128)(2,1)} %collective-permute-done.11.refs_0_, f32[1152,128]{1,0:T(8,128)S(1)} %attend.4.refs_1_), custom_call_target="tpu_custom_call" | custom-call | flops 603979776 | bytes 1048576 | tf_op jit(solution)/shard_map/attend/pallas_call | solution.py:164
  93.0 10.3 %all_to_all.11 = bf16[4,144,256]{2,1,0:T(8,128)(2,1)S(1)} all-to-all(bf16[4,144,256]{2,1,0:T(8,128)(2,1)S(1)} %bitcast.5), channel_id=1, replica_groups=mesh['batch'=16,'y'=4,'z'=8] {'y'}, dimensions={0} | all-to-all | bytes 589824 | tf_op jit(solution)/shard_map/all_to_all | solution.py:243
  (46 shorter events, 6.0 us)
Async XLA Ops:
  2.8 9.9 %collective-permute-start = (bf16[256,256]{1,0:T(8,128)(2,1)}, bf16[256,256]{1,0:T(8,128)(2,1)S(1)}, u32[]{:S(2)}, u32[]{:S(2)}) collective-permute-start(bf16[256,256]{1,0:T(8,128)(2,1)} %get-tuple-element.18), channel_id=1, source_target_pairs={{0,8},{8,16},{16,24},{24,0},{1,9},{9,17},{17,25},{25,1},{2,10},{10... | collective-permute-start | bytes 393224 | tf_op jit(solution)/shard_map/ppermute | solution.py:213
  7.6 12.5 %collective-permute-start.1 = (bf16[256,256]{1,0:T(8,128)(2,1)}, bf16[256,256]{1,0:T(8,128)(2,1)S(1)}, u32[]{:S(2)}, u32[]{:S(2)}) collective-permute-start(bf16[256,256]{1,0:T(8,128)(2,1)} %get-tuple-element.19), channel_id=1, source_target_pairs={{0,16},{8,24},{16,0},{24,8},{1,17},{9,25},{17,1},{25,9},{2,18},{10... | collective-permute-start | bytes 393224 | tf_op jit(solution)/shard_map/ppermute | solution.py:213
  9.5 10.6 %collective-permute-start.2 = (bf16[256,256]{1,0:T(8,128)(2,1)}, bf16[256,256]{1,0:T(8,128)(2,1)S(1)}, u32[]{:S(2)}, u32[]{:S(2)}) collective-permute-start(bf16[256,256]{1,0:T(8,128)(2,1)} %get-tuple-element.20), channel_id=1, source_target_pairs={{0,24},{8,0},{16,8},{24,16},{1,25},{9,1},{17,9},{25,17},{2,26},{10... | collective-permute-start | bytes 393224 | tf_op jit(solution)/shard_map/ppermute | solution.py:213
  21.0 13.1 %copy-start.15 = (bf16[144,256]{1,0:T(8,128)(2,1)S(1)}, bf16[144,256]{1,0:T(8,128)(2,1)}, u32[]{:S(2)}) copy-start(bf16[144,256]{1,0:T(8,128)(2,1)} %get-tuple-element.26) | copy-start | bytes 221188
  21.0 25.2 %copy-start.14 = (bf16[144,256]{1,0:T(8,128)(2,1)S(1)}, bf16[144,256]{1,0:T(8,128)(2,1)}, u32[]{:S(2)}) copy-start(bf16[144,256]{1,0:T(8,128)(2,1)} %get-tuple-element.21) | copy-start | bytes 221188
  21.0 41.6 %copy-start.13 = (bf16[144,256]{1,0:T(8,128)(2,1)S(1)}, bf16[144,256]{1,0:T(8,128)(2,1)}, u32[]{:S(2)}) copy-start(bf16[144,256]{1,0:T(8,128)(2,1)} %get-tuple-element.24) | copy-start | bytes 221188
  21.0 57.1 %copy-start.10 = (s32[1024]{0:T(1024)S(1)}, s32[1024]{0:T(1024)}, u32[]{:S(2)}) copy-start(s32[1024]{0:T(1024)} %param.24) | copy-start | bytes 12292
  21.1 58.0 %copy-start.5 = (bf16[144,256]{1,0:T(8,128)(2,1)S(1)}, bf16[144,256]{1,0:T(8,128)(2,1)}, u32[]{:S(2)}) copy-start(bf16[144,256]{1,0:T(8,128)(2,1)} %get-tuple-element.16.refs_0_) | copy-start | bytes 221188
  21.1 23.2 %collective-permute-start.7 = (bf16[1024,256]{1,0:T(8,128)(2,1)S(1)}, bf16[1024,256]{1,0:T(8,128)(2,1)S(1)}, u32[]{:S(2)}, u32[]{:S(2)}) collective-permute-start(bf16[1024,256]{1,0:T(8,128)(2,1)S(1)} %shard_map.150.refs_0_), channel_id=1, source_target_pairs={{0,1},{1,2},{2,3},{3,4},{4,5},{5,6},{6,7},{7,0},{8,9},{9,10},{10,1... | collective-permute-start | bytes 1572872 | tf_op jit(solution)/shard_map/ppermute | solution.py:213
  25.5 26.9 %collective-permute-start.3 = (bf16[1024,256]{1,0:T(8,128)(2,1)S(1)}, bf16[1024,256]{1,0:T(8,128)(2,1)S(1)}, u32[]{:S(2)}, u32[]{:S(2)}) collective-permute-start(bf16[1024,256]{1,0:T(8,128)(2,1)S(1)} %shard_map.150.refs_0_), channel_id=1, source_target_pairs={{0,7},{1,0},{2,1},{3,2},{4,3},{5,4},{6,5},{7,6},{8,15},{9,8},{10,9... | collective-permute-start | bytes 1572872 | tf_op jit(solution)/shard_map/ppermute | solution.py:213
  34.1 8.0 %collective-permute-start.8 = (bf16[144,256]{1,0:T(8,128)(2,1)S(1)}, bf16[144,256]{1,0:T(8,128)(2,1)S(1)}, u32[]{:S(2)}, u32[]{:S(2)}) collective-permute-start(bf16[144,256]{1,0:T(8,128)(2,1)S(1)} %copy-done.15), channel_id=1, source_target_pairs={{0,24},{8,0},{16,8},{24,16},{1,25},{9,1},{17,9},{25,17},{2,26},{10... | collective-permute-start | bytes 221192 | tf_op jit(solution)/shard_map/ppermute | solution.py:213
  44.2 16.4 %collective-permute-start.9 = (bf16[1024,256]{1,0:T(8,128)(2,1)S(1)}, bf16[1024,256]{1,0:T(8,128)(2,1)S(1)}, u32[]{:S(2)}, u32[]{:S(2)}) collective-permute-start(bf16[1024,256]{1,0:T(8,128)(2,1)S(1)} %collective-permute-done.7.refs_1_), channel_id=1, source_target_pairs={{0,1},{1,2},{2,3},{3,4},{4,5},{5,6},{6,7},{7,0},{8,9},{9,10},{10,1... | collective-permute-start | bytes 1572872 | tf_op jit(solution)/shard_map/ppermute | solution.py:213
  46.2 6.2 %collective-permute-start.4 = (bf16[144,256]{1,0:T(8,128)(2,1)S(1)}, bf16[144,256]{1,0:T(8,128)(2,1)S(1)}, u32[]{:S(2)}, u32[]{:S(2)}) collective-permute-start(bf16[144,256]{1,0:T(8,128)(2,1)S(1)} %copy-done.14), channel_id=1, source_target_pairs={{0,8},{8,16},{16,24},{24,0},{1,9},{9,17},{17,25},{25,1},{2,10},{10... | collective-permute-start | bytes 221192 | tf_op jit(solution)/shard_map/ppermute | solution.py:213
  52.4 18.0 %collective-permute-start.5 = (bf16[1024,256]{1,0:T(8,128)(2,1)S(1)}, bf16[1024,256]{1,0:T(8,128)(2,1)S(1)}, u32[]{:S(2)}, u32[]{:S(2)}) collective-permute-start(bf16[1024,256]{1,0:T(8,128)(2,1)S(1)} %collective-permute-done.3.refs_2_), channel_id=1, source_target_pairs={{0,7},{1,0},{2,1},{3,2},{4,3},{5,4},{6,5},{7,6},{8,15},{9,8},{10,9... | collective-permute-start | bytes 1572872 | tf_op jit(solution)/shard_map/ppermute | solution.py:213
  60.7 15.5 %collective-permute-start.10 = (bf16[1024,256]{1,0:T(8,128)(2,1)S(1)}, bf16[1024,256]{1,0:T(8,128)(2,1)S(1)}, u32[]{:S(2)}, u32[]{:S(2)}) collective-permute-start(bf16[1024,256]{1,0:T(8,128)(2,1)S(1)} %collective-permute-done.9.refs_3_), channel_id=1, source_target_pairs={{0,1},{1,2},{2,3},{3,4},{4,5},{5,6},{6,7},{7,0},{8,9},{9,10},{10,1... | collective-permute-start | bytes 1572872 | tf_op jit(solution)/shard_map/ppermute | solution.py:213
  62.6 7.8 %collective-permute-start.6 = (bf16[144,256]{1,0:T(8,128)(2,1)S(1)}, bf16[144,256]{1,0:T(8,128)(2,1)S(1)}, u32[]{:S(2)}, u32[]{:S(2)}) collective-permute-start(bf16[144,256]{1,0:T(8,128)(2,1)S(1)} %copy-done.13), channel_id=1, source_target_pairs={{0,16},{8,24},{16,0},{24,8},{1,17},{9,25},{17,1},{25,9},{2,18},{10... | collective-permute-start | bytes 221192 | tf_op jit(solution)/shard_map/ppermute | solution.py:213
  70.4 14.5 %collective-permute-start.12 = (bf16[1024,256]{1,0:T(8,128)(2,1)S(1)}, bf16[1024,256]{1,0:T(8,128)(2,1)}, u32[]{:S(2)}, u32[]{:S(2)}) collective-permute-start(bf16[1024,256]{1,0:T(8,128)(2,1)S(1)} %collective-permute-done.5.refs_4_), channel_id=1, source_target_pairs={{0,7},{1,0},{2,1},{3,2},{4,3},{5,4},{6,5},{7,6},{8,15},{9,8},{10,9... | collective-permute-start | bytes 1572872 | tf_op jit(solution)/shard_map/ppermute | solution.py:213
  76.1 14.7 %collective-permute-start.11 = (bf16[1024,256]{1,0:T(8,128)(2,1)S(1)}, bf16[1024,256]{1,0:T(8,128)(2,1)}, u32[]{:S(2)}, u32[]{:S(2)}) collective-permute-start(bf16[1024,256]{1,0:T(8,128)(2,1)S(1)} %collective-permute-done.10.refs_0_), channel_id=1, source_target_pairs={{0,1},{1,2},{2,3},{3,4},{4,5},{5,6},{6,7},{7,0},{8,9},{9,10},{10,1... | collective-permute-start | bytes 1572872 | tf_op jit(solution)/shard_map/ppermute | solution.py:213
  87.9 15.4 %copy-start = (bf16[512,1024]{1,0:T(8,128)(2,1)S(1)}, bf16[512,1024]{1,0:T(8,128)(2,1)}, u32[]{:S(2)}) copy-start(bf16[512,1024]{1,0:T(8,128)(2,1)} %w_ref.1) | copy-start | bytes 3145732
  90.8 12.5 %copy-start.2 = (bf16[256,512]{1,0:T(8,128)(2,1)S(1)}, bf16[256,512]{1,0:T(8,128)(2,1)}, u32[]{:S(2)}) copy-start(bf16[256,512]{1,0:T(8,128)(2,1)} %hg.1) | copy-start | bytes 786436
  90.8 12.5 %copy-start.6 = (bf16[32,1024]{1,0:T(8,128)(2,1)S(1)}, bf16[32,1024]{1,0:T(8,128)(2,1)}, u32[]{:S(2)}) copy-start(bf16[32,1024]{1,0:T(8,128)(2,1)} %cx.1) | copy-start | bytes 196612
  90.8 12.5 %copy-start.8 = (bf16[32,512]{1,0:T(8,128)(2,1)S(1)}, bf16[32,512]{1,0:T(8,128)(2,1)}, u32[]{:S(2)}) copy-start(bf16[32,512]{1,0:T(8,128)(2,1)} %cv.1) | copy-start | bytes 98308
  90.8 12.5 %copy-start.9 = (bf16[32,512]{1,0:T(8,128)(2,1)S(1)}, bf16[32,512]{1,0:T(8,128)(2,1)}, u32[]{:S(2)}) copy-start(bf16[32,512]{1,0:T(8,128)(2,1)} %cg.1) | copy-start | bytes 98308
  93.0 10.4 %copy-start.1 = (bf16[256,1024]{1,0:T(8,128)(2,1)S(1)}, bf16[256,1024]{1,0:T(8,128)(2,1)}, u32[]{:S(2)}) copy-start(bf16[256,1024]{1,0:T(8,128)(2,1)} %hx.1) | copy-start | bytes 1572868
  (5 other events, 22.9 us)
